TPU v7x, 256 devices: a whole 4x4x8 slice. The times are simulated.
256 devices in a mesh: dp: 32 (over z_hi, x, y), tensor: 8 (over z_lo, core).
Axes of the slice: x: 4, y: 4, z: 8 (z_hi: 2, z_lo: 4; z = z_hi * 4 + z_lo), core: 2. Of those that a mesh axis runs over, the one named last changes fastest.
Arguments:
- hidden: bfloat16 [1024, 8192], P('tensor'), may hold values from -6 to 6
- norm_gain: float32 [8192], replicated, may hold values from 0.1 to 1.9
- gate_pre: bfloat16 [1024, 28672], P('tensor', 'dp'), may hold values from -6 to 6
- out_grad: bfloat16 [1024, 28672], P('tensor', 'dp'), may hold values from -6 to 6
- grad_basis: bfloat16 [28672, 14336], P('dp', 'tensor'), may hold values from -0.03125 to 0.03125
- act_basis: bfloat16 [8192, 4096], P('dp'), may hold values from -0.125 to 0.125
Outputs:
- correction: float32 [14336, 4096], P('tensor', 'dp')
All inputs are finite; a program needn't handle non-finite values.
Results may differ from a plain program's by a relative error of at most 0.00091.
Values may be sent and summed in bfloat16 or wider, within the bound.
No kernel may reach another device: no remote copies, remote signals or barrier semaphores. Data moves between devices by JAX's collectives and lax.ppermute only.
A program may use at most 128 MiB of HBM per device.

v0:
```python
import jax
import jax.numpy as jnp
from jax import lax
from jax.sharding import PartitionSpec as P


def per_device(hidden, norm_gain, gate_pre, out_grad, grad_basis, act_basis):
    wide = hidden.astype(jnp.float32)
    stat = jnp.mean(wide * wide, axis=-1, keepdims=True)
    normed = (wide * lax.rsqrt(stat + 1e-05) * norm_gain).astype(jnp.bfloat16)
    width = act_basis.shape[0]
    normed_part = lax.dynamic_slice_in_dim(normed, lax.axis_index("dp") * width, width, 1)
    act_partial = jnp.dot(
        lax.all_gather(normed_part, "tensor", axis=0, tiled=True),
        act_basis,
        preferred_element_type=jnp.float32,
    )
    act_proj = lax.psum_scatter(act_partial, "dp", scatter_dimension=1, tiled=True)
    act_sq = (act_proj * act_proj).astype(jnp.bfloat16)
    up_grad = (out_grad.astype(jnp.float32) * jax.nn.silu(gate_pre.astype(jnp.float32))).astype(
        jnp.bfloat16
    )
    grad_rows = lax.all_gather(up_grad, "tensor", axis=0, tiled=True)
    all_tokens = grad_rows.shape[0]
    grad_proj = lax.psum(jnp.dot(grad_rows, grad_basis, preferred_element_type=jnp.float32), "dp")
    grad_sq = (grad_proj * grad_proj).astype(jnp.bfloat16)
    total = lax.dot_general(
        grad_sq, act_sq, (((0,), (0,)), ((), ())), preferred_element_type=jnp.float32
    )
    return total / jnp.float32(all_tokens)


def solution(mesh):
    placed = (
        P("tensor", None),
        P(),
        P("tensor", "dp"),
        P("tensor", "dp"),
        P("dp", "tensor"),
        P("dp", None),
    )
    return jax.shard_map(
        per_device, mesh=mesh, in_specs=placed, out_specs=P("tensor", "dp"), check_vma=False
    )
```

profile of v0, /device:TPU:64, one launch (start us, length us, event | category | flops | bytes accessed | tf_op | source)
XLA Modules:
  0.0 987.4 jit_solution(14064264488315452223)
XLA Ops:
  6.5 0.0 copy-start
  6.5 0.0 all-gather.2.cloned.1.call-start
  6.5 2.0 fusion.6
  8.6 0.0 all-gather.2.cloned.1.call-update
  8.6 0.0 all-reduce.2.cloned.1.call-start
  8.6 36.3 %all-gather.2.cloned.1.call-done = bf16[1024,896]{1,0:T(8,128)(2,1)} async-done(((bf16[128,896]{1,0:T(8,128)(2,1)}), bf16[1024,896]{1,0:T(8,128)(2,1)}) %all-gather.2.cloned.1.call-update) | async-done | bytes 1835024 | tf_op jit(solution)/shard_map/all_gather | solution.py:23
  45.0 0.0 copy-done
  45.0 8.5 fusion.9
  53.4 0.0 all-reduce.2.cloned.1.call-update
  53.5 0.0 reduce-scatter.2.cloned.1.call-start
  53.5 4.0 convert_element_type.25
  57.5 0.0 copy-start.1
  57.5 0.9 dynamic-slice
  58.4 2.1 multiply_reduce_fusion
  60.5 1.0 fusion.8
  61.5 19.2 %all_gather.7 = bf16[1024,256]{1,0:T(8,128)(2,1)S(1)} all-gather(bf16[128,256]{1,0:T(8,128)(2,1)S(1)} %fusion.8), channel_id=1, replica_groups=mesh['dp'=32,'tensor'=8] {'tensor'}, dimensions={0}, use_global_device_ids=true | all-gather | bytes 589824 | tf_op jit(solution)/shard_map/all_gather | solution.py:14
  80.7 0.0 copy-done.1
  80.7 8.1 fusion.10
  88.8 0.0 reduce-scatter.2.cloned.1.call-update
  88.8 465.1 %all-reduce.2.cloned.1.call-done = f32[1024,1792]{1,0:T(8,128)} async-done(((f32[1024,1792]{1,0:T(8,128)}), f32[1024,1792]{1,0:T(8,128)}) %all-reduce.2.cloned.1.call-update) | async-done | bytes 7340048 | tf_op jit(solution)/shard_map/psum | solution.py:25
  553.9 421.8 %reduce-scatter.2.cloned.1.call-done = f32[1024,128]{1,0:T(8,128)} async-done(((f32[1024,4096]{1,0:T(8,128)}), f32[1024,128]{1,0:T(8,128)}) %reduce-scatter.2.cloned.1.call-update) | async-done | bytes 524304 | tf_op jit(solution)/shard_map/reduce_scatter | solution.py:18
  975.7 5.2 fusion.1
  (1 shorter events, 0.0 us)
Async XLA Ops:
  6.5 38.4 %copy-start = (bf16[896,1792]{1,0:T(8,128)(2,1)S(1)}, bf16[896,1792]{1,0:T(8,128)(2,1)}, u32[]{:S(2)}) copy-start(bf16[896,1792]{1,0:T(8,128)(2,1)} %param.10) | copy-start | bytes 9633796
  6.5 38.4 %all-gather.2.cloned.1.call-start = ((), (), s32[]{:S(2)}) async-start(), calls=%async_computation.1 | async-start | bytes 2064384 | tf_op jit(solution)/shard_map/all_gather | solution.py:23
  8.6 545.3 %all-reduce.2.cloned.1.call-start = ((), (), s32[]{:S(2)}) async-start(), calls=%async_computation.2 | async-start | bytes 14680064 | tf_op jit(solution)/shard_map/psum | solution.py:25
  53.5 922.2 %reduce-scatter.2.cloned.1.call-start = ((), (), s32[]{:S(2)}) async-start(), calls=%async_computation.3 | async-start | bytes 17301504 | tf_op jit(solution)/shard_map/reduce_scatter | solution.py:18
  57.5 23.2 %copy-start.1 = (bf16[256,4096]{1,0:T(8,128)(2,1)S(1)}, bf16[256,4096]{1,0:T(8,128)(2,1)}, u32[]{:S(2)}) copy-start(bf16[256,4096]{1,0:T(8,128)(2,1)} %param.11) | copy-start | bytes 6291460
Sparse Core Ops, SparseCore 0:
  9.1 35.7 all-gather.1
  53.6 500.2 all-reduce.1
  556.4 419.1 reduce-scatter.1
where the time goes:
time: 988 us; the launch traced here: 987 us
  waiting for transfers between devices  923 us (93%)
  matrix products  21.8 us (2%)
  blocking collectives  19.2 us (2%)
  between operations  13.1 us (1%)
    psum x1, waiting for transfers between devices, per_device(): lax.psum(jnp.dot(grad_rows, grad_basis, preferred_element_type=jnp.float3...  465 us
    reduce_scatter x1, waiting for transfers between devices, per_device(): lax.psum_scatter(act_partial, 'dp', scatter_dimension=1, tiled=True)  422 us
    all_gather x1, waiting for transfers between devices, per_device(): grad_rows = lax.all_gather(up_grad, 'tensor', axis=0, tiled=True)  36.3 us
  transfers between devices with their start and end apart: 3, of which 3 were waited for; matrix products, arithmetic and copies ran while one was open for 2% of the time, Pallas kernels for 0%

commit v1 on v0

v1 whole, which is shorter than its diff:
```python
import jax
import jax.numpy as jnp
from jax import lax
from jax.sharding import Mesh
from jax.sharding import PartitionSpec as P

AXES = ("z_hi", "x", "y", "z_lo", "core")
SIZES = (2, 4, 4, 4, 2)
DP = ("z_hi", "x", "y")
TENSOR = ("z_lo", "core")


def shifted(value, axis, step):
    size = SIZES[AXES.index(axis)]
    return lax.ppermute(value, axis, [(i, (i + step) % size) for i in range(size)])


def act_squares(hidden, norm_gain, act_basis):
    wide = hidden.astype(jnp.float32)
    stat = jnp.mean(wide * wide, axis=-1, keepdims=True)
    width = act_basis.shape[0]
    start = lax.axis_index(DP) * width
    part = lax.dynamic_slice_in_dim(hidden, start, width, 1).astype(jnp.float32)
    gain = lax.dynamic_slice_in_dim(norm_gain, start, width, 0)
    normed = (part * lax.rsqrt(stat + 1e-05) * gain).astype(jnp.bfloat16)
    partial = jnp.dot(normed, act_basis, preferred_element_type=jnp.float32).astype(jnp.bfloat16)
    tokens, columns = partial.shape
    block = columns // 32
    pieces = partial.reshape(tokens, 2, 4, 4, block).transpose(3, 2, 0, 1, 4)
    pieces = pieces.reshape(16, tokens, 2 * block)
    got = lax.all_to_all(pieces, ("y", "x"), 0, 0, tiled=True)
    summed = jnp.sum(got.astype(jnp.float32), axis=0).reshape(tokens, 2, block)
    z_hi = lax.axis_index("z_hi")
    kept = lax.dynamic_index_in_dim(summed, z_hi, 1, keepdims=False)
    given = lax.dynamic_index_in_dim(summed, 1 - z_hi, 1, keepdims=False)
    total = kept + shifted(given.astype(jnp.bfloat16), "z_hi", 1).astype(jnp.float32)
    square = (total * total).astype(jnp.bfloat16)
    spread = lax.all_gather(square, ("x",) + TENSOR, axis=0, tiled=False)
    return spread.reshape(4, 4, 2 * tokens, block)


def per_device(hidden, norm_gain, gate_pre, out_grad, grad_basis, act_basis):
    up_grad = (out_grad.astype(jnp.float32) * jax.nn.silu(gate_pre.astype(jnp.float32))).astype(
        jnp.bfloat16
    )
    moved = [up_grad] + [shifted(up_grad, "z_lo", step) for step in (1, 2, 3)]
    act_sq = act_squares(hidden, norm_gain, act_basis)
    first = lax.axis_index("core") == 0
    partials = []
    for own in moved:
        other = shifted(own, "core", 1)
        rows = jnp.concatenate(
            [jnp.where(first, own, other), jnp.where(first, other, own)], axis=0
        )
        partials.append(
            lax.dot_general(
                grad_basis, rows, (((0,), (1,)), ((), ())), preferred_element_type=jnp.float32
            ).astype(jnp.bfloat16)
        )
    columns, quarter = partials[0].shape
    pieces = jnp.concatenate(partials, axis=0).reshape(16, columns // 4, quarter)
    got = lax.all_to_all(pieces, ("y", "x"), 0, 0, tiled=True)
    summed = jnp.sum(got.astype(jnp.float32), axis=0)
    total = summed + shifted(summed.astype(jnp.bfloat16), "z_hi", 1).astype(jnp.float32)
    square = (total * total).astype(jnp.bfloat16)
    grad_sq = lax.all_to_all(
        jnp.broadcast_to(square[None], (4,) + square.shape), "y", 0, 0, tiled=True
    )
    z_lo = lax.axis_index("z_lo")
    act_by_step = jnp.stack(
        [
            lax.dynamic_index_in_dim(act_sq, lax.rem(z_lo + 4 - step, 4), 1, keepdims=False)
            for step in range(4)
        ]
    )
    out = jnp.einsum("snt,sxtm->xnm", grad_sq, act_by_step, preferred_element_type=jnp.float32)
    out = out / jnp.float32(4 * quarter)
    out = lax.all_to_all(out, "x", 0, 0, tiled=True)
    return out.reshape(columns, -1)


def solution(mesh):
    fine = Mesh(mesh.devices.reshape(SIZES), AXES)
    placed = (
        P(TENSOR, None),
        P(),
        P(TENSOR, DP),
        P(TENSOR, DP),
        P(DP, TENSOR),
        P(DP, None),
    )
    return jax.shard_map(
        per_device, mesh=fine, in_specs=placed, out_specs=P(TENSOR, DP), check_vma=False
    )
```

time: 988 us -> 178 us (0.18)
  the two profiles are of different devices: /device:TPU:64 before, /device:TPU:32 now
where the time goes in v1:
time: 178 us; the launch traced here: 177 us
  waiting for transfers between devices  73.9 us (42%)
  starting transfers between devices  34.1 us (19%)
  local copies, waits for them, and re-layouts  16.2 us (9%)
  blocking collectives  15.7 us (9%)
  other arithmetic  14.1 us (8%)
  between operations  13.6 us (8%)
  matrix products  9.67 us (5%)
    all_to_all x1, waiting for transfers between devices, per_device(): got = lax.all_to_all(pieces, ('y', 'x'), 0, 0, tiled=True)  47.7 us
    ppermute x9, starting transfers between devices, shifted(): lax.ppermute(value, axis, [(i, (i + step) % size) for i in range(size)])  17 us
    all_to_all x1, blocking collectives, per_device(): out = lax.all_to_all(out, 'x', 0, 0, tiled=True)  15.7 us
    ppermute x9, waiting for transfers between devices, shifted(): lax.ppermute(value, axis, [(i, (i + step) % size) for i in range(size)])  12.7 us
    all_to_all x1, waiting for transfers between devices, per_device(): lax.all_to_all(jnp.broadcast_to(square[None], (4,) + square.shape), 'y',...  12 us
    all_to_all x1, starting transfers between devices, act_squares(): got = lax.all_to_all(pieces, ('y', 'x'), 0, 0, tiled=True)  7.09 us
    concatenate x1, local copies, waits for them, and re-layouts, per_device(): jnp.concatenate(partials, axis=0).reshape(16, columns // 4, quarter)  5.92 us
    all_to_all x1, starting transfers between devices, per_device(): got = lax.all_to_all(pieces, ('y', 'x'), 0, 0, tiled=True)  5.73 us
  transfers between devices with their start and end apart: 13, of which 5 were waited for; matrix products, arithmetic and copies ran while one was open for 20% of the time, Pallas kernels for 0%

profile of v1, /device:TPU:32, one launch (start us, length us, event | category | flops | bytes accessed | tf_op | source)
XLA Modules:
  0.0 177.3 jit_solution(13959246452012191315)
XLA Ops:
  6.5 1.3 fusion.30
  7.9 2.0 %collective-permute-start.2 = (bf16[128,896]{1,0:T(8,128)(2,1)S(1)}, bf16[128,896]{1,0:T(8,128)(2,1)}, u32[]{:S(2)}, u32[]{:S(2)}) collective-permute-start(bf16[128,896]{1,0:T(8,128)(2,1)S(1)} %fusion.30), channel_id=1, source_target_pairs={{0,2},{2,4},{4,6},{6,0},{1,3},{3,5},{5,7},{7,1},{8,10},{10,12},{12... | collective-permute-start | bytes 688136 | tf_op jit(solution)/shard_map/ppermute | solution.py:15
  9.9 2.3 %collective-permute-start.4 = (bf16[128,896]{1,0:T(8,128)(2,1)S(1)}, bf16[128,896]{1,0:T(8,128)(2,1)}, u32[]{:S(2)}, u32[]{:S(2)}) collective-permute-start(bf16[128,896]{1,0:T(8,128)(2,1)S(1)} %fusion.30), channel_id=1, source_target_pairs={{0,4},{2,6},{4,0},{6,2},{1,5},{3,7},{5,1},{7,3},{8,12},{10,14},{12... | collective-permute-start | bytes 688136 | tf_op jit(solution)/shard_map/ppermute | solution.py:15
  12.2 1.1 collective-permute-start.6
  13.3 2.1 %multiply_reduce_fusion = f32[128]{0:T(128)S(1)} fusion(bf16[128,8192]{1,0:T(8,128)(2,1)} %param.6), kind=kLoop, calls=%fused_computation.2 | loop fusion | flops 3145600 | bytes 2097664 | tf_op jit(solution)/shard_map/reduce_sum | solution.py:20
  16.1 3.1 %convolution_convert_fusion = bf16[128,4096]{1,0:T(8,128)(2,1)} fusion(bf16[256,4096]{1,0:T(8,128)(2,1)} %param.11, f32[256]{0:T(256)S(1)} %dynamic_slice.27, f32[128]{0:T(128)S(1)} %add_rsqrt_fusion, bf16[128,8192]{1,0:T(8,128)(2,1)} %param.6, s32[]{:T(128)S(6)} %select_n.60), kind=kOutput, calls=%fused_computation.1 | convolution fusion | flops 269090816 | bytes 3212804 | tf_op jit(solution)/shard_map/dot_general | solution.py:26
  19.2 2.6 %reshape.33 = bf16[128,2,4,4,128]{4,3,2,1,0:T(4,128)(2,1)} reshape(bf16[128,4096]{1,0:T(8,128)(2,1)} %convolution_convert_fusion) | data formatting | bytes 2097152 | tf_op jit(solution)/shard_map/reshape | solution.py:29
  21.8 2.7 %copy.12 = bf16[128,2,4,4,128]{0,4,1,2,3:T(8,128)(2,1)} copy(bf16[128,2,4,4,128]{4,3,2,1,0:T(4,128)(2,1)} %reshape.33) | data formatting | bytes 2097152 | tf_op jit(solution)/shard_map/reshape | solution.py:29
  24.5 7.1 %all-to-all-start = ((bf16[16,128,256]{1,2,0:T(8,128)(2,1)}), bf16[16,128,256]{1,2,0:T(8,128)(2,1)}, u32[]{:S(2)}, u32[]{:S(2)}) async-start(bf16[16,128,256]{1,2,0:T(8,128)(2,1)} %bitcast.48), calls=%async_computation | async-start | bytes 2097152 | tf_op jit(solution)/shard_map/all_to_all | solution.py:31
  33.5 1.1 fusion
  34.6 1.0 broadcast_select_fusion.5
  35.6 1.1 fusion.1
  36.8 1.0 broadcast_select_fusion.3
  37.7 1.1 fusion.2
  38.9 1.0 broadcast_select_fusion.1
  39.9 1.1 fusion.3
  41.0 2.1 %pad_maximum_fusion = bf16[7168,256]{0,1:T(8,128)(2,1)} fusion(bf16[1792,256]{0,1:T(8,128)(2,1)S(1)} %fusion.3, bf16[1792,256]{0,1:T(8,128)(2,1)S(1)} %fusion.2, bf16[1792,256]{0,1:T(8,128)(2,1)S(1)} %fusion.1, bf16[1792,256]{0,1:T(8,128)(2,1)S(1)} %fusion), kind=kLoop, calls=%fused_computation.3 | loop fusion | flops 14680064 | bytes 7340032 | tf_op jit(solution)/shard_map/concatenate | solution.py:61
  43.1 5.9 %copy.15 = bf16[7168,256]{1,0:T(8,128)(2,1)} copy(bf16[7168,256]{0,1:T(8,128)(2,1)} %pad_maximum_fusion) | data formatting | bytes 7340032 | tf_op jit(solution)/shard_map/concatenate | solution.py:61
  49.0 1.4 all-to-all-done
  50.4 5.7 %all-to-all-start.1 = ((bf16[16,448,256]{2,1,0:T(8,128)(2,1)}), bf16[16,448,256]{2,1,0:T(8,128)(2,1)}, u32[]{:S(2)}, u32[]{:S(2)}) async-start(bf16[16,448,256]{2,1,0:T(8,128)(2,1)} %bitcast.47), calls=%async_computation.1 | async-start | bytes 7340032 | tf_op jit(solution)/shard_map/all_to_all | solution.py:62
  56.1 1.4 convert_reduce_fusion.1
  57.7 5.3 %collective-permute-start = (bf16[128,128]{1,0:T(8,128)(2,1)S(1)}, bf16[128,128]{1,0:T(8,128)(2,1)S(1)}, u32[]{:S(2)}, u32[]{:S(2)}) collective-permute-start(bf16[128,128]{1,0:T(8,128)(2,1)S(1)} %bitcast.53), channel_id=1, source_target_pairs={{0,128},{128,0},{1,129},{129,1},{2,130},{130,2},{3,131},{131,3},{4... | collective-permute-start | bytes 98312 | tf_op jit(solution)/shard_map/ppermute | solution.py:15
  63.1 2.5 %collective-permute-done = bf16[128,128]{1,0:T(8,128)(2,1)S(1)} collective-permute-done((bf16[128,128]{1,0:T(8,128)(2,1)S(1)}, bf16[128,128]{1,0:T(8,128)(2,1)S(1)}, u32[]{:S(2)}, u32[]{:S(2)}) %collective-permute-start) | collective-permute-done | bytes 32800 | tf_op jit(solution)/shard_map/ppermute | solution.py:15
  66.2 47.7 %all-to-all-done.1 = bf16[16,448,256]{2,1,0:T(8,128)(2,1)} async-done(((bf16[16,448,256]{2,1,0:T(8,128)(2,1)}), bf16[16,448,256]{2,1,0:T(8,128)(2,1)}, u32[]{:S(2)}, u32[]{:S(2)}) %all-to-all-start.1) | async-done | bytes 3670048 | tf_op jit(solution)/shard_map/all_to_all | solution.py:62
  114.0 2.6 %convert_reduce_fusion = f32[448,256]{1,0:T(8,128)S(1)} fusion(bf16[16,448,256]{2,1,0:T(8,128)(2,1)} %all-to-all-done.1), kind=kLoop, calls=%fused_computation | loop fusion | flops 3555328 | bytes 4128768 | tf_op jit(solution)/shard_map/reduce_sum | solution.py:63
  116.6 5.5 %collective-permute-start.8 = (bf16[448,256]{1,0:T(8,128)(2,1)S(1)}, bf16[448,256]{1,0:T(8,128)(2,1)S(1)}, u32[]{:S(2)}, u32[]{:S(2)}) collective-permute-start(bf16[448,256]{1,0:T(8,128)(2,1)S(1)} %convert_element_type.93), channel_id=1, source_target_pairs={{0,128},{128,0},{1,129},{129,1},{2,130},{130,2},{3,131},{131,3},{4... | collective-permute-start | bytes 688136 | tf_op jit(solution)/shard_map/ppermute | solution.py:15
  122.1 10.2 %collective-permute-done.8 = bf16[448,256]{1,0:T(8,128)(2,1)S(1)} collective-permute-done((bf16[448,256]{1,0:T(8,128)(2,1)S(1)}, bf16[448,256]{1,0:T(8,128)(2,1)S(1)}, u32[]{:S(2)}, u32[]{:S(2)}) %collective-permute-start.8) | collective-permute-done | bytes 229408 | tf_op jit(solution)/shard_map/ppermute | solution.py:15
  133.4 4.2 %all-to-all-start.2 = ((bf16[4,448,256]{2,1,0:T(8,128)(2,1)}), bf16[4,448,256]{2,1,0:T(8,128)(2,1)}, u32[]{:S(2)}, u32[]{:S(2)}) async-start(bf16[4,448,256]{2,1,0:T(8,128)(2,1)} %broadcast_in_dim.2), calls=%async_computation.2 | async-start | bytes 1835008 | tf_op jit(solution)/shard_map/all_to_all | solution.py:66
  137.6 2.1 %dynamic-slice_bitcast_fusion.3 = (bf16[1,4,256,128]{3,2,0,1:T(8,128)(2,1)S(1)}, bf16[1,4,256,128]{3,2,0,1:T(8,128)(2,1)}, bf16[1,4,256,128]{3,2,0,1:T(8,128)(2,1)}, bf16[1,4,256,128]{3,2,0,1:T(8,128)(2,1)}) fusion(bf16[4,4,256,128]{3,2,1,0:T(8,128)(2,1)} %bitcast.50, s32[]{:T(128)S(6)} %select_n.63, s32[]{:T(128)S(6)} %select_n.66, s32[]{:T(128)S(6)} %select_n.65, ...), kind=kLoop, calls=%fused_computation.47 | loop fusion | bytes 2097168 | tf_op jit(solution)/shard_map/stack | solution.py:70
  139.8 12.0 %all-to-all-done.2 = bf16[4,448,256]{2,1,0:T(8,128)(2,1)} async-done(((bf16[4,448,256]{2,1,0:T(8,128)(2,1)}), bf16[4,448,256]{2,1,0:T(8,128)(2,1)}, u32[]{:S(2)}, u32[]{:S(2)}) %all-to-all-start.2) | async-done | bytes 917536 | tf_op jit(solution)/shard_map/all_to_all | solution.py:66
  151.8 2.0 %fusion.5 = f32[4,448,128]{2,1,0:T(8,128)S(1)} fusion(bf16[1,4,256,128]{3,2,0,1:T(8,128)(2,1)} %get-tuple-element.6, bf16[1,4,256,128]{3,2,0,1:T(8,128)(2,1)} %get-tuple-element.7, bf16[1,4,256,128]{3,2,0,1:T(8,128)(2,1)} %get-tuple-element.8, bf16[1,4,256,128]{3,2,0,1:T(8,128)(2,1)S(1)} %get-tuple-element.5, bf16[4,448,256]{2,1,0:T(8,128)(2,1)} %all-to-all-done.2), kind=kOutput, calls=%fused_computation.15 | convolution fusion | flops 474185728 | bytes 2883584 | tf_op jit(solution)/shard_map/snt,sxtm->xnm/dot_general | solution.py:76
  153.8 15.7 %all_to_all.20 = f32[4,448,128]{2,1,0:T(8,128)S(1)} all-to-all(f32[4,448,128]{2,1,0:T(8,128)S(1)} %fusion.5), channel_id=1, replica_groups=mesh['z_hi'=2,'x'=4,'y'=4,'z_lo'=4,'core'=2] {'x'}, dimensions={0} | all-to-all | bytes 1835008 | tf_op jit(solution)/shard_map/all_to_all | solution.py:78
  (28 shorter events, 5.5 us)
Async XLA Ops:
  6.5 26.9 %copy-start = (bf16[896,1792]{1,0:T(8,128)(2,1)S(1)}, bf16[896,1792]{1,0:T(8,128)(2,1)}, u32[]{:S(2)}) copy-start(bf16[896,1792]{1,0:T(8,128)(2,1)} %param.10) | copy-start | bytes 9633796
  7.9 23.7 %collective-permute-start.2 = (bf16[128,896]{1,0:T(8,128)(2,1)S(1)}, bf16[128,896]{1,0:T(8,128)(2,1)}, u32[]{:S(2)}, u32[]{:S(2)}) collective-permute-start(bf16[128,896]{1,0:T(8,128)(2,1)S(1)} %fusion.30), channel_id=1, source_target_pairs={{0,2},{2,4},{4,6},{6,0},{1,3},{3,5},{5,7},{7,1},{8,10},{10,12},{12... | collective-permute-start | bytes 688136 | tf_op jit(solution)/shard_map/ppermute | solution.py:15
  9.9 22.1 %collective-permute-start.4 = (bf16[128,896]{1,0:T(8,128)(2,1)S(1)}, bf16[128,896]{1,0:T(8,128)(2,1)}, u32[]{:S(2)}, u32[]{:S(2)}) collective-permute-start(bf16[128,896]{1,0:T(8,128)(2,1)S(1)} %fusion.30), channel_id=1, source_target_pairs={{0,4},{2,6},{4,0},{6,2},{1,5},{3,7},{5,1},{7,3},{8,12},{10,14},{12... | collective-permute-start | bytes 688136 | tf_op jit(solution)/shard_map/ppermute | solution.py:15
  12.2 20.1 %collective-permute-start.6 = (bf16[128,896]{1,0:T(8,128)(2,1)S(1)}, bf16[128,896]{1,0:T(8,128)(2,1)}, u32[]{:S(2)}, u32[]{:S(2)}) collective-permute-start(bf16[128,896]{1,0:T(8,128)(2,1)S(1)} %fusion.30), channel_id=1, source_target_pairs={{0,6},{2,0},{4,2},{6,4},{1,7},{3,1},{5,3},{7,5},{8,14},{10,8},{12,... | collective-permute-start | bytes 688136 | tf_op jit(solution)/shard_map/ppermute | solution.py:15
  13.3 19.2 %collective-permute-start.1 = (bf16[128,896]{1,0:T(8,128)(2,1)S(1)}, bf16[128,896]{1,0:T(8,128)(2,1)}, u32[]{:S(2)}, u32[]{:S(2)}) collective-permute-start(bf16[128,896]{1,0:T(8,128)(2,1)S(1)} %fusion.30), channel_id=1, source_target_pairs={{0,1},{1,0},{2,3},{3,2},{4,5},{5,4},{6,7},{7,6},{8,9},{9,8},{10,11... | collective-permute-start | bytes 688136 | tf_op jit(solution)/shard_map/ppermute | solution.py:15
  24.5 25.9 %all-to-all-start = ((bf16[16,128,256]{1,2,0:T(8,128)(2,1)}), bf16[16,128,256]{1,2,0:T(8,128)(2,1)}, u32[]{:S(2)}, u32[]{:S(2)}) async-start(bf16[16,128,256]{1,2,0:T(8,128)(2,1)} %bitcast.48), calls=%async_computation | async-start | bytes 2097152 | tf_op jit(solution)/shard_map/all_to_all | solution.py:31
  31.6 3.0 %collective-permute-start.3 = (bf16[128,896]{1,0:T(8,128)(2,1)}, bf16[128,896]{1,0:T(8,128)(2,1)S(1)}, u32[]{:S(2)}, u32[]{:S(2)}) collective-permute-start(bf16[128,896]{1,0:T(8,128)(2,1)} %collective-permute-done.2), channel_id=1, source_target_pairs={{0,1},{1,0},{2,3},{3,2},{4,5},{5,4},{6,7},{7,6},{8,9},{9,8},{10,11... | collective-permute-start | bytes 688136 | tf_op jit(solution)/shard_map/ppermute | solution.py:15
  31.9 4.8 %collective-permute-start.5 = (bf16[128,896]{1,0:T(8,128)(2,1)}, bf16[128,896]{1,0:T(8,128)(2,1)S(1)}, u32[]{:S(2)}, u32[]{:S(2)}) collective-permute-start(bf16[128,896]{1,0:T(8,128)(2,1)} %collective-permute-done.4), channel_id=1, source_target_pairs={{0,1},{1,0},{2,3},{3,2},{4,5},{5,4},{6,7},{7,6},{8,9},{9,8},{10,11... | collective-permute-start | bytes 688136 | tf_op jit(solution)/shard_map/ppermute | solution.py:15
  32.2 6.7 %collective-permute-start.7 = (bf16[128,896]{1,0:T(8,128)(2,1)}, bf16[128,896]{1,0:T(8,128)(2,1)S(1)}, u32[]{:S(2)}, u32[]{:S(2)}) collective-permute-start(bf16[128,896]{1,0:T(8,128)(2,1)} %collective-permute-done.6), channel_id=1, source_target_pairs={{0,1},{1,0},{2,3},{3,2},{4,5},{5,4},{6,7},{7,6},{8,9},{9,8},{10,11... | collective-permute-start | bytes 688136 | tf_op jit(solution)/shard_map/ppermute | solution.py:15
  50.4 63.6 %all-to-all-start.1 = ((bf16[16,448,256]{2,1,0:T(8,128)(2,1)}), bf16[16,448,256]{2,1,0:T(8,128)(2,1)}, u32[]{:S(2)}, u32[]{:S(2)}) async-start(bf16[16,448,256]{2,1,0:T(8,128)(2,1)} %bitcast.47), calls=%async_computation.1 | async-start | bytes 7340032 | tf_op jit(solution)/shard_map/all_to_all | solution.py:62
  56.1 81.5 %all-gather.3.cloned.1.call-start = ((), (), s32[]{:S(2)}) async-start(), calls=%async_computation.4 | async-start | bytes 1081344 | tf_op jit(solution)/shard_map/all_gather | solution.py:38
  57.7 7.9 %collective-permute-start = (bf16[128,128]{1,0:T(8,128)(2,1)S(1)}, bf16[128,128]{1,0:T(8,128)(2,1)S(1)}, u32[]{:S(2)}, u32[]{:S(2)}) collective-permute-start(bf16[128,128]{1,0:T(8,128)(2,1)S(1)} %bitcast.53), channel_id=1, source_target_pairs={{0,128},{128,0},{1,129},{129,1},{2,130},{130,2},{3,131},{131,3},{4... | collective-permute-start | bytes 98312 | tf_op jit(solution)/shard_map/ppermute | solution.py:15
  116.6 15.7 %collective-permute-start.8 = (bf16[448,256]{1,0:T(8,128)(2,1)S(1)}, bf16[448,256]{1,0:T(8,128)(2,1)S(1)}, u32[]{:S(2)}, u32[]{:S(2)}) collective-permute-start(bf16[448,256]{1,0:T(8,128)(2,1)S(1)} %convert_element_type.93), channel_id=1, source_target_pairs={{0,128},{128,0},{1,129},{129,1},{2,130},{130,2},{3,131},{131,3},{4... | collective-permute-start | bytes 688136 | tf_op jit(solution)/shard_map/ppermute | solution.py:15
  133.4 18.4 %all-to-all-start.2 = ((bf16[4,448,256]{2,1,0:T(8,128)(2,1)}), bf16[4,448,256]{2,1,0:T(8,128)(2,1)}, u32[]{:S(2)}, u32[]{:S(2)}) async-start(bf16[4,448,256]{2,1,0:T(8,128)(2,1)} %broadcast_in_dim.2), calls=%async_computation.2 | async-start | bytes 1835008 | tf_op jit(solution)/shard_map/all_to_all | solution.py:66
Sparse Core Ops, SparseCore 0:
  66.3 66.8 all-gather.2

commit v2 on v1

v2 whole, which is shorter than its diff:
```python
import jax
import jax.numpy as jnp
from jax import lax
from jax.experimental import pallas as pl
from jax.experimental.pallas import tpu as pltpu
from jax.sharding import Mesh
from jax.sharding import PartitionSpec as P

AXES = ("z_hi", "x", "y", "z_lo", "core")
SIZES = (2, 4, 4, 4, 2)
DP = ("z_hi", "x", "y")
TENSOR = ("z_lo", "core")
VMEM_LIMIT = 48 * 1024 * 1024
SMEM = pl.BlockSpec(memory_space=pltpu.SMEM)
VMEM = pl.BlockSpec(memory_space=pltpu.VMEM)


def shifted(value, axis, step):
    size = SIZES[AXES.index(axis)]
    return lax.ppermute(value, axis, [(i, (i + step) % size) for i in range(size)])


def act_kernel(place, hidden, gain, basis, out):
    tokens, features = hidden.shape
    depth = basis.shape[0]
    squares = jnp.zeros((tokens, 128), jnp.float32)
    for at in range(0, features, 128):
        wide = hidden[:, at : at + 128].astype(jnp.float32)
        squares += wide * wide
    stat = jnp.sum(squares, axis=-1, keepdims=True) / features
    mine = pl.ds(pl.multiple_of(place[0] * depth, depth), depth)
    scaled = hidden[:, mine].astype(jnp.float32) * lax.rsqrt(stat + 1e-05)
    normed = (scaled * gain[:, mine]).astype(jnp.bfloat16)
    block = out.shape[2] // 2
    for z_hi in range(2):
        for x in range(4):
            at = (z_hi * 16 + x * 4) * block
            part = jnp.dot(
                normed, basis[:, at : at + 4 * block], preferred_element_type=jnp.float32
            )
            for y in range(4):
                out[x * 4 + y, :, z_hi * block : (z_hi + 1) * block] = part[
                    :, y * block : (y + 1) * block
                ].astype(jnp.bfloat16)


def grad_kernel(*refs):
    *rows, basis, out = refs
    together = jnp.concatenate([part[...] for part in rows], axis=0)
    for at in range(0, basis.shape[1], 256):
        part = jnp.dot(together, basis[:, at : at + 256], preferred_element_type=jnp.float32)
        out[at : at + 256, :] = part.T.astype(jnp.bfloat16)


def correct_kernel(steps, tokens, *refs):
    place, grad_sq, act_sq, *before, out, act = refs
    block = act_sq.shape[3]
    at = 0
    for step in steps:
        chip = lax.rem(place[0] + 4 - step, 4)
        for flip in range(2):
            core = lax.rem(place[1] + flip, 2)
            for x in range(4):
                act[at : at + block, x * 128 : (x + 1) * 128] = act_sq[chip, core, x]
            at += block
    rows = grad_sq.shape[1]
    for y in range(4):
        part = jnp.dot(grad_sq[y], act[...], preferred_element_type=jnp.float32)
        part = part * (1.0 / tokens)
        for x in range(4):
            here = part[:, x * 128 : (x + 1) * 128]
            if before:
                here = before[0][x, y * rows : (y + 1) * rows, :] + here
            out[x, y * rows : (y + 1) * rows, :] = here


def act_squares(hidden, norm_gain, act_basis):
    tokens = hidden.shape[0]
    columns = act_basis.shape[1]
    block = columns // 32
    place = lax.axis_index(DP).astype(jnp.int32).reshape(1)
    pieces = pl.pallas_call(
        act_kernel,
        out_shape=jax.ShapeDtypeStruct((16, tokens, 2 * block), jnp.bfloat16),
        in_specs=[SMEM, VMEM, VMEM, VMEM],
        out_specs=VMEM,
        compiler_params=pltpu.CompilerParams(vmem_limit_bytes=VMEM_LIMIT),
        name="act",
    )(place, hidden, norm_gain.reshape(1, -1), act_basis)
    got = lax.all_to_all(pieces, ("x", "y"), 0, 0, tiled=True)
    summed = jnp.sum(got.astype(jnp.float32), axis=0).reshape(tokens, 2, block)
    z_hi = lax.axis_index("z_hi")
    kept = lax.dynamic_index_in_dim(summed, z_hi, 1, keepdims=False)
    given = lax.dynamic_index_in_dim(summed, 1 - z_hi, 1, keepdims=False)
    total = kept + shifted(given, "z_hi", 1)
    square = (total * total).astype(jnp.bfloat16)
    row = lax.all_gather(square, "x", axis=0, tiled=False)
    spread = lax.all_gather(row, TENSOR, axis=0, tiled=False)
    return spread.reshape(4, 2, 4, tokens, block)


def grad_squares(rows, basis):
    tokens = sum(part.shape[0] for part in rows)
    columns = basis.shape[1]
    partial = pl.pallas_call(
        grad_kernel,
        out_shape=jax.ShapeDtypeStruct((columns, tokens), jnp.bfloat16),
        in_specs=[VMEM] * (len(rows) + 1),
        out_specs=VMEM,
        compiler_params=pltpu.CompilerParams(vmem_limit_bytes=VMEM_LIMIT),
        name="grad",
    )(*rows, basis)
    got = lax.all_to_all(partial.reshape(16, columns // 16, tokens), ("x", "y"), 0, 0, tiled=True)
    summed = jnp.sum(got.astype(jnp.float32), axis=0)
    total = summed + shifted(summed.astype(jnp.bfloat16), "z_hi", 1).astype(jnp.float32)
    square = (total * total).astype(jnp.bfloat16)
    return lax.all_to_all(
        jnp.broadcast_to(square[None], (4,) + square.shape), "y", 0, 0, tiled=True
    )


def corrected(steps, place, grad_sq, act_sq, tokens, *before):
    _, rows, here = grad_sq.shape
    block = act_sq.shape[4]
    return pl.pallas_call(
        lambda *refs: correct_kernel(steps, tokens, *refs),
        out_shape=jax.ShapeDtypeStruct((4, 4 * rows, block), jnp.float32),
        in_specs=[SMEM] + [VMEM] * (2 + len(before)),
        out_specs=VMEM,
        scratch_shapes=[pltpu.VMEM((here, 4 * block), jnp.bfloat16)],
        compiler_params=pltpu.CompilerParams(vmem_limit_bytes=VMEM_LIMIT),
        name="correct",
    )(place, grad_sq, act_sq, *before)


def per_device(hidden, norm_gain, gate_pre, out_grad, grad_basis, act_basis):
    up_grad = (out_grad.astype(jnp.float32) * jax.nn.silu(gate_pre.astype(jnp.float32))).astype(
        jnp.bfloat16
    )
    moved = [up_grad] + [shifted(up_grad, "z_lo", step) for step in (1, 2, 3)]
    act_sq = act_squares(hidden, norm_gain, act_basis)
    both = [(own, shifted(own, "core", 1)) for own in moved]
    place = jnp.stack([lax.axis_index("z_lo"), lax.axis_index("core")]).astype(jnp.int32)
    tokens = 8 * hidden.shape[0]
    out = []
    for steps in ((0, 1), (2, 3)):
        rows = [part for step in steps for part in both[step]]
        grad_sq = grad_squares(rows, grad_basis)
        out = [corrected(steps, place, grad_sq, act_sq, tokens, *out)]
    out = lax.all_to_all(out[0], "x", 0, 0, tiled=True)
    return out.reshape(grad_basis.shape[1], -1)


def solution(mesh):
    fine = Mesh(mesh.devices.reshape(SIZES), AXES)
    placed = (
        P(TENSOR, None),
        P(),
        P(TENSOR, DP),
        P(TENSOR, DP),
        P(DP, TENSOR),
        P(DP, None),
    )
    return jax.shard_map(
        per_device, mesh=fine, in_specs=placed, out_specs=P(TENSOR, DP), check_vma=False
    )
```

time: 178 us -> 168 us (0.944)
  the two profiles are of different devices: /device:TPU:32 before, /device:TPU:8 now
where the time goes in v2:
time: 168 us; the launch traced here: 167 us
  waiting for transfers between devices  50.3 us (30%)
  starting transfers between devices  45.2 us (27%)
  blocking collectives  34.1 us (20%)
  between operations  13.6 us (8%)
  local copies, waits for them, and re-layouts  11.6 us (7%)
  Pallas kernels  7.4 us (4%)
  other arithmetic  4.79 us (3%)
    ppermute x10, waiting for transfers between devices, shifted(): lax.ppermute(value, axis, [(i, (i + step) % size) for i in range(size)])  31.3 us
    all_gather x1, blocking collectives, act_squares(): row = lax.all_gather(square, 'x', axis=0, tiled=False)  19.8 us
    ppermute x10, starting transfers between devices, shifted(): lax.ppermute(value, axis, [(i, (i + step) % size) for i in range(size)])  17.8 us
    all_to_all x1, blocking collectives, per_device(): out = lax.all_to_all(out[0], 'x', 0, 0, tiled=True)  14.3 us
    all_to_all x2, starting transfers between devices, grad_squares(): lax.all_to_all(partial.reshape(16, columns // 16, tokens), ('x', 'y'), 0,...  11.6 us
    unnamed x19, local copies, waits for them, and re-layouts  9.68 us
    all_to_all x2, starting transfers between devices, grad_squares(): lax.all_to_all(jnp.broadcast_to(square[None], (4,) + square.shape), 'y',...  8.35 us
    all_to_all x2, waiting for transfers between devices, grad_squares(): lax.all_to_all(jnp.broadcast_to(square[None], (4,) + square.shape), 'y',...  7.9 us
  transfers between devices with their start and end apart: 16, of which 11 were waited for; matrix products, arithmetic and copies ran while one was open for 4% of the time, Pallas kernels for 3%

profile of v2, /device:TPU:8, one launch (start us, length us, event | category | flops | bytes accessed | tf_op | source)
XLA Modules:
  0.0 166.9 jit_solution(246672468839667152)
XLA Ops:
  6.5 1.6 copy-done.6
  8.1 1.6 copy-done.7
  12.4 7.4 %all-to-all-start.2 = ((bf16[16,128,256]{2,1,0:T(8,128)(2,1)}), bf16[16,128,256]{2,1,0:T(8,128)(2,1)}, u32[]{:S(2)}, u32[]{:S(2)}) async-start(bf16[16,128,256]{2,1,0:T(8,128)(2,1)} %copy-done.5), calls=%async_computation.2 | async-start | bytes 2097152 | tf_op jit(solution)/shard_map/all_to_all | solution.py:90
  19.8 1.2 fusion.4.refs_0_
  21.0 2.0 %collective-permute-start.7 = (bf16[128,896]{1,0:T(8,128)(2,1)S(1)}, bf16[128,896]{1,0:T(8,128)(2,1)S(1)}, u32[]{:S(2)}, u32[]{:S(2)}) collective-permute-start(bf16[128,896]{1,0:T(8,128)(2,1)S(1)} %fusion.4.refs_0_), channel_id=1, source_target_pairs={{0,2},{2,4},{4,6},{6,0},{1,3},{3,5},{5,7},{7,1},{8,10},{10,12},{12... | collective-permute-start | bytes 688136 | tf_op jit(solution)/shard_map/ppermute | solution.py:20
  23.0 7.7 %collective-permute-done.7.refs_2_ = bf16[128,896]{1,0:T(8,128)(2,1)S(1)} collective-permute-done((bf16[128,896]{1,0:T(8,128)(2,1)S(1)}, bf16[128,896]{1,0:T(8,128)(2,1)S(1)}, u32[]{:S(2)}, u32[]{:S(2)}) %collective-permute-start.7) | collective-permute-done | bytes 229408 | tf_op jit(solution)/shard_map/ppermute | solution.py:20
  30.7 1.5 collective-permute-done.8.refs_3_
  32.2 2.2 %grad.3 = bf16[1792,512]{1,0:T(8,128)(2,1)S(1)} custom-call(bf16[128,896]{1,0:T(8,128)(2,1)S(1)} %fusion.4.refs_0_, bf16[128,896]{1,0:T(8,128)(2,1)S(1)} %collective-permute-done.6.refs_1_, bf16[128,896]{1,0:T(8,128)(2,1)S(1)} %collective-permute-done.7.refs_2_, bf16[128,896]{1,0:T(8,128)(2,1)S(1)} %collective-permute-done.8.refs_3_, ...), custom_call_target="tpu_custom_call" | custom-call | tf_op jit(solution)/shard_map/grad/pallas_call | solution.py:105
  34.4 1.2 copy-done.2
  36.2 6.6 %all-to-all-start.3 = ((bf16[16,112,512]{2,1,0:T(8,128)(2,1)}), bf16[16,112,512]{2,1,0:T(8,128)(2,1)}, u32[]{:S(2)}, u32[]{:S(2)}) async-start(bf16[16,112,512]{2,1,0:T(8,128)(2,1)} %bitcast.18), calls=%async_computation.3 | async-start | bytes 3670016 | tf_op jit(solution)/shard_map/all_to_all | solution.py:113
  42.9 3.6 %collective-permute-start.2 = (bf16[128,896]{1,0:T(8,128)(2,1)S(1)}, bf16[128,896]{1,0:T(8,128)(2,1)S(1)}, u32[]{:S(2)}, u32[]{:S(2)}) collective-permute-start(bf16[128,896]{1,0:T(8,128)(2,1)S(1)} %fusion.4.refs_0_), channel_id=1, source_target_pairs={{0,6},{2,0},{4,2},{6,4},{1,7},{3,1},{5,3},{7,5},{8,14},{10,8},{12,... | collective-permute-start | bytes 688136 | tf_op jit(solution)/shard_map/ppermute | solution.py:20
  46.5 5.3 %collective-permute-done.2.refs_2_ = bf16[128,896]{1,0:T(8,128)(2,1)S(1)} collective-permute-done((bf16[128,896]{1,0:T(8,128)(2,1)S(1)}, bf16[128,896]{1,0:T(8,128)(2,1)S(1)}, u32[]{:S(2)}, u32[]{:S(2)}) %collective-permute-start.2) | collective-permute-done | bytes 229408 | tf_op jit(solution)/shard_map/ppermute | solution.py:20
  51.7 7.3 %collective-permute-done.refs_0_ = bf16[128,896]{1,0:T(8,128)(2,1)S(1)} collective-permute-done((bf16[128,896]{1,0:T(8,128)(2,1)S(1)}, bf16[128,896]{1,0:T(8,128)(2,1)S(1)}, u32[]{:S(2)}, u32[]{:S(2)}) %collective-permute-start) | collective-permute-done | bytes 229408 | tf_op jit(solution)/shard_map/ppermute | solution.py:20
  59.0 1.5 collective-permute-done.1.refs_1_
  60.5 2.2 %grad.2 = bf16[1792,512]{1,0:T(8,128)(2,1)S(1)} custom-call(bf16[128,896]{1,0:T(8,128)(2,1)S(1)} %collective-permute-done.refs_0_, bf16[128,896]{1,0:T(8,128)(2,1)S(1)} %collective-permute-done.1.refs_1_, bf16[128,896]{1,0:T(8,128)(2,1)S(1)} %collective-permute-done.2.refs_2_, bf16[128,896]{1,0:T(8,128)(2,1)S(1)} %collective-permute-done.3.refs_3_, ...), custom_call_target="tpu_custom_call" | custom-call | tf_op jit(solution)/shard_map/grad/pallas_call | solution.py:105
  62.7 1.2 copy-done.1
  63.9 5.3 %all-to-all-done.3 = bf16[16,112,512]{2,1,0:T(8,128)(2,1)} async-done(((bf16[16,112,512]{2,1,0:T(8,128)(2,1)}), bf16[16,112,512]{2,1,0:T(8,128)(2,1)}, u32[]{:S(2)}, u32[]{:S(2)}) %all-to-all-start.3) | async-done | bytes 1835040 | tf_op jit(solution)/shard_map/all_to_all | solution.py:113
  69.2 5.0 %all-to-all-start = ((bf16[16,112,512]{2,1,0:T(8,128)(2,1)}), bf16[16,112,512]{2,1,0:T(8,128)(2,1)S(1)}, u32[]{:S(2)}, u32[]{:S(2)}) async-start(bf16[16,112,512]{2,1,0:T(8,128)(2,1)} %bitcast.17), calls=%async_computation | async-start | bytes 3670016 | tf_op jit(solution)/shard_map/all_to_all | solution.py:113
  74.3 1.4 convert_reduce_fusion.2
  75.8 6.1 %collective-permute-start.5 = (f32[128,128]{1,0:T(8,128)S(1)}, f32[128,128]{1,0:T(8,128)S(1)}, u32[]{:S(2)}, u32[]{:S(2)}) collective-permute-start(f32[128,128]{1,0:T(8,128)S(1)} %bitcast.25), channel_id=1, source_target_pairs={{0,128},{128,0},{1,129},{129,1},{2,130},{130,2},{3,131},{131,3},{4... | collective-permute-start | bytes 196616 | tf_op jit(solution)/shard_map/ppermute | solution.py:20
  82.1 2.2 %collective-permute-done.5 = f32[128,128]{1,0:T(8,128)S(1)} collective-permute-done((f32[128,128]{1,0:T(8,128)S(1)}, f32[128,128]{1,0:T(8,128)S(1)}, u32[]{:S(2)}, u32[]{:S(2)}) %collective-permute-start.5) | collective-permute-done | bytes 65568 | tf_op jit(solution)/shard_map/ppermute | solution.py:20
  84.2 19.8 %all-gather = bf16[512,128]{1,0:T(8,128)(2,1)} all-gather(bf16[128,128]{1,0:T(8,128)(2,1)S(1)} %fusion.6), channel_id=2, replica_groups=mesh['z_hi'=2,'x'=4,'y'=4,'z_lo'=4,'core'=2] {'x'}, dimensions={0}, use_global_device_ids=true | all-gather | bytes 163840 | tf_op jit(solution)/shard_map/all_gather | solution.py:97
  104.0 1.8 %convert_reduce_fusion = f32[112,512]{1,0:T(8,128)S(1)} fusion(bf16[16,112,512]{2,1,0:T(8,128)(2,1)} %all-to-all-done.3), kind=kLoop, calls=%fused_computation | loop fusion | flops 1777664 | bytes 2064384 | tf_op jit(solution)/shard_map/reduce_sum | solution.py:114
  105.8 5.8 %collective-permute-start.9 = (bf16[112,512]{1,0:T(8,128)(2,1)S(1)}, bf16[112,512]{1,0:T(8,128)(2,1)S(1)}, u32[]{:S(2)}, u32[]{:S(2)}) collective-permute-start(bf16[112,512]{1,0:T(8,128)(2,1)S(1)} %convert_element_type.49), channel_id=1, source_target_pairs={{0,128},{128,0},{1,129},{129,1},{2,130},{130,2},{3,131},{131,3},{4... | collective-permute-start | bytes 344072 | tf_op jit(solution)/shard_map/ppermute | solution.py:20
  112.2 5.9 %collective-permute-done.9 = bf16[112,512]{1,0:T(8,128)(2,1)S(1)} collective-permute-done((bf16[112,512]{1,0:T(8,128)(2,1)S(1)}, bf16[112,512]{1,0:T(8,128)(2,1)S(1)}, u32[]{:S(2)}, u32[]{:S(2)}) %collective-permute-start.9) | collective-permute-done | bytes 114720 | tf_op jit(solution)/shard_map/ppermute | solution.py:20
  118.9 3.5 %all-to-all-start.4 = ((bf16[4,112,512]{2,1,0:T(8,128)(2,1)}), bf16[4,112,512]{2,1,0:T(8,128)(2,1)S(1)}, u32[]{:S(2)}, u32[]{:S(2)}) async-start(bf16[4,112,512]{2,1,0:T(8,128)(2,1)} %broadcast_in_dim.5), calls=%async_computation.4 | async-start | bytes 917504 | tf_op jit(solution)/shard_map/all_to_all | solution.py:117
  122.4 7.9 %all-to-all-done.4.refs_1_ = bf16[4,112,512]{2,1,0:T(8,128)(2,1)S(1)} async-done(((bf16[4,112,512]{2,1,0:T(8,128)(2,1)}), bf16[4,112,512]{2,1,0:T(8,128)(2,1)S(1)}, u32[]{:S(2)}, u32[]{:S(2)}) %all-to-all-start.4) | async-done | bytes 458784 | tf_op jit(solution)/shard_map/all_to_all | solution.py:117
  131.1 4.9 %all-to-all-start.1 = ((bf16[4,112,512]{2,1,0:T(8,128)(2,1)}), bf16[4,112,512]{2,1,0:T(8,128)(2,1)S(1)}, u32[]{:S(2)}, u32[]{:S(2)}) async-start(bf16[4,112,512]{2,1,0:T(8,128)(2,1)} %broadcast_in_dim.4), calls=%async_computation.1 | async-start | bytes 917504 | tf_op jit(solution)/shard_map/all_to_all | solution.py:117
  136.1 5.1 %all-gather.4.cloned.1.call-done = bf16[32,128,128]{2,1,0:T(8,128)(2,1)} async-done(((bf16[4,128,128]{2,1,0:T(8,128)(2,1)}), bf16[32,128,128]{2,1,0:T(8,128)(2,1)}) %all-gather.4.cloned.1.call-update) | async-done | bytes 1048592 | tf_op jit(solution)/shard_map/all_gather | solution.py:98
  141.2 1.2 copy-done.3
  143.7 1.1 correct.3
  144.8 14.3 %all_to_all.30 = f32[4,448,128]{2,1,0:T(8,128)S(1)} all-to-all(f32[4,448,128]{2,1,0:T(8,128)S(1)} %correct.3), channel_id=1, replica_groups=mesh['z_hi'=2,'x'=4,'y'=4,'z_lo'=4,'core'=2] {'x'}, dimensions={0} | all-to-all | bytes 1835008 | tf_op jit(solution)/shard_map/all_to_all | solution.py:150
  (43 shorter events, 8.1 us)
Async XLA Ops:
  6.5 1.6 copy-start.6
  8.1 1.6 copy-start.7
  9.7 0.8 copy-start.8
  10.5 21.7 %copy-start = (bf16[896,1792]{1,0:T(8,128)(2,1)S(1)}, bf16[896,1792]{1,0:T(8,128)(2,1)}, u32[]{:S(2)}) copy-start(bf16[896,1792]{1,0:T(8,128)(2,1)} %refs_4_.3) | copy-start | bytes 9633796
  11.4 1.0 copy-start.5
  12.4 23.8 %all-to-all-start.2 = ((bf16[16,128,256]{2,1,0:T(8,128)(2,1)}), bf16[16,128,256]{2,1,0:T(8,128)(2,1)}, u32[]{:S(2)}, u32[]{:S(2)}) async-start(bf16[16,128,256]{2,1,0:T(8,128)(2,1)} %copy-done.5), calls=%async_computation.2 | async-start | bytes 2097152 | tf_op jit(solution)/shard_map/all_to_all | solution.py:90
  21.0 9.7 %collective-permute-start.7 = (bf16[128,896]{1,0:T(8,128)(2,1)S(1)}, bf16[128,896]{1,0:T(8,128)(2,1)S(1)}, u32[]{:S(2)}, u32[]{:S(2)}) collective-permute-start(bf16[128,896]{1,0:T(8,128)(2,1)S(1)} %fusion.4.refs_0_), channel_id=1, source_target_pairs={{0,2},{2,4},{4,6},{6,0},{1,3},{3,5},{5,7},{7,1},{8,10},{10,12},{12... | collective-permute-start | bytes 688136 | tf_op jit(solution)/shard_map/ppermute | solution.py:20
  23.0 7.8 %collective-permute-start.6 = (bf16[128,896]{1,0:T(8,128)(2,1)S(1)}, bf16[128,896]{1,0:T(8,128)(2,1)S(1)}, u32[]{:S(2)}, u32[]{:S(2)}) collective-permute-start(bf16[128,896]{1,0:T(8,128)(2,1)S(1)} %fusion.4.refs_0_), channel_id=1, source_target_pairs={{0,1},{1,0},{2,3},{3,2},{4,5},{5,4},{6,7},{7,6},{8,9},{9,8},{10,11... | collective-permute-start | bytes 688136 | tf_op jit(solution)/shard_map/ppermute | solution.py:20
  30.7 1.5 collective-permute-start.8
  34.4 1.2 copy-start.2
  36.2 33.0 %all-to-all-start.3 = ((bf16[16,112,512]{2,1,0:T(8,128)(2,1)}), bf16[16,112,512]{2,1,0:T(8,128)(2,1)}, u32[]{:S(2)}, u32[]{:S(2)}) async-start(bf16[16,112,512]{2,1,0:T(8,128)(2,1)} %bitcast.18), calls=%async_computation.3 | async-start | bytes 3670016 | tf_op jit(solution)/shard_map/all_to_all | solution.py:113
  42.9 8.8 %collective-permute-start.2 = (bf16[128,896]{1,0:T(8,128)(2,1)S(1)}, bf16[128,896]{1,0:T(8,128)(2,1)S(1)}, u32[]{:S(2)}, u32[]{:S(2)}) collective-permute-start(bf16[128,896]{1,0:T(8,128)(2,1)S(1)} %fusion.4.refs_0_), channel_id=1, source_target_pairs={{0,6},{2,0},{4,2},{6,4},{1,7},{3,1},{5,3},{7,5},{8,14},{10,8},{12,... | collective-permute-start | bytes 688136 | tf_op jit(solution)/shard_map/ppermute | solution.py:20
  46.5 12.6 %collective-permute-start = (bf16[128,896]{1,0:T(8,128)(2,1)S(1)}, bf16[128,896]{1,0:T(8,128)(2,1)S(1)}, u32[]{:S(2)}, u32[]{:S(2)}) collective-permute-start(bf16[128,896]{1,0:T(8,128)(2,1)S(1)} %fusion.4.refs_0_), channel_id=1, source_target_pairs={{0,4},{2,6},{4,0},{6,2},{1,5},{3,7},{5,1},{7,3},{8,12},{10,14},{12... | collective-permute-start | bytes 688136 | tf_op jit(solution)/shard_map/ppermute | solution.py:20
  51.7 7.3 %collective-permute-start.3 = (bf16[128,896]{1,0:T(8,128)(2,1)S(1)}, bf16[128,896]{1,0:T(8,128)(2,1)S(1)}, u32[]{:S(2)}, u32[]{:S(2)}) collective-permute-start(bf16[128,896]{1,0:T(8,128)(2,1)S(1)} %collective-permute-done.2.refs_2_), channel_id=1, source_target_pairs={{0,1},{1,0},{2,3},{3,2},{4,5},{5,4},{6,7},{7,6},{8,9},{9,8},{10,11... | collective-permute-start | bytes 688136 | tf_op jit(solution)/shard_map/ppermute | solution.py:20
  59.0 1.5 collective-permute-start.1
  62.7 1.2 copy-start.1
  69.2 42.4 %all-to-all-start = ((bf16[16,112,512]{2,1,0:T(8,128)(2,1)}), bf16[16,112,512]{2,1,0:T(8,128)(2,1)S(1)}, u32[]{:S(2)}, u32[]{:S(2)}) async-start(bf16[16,112,512]{2,1,0:T(8,128)(2,1)} %bitcast.17), calls=%async_computation | async-start | bytes 3670016 | tf_op jit(solution)/shard_map/all_to_all | solution.py:113
  74.2 67.0 %all-gather.4.cloned.1.call-start = ((), (), s32[]{:S(2)}) async-start(), calls=%async_computation.6 | async-start | bytes 1179648 | tf_op jit(solution)/shard_map/all_gather | solution.py:98
  75.8 8.4 %collective-permute-start.5 = (f32[128,128]{1,0:T(8,128)S(1)}, f32[128,128]{1,0:T(8,128)S(1)}, u32[]{:S(2)}, u32[]{:S(2)}) collective-permute-start(f32[128,128]{1,0:T(8,128)S(1)} %bitcast.25), channel_id=1, source_target_pairs={{0,128},{128,0},{1,129},{129,1},{2,130},{130,2},{3,131},{131,3},{4... | collective-permute-start | bytes 196616 | tf_op jit(solution)/shard_map/ppermute | solution.py:20
  105.8 12.3 %collective-permute-start.9 = (bf16[112,512]{1,0:T(8,128)(2,1)S(1)}, bf16[112,512]{1,0:T(8,128)(2,1)S(1)}, u32[]{:S(2)}, u32[]{:S(2)}) collective-permute-start(bf16[112,512]{1,0:T(8,128)(2,1)S(1)} %convert_element_type.49), channel_id=1, source_target_pairs={{0,128},{128,0},{1,129},{129,1},{2,130},{130,2},{3,131},{131,3},{4... | collective-permute-start | bytes 344072 | tf_op jit(solution)/shard_map/ppermute | solution.py:20
  111.9 10.5 %collective-permute-start.4 = (bf16[112,512]{1,0:T(8,128)(2,1)S(1)}, bf16[112,512]{1,0:T(8,128)(2,1)S(1)}, u32[]{:S(2)}, u32[]{:S(2)}) collective-permute-start(bf16[112,512]{1,0:T(8,128)(2,1)S(1)} %convert_element_type.43), channel_id=1, source_target_pairs={{0,128},{128,0},{1,129},{129,1},{2,130},{130,2},{3,131},{131,3},{4... | collective-permute-start | bytes 344072 | tf_op jit(solution)/shard_map/ppermute | solution.py:20
  118.9 11.4 %all-to-all-start.4 = ((bf16[4,112,512]{2,1,0:T(8,128)(2,1)}), bf16[4,112,512]{2,1,0:T(8,128)(2,1)S(1)}, u32[]{:S(2)}, u32[]{:S(2)}) async-start(bf16[4,112,512]{2,1,0:T(8,128)(2,1)} %broadcast_in_dim.5), calls=%async_computation.4 | async-start | bytes 917504 | tf_op jit(solution)/shard_map/all_to_all | solution.py:117
  131.1 12.4 %all-to-all-start.1 = ((bf16[4,112,512]{2,1,0:T(8,128)(2,1)}), bf16[4,112,512]{2,1,0:T(8,128)(2,1)S(1)}, u32[]{:S(2)}, u32[]{:S(2)}) async-start(bf16[4,112,512]{2,1,0:T(8,128)(2,1)} %broadcast_in_dim.4), calls=%async_computation.1 | async-start | bytes 917504 | tf_op jit(solution)/shard_map/all_to_all | solution.py:117
  141.2 1.2 copy-start.3
  142.4 1.2 copy-start.4
Sparse Core Ops, SparseCore 0:
  104.1 37.0 all-gather.3

commit v3 on v0

v3 whole, which is shorter than its diff:
```python
import jax
import jax.numpy as jnp
from jax import lax
from jax.experimental import pallas as pl
from jax.experimental.pallas import tpu as pltpu
from jax.sharding import Mesh
from jax.sharding import PartitionSpec as P

AXES = ("z_hi", "x", "y", "z_lo", "core")
SIZES = (2, 4, 4, 4, 2)
DP = ("z_hi", "x", "y")
TENSOR = ("z_lo", "core")
SMEM = pl.BlockSpec(memory_space=pltpu.SMEM)
VMEM = pl.BlockSpec(memory_space=pltpu.VMEM)
HBM = pl.BlockSpec(memory_space=pl.ANY)
PARAMS = pltpu.CompilerParams(vmem_limit_bytes=48 * 1024 * 1024)


def shifted(value, axis, step):
    size = SIZES[AXES.index(axis)]
    return lax.ppermute(value, axis, [(i, (i + step) % size) for i in range(size)])


def first_kernel(place, gain, own, other, hidden_at, act_at, grad_at, out_at,
                 hidden, act_basis, grad_basis, rows, out, sems):
    loads = [
        pltpu.make_async_copy(src, dst, sems.at[i])
        for i, (src, dst) in enumerate(
            ((hidden_at, hidden), (act_at, act_basis), (grad_at, grad_basis))
        )
    ]
    for load in loads:
        load.start()
    tokens, features = hidden.shape
    depth = act_basis.shape[0]
    rows[:tokens, :] = own[...]
    rows[tokens:, :] = other[...]
    loads[0].wait()
    squares = jnp.zeros((tokens, 128), jnp.float32)
    for at in range(0, features, 128):
        wide = hidden[:, at : at + 128].astype(jnp.float32)
        squares += wide * wide
    stat = jnp.sum(squares, axis=-1, keepdims=True) / features
    mine = pl.ds(pl.multiple_of(place[0] * depth, depth), depth)
    scaled = hidden[:, mine].astype(jnp.float32) * lax.rsqrt(stat + 1e-05)
    normed = (scaled * gain[:, mine]).astype(jnp.bfloat16)
    loads[1].wait()
    block = act_basis.shape[1] // 32
    for z_hi in range(2):
        for x in range(4):
            at = (z_hi * 16 + x * 4) * block
            part = jnp.dot(
                normed, act_basis[:, at : at + 4 * block], preferred_element_type=jnp.float32
            )
            for y in range(4):
                out[x * 4 + y, :tokens, z_hi * block : (z_hi + 1) * block] = part[
                    :, y * block : (y + 1) * block
                ].astype(jnp.bfloat16)
    act_rows = pl.ds(0, tokens)
    act_store = pltpu.make_async_copy(out.at[:, act_rows], out_at.at[:, act_rows], sems.at[3])
    act_store.start()
    loads[2].wait()
    columns = grad_basis.shape[1]
    share = columns // 16
    for at in range(0, columns, 256):
        part = jnp.dot(rows[...], grad_basis[:, at : at + 256], preferred_element_type=jnp.float32)
        part = part.T.astype(jnp.bfloat16)
        for owner in range(at // share, (at + 255) // share + 1):
            low, high = max(at, owner * share), min(at + 256, (owner + 1) * share)
            to = tokens + low - owner * share
            out[owner, to : to + high - low, :] = part[low - at : high - at, :]
    grad_rows = pl.ds(tokens, share)
    grad_store = pltpu.make_async_copy(out.at[:, grad_rows], out_at.at[:, grad_rows], sems.at[4])
    grad_store.start()
    act_store.wait()
    grad_store.wait()


def first_partials(hidden, norm_gain, act_basis, grad_basis, own, other):
    tokens, features = hidden.shape
    shape = (16, tokens + grad_basis.shape[1] // 16, 2 * tokens)
    place = lax.axis_index(DP).astype(jnp.int32).reshape(1)
    return pl.pallas_call(
        first_kernel,
        out_shape=jax.ShapeDtypeStruct(shape, jnp.bfloat16),
        in_specs=[SMEM, VMEM, VMEM, VMEM, HBM, HBM, HBM],
        out_specs=HBM,
        scratch_shapes=[
            pltpu.VMEM(hidden.shape, jnp.bfloat16),
            pltpu.VMEM(act_basis.shape, jnp.bfloat16),
            pltpu.VMEM(grad_basis.shape, jnp.bfloat16),
            pltpu.VMEM((2 * tokens, own.shape[1]), jnp.bfloat16),
            pltpu.VMEM(shape, jnp.bfloat16),
            pltpu.SemaphoreType.DMA((5,)),
        ],
        compiler_params=PARAMS,
        name="first",
    )(place, norm_gain.reshape(1, -1), own, other, hidden, act_basis, grad_basis)


def grad_kernel(count, *refs):
    parts, basis, out, rows = refs[:count], refs[count], refs[-2], refs[-1]

    @pl.when(pl.program_id(0) == 0)
    def _():
        at = 0
        for part in parts:
            rows[at : at + part.shape[0], :] = part[...]
            at += part.shape[0]

    part = jnp.dot(rows[...], basis[...], preferred_element_type=jnp.float32)
    out[...] = part.T.astype(jnp.bfloat16)


def grad_partials(parts, basis, *after):
    depth, columns = basis.shape
    tokens = sum(part.shape[0] for part in parts)
    whole = pl.BlockSpec(parts[0].shape, lambda i: (0, 0))
    return pl.pallas_call(
        lambda *refs: grad_kernel(len(parts), *refs),
        grid=(columns // 256,),
        out_shape=jax.ShapeDtypeStruct((columns, tokens), jnp.bfloat16),
        in_specs=[whole] * len(parts)
        + [pl.BlockSpec((depth, 256), lambda i: (0, i))]
        + [HBM] * len(after),
        out_specs=pl.BlockSpec((256, tokens), lambda i: (i, 0)),
        scratch_shapes=[pltpu.VMEM((tokens, depth), jnp.bfloat16)],
        compiler_params=PARAMS,
        name="grad",
    )(*parts, basis, *after)


def spread_sum_kernel(place, got, kept, grad, given):
    tokens = kept.shape[0]
    half = tokens // 2
    act = jnp.zeros((tokens, 2 * kept.shape[1]), jnp.float32)
    for source in range(got.shape[0]):
        act += got[source, :tokens, :].astype(jnp.float32)
    low, high = act[:, : kept.shape[1]], act[:, kept.shape[1] :]
    first = place[0] == 0
    kept[...] = jnp.where(first, low, high)
    away = jnp.where(first, high, low).astype(jnp.bfloat16)
    given[:half, : kept.shape[1]] = away[:half]
    given[:half, kept.shape[1] :] = away[half:]
    total = jnp.zeros(grad.shape, jnp.float32)
    for source in range(got.shape[0]):
        total += got[source, tokens:, :].astype(jnp.float32)
    grad[...] = total
    given[half:, :] = total.astype(jnp.bfloat16)


def square_kernel(kept, grad, got, act_sq, grad_sq):
    tokens, block = kept.shape
    half = tokens // 2
    for part in range(2):
        rows = slice(part * half, (part + 1) * half)
        total = kept[rows, :] + got[:half, part * block : (part + 1) * block].astype(jnp.float32)
        act_sq[rows, :] = (total * total).astype(jnp.bfloat16)
    total = grad[...] + got[half:, :].astype(jnp.float32)
    grad_sq[...] = (total * total).astype(jnp.bfloat16)


def first_squares(got, tokens):
    share = got.shape[1] - tokens
    wide = got.shape[2]
    block = wide // 2
    place = lax.axis_index("z_hi").astype(jnp.int32).reshape(1)
    kept, grad, given = pl.pallas_call(
        spread_sum_kernel,
        out_shape=(
            jax.ShapeDtypeStruct((tokens, block), jnp.float32),
            jax.ShapeDtypeStruct((share, wide), jnp.float32),
            jax.ShapeDtypeStruct((tokens // 2 + share, wide), jnp.bfloat16),
        ),
        in_specs=[SMEM, VMEM],
        out_specs=(VMEM, VMEM, VMEM),
        compiler_params=PARAMS,
        name="spread_sum",
    )(place, got)
    return pl.pallas_call(
        square_kernel,
        out_shape=(
            jax.ShapeDtypeStruct((tokens, block), jnp.bfloat16),
            jax.ShapeDtypeStruct((share, wide), jnp.bfloat16),
        ),
        in_specs=[VMEM] * 3,
        out_specs=(VMEM, VMEM),
        compiler_params=PARAMS,
        name="square",
    )(kept, grad, shifted(given, "z_hi", 1))


def exchanged(partial):
    columns, tokens = partial.shape
    return lax.all_to_all(partial.reshape(16, columns // 16, tokens), ("x", "y"), 0, 0, tiled=True)


def squared(got):
    summed = jnp.sum(got.astype(jnp.float32), axis=0)
    total = summed + shifted(summed.astype(jnp.bfloat16), "z_hi", 1).astype(jnp.float32)
    return (total * total).astype(jnp.bfloat16)


def correct_kernel(steps, *refs):
    place, *pieces, act_sq, out, act = refs
    pieces, before = pieces[:4], pieces[4:]
    tokens, block = act_sq.shape[2:]
    for i, step in enumerate(steps):
        chip = lax.rem(place[0] + 4 - step, 4)
        for x in range(4):
            act[i * tokens : (i + 1) * tokens, x * block : (x + 1) * block] = act_sq[x, chip]
    rows = pieces[0].shape[0]
    for piece, behind in zip(pieces, (0, 1, 2, 3)):
        part = jnp.dot(piece[...], act[...], preferred_element_type=jnp.float32)
        part = part * (1.0 / (4 * tokens))
        at = pl.ds(pl.multiple_of(lax.rem(place[1] + 4 - behind, 4) * rows, rows), rows)
        for x in range(4):
            here = part[:, x * block : (x + 1) * block]
            if before:
                here = before[0][x, at, :] + here
            out[x, at, :] = here


def corrected(steps, grad_sq, act_sq, *before):
    rows, tokens = grad_sq.shape
    block = act_sq.shape[3]
    place = jnp.stack([lax.axis_index("z_lo"), lax.axis_index("y")]).astype(jnp.int32)
    pieces = [grad_sq] + [shifted(grad_sq, "y", step) for step in (1, 2, 3)]
    return pl.pallas_call(
        lambda *refs: correct_kernel(steps, *refs),
        out_shape=jax.ShapeDtypeStruct((4, 4 * rows, block), jnp.float32),
        in_specs=[SMEM] + [VMEM] * (5 + len(before)),
        out_specs=VMEM,
        scratch_shapes=[pltpu.VMEM((tokens, 4 * block), jnp.bfloat16)],
        compiler_params=PARAMS,
        name="correct",
    )(place, *pieces, *before, act_sq)


def per_device(hidden, norm_gain, gate_pre, out_grad, grad_basis, act_basis):
    tokens = hidden.shape[0]
    up_grad = (out_grad.astype(jnp.float32) * jax.nn.silu(gate_pre.astype(jnp.float32))).astype(
        jnp.bfloat16
    )
    moved = [up_grad] + [shifted(up_grad, "z_lo", step) for step in (1, 2, 3)]
    both = [(own, shifted(own, "core", 1)) for own in moved]
    first = first_partials(hidden, norm_gain, act_basis, grad_basis, *both[0])
    got_first = lax.all_to_all(first, ("x", "y"), 0, 0, tiled=True)
    got_middle = exchanged(grad_partials(both[1] + both[2], grad_basis))
    act_own, grad_first = first_squares(got_first, tokens)
    act_chip = jnp.concatenate([act_own, shifted(act_own, "core", 1)], axis=0)
    act_sq = lax.all_gather(act_chip, ("x", "z_lo"), axis=0, tiled=False)
    act_sq = act_sq.reshape(4, 4, 2 * tokens, -1)
    got_last = exchanged(grad_partials(both[3], grad_basis, act_chip))
    grad_most = jnp.concatenate([grad_first, squared(got_middle)], axis=1)
    most = corrected((0, 1, 2), grad_most, act_sq)
    out = corrected((3,), squared(got_last), act_sq, most)
    out = lax.all_to_all(out, "x", 0, 0, tiled=True)
    return out.reshape(grad_basis.shape[1], -1)


def solution(mesh):
    fine = Mesh(mesh.devices.reshape(SIZES), AXES)
    placed = (
        P(TENSOR, None),
        P(),
        P(TENSOR, DP),
        P(TENSOR, DP),
        P(DP, TENSOR),
        P(DP, None),
    )
    return jax.shard_map(
        per_device, mesh=fine, in_specs=placed, out_specs=P(TENSOR, DP), check_vma=False
    )
```

time: 988 us -> 183 us (0.19)
  the two profiles are of different devices: /device:TPU:64 before, /device:TPU:16 now
where the time goes in v3:
time: 183 us
  waiting for transfers between devices  73 us (40%)
  starting transfers between devices  55.4 us (30%)
  Pallas kernels  14.9 us (8%)
  between operations  13.6 us (7%)
  blocking collectives  12.6 us (7%)
  local copies, waits for them, and re-layouts  9.89 us (5%)
  other arithmetic  3.27 us (2%)
    ppermute x17, waiting for transfers between devices, shifted(): lax.ppermute(value, axis, [(i, (i + step) % size) for i in range(size)])  38.3 us
    ppermute x17, starting transfers between devices, shifted(): lax.ppermute(value, axis, [(i, (i + step) % size) for i in range(size)])  33.5 us
    all_gather x1, waiting for transfers between devices, per_device(): act_sq = lax.all_gather(act_chip, ('x', 'z_lo'), axis=0, tiled=False)  32.1 us
    all_to_all x2, starting transfers between devices, exchanged(): lax.all_to_all(partial.reshape(16, columns // 16, tokens), ('x', 'y'), 0,...  14.4 us
    all_to_all x1, blocking collectives, per_device(): out = lax.all_to_all(out, 'x', 0, 0, tiled=True)  12.6 us
    unnamed x24, local copies, waits for them, and re-layouts  9.88 us
    all_to_all x1, starting transfers between devices, per_device(): got_first = lax.all_to_all(first, ('x', 'y'), 0, 0, tiled=True)  7.54 us
    pallas_call x2, Pallas kernels, grad_partials(): pl.pallas_call(lambda *refs: grad_kernel(len(parts), *refs), grid=(column...  6.93 us
  transfers between devices with their start and end apart: 21, of which 16 were waited for; matrix products, arithmetic and copies ran while one was open for 1% of the time, Pallas kernels for 5%

profile of v3, /device:TPU:16, one launch (start us, length us, event | category | flops | bytes accessed | tf_op | source)
XLA Modules:
  0.0 182.7 jit_solution(14771555844763983705)
XLA Ops:
  7.8 1.5 collective-permute-done.2.other
  9.3 1.6 copy-done.5
  11.7 4.0 %first.1 = bf16[16,240,256]{2,1,0:T(8,128)(2,1)S(1)} custom-call(s32[1]{0:T(128)} %bitcast.3.place, f32[1,8192]{1,0:T(1,128)S(1)} %bitcast.13, bf16[128,896]{1,0:T(8,128)(2,1)S(1)} %fusion.4.own, bf16[128,896]{1,0:T(8,128)(2,1)S(1)} %collective-permute-done.2.other, bf16[128,8192]{1,0:T(8,128)(2,1)S(1)} %copy-done.5, bf16[256,4096]{1,0:T(8,128)(2,1)} %act_at.1, ...), custom_call_target="tpu_custom_call" | custom-call | tf_op jit(solution)/shard_map/first/pallas_call | solution.py:83
  15.7 1.3 copy-done.1
  17.0 7.5 %all-to-all-start = ((bf16[16,240,256]{2,1,0:T(8,128)(2,1)}), bf16[16,240,256]{2,1,0:T(8,128)(2,1)}, u32[]{:S(2)}, u32[]{:S(2)}) async-start(bf16[16,240,256]{2,1,0:T(8,128)(2,1)} %copy-done.1), calls=%async_computation | async-start | bytes 3932160 | tf_op jit(solution)/shard_map/all_to_all | solution.py:248
  24.5 1.9 %collective-permute-start.9 = (bf16[128,896]{1,0:T(8,128)(2,1)S(1)}, bf16[128,896]{1,0:T(8,128)(2,1)S(1)}, u32[]{:S(2)}, u32[]{:S(2)}) collective-permute-start(bf16[128,896]{1,0:T(8,128)(2,1)S(1)} %fusion.4.own), channel_id=1, source_target_pairs={{0,2},{2,4},{4,6},{6,0},{1,3},{3,5},{5,7},{7,1},{8,10},{10,12},{12... | collective-permute-start | bytes 688136 | tf_op jit(solution)/shard_map/ppermute | solution.py:21
  26.4 3.3 %collective-permute-start.11 = (bf16[128,896]{1,0:T(8,128)(2,1)S(1)}, bf16[128,896]{1,0:T(8,128)(2,1)S(1)}, u32[]{:S(2)}, u32[]{:S(2)}) collective-permute-start(bf16[128,896]{1,0:T(8,128)(2,1)S(1)} %fusion.4.own), channel_id=1, source_target_pairs={{0,4},{2,6},{4,0},{6,2},{1,5},{3,7},{5,1},{7,3},{8,12},{10,14},{12... | collective-permute-start | bytes 688136 | tf_op jit(solution)/shard_map/ppermute | solution.py:21
  29.7 6.0 %collective-permute-done.9.refs_0_ = bf16[128,896]{1,0:T(8,128)(2,1)S(1)} collective-permute-done((bf16[128,896]{1,0:T(8,128)(2,1)S(1)}, bf16[128,896]{1,0:T(8,128)(2,1)S(1)}, u32[]{:S(2)}, u32[]{:S(2)}) %collective-permute-start.9) | collective-permute-done | bytes 229408 | tf_op jit(solution)/shard_map/ppermute | solution.py:21
  35.7 8.6 %collective-permute-done.11.refs_2_ = bf16[128,896]{1,0:T(8,128)(2,1)S(1)} collective-permute-done((bf16[128,896]{1,0:T(8,128)(2,1)S(1)}, bf16[128,896]{1,0:T(8,128)(2,1)S(1)}, u32[]{:S(2)}, u32[]{:S(2)}) %collective-permute-start.11) | collective-permute-done | bytes 229408 | tf_op jit(solution)/shard_map/ppermute | solution.py:21
  44.4 1.4 collective-permute-done.12.refs_3_
  45.8 4.0 %grad.3 = bf16[1792,512]{1,0:T(8,128)(2,1)S(1)} custom-call(bf16[128,896]{1,0:T(8,128)(2,1)S(1)} %collective-permute-done.9.refs_0_, bf16[128,896]{1,0:T(8,128)(2,1)S(1)} %collective-permute-done.10.refs_1_, bf16[128,896]{1,0:T(8,128)(2,1)S(1)} %collective-permute-done.11.refs_2_, bf16[128,896]{1,0:T(8,128)(2,1)S(1)} %collective-permute-done.12.refs_3_, ...), custom_call_target="tpu_custom_call" | custom-call | tf_op jit(solution)/shard_map/grad/pallas_call | solution.py:119
  49.8 1.2 copy-done.2
  51.2 7.1 %all-to-all-start.2 = ((bf16[16,112,512]{2,1,0:T(8,128)(2,1)}), bf16[16,112,512]{2,1,0:T(8,128)(2,1)}, u32[]{:S(2)}, u32[]{:S(2)}) async-start(bf16[16,112,512]{2,1,0:T(8,128)(2,1)} %bitcast.9), calls=%async_computation.2 | async-start | bytes 3670016 | tf_op jit(solution)/shard_map/all_to_all | solution.py:195
  58.3 1.8 spread_sum.1
  60.1 7.3 %collective-permute-start.3 = (bf16[176,256]{1,0:T(8,128)(2,1)S(1)}, bf16[176,256]{1,0:T(8,128)(2,1)S(1)}, u32[]{:S(2)}, u32[]{:S(2)}) collective-permute-start(bf16[176,256]{1,0:T(8,128)(2,1)S(1)} %get-tuple-element.12), channel_id=1, source_target_pairs={{0,128},{128,0},{1,129},{129,1},{2,130},{130,2},{3,131},{131,3},{4... | collective-permute-start | bytes 270344 | tf_op jit(solution)/shard_map/ppermute | solution.py:21
  67.4 2.6 %collective-permute-done.3.got = bf16[176,256]{1,0:T(8,128)(2,1)S(1)} collective-permute-done((bf16[176,256]{1,0:T(8,128)(2,1)S(1)}, bf16[176,256]{1,0:T(8,128)(2,1)S(1)}, u32[]{:S(2)}, u32[]{:S(2)}) %collective-permute-start.3) | collective-permute-done | bytes 90144 | tf_op jit(solution)/shard_map/ppermute | solution.py:21
  72.0 4.2 %collective-permute-start = (bf16[128,896]{1,0:T(8,128)(2,1)S(1)}, bf16[128,896]{1,0:T(8,128)(2,1)S(1)}, u32[]{:S(2)}, u32[]{:S(2)}) collective-permute-start(bf16[128,896]{1,0:T(8,128)(2,1)S(1)} %fusion.4.own), channel_id=1, source_target_pairs={{0,6},{2,0},{4,2},{6,4},{1,7},{3,1},{5,3},{7,5},{8,14},{10,8},{12,... | collective-permute-start | bytes 688136 | tf_op jit(solution)/shard_map/ppermute | solution.py:21
  76.2 5.2 %collective-permute-done.refs_0_ = bf16[128,896]{1,0:T(8,128)(2,1)S(1)} collective-permute-done((bf16[128,896]{1,0:T(8,128)(2,1)S(1)}, bf16[128,896]{1,0:T(8,128)(2,1)S(1)}, u32[]{:S(2)}, u32[]{:S(2)}) %collective-permute-start) | collective-permute-done | bytes 229408 | tf_op jit(solution)/shard_map/ppermute | solution.py:21
  81.4 1.5 collective-permute-done.1.refs_1_
  83.7 3.0 %grad.2 = bf16[1792,256]{1,0:T(8,128)(2,1)S(1)} custom-call(bf16[128,896]{1,0:T(8,128)(2,1)S(1)} %collective-permute-done.refs_0_, bf16[128,896]{1,0:T(8,128)(2,1)S(1)} %collective-permute-done.1.refs_1_, bf16[896,1792]{1,0:T(8,128)(2,1)S(1)} %copy-done, bf16[256,128]{1,0:T(8,128)(2,1)S(1)} %copy-done.7), custom_call_target="tpu_custom_call" | custom-call | tf_op jit(solution)/shard_map/grad/pallas_call | solution.py:119
  87.6 7.3 %all-to-all-start.1 = ((bf16[16,112,256]{2,1,0:T(8,128)(2,1)}), bf16[16,112,256]{2,1,0:T(8,128)(2,1)S(1)}, u32[]{:S(2)}, u32[]{:S(2)}) async-start(bf16[16,112,256]{2,1,0:T(8,128)(2,1)} %bitcast.12), calls=%async_computation.1 | async-start | bytes 1835008 | tf_op jit(solution)/shard_map/all_to_all | solution.py:195
  94.9 1.8 convert_reduce_fusion
  96.7 4.7 %collective-permute-start.13 = (bf16[112,512]{1,0:T(8,128)(2,1)S(1)}, bf16[112,512]{1,0:T(8,128)(2,1)S(1)}, u32[]{:S(2)}, u32[]{:S(2)}) collective-permute-start(bf16[112,512]{1,0:T(8,128)(2,1)S(1)} %convert_element_type.41), channel_id=1, source_target_pairs={{0,128},{128,0},{1,129},{129,1},{2,130},{130,2},{3,131},{131,3},{4... | collective-permute-start | bytes 344072 | tf_op jit(solution)/shard_map/ppermute | solution.py:21
  101.5 6.7 %collective-permute-done.13 = bf16[112,512]{1,0:T(8,128)(2,1)S(1)} collective-permute-done((bf16[112,512]{1,0:T(8,128)(2,1)S(1)}, bf16[112,512]{1,0:T(8,128)(2,1)S(1)}, u32[]{:S(2)}, u32[]{:S(2)}) %collective-permute-start.13) | collective-permute-done | bytes 114720 | tf_op jit(solution)/shard_map/ppermute | solution.py:21
  108.2 2.4 %all-to-all-done.1 = bf16[16,112,256]{2,1,0:T(8,128)(2,1)S(1)} async-done(((bf16[16,112,256]{2,1,0:T(8,128)(2,1)}), bf16[16,112,256]{2,1,0:T(8,128)(2,1)S(1)}, u32[]{:S(2)}, u32[]{:S(2)}) %all-to-all-start.1) | async-done | bytes 917536 | tf_op jit(solution)/shard_map/all_to_all | solution.py:195
  110.8 4.2 %collective-permute-start.5 = (bf16[112,256]{1,0:T(8,128)(2,1)S(1)}, bf16[112,256]{1,0:T(8,128)(2,1)S(1)}, u32[]{:S(2)}, u32[]{:S(2)}) collective-permute-start(bf16[112,256]{1,0:T(8,128)(2,1)S(1)} %convert_element_type.37), channel_id=1, source_target_pairs={{0,128},{128,0},{1,129},{129,1},{2,130},{130,2},{3,131},{131,3},{4... | collective-permute-start | bytes 172040 | tf_op jit(solution)/shard_map/ppermute | solution.py:21
  115.0 1.2 collective-permute-start.14
  116.2 2.0 %collective-permute-start.15 = (bf16[112,768]{1,0:T(8,128)(2,1)S(1)}, bf16[112,768]{1,0:T(8,128)(2,1)S(1)}, u32[]{:S(2)}, u32[]{:S(2)}) collective-permute-start(bf16[112,768]{1,0:T(8,128)(2,1)S(1)} %pad_maximum_fusion.refs_1_), channel_id=1, source_target_pairs={{0,16},{8,24},{16,0},{24,8},{1,17},{9,25},{17,1},{25,9},{2,18},{10... | collective-permute-start | bytes 516104 | tf_op jit(solution)/shard_map/ppermute | solution.py:21
  118.2 2.1 %collective-permute-start.16 = (bf16[112,768]{1,0:T(8,128)(2,1)S(1)}, bf16[112,768]{1,0:T(8,128)(2,1)S(1)}, u32[]{:S(2)}, u32[]{:S(2)}) collective-permute-start(bf16[112,768]{1,0:T(8,128)(2,1)S(1)} %pad_maximum_fusion.refs_1_), channel_id=1, source_target_pairs={{0,24},{8,0},{16,8},{24,16},{1,25},{9,1},{17,9},{25,17},{2,26},{10... | collective-permute-start | bytes 516104 | tf_op jit(solution)/shard_map/ppermute | solution.py:21
  124.0 1.7 collective-permute-done.15.refs_3_
  126.8 32.1 %all-gather.3.cloned.1.call-done = bf16[4096,128]{1,0:T(8,128)(2,1)} async-done(((bf16[256,128]{1,0:T(8,128)(2,1)}), bf16[4096,128]{1,0:T(8,128)(2,1)}) %all-gather.3.cloned.1.call-update) | async-done | bytes 1048592 | tf_op jit(solution)/shard_map/all_gather | solution.py:252
  162.3 12.6 %all_to_all.20 = f32[4,448,128]{2,1,0:T(8,128)S(1)} all-to-all(f32[4,448,128]{2,1,0:T(8,128)S(1)} %correct.3), channel_id=1, replica_groups=mesh['z_hi'=2,'x'=4,'y'=4,'z_lo'=4,'core'=2] {'x'}, dimensions={0} | all-to-all | bytes 1835008 | tf_op jit(solution)/shard_map/all_to_all | solution.py:258
  (53 shorter events, 15.4 us)
Async XLA Ops:
  7.7 1.6 collective-permute-start.2
  9.3 1.6 copy-start.5
  10.9 0.8 copy-start.10
  15.7 1.3 copy-start.1
  17.0 28.8 %copy-start = (bf16[896,1792]{1,0:T(8,128)(2,1)S(1)}, bf16[896,1792]{1,0:T(8,128)(2,1)}, u32[]{:S(2)}) copy-start(bf16[896,1792]{1,0:T(8,128)(2,1)} %refs_4_.1) | copy-start | bytes 9633796
  17.0 34.2 %all-to-all-start = ((bf16[16,240,256]{2,1,0:T(8,128)(2,1)}), bf16[16,240,256]{2,1,0:T(8,128)(2,1)}, u32[]{:S(2)}, u32[]{:S(2)}) async-start(bf16[16,240,256]{2,1,0:T(8,128)(2,1)} %copy-done.1), calls=%async_computation | async-start | bytes 3932160 | tf_op jit(solution)/shard_map/all_to_all | solution.py:248
  24.5 11.2 %collective-permute-start.9 = (bf16[128,896]{1,0:T(8,128)(2,1)S(1)}, bf16[128,896]{1,0:T(8,128)(2,1)S(1)}, u32[]{:S(2)}, u32[]{:S(2)}) collective-permute-start(bf16[128,896]{1,0:T(8,128)(2,1)S(1)} %fusion.4.own), channel_id=1, source_target_pairs={{0,2},{2,4},{4,6},{6,0},{1,3},{3,5},{5,7},{7,1},{8,10},{10,12},{12... | collective-permute-start | bytes 688136 | tf_op jit(solution)/shard_map/ppermute | solution.py:21
  26.4 17.9 %collective-permute-start.11 = (bf16[128,896]{1,0:T(8,128)(2,1)S(1)}, bf16[128,896]{1,0:T(8,128)(2,1)S(1)}, u32[]{:S(2)}, u32[]{:S(2)}) collective-permute-start(bf16[128,896]{1,0:T(8,128)(2,1)S(1)} %fusion.4.own), channel_id=1, source_target_pairs={{0,4},{2,6},{4,0},{6,2},{1,5},{3,7},{5,1},{7,3},{8,12},{10,14},{12... | collective-permute-start | bytes 688136 | tf_op jit(solution)/shard_map/ppermute | solution.py:21
  35.7 8.7 %collective-permute-start.10 = (bf16[128,896]{1,0:T(8,128)(2,1)S(1)}, bf16[128,896]{1,0:T(8,128)(2,1)S(1)}, u32[]{:S(2)}, u32[]{:S(2)}) collective-permute-start(bf16[128,896]{1,0:T(8,128)(2,1)S(1)} %collective-permute-done.9.refs_0_), channel_id=1, source_target_pairs={{0,1},{1,0},{2,3},{3,2},{4,5},{5,4},{6,7},{7,6},{8,9},{9,8},{10,11... | collective-permute-start | bytes 688136 | tf_op jit(solution)/shard_map/ppermute | solution.py:21
  44.3 1.5 collective-permute-start.12
  49.8 1.2 copy-start.2
  51.2 36.5 %all-to-all-start.2 = ((bf16[16,112,512]{2,1,0:T(8,128)(2,1)}), bf16[16,112,512]{2,1,0:T(8,128)(2,1)}, u32[]{:S(2)}, u32[]{:S(2)}) async-start(bf16[16,112,512]{2,1,0:T(8,128)(2,1)} %bitcast.9), calls=%async_computation.2 | async-start | bytes 3670016 | tf_op jit(solution)/shard_map/all_to_all | solution.py:195
  58.3 100.7 %all-gather.3.cloned.1.call-start = ((), (), s32[]{:S(2)}) async-start(), calls=%async_computation.4 | async-start | bytes 1114112 | tf_op jit(solution)/shard_map/all_gather | solution.py:252
  60.1 9.9 %collective-permute-start.3 = (bf16[176,256]{1,0:T(8,128)(2,1)S(1)}, bf16[176,256]{1,0:T(8,128)(2,1)S(1)}, u32[]{:S(2)}, u32[]{:S(2)}) collective-permute-start(bf16[176,256]{1,0:T(8,128)(2,1)S(1)} %get-tuple-element.12), channel_id=1, source_target_pairs={{0,128},{128,0},{1,129},{129,1},{2,130},{130,2},{3,131},{131,3},{4... | collective-permute-start | bytes 270344 | tf_op jit(solution)/shard_map/ppermute | solution.py:21
  70.0 0.6 copy-start.8
  70.0 1.3 collective-permute-start.4
  71.3 0.6 copy-start.6
  72.0 9.4 %collective-permute-start = (bf16[128,896]{1,0:T(8,128)(2,1)S(1)}, bf16[128,896]{1,0:T(8,128)(2,1)S(1)}, u32[]{:S(2)}, u32[]{:S(2)}) collective-permute-start(bf16[128,896]{1,0:T(8,128)(2,1)S(1)} %fusion.4.own), channel_id=1, source_target_pairs={{0,6},{2,0},{4,2},{6,4},{1,7},{3,1},{5,3},{7,5},{8,14},{10,8},{12,... | collective-permute-start | bytes 688136 | tf_op jit(solution)/shard_map/ppermute | solution.py:21
  81.4 1.5 collective-permute-start.1
  82.9 0.8 copy-start.7
  86.7 0.9 copy-start.4
  87.6 23.0 %all-to-all-start.1 = ((bf16[16,112,256]{2,1,0:T(8,128)(2,1)}), bf16[16,112,256]{2,1,0:T(8,128)(2,1)S(1)}, u32[]{:S(2)}, u32[]{:S(2)}) async-start(bf16[16,112,256]{2,1,0:T(8,128)(2,1)} %bitcast.12), calls=%async_computation.1 | async-start | bytes 1835008 | tf_op jit(solution)/shard_map/all_to_all | solution.py:195
  94.9 20.0 %copy-start.9 = (bf16[112,256]{1,0:T(8,128)(2,1)S(1)}, bf16[112,256]{1,0:T(8,128)(2,1)}, u32[]{:S(2)}) copy-start(bf16[112,256]{1,0:T(8,128)(2,1)} %copy-done.8) | copy-start | bytes 172036
  96.7 11.4 %collective-permute-start.13 = (bf16[112,512]{1,0:T(8,128)(2,1)S(1)}, bf16[112,512]{1,0:T(8,128)(2,1)S(1)}, u32[]{:S(2)}, u32[]{:S(2)}) collective-permute-start(bf16[112,512]{1,0:T(8,128)(2,1)S(1)} %convert_element_type.41), channel_id=1, source_target_pairs={{0,128},{128,0},{1,129},{129,1},{2,130},{130,2},{3,131},{131,3},{4... | collective-permute-start | bytes 344072 | tf_op jit(solution)/shard_map/ppermute | solution.py:21
  110.8 9.9 %collective-permute-start.5 = (bf16[112,256]{1,0:T(8,128)(2,1)S(1)}, bf16[112,256]{1,0:T(8,128)(2,1)S(1)}, u32[]{:S(2)}, u32[]{:S(2)}) collective-permute-start(bf16[112,256]{1,0:T(8,128)(2,1)S(1)} %convert_element_type.37), channel_id=1, source_target_pairs={{0,128},{128,0},{1,129},{129,1},{2,130},{130,2},{3,131},{131,3},{4... | collective-permute-start | bytes 172040 | tf_op jit(solution)/shard_map/ppermute | solution.py:21
  115.0 7.9 %collective-permute-start.14 = (bf16[112,768]{1,0:T(8,128)(2,1)S(1)}, bf16[112,768]{1,0:T(8,128)(2,1)S(1)}, u32[]{:S(2)}, u32[]{:S(2)}) collective-permute-start(bf16[112,768]{1,0:T(8,128)(2,1)S(1)} %pad_maximum_fusion.refs_1_), channel_id=1, source_target_pairs={{0,8},{8,16},{16,24},{24,0},{1,9},{9,17},{17,25},{25,1},{2,10},{10... | collective-permute-start | bytes 516104 | tf_op jit(solution)/shard_map/ppermute | solution.py:21
  116.2 9.5 %collective-permute-start.15 = (bf16[112,768]{1,0:T(8,128)(2,1)S(1)}, bf16[112,768]{1,0:T(8,128)(2,1)S(1)}, u32[]{:S(2)}, u32[]{:S(2)}) collective-permute-start(bf16[112,768]{1,0:T(8,128)(2,1)S(1)} %pad_maximum_fusion.refs_1_), channel_id=1, source_target_pairs={{0,16},{8,24},{16,0},{24,8},{1,17},{9,25},{17,1},{25,9},{2,18},{10... | collective-permute-start | bytes 516104 | tf_op jit(solution)/shard_map/ppermute | solution.py:21
  118.2 8.5 %collective-permute-start.16 = (bf16[112,768]{1,0:T(8,128)(2,1)S(1)}, bf16[112,768]{1,0:T(8,128)(2,1)S(1)}, u32[]{:S(2)}, u32[]{:S(2)}) collective-permute-start(bf16[112,768]{1,0:T(8,128)(2,1)S(1)} %pad_maximum_fusion.refs_1_), channel_id=1, source_target_pairs={{0,24},{8,0},{16,8},{24,16},{1,25},{9,1},{17,9},{25,17},{2,26},{10... | collective-permute-start | bytes 516104 | tf_op jit(solution)/shard_map/ppermute | solution.py:21
  120.7 40.7 %collective-permute-start.6 = (bf16[112,256]{1,0:T(8,128)(2,1)S(1)}, bf16[112,256]{1,0:T(8,128)(2,1)S(1)}, u32[]{:S(2)}, u32[]{:S(2)}) collective-permute-start(bf16[112,256]{1,0:T(8,128)(2,1)S(1)} %multiply_convert_fusion.1.refs_1_), channel_id=1, source_target_pairs={{0,8},{8,16},{16,24},{24,0},{1,9},{9,17},{17,25},{25,1},{2,10},{10... | collective-permute-start | bytes 172040 | tf_op jit(solution)/shard_map/ppermute | solution.py:21
  121.9 39.5 %collective-permute-start.7 = (bf16[112,256]{1,0:T(8,128)(2,1)S(1)}, bf16[112,256]{1,0:T(8,128)(2,1)S(1)}, u32[]{:S(2)}, u32[]{:S(2)}) collective-permute-start(bf16[112,256]{1,0:T(8,128)(2,1)S(1)} %multiply_convert_fusion.1.refs_1_), channel_id=1, source_target_pairs={{0,16},{8,24},{16,0},{24,8},{1,17},{9,25},{17,1},{25,9},{2,18},{10... | collective-permute-start | bytes 172040 | tf_op jit(solution)/shard_map/ppermute | solution.py:21
  122.9 38.5 %collective-permute-start.8 = (bf16[112,256]{1,0:T(8,128)(2,1)S(1)}, bf16[112,256]{1,0:T(8,128)(2,1)S(1)}, u32[]{:S(2)}, u32[]{:S(2)}) collective-permute-start(bf16[112,256]{1,0:T(8,128)(2,1)S(1)} %multiply_convert_fusion.1.refs_1_), channel_id=1, source_target_pairs={{0,24},{8,0},{16,8},{24,16},{1,25},{9,1},{17,9},{25,17},{2,26},{10... | collective-permute-start | bytes 172040 | tf_op jit(solution)/shard_map/ppermute | solution.py:21
  158.9 1.2 copy-start.3
Sparse Core Ops, SparseCore 0:
  72.1 86.7 all-gather.2

commit v4 on v0

v4 whole, which is shorter than its diff:
```python
import jax
import jax.numpy as jnp
from jax import lax
from jax.experimental import pallas as pl
from jax.experimental.pallas import tpu as pltpu
from jax.sharding import Mesh
from jax.sharding import PartitionSpec as P

AXES = ("z_hi", "x", "y", "z_lo", "core")
SIZES = (2, 4, 4, 4, 2)
DP = ("z_hi", "x", "y")
TENSOR = ("z_lo", "core")
SMEM = pl.BlockSpec(memory_space=pltpu.SMEM)
VMEM = pl.BlockSpec(memory_space=pltpu.VMEM)
ANY = pl.BlockSpec(memory_space=pl.ANY)
PARAMS = pltpu.CompilerParams(vmem_limit_bytes=32 * 1024 * 1024)
WHOLE = pltpu.CompilerParams(vmem_limit_bytes=60 * 1024 * 1024)


def shifted(value, axis, step):
    size = SIZES[AXES.index(axis)]
    return lax.ppermute(value, axis, [(i, (i + step) % size) for i in range(size)])


def act_kernel(place, gain, hidden_at, basis_at, out_at, hidden, basis, out, sems):
    tokens, features = hidden.shape
    depth = basis.shape[0]
    strip = tokens // 4
    loads = [
        pltpu.make_async_copy(hidden_at.at[here], hidden.at[here], sems.at[i])
        for i, here in enumerate(pl.ds(at, strip) for at in range(0, tokens, strip))
    ]
    load_basis = pltpu.make_async_copy(basis_at, basis, sems.at[4])
    for load in loads:
        load.start()
    load_basis.start()
    stats = []
    for i, load in enumerate(loads):
        load.wait()
        squares = jnp.zeros((strip, 128), jnp.float32)
        for at in range(0, features, 128):
            wide = hidden[i * strip : (i + 1) * strip, at : at + 128].astype(jnp.float32)
            squares += wide * wide
        stats.append(jnp.sum(squares, axis=-1, keepdims=True) / features)
    stat = jnp.concatenate(stats, axis=0)
    mine = pl.ds(pl.multiple_of(place[0] * depth, depth), depth)
    scaled = hidden[:, mine].astype(jnp.float32) * lax.rsqrt(stat + 1e-05)
    normed = (scaled * gain[:, mine]).astype(jnp.bfloat16)
    load_basis.wait()
    block = basis.shape[1] // 32
    stores = []
    for x in range(4):
        for z_hi in range(2):
            at = (z_hi * 16 + x * 4) * block
            part = jnp.dot(
                normed, basis[:, at : at + 4 * block], preferred_element_type=jnp.float32
            )
            for y in range(4):
                here = part[:, y * block : (y + 1) * block]
                to = slice(z_hi * block, (z_hi + 1) * block)
                out[x * 4 + y, :, to] = here.astype(jnp.bfloat16)
        here = pl.ds(x * 4, 4)
        stores.append(pltpu.make_async_copy(out.at[here], out_at.at[here], sems.at[5 + x]))
        stores[-1].start()
    for store in stores:
        store.wait()


def act_partials(hidden, norm_gain, act_basis):
    tokens = hidden.shape[0]
    shape = (16, tokens, act_basis.shape[1] // 16)
    place = lax.axis_index(DP).astype(jnp.int32).reshape(1)
    return pl.pallas_call(
        act_kernel,
        out_shape=pltpu.HBM(shape, jnp.bfloat16),
        in_specs=[SMEM, VMEM, ANY, ANY],
        out_specs=ANY,
        scratch_shapes=[
            pltpu.VMEM(hidden.shape, jnp.bfloat16),
            pltpu.VMEM(act_basis.shape, jnp.bfloat16),
            pltpu.VMEM(shape, jnp.bfloat16),
            pltpu.SemaphoreType.DMA((9,)),
        ],
        compiler_params=WHOLE,
        name="act",
    )(place, norm_gain.reshape(1, -1), hidden, act_basis)


def grad_kernel(count, *refs):
    parts, basis, out_at, rows, out, sem = refs[:count], refs[count], *refs[-4:]
    at = 0
    for part in parts:
        rows[at : at + part.shape[0], :] = part[...]
        at += part.shape[0]
    stores = []
    for at in range(0, basis.shape[1], 256):
        here = pl.ds(at, 256)
        part = jnp.dot(rows[...], basis[:, here], preferred_element_type=jnp.float32)
        out[here, :] = part.T.astype(jnp.bfloat16)
        stores.append(
            pltpu.make_async_copy(out.at[here], out_at.at[here], sem.at[at // 256])
        )
        stores[-1].start()
    for store in stores:
        store.wait()


def grad_partials(parts, basis, *after):
    depth, columns = basis.shape
    tokens = sum(part.shape[0] for part in parts)
    shape = (columns, tokens)
    return pl.pallas_call(
        lambda *refs: grad_kernel(len(parts), *refs),
        out_shape=pltpu.HBM(shape, jnp.bfloat16),
        in_specs=[VMEM] * (len(parts) + 1) + [ANY] * len(after),
        out_specs=ANY,
        scratch_shapes=[
            pltpu.VMEM((tokens, depth), jnp.bfloat16),
            pltpu.VMEM(shape, jnp.bfloat16),
            pltpu.SemaphoreType.DMA((columns // 256,)),
        ],
        compiler_params=PARAMS,
        name="grad",
    )(*parts, basis, *after)


def act_sum_kernel(place, got, kept, given):
    total = got[0].astype(jnp.float32)
    for source in range(1, got.shape[0]):
        total += got[source].astype(jnp.float32)
    low, high = total[:, : kept.shape[1]], total[:, kept.shape[1] :]
    first = place[0] == 0
    kept[...] = jnp.where(first, low, high)
    given[...] = jnp.where(first, high, low)


def act_squares(partials):
    got = lax.all_to_all(partials, ("x", "y"), 0, 0, tiled=True)
    _, tokens, wide = got.shape
    half = jax.ShapeDtypeStruct((tokens, wide // 2), jnp.float32)
    place = lax.axis_index("z_hi").astype(jnp.int32).reshape(1)
    kept, given = pl.pallas_call(
        act_sum_kernel,
        out_shape=(half, half),
        in_specs=[SMEM, VMEM],
        out_specs=(VMEM, VMEM),
        compiler_params=PARAMS,
        name="act_sum",
    )(place, got)
    total = kept + shifted(given, "z_hi", 1)
    square = (total * total).astype(jnp.bfloat16)
    row = [square] + [shifted(square, "x", step) for step in (1, 2, 3)]
    spread = lax.all_gather(jnp.stack(row), TENSOR, axis=0, tiled=False)
    return row, spread.reshape(4, 2, 4, tokens, wide // 2)


def gate_kernel(*refs):
    del refs


def gated(value, *after):
    return pl.pallas_call(
        gate_kernel,
        out_shape=pltpu.HBM(value.shape, value.dtype),
        in_specs=[ANY] * (1 + len(after)),
        out_specs=ANY,
        input_output_aliases={0: 0},
        compiler_params=PARAMS,
        name="gate",
    )(value, *after)


def exchanged(partial):
    columns, tokens = partial.shape
    return lax.all_to_all(partial.reshape(16, columns // 16, tokens), ("x", "y"), 0, 0, tiled=True)


def squared(got):
    summed = jnp.sum(got.astype(jnp.float32), axis=0)
    total = summed + shifted(summed.astype(jnp.bfloat16), "z_hi", 1).astype(jnp.float32)
    return (total * total).astype(jnp.bfloat16)


def correct_kernel(steps, *refs):
    place, *pieces, act_sq, out, act = refs
    pieces, before = pieces[:4], pieces[4:]
    tokens, block = act_sq.shape[3:]
    at = 0
    for step in steps:
        chip = lax.rem(place[0] + 4 - step, 4)
        for flip in range(2):
            core = lax.rem(place[1] + flip, 2)
            for behind in range(4):
                to = slice(behind * block, (behind + 1) * block)
                act[at : at + tokens, to] = act_sq[chip, core, behind]
            at += tokens
    rows = pieces[0].shape[0]
    for y_behind, piece in enumerate(pieces):
        part = jnp.dot(piece[...], act[...], preferred_element_type=jnp.float32)
        part = part * (1.0 / (8 * tokens))
        at = pl.ds(pl.multiple_of(lax.rem(place[3] + 4 - y_behind, 4) * rows, rows), rows)
        for behind in range(4):
            x = lax.rem(place[2] + 4 - behind, 4)
            here = part[:, behind * block : (behind + 1) * block]
            if before:
                here = before[0][x, at, :] + here
            out[x, at, :] = here


def corrected(steps, grad_sq, act_sq, *before):
    rows, tokens = grad_sq.shape
    block = act_sq.shape[4]
    place = jnp.stack([lax.axis_index(a) for a in ("z_lo", "core", "x", "y")]).astype(jnp.int32)
    pieces = [grad_sq] + [shifted(grad_sq, "y", step) for step in (1, 2, 3)]
    return pl.pallas_call(
        lambda *refs: correct_kernel(steps, *refs),
        out_shape=jax.ShapeDtypeStruct((4, 4 * rows, block), jnp.float32),
        in_specs=[SMEM] + [VMEM] * (5 + len(before)),
        out_specs=VMEM,
        scratch_shapes=[pltpu.VMEM((tokens, 4 * block), jnp.bfloat16)],
        compiler_params=PARAMS,
        name="correct",
    )(place, *pieces, *before, act_sq)


CHUNKS = ((0, 1), (2, 3))


def per_device(hidden, norm_gain, gate_pre, out_grad, grad_basis, act_basis):
    up_grad = (out_grad.astype(jnp.float32) * jax.nn.silu(gate_pre.astype(jnp.float32))).astype(
        jnp.bfloat16
    )
    moved = [up_grad] + [shifted(up_grad, "z_lo", step) for step in (1, 2, 3)]
    both = [(own, shifted(own, "core", 1)) for own in moved]
    act_row, act_sq = act_squares(act_partials(hidden, norm_gain, act_basis))
    grad_got = []
    for chunk, steps in enumerate(CHUNKS):
        partial = grad_partials([part for step in steps for part in both[step]], grad_basis)
        if chunk:
            partial = gated(partial, *act_row)
        grad_got.append(exchanged(partial))
    out = []
    for steps, got in zip(CHUNKS, grad_got):
        out = [corrected(steps, squared(got), act_sq, *out)]
    out = lax.all_to_all(out[0], "x", 0, 0, tiled=True)
    return out.reshape(grad_basis.shape[1], -1)


def solution(mesh):
    fine = Mesh(mesh.devices.reshape(SIZES), AXES)
    placed = (
        P(TENSOR, None),
        P(),
        P(TENSOR, DP),
        P(TENSOR, DP),
        P(DP, TENSOR),
        P(DP, None),
    )
    return jax.shard_map(
        per_device, mesh=fine, in_specs=placed, out_specs=P(TENSOR, DP), check_vma=False
    )
```

time: 988 us -> 144 us (0.15)
  waiting for transfers between devices: 923 us -> 40.7 us
  starting transfers between devices: 0.09 us -> 51.5 us
  matrix products: 21.8 us -> 0 us
  Pallas kernels: 0 us -> 14.1 us
    psum x1 -> x0, waiting for transfers between devices: 465 us -> none  [per_device(): lax.psum(jnp.dot(grad_rows, grad_basis, preferred_element_type=jnp.float3...]
    reduce_scatter x1 -> x0, waiting for transfers between devices: 422 us -> none  [per_device(): lax.psum_scatter(act_partial, 'dp', scatter_dimension=1, tiled=True)]
    all_gather x1, waiting for transfers between devices: 36.3 us -> 0.02 us  [act_squares(): spread = lax.all_gather(jnp.stack(row), TENSOR, axis=0, tiled=False)]
    ppermute x0 -> x19, starting transfers between devices: none -> 34.2 us  [shifted(): lax.ppermute(value, axis, [(i, (i + step) % size) for i in range(size)])]
    all_to_all x0 -> x3, waiting for transfers between devices: none -> 22.1 us  [the longest x2 17.2 us: exchanged(): lax.all_to_all(partial.reshape(16, columns // 16, tokens), ('x', 'y'), 0,...]
    dot_general x3 -> x0, matrix products: 21.8 us -> none  [the longest x1 8.47 us: per_device(): jnp.dot(grad_rows, grad_basis, preferred_element_type=jnp.float32)]
    all_gather x1 -> x0, blocking collectives: 19.2 us -> none  [per_device(): lax.all_gather(normed_part, 'tensor', axis=0, tiled=True)]
    ppermute x0 -> x19, waiting for transfers between devices: none -> 18.6 us  [shifted(): lax.ppermute(value, axis, [(i, (i + step) % size) for i in range(size)])]
  transfers between devices with their start and end apart: 3 -> 23, of which waited for: 3 -> 10; matrix products, arithmetic and copies ran while one was open for 2% -> 3% of each run, Pallas kernels for 0% -> 6%
where the time goes in v4:
time: 144 us; the launch traced here: 142 us
  starting transfers between devices  51.5 us (36%)
  waiting for transfers between devices  40.7 us (28%)
  blocking collectives  15.5 us (11%)
  Pallas kernels  14.1 us (10%)
  between operations  13.6 us (9%)
  other arithmetic  4.09 us (3%)
  local copies, waits for them, and re-layouts  2.15 us (1%)
    ppermute x19, starting transfers between devices, shifted(): lax.ppermute(value, axis, [(i, (i + step) % size) for i in range(size)])  34.2 us
    ppermute x19, waiting for transfers between devices, shifted(): lax.ppermute(value, axis, [(i, (i + step) % size) for i in range(size)])  18.6 us
    all_to_all x2, waiting for transfers between devices, exchanged(): lax.all_to_all(partial.reshape(16, columns // 16, tokens), ('x', 'y'), 0,...  17.2 us
    all_to_all x1, blocking collectives, per_device(): out = lax.all_to_all(out[0], 'x', 0, 0, tiled=True)  15.5 us
    all_to_all x2, starting transfers between devices, exchanged(): lax.all_to_all(partial.reshape(16, columns // 16, tokens), ('x', 'y'), 0,...  10.2 us
    all_to_all x1, starting transfers between devices, act_squares(): got = lax.all_to_all(partials, ('x', 'y'), 0, 0, tiled=True)  7.09 us
    pallas_call x2, Pallas kernels, grad_partials(): pl.pallas_call(lambda *refs: grad_kernel(len(parts), *refs), out_shape=pl...  6.03 us
    all_to_all x1, waiting for transfers between devices, act_squares(): got = lax.all_to_all(partials, ('x', 'y'), 0, 0, tiled=True)  4.91 us
  transfers between devices with their start and end apart: 23, of which 10 were waited for; matrix products, arithmetic and copies ran while one was open for 3% of the time, Pallas kernels for 6%

profile of v4, /device:TPU:64, one launch (start us, length us, event | category | flops | bytes accessed | tf_op | source)
XLA Modules:
  0.0 141.7 jit_solution(14450587426509601534)
XLA Ops:
  6.5 4.5 %act.1 = bf16[16,128,256]{2,1,0:T(8,128)(2,1)} custom-call(s32[1]{0:T(128)} %bitcast.5.place, f32[1,8192]{1,0:T(1,128)} %bitcast.24, bf16[128,8192]{1,0:T(8,128)(2,1)} %hidden_at.1, bf16[256,4096]{1,0:T(8,128)(2,1)} %basis_at.1), custom_call_target="tpu_custom_call" | custom-call | tf_op jit(solution)/shard_map/act/pallas_call | solution.py:73
  11.1 7.1 %all-to-all-start = ((bf16[16,128,256]{2,1,0:T(8,128)(2,1)}), bf16[16,128,256]{2,1,0:T(8,128)(2,1)}, u32[]{:S(2)}, u32[]{:S(2)}) async-start(bf16[16,128,256]{2,1,0:T(8,128)(2,1)} %act.1), calls=%async_computation | async-start | bytes 2097152 | tf_op jit(solution)/shard_map/all_to_all | solution.py:138
  18.2 1.2 fusion.4.refs_0_
  19.4 2.0 %collective-permute-start.13 = (bf16[128,896]{1,0:T(8,128)(2,1)S(1)}, bf16[128,896]{1,0:T(8,128)(2,1)S(1)}, u32[]{:S(2)}, u32[]{:S(2)}) collective-permute-start(bf16[128,896]{1,0:T(8,128)(2,1)S(1)} %fusion.4.refs_0_), channel_id=1, source_target_pairs={{0,2},{2,4},{4,6},{6,0},{1,3},{3,5},{5,7},{7,1},{8,10},{10,12},{12... | collective-permute-start | bytes 688136 | tf_op jit(solution)/shard_map/ppermute | solution.py:22
  21.4 5.1 %collective-permute-done.13.refs_2_ = bf16[128,896]{1,0:T(8,128)(2,1)S(1)} collective-permute-done((bf16[128,896]{1,0:T(8,128)(2,1)S(1)}, bf16[128,896]{1,0:T(8,128)(2,1)S(1)}, u32[]{:S(2)}, u32[]{:S(2)}) %collective-permute-start.13) | collective-permute-done | bytes 229408 | tf_op jit(solution)/shard_map/ppermute | solution.py:22
  26.5 1.5 %collective-permute-done.14.refs_3_ = bf16[128,896]{1,0:T(8,128)(2,1)S(1)} collective-permute-done((bf16[128,896]{1,0:T(8,128)(2,1)S(1)}, bf16[128,896]{1,0:T(8,128)(2,1)S(1)}, u32[]{:S(2)}, u32[]{:S(2)}) %collective-permute-start.14) | collective-permute-done | bytes 229408 | tf_op jit(solution)/shard_map/ppermute | solution.py:22
  28.0 3.0 %grad.3 = bf16[1792,512]{1,0:T(8,128)(2,1)} custom-call(bf16[128,896]{1,0:T(8,128)(2,1)S(1)} %fusion.4.refs_0_, bf16[128,896]{1,0:T(8,128)(2,1)S(1)} %collective-permute-done.12.refs_1_, bf16[128,896]{1,0:T(8,128)(2,1)S(1)} %collective-permute-done.13.refs_2_, bf16[128,896]{1,0:T(8,128)(2,1)S(1)} %collective-permute-done.14.refs_3_, ...), custom_call_target="tpu_custom_call" | custom-call | tf_op jit(solution)/shard_map/grad/pallas_call | solution.py:112
  31.0 4.9 %all-to-all-done.got = bf16[16,128,256]{2,1,0:T(8,128)(2,1)} async-done(((bf16[16,128,256]{2,1,0:T(8,128)(2,1)}), bf16[16,128,256]{2,1,0:T(8,128)(2,1)}, u32[]{:S(2)}, u32[]{:S(2)}) %all-to-all-start) | async-done | bytes 1048608 | tf_op jit(solution)/shard_map/all_to_all | solution.py:138
  35.9 4.4 %all-to-all-start.2 = ((bf16[16,112,512]{2,1,0:T(8,128)(2,1)}), bf16[16,112,512]{2,1,0:T(8,128)(2,1)}, u32[]{:S(2)}, u32[]{:S(2)}) async-start(bf16[16,112,512]{2,1,0:T(8,128)(2,1)} %bitcast.22), calls=%async_computation.2 | async-start | bytes 3670016 | tf_op jit(solution)/shard_map/all_to_all | solution.py:175
  40.6 3.2 %collective-permute-start.2 = (bf16[128,896]{1,0:T(8,128)(2,1)S(1)}, bf16[128,896]{1,0:T(8,128)(2,1)S(1)}, u32[]{:S(2)}, u32[]{:S(2)}) collective-permute-start(bf16[128,896]{1,0:T(8,128)(2,1)S(1)} %fusion.4.refs_0_), channel_id=1, source_target_pairs={{0,6},{2,0},{4,2},{6,4},{1,7},{3,1},{5,3},{7,5},{8,14},{10,8},{12,... | collective-permute-start | bytes 688136 | tf_op jit(solution)/shard_map/ppermute | solution.py:22
  43.8 1.4 act_sum.1
  45.2 4.6 %collective-permute-start.4 = (f32[128,128]{1,0:T(8,128)S(1)}, f32[128,128]{1,0:T(8,128)S(1)}, u32[]{:S(2)}, u32[]{:S(2)}) collective-permute-start(f32[128,128]{1,0:T(8,128)S(1)} %get-tuple-element.8), channel_id=1, source_target_pairs={{0,128},{128,0},{1,129},{129,1},{2,130},{130,2},{3,131},{131,3},{4... | collective-permute-start | bytes 196616 | tf_op jit(solution)/shard_map/ppermute | solution.py:22
  49.9 6.8 %collective-permute-done.2.refs_2_ = bf16[128,896]{1,0:T(8,128)(2,1)S(1)} collective-permute-done((bf16[128,896]{1,0:T(8,128)(2,1)S(1)}, bf16[128,896]{1,0:T(8,128)(2,1)S(1)}, u32[]{:S(2)}, u32[]{:S(2)}) %collective-permute-start.2) | collective-permute-done | bytes 229408 | tf_op jit(solution)/shard_map/ppermute | solution.py:22
  56.6 2.0 %collective-permute-start.5 = (bf16[128,128]{1,0:T(8,128)(2,1)S(1)}, bf16[128,128]{1,0:T(8,128)(2,1)S(1)}, u32[]{:S(2)}, u32[]{:S(2)}) collective-permute-start(bf16[128,128]{1,0:T(8,128)(2,1)S(1)} %multiply_convert_fusion.2.refs_1_), channel_id=1, source_target_pairs={{0,32},{32,64},{64,96},{96,0},{1,33},{33,65},{65,97},{97,1},{2,34}... | collective-permute-start | bytes 98312 | tf_op jit(solution)/shard_map/ppermute | solution.py:22
  58.6 2.8 %collective-permute-start.6 = (bf16[128,128]{1,0:T(8,128)(2,1)S(1)}, bf16[128,128]{1,0:T(8,128)(2,1)S(1)}, u32[]{:S(2)}, u32[]{:S(2)}) collective-permute-start(bf16[128,128]{1,0:T(8,128)(2,1)S(1)} %multiply_convert_fusion.2.refs_1_), channel_id=1, source_target_pairs={{0,64},{32,96},{64,0},{96,32},{1,65},{33,97},{65,1},{97,33},{2,66}... | collective-permute-start | bytes 98312 | tf_op jit(solution)/shard_map/ppermute | solution.py:22
  61.4 1.4 %collective-permute-start.7 = (bf16[128,128]{1,0:T(8,128)(2,1)S(1)}, bf16[128,128]{1,0:T(8,128)(2,1)S(1)}, u32[]{:S(2)}, u32[]{:S(2)}) collective-permute-start(bf16[128,128]{1,0:T(8,128)(2,1)S(1)} %multiply_convert_fusion.2.refs_1_), channel_id=1, source_target_pairs={{0,96},{32,0},{64,32},{96,64},{1,97},{33,1},{65,33},{97,65},{2,98}... | collective-permute-start | bytes 98312 | tf_op jit(solution)/shard_map/ppermute | solution.py:22
  62.8 3.0 %grad.2.refs_0_ = bf16[1792,512]{1,0:T(8,128)(2,1)} custom-call(bf16[128,896]{1,0:T(8,128)(2,1)S(1)} %collective-permute-done.refs_0_, bf16[128,896]{1,0:T(8,128)(2,1)S(1)} %collective-permute-done.1.refs_1_, bf16[128,896]{1,0:T(8,128)(2,1)S(1)} %collective-permute-done.2.refs_2_, bf16[128,896]{1,0:T(8,128)(2,1)S(1)} %collective-permute-done.3.refs_3_, ...), custom_call_target="tpu_custom_call" | custom-call | tf_op jit(solution)/shard_map/grad/pallas_call | solution.py:112
  65.9 5.8 %all-to-all-start.1 = ((bf16[16,112,512]{2,1,0:T(8,128)(2,1)}), bf16[16,112,512]{2,1,0:T(8,128)(2,1)S(1)}, u32[]{:S(2)}, u32[]{:S(2)}) async-start(bf16[16,112,512]{2,1,0:T(8,128)(2,1)} %bitcast.21), calls=%async_computation.1 | async-start | bytes 3670016 | tf_op jit(solution)/shard_map/all_to_all | solution.py:175
  72.5 1.8 %convert_reduce_fusion = f32[112,512]{1,0:T(8,128)S(1)} fusion(bf16[16,112,512]{2,1,0:T(8,128)(2,1)} %all-to-all-done.2), kind=kLoop, calls=%fused_computation | loop fusion | flops 1777664 | bytes 2064384 | tf_op jit(solution)/shard_map/reduce_sum | solution.py:179
  74.3 6.0 %collective-permute-start.15 = (bf16[112,512]{1,0:T(8,128)(2,1)S(1)}, bf16[112,512]{1,0:T(8,128)(2,1)S(1)}, u32[]{:S(2)}, u32[]{:S(2)}) collective-permute-start(bf16[112,512]{1,0:T(8,128)(2,1)S(1)} %convert_element_type.45), channel_id=1, source_target_pairs={{0,128},{128,0},{1,129},{129,1},{2,130},{130,2},{3,131},{131,3},{4... | collective-permute-start | bytes 344072 | tf_op jit(solution)/shard_map/ppermute | solution.py:22
  80.3 17.2 %all-to-all-done.1 = bf16[16,112,512]{2,1,0:T(8,128)(2,1)S(1)} async-done(((bf16[16,112,512]{2,1,0:T(8,128)(2,1)}), bf16[16,112,512]{2,1,0:T(8,128)(2,1)S(1)}, u32[]{:S(2)}, u32[]{:S(2)}) %all-to-all-start.1) | async-done | bytes 1835040 | tf_op jit(solution)/shard_map/all_to_all | solution.py:175
  97.8 6.0 %collective-permute-start.8 = (bf16[112,512]{1,0:T(8,128)(2,1)S(1)}, bf16[112,512]{1,0:T(8,128)(2,1)S(1)}, u32[]{:S(2)}, u32[]{:S(2)}) collective-permute-start(bf16[112,512]{1,0:T(8,128)(2,1)S(1)} %convert_element_type.41), channel_id=1, source_target_pairs={{0,128},{128,0},{1,129},{129,1},{2,130},{130,2},{3,131},{131,3},{4... | collective-permute-start | bytes 344072 | tf_op jit(solution)/shard_map/ppermute | solution.py:22
  105.1 2.1 %collective-permute-start.18 = (bf16[112,512]{1,0:T(8,128)(2,1)S(1)}, bf16[112,512]{1,0:T(8,128)(2,1)S(1)}, u32[]{:S(2)}, u32[]{:S(2)}) collective-permute-start(bf16[112,512]{1,0:T(8,128)(2,1)S(1)} %multiply_convert_fusion.refs_1_), channel_id=1, source_target_pairs={{0,24},{8,0},{16,8},{24,16},{1,25},{9,1},{17,9},{25,17},{2,26},{10... | collective-permute-start | bytes 344072 | tf_op jit(solution)/shard_map/ppermute | solution.py:22
  107.2 1.9 %collective-permute-done.8 = bf16[112,512]{1,0:T(8,128)(2,1)S(1)} collective-permute-done((bf16[112,512]{1,0:T(8,128)(2,1)S(1)}, bf16[112,512]{1,0:T(8,128)(2,1)S(1)}, u32[]{:S(2)}, u32[]{:S(2)}) %collective-permute-start.8) | collective-permute-done | bytes 114720 | tf_op jit(solution)/shard_map/ppermute | solution.py:22
  109.3 1.8 %collective-permute-start.10 = (bf16[112,512]{1,0:T(8,128)(2,1)S(1)}, bf16[112,512]{1,0:T(8,128)(2,1)S(1)}, u32[]{:S(2)}, u32[]{:S(2)}) collective-permute-start(bf16[112,512]{1,0:T(8,128)(2,1)S(1)} %multiply_convert_fusion.1.refs_1_), channel_id=1, source_target_pairs={{0,16},{8,24},{16,0},{24,8},{1,17},{9,25},{17,1},{25,9},{2,18},{10... | collective-permute-start | bytes 344072 | tf_op jit(solution)/shard_map/ppermute | solution.py:22
  111.1 1.3 collective-permute-done.16.refs_2_
  113.0 1.2 copy-done.1
  114.3 1.1 correct.2.refs_5_
  115.3 1.1 collective-permute-done.9.refs_2_
  117.3 1.1 correct.3
  118.4 15.5 %all_to_all.20 = f32[4,448,128]{2,1,0:T(8,128)S(1)} all-to-all(f32[4,448,128]{2,1,0:T(8,128)S(1)} %correct.3), channel_id=1, replica_groups=mesh['z_hi'=2,'x'=4,'y'=4,'z_lo'=4,'core'=2] {'x'}, dimensions={0} | all-to-all | bytes 1835008 | tf_op jit(solution)/shard_map/all_to_all | solution.py:245
  133.9 0.9 copy.10
  (40 shorter events, 4.5 us)
Async XLA Ops:
  6.5 21.5 %copy-start = (bf16[896,1792]{1,0:T(8,128)(2,1)S(1)}, bf16[896,1792]{1,0:T(8,128)(2,1)}, u32[]{:S(2)}) copy-start(bf16[896,1792]{1,0:T(8,128)(2,1)} %refs_4_.3) | copy-start | bytes 9633796
  11.1 24.9 %all-to-all-start = ((bf16[16,128,256]{2,1,0:T(8,128)(2,1)}), bf16[16,128,256]{2,1,0:T(8,128)(2,1)}, u32[]{:S(2)}, u32[]{:S(2)}) async-start(bf16[16,128,256]{2,1,0:T(8,128)(2,1)} %act.1), calls=%async_computation | async-start | bytes 2097152 | tf_op jit(solution)/shard_map/all_to_all | solution.py:138
  19.4 7.1 %collective-permute-start.13 = (bf16[128,896]{1,0:T(8,128)(2,1)S(1)}, bf16[128,896]{1,0:T(8,128)(2,1)S(1)}, u32[]{:S(2)}, u32[]{:S(2)}) collective-permute-start(bf16[128,896]{1,0:T(8,128)(2,1)S(1)} %fusion.4.refs_0_), channel_id=1, source_target_pairs={{0,2},{2,4},{4,6},{6,0},{1,3},{3,5},{5,7},{7,1},{8,10},{10,12},{12... | collective-permute-start | bytes 688136 | tf_op jit(solution)/shard_map/ppermute | solution.py:22
  21.4 5.2 %collective-permute-start.12 = (bf16[128,896]{1,0:T(8,128)(2,1)S(1)}, bf16[128,896]{1,0:T(8,128)(2,1)S(1)}, u32[]{:S(2)}, u32[]{:S(2)}) collective-permute-start(bf16[128,896]{1,0:T(8,128)(2,1)S(1)} %fusion.4.refs_0_), channel_id=1, source_target_pairs={{0,1},{1,0},{2,3},{3,2},{4,5},{5,4},{6,7},{7,6},{8,9},{9,8},{10,11... | collective-permute-start | bytes 688136 | tf_op jit(solution)/shard_map/ppermute | solution.py:22
  26.5 1.5 %collective-permute-start.14 = (bf16[128,896]{1,0:T(8,128)(2,1)S(1)}, bf16[128,896]{1,0:T(8,128)(2,1)S(1)}, u32[]{:S(2)}, u32[]{:S(2)}) collective-permute-start(bf16[128,896]{1,0:T(8,128)(2,1)S(1)} %collective-permute-done.13.refs_2_), channel_id=1, source_target_pairs={{0,1},{1,0},{2,3},{3,2},{4,5},{5,4},{6,7},{7,6},{8,9},{9,8},{10,11... | collective-permute-start | bytes 688136 | tf_op jit(solution)/shard_map/ppermute | solution.py:22
  35.9 30.0 %all-to-all-start.2 = ((bf16[16,112,512]{2,1,0:T(8,128)(2,1)}), bf16[16,112,512]{2,1,0:T(8,128)(2,1)}, u32[]{:S(2)}, u32[]{:S(2)}) async-start(bf16[16,112,512]{2,1,0:T(8,128)(2,1)} %bitcast.22), calls=%async_computation.2 | async-start | bytes 3670016 | tf_op jit(solution)/shard_map/all_to_all | solution.py:175
  40.4 9.5 %collective-permute-start = (bf16[128,896]{1,0:T(8,128)(2,1)S(1)}, bf16[128,896]{1,0:T(8,128)(2,1)S(1)}, u32[]{:S(2)}, u32[]{:S(2)}) collective-permute-start(bf16[128,896]{1,0:T(8,128)(2,1)S(1)} %fusion.4.refs_0_), channel_id=1, source_target_pairs={{0,4},{2,6},{4,0},{6,2},{1,5},{3,7},{5,1},{7,3},{8,12},{10,14},{12... | collective-permute-start | bytes 688136 | tf_op jit(solution)/shard_map/ppermute | solution.py:22
  40.6 16.0 %collective-permute-start.2 = (bf16[128,896]{1,0:T(8,128)(2,1)S(1)}, bf16[128,896]{1,0:T(8,128)(2,1)S(1)}, u32[]{:S(2)}, u32[]{:S(2)}) collective-permute-start(bf16[128,896]{1,0:T(8,128)(2,1)S(1)} %fusion.4.refs_0_), channel_id=1, source_target_pairs={{0,6},{2,0},{4,2},{6,4},{1,7},{3,1},{5,3},{7,5},{8,14},{10,8},{12,... | collective-permute-start | bytes 688136 | tf_op jit(solution)/shard_map/ppermute | solution.py:22
  45.2 11.4 %collective-permute-start.4 = (f32[128,128]{1,0:T(8,128)S(1)}, f32[128,128]{1,0:T(8,128)S(1)}, u32[]{:S(2)}, u32[]{:S(2)}) collective-permute-start(f32[128,128]{1,0:T(8,128)S(1)} %get-tuple-element.8), channel_id=1, source_target_pairs={{0,128},{128,0},{1,129},{129,1},{2,130},{130,2},{3,131},{131,3},{4... | collective-permute-start | bytes 196616 | tf_op jit(solution)/shard_map/ppermute | solution.py:22
  49.9 13.0 %collective-permute-start.1 = (bf16[128,896]{1,0:T(8,128)(2,1)S(1)}, bf16[128,896]{1,0:T(8,128)(2,1)S(1)}, u32[]{:S(2)}, u32[]{:S(2)}) collective-permute-start(bf16[128,896]{1,0:T(8,128)(2,1)S(1)} %collective-permute-done.refs_0_), channel_id=1, source_target_pairs={{0,1},{1,0},{2,3},{3,2},{4,5},{5,4},{6,7},{7,6},{8,9},{9,8},{10,11... | collective-permute-start | bytes 688136 | tf_op jit(solution)/shard_map/ppermute | solution.py:22
  56.6 6.2 %collective-permute-start.3 = (bf16[128,896]{1,0:T(8,128)(2,1)S(1)}, bf16[128,896]{1,0:T(8,128)(2,1)S(1)}, u32[]{:S(2)}, u32[]{:S(2)}) collective-permute-start(bf16[128,896]{1,0:T(8,128)(2,1)S(1)} %collective-permute-done.2.refs_2_), channel_id=1, source_target_pairs={{0,1},{1,0},{2,3},{3,2},{4,5},{5,4},{6,7},{7,6},{8,9},{9,8},{10,11... | collective-permute-start | bytes 688136 | tf_op jit(solution)/shard_map/ppermute | solution.py:22
  56.6 9.2 %collective-permute-start.5 = (bf16[128,128]{1,0:T(8,128)(2,1)S(1)}, bf16[128,128]{1,0:T(8,128)(2,1)S(1)}, u32[]{:S(2)}, u32[]{:S(2)}) collective-permute-start(bf16[128,128]{1,0:T(8,128)(2,1)S(1)} %multiply_convert_fusion.2.refs_1_), channel_id=1, source_target_pairs={{0,32},{32,64},{64,96},{96,0},{1,33},{33,65},{65,97},{97,1},{2,34}... | collective-permute-start | bytes 98312 | tf_op jit(solution)/shard_map/ppermute | solution.py:22
  58.6 7.3 %collective-permute-start.6 = (bf16[128,128]{1,0:T(8,128)(2,1)S(1)}, bf16[128,128]{1,0:T(8,128)(2,1)S(1)}, u32[]{:S(2)}, u32[]{:S(2)}) collective-permute-start(bf16[128,128]{1,0:T(8,128)(2,1)S(1)} %multiply_convert_fusion.2.refs_1_), channel_id=1, source_target_pairs={{0,64},{32,96},{64,0},{96,32},{1,65},{33,97},{65,1},{97,33},{2,66}... | collective-permute-start | bytes 98312 | tf_op jit(solution)/shard_map/ppermute | solution.py:22
  61.4 4.5 %collective-permute-start.7 = (bf16[128,128]{1,0:T(8,128)(2,1)S(1)}, bf16[128,128]{1,0:T(8,128)(2,1)S(1)}, u32[]{:S(2)}, u32[]{:S(2)}) collective-permute-start(bf16[128,128]{1,0:T(8,128)(2,1)S(1)} %multiply_convert_fusion.2.refs_1_), channel_id=1, source_target_pairs={{0,96},{32,0},{64,32},{96,64},{1,97},{33,1},{65,33},{97,65},{2,98}... | collective-permute-start | bytes 98312 | tf_op jit(solution)/shard_map/ppermute | solution.py:22
  65.9 31.6 %all-to-all-start.1 = ((bf16[16,112,512]{2,1,0:T(8,128)(2,1)}), bf16[16,112,512]{2,1,0:T(8,128)(2,1)S(1)}, u32[]{:S(2)}, u32[]{:S(2)}) async-start(bf16[16,112,512]{2,1,0:T(8,128)(2,1)} %bitcast.21), calls=%async_computation.1 | async-start | bytes 3670016 | tf_op jit(solution)/shard_map/all_to_all | solution.py:175
  71.8 41.3 %all-gather.3.cloned.1.call-start = ((), (), s32[]{:S(2)}) async-start(), calls=%async_computation.4 | async-start | bytes 1179648 | tf_op jit(solution)/shard_map/all_gather | solution.py:153
  74.3 29.5 %collective-permute-start.15 = (bf16[112,512]{1,0:T(8,128)(2,1)S(1)}, bf16[112,512]{1,0:T(8,128)(2,1)S(1)}, u32[]{:S(2)}, u32[]{:S(2)}) collective-permute-start(bf16[112,512]{1,0:T(8,128)(2,1)S(1)} %convert_element_type.45), channel_id=1, source_target_pairs={{0,128},{128,0},{1,129},{129,1},{2,130},{130,2},{3,131},{131,3},{4... | collective-permute-start | bytes 344072 | tf_op jit(solution)/shard_map/ppermute | solution.py:22
  97.8 11.3 %collective-permute-start.8 = (bf16[112,512]{1,0:T(8,128)(2,1)S(1)}, bf16[112,512]{1,0:T(8,128)(2,1)S(1)}, u32[]{:S(2)}, u32[]{:S(2)}) collective-permute-start(bf16[112,512]{1,0:T(8,128)(2,1)S(1)} %convert_element_type.41), channel_id=1, source_target_pairs={{0,128},{128,0},{1,129},{129,1},{2,130},{130,2},{3,131},{131,3},{4... | collective-permute-start | bytes 344072 | tf_op jit(solution)/shard_map/ppermute | solution.py:22
  103.8 8.5 %collective-permute-start.16 = (bf16[112,512]{1,0:T(8,128)(2,1)S(1)}, bf16[112,512]{1,0:T(8,128)(2,1)S(1)}, u32[]{:S(2)}, u32[]{:S(2)}) collective-permute-start(bf16[112,512]{1,0:T(8,128)(2,1)S(1)} %multiply_convert_fusion.refs_1_), channel_id=1, source_target_pairs={{0,8},{8,16},{16,24},{24,0},{1,9},{9,17},{17,25},{25,1},{2,10},{10... | collective-permute-start | bytes 344072 | tf_op jit(solution)/shard_map/ppermute | solution.py:22
  104.4 8.6 %collective-permute-start.17 = (bf16[112,512]{1,0:T(8,128)(2,1)S(1)}, bf16[112,512]{1,0:T(8,128)(2,1)S(1)}, u32[]{:S(2)}, u32[]{:S(2)}) collective-permute-start(bf16[112,512]{1,0:T(8,128)(2,1)S(1)} %multiply_convert_fusion.refs_1_), channel_id=1, source_target_pairs={{0,16},{8,24},{16,0},{24,8},{1,17},{9,25},{17,1},{25,9},{2,18},{10... | collective-permute-start | bytes 344072 | tf_op jit(solution)/shard_map/ppermute | solution.py:22
  105.1 7.9 %collective-permute-start.18 = (bf16[112,512]{1,0:T(8,128)(2,1)S(1)}, bf16[112,512]{1,0:T(8,128)(2,1)S(1)}, u32[]{:S(2)}, u32[]{:S(2)}) collective-permute-start(bf16[112,512]{1,0:T(8,128)(2,1)S(1)} %multiply_convert_fusion.refs_1_), channel_id=1, source_target_pairs={{0,24},{8,0},{16,8},{24,16},{1,25},{9,1},{17,9},{25,17},{2,26},{10... | collective-permute-start | bytes 344072 | tf_op jit(solution)/shard_map/ppermute | solution.py:22
  109.1 7.3 %collective-permute-start.9 = (bf16[112,512]{1,0:T(8,128)(2,1)S(1)}, bf16[112,512]{1,0:T(8,128)(2,1)S(1)}, u32[]{:S(2)}, u32[]{:S(2)}) collective-permute-start(bf16[112,512]{1,0:T(8,128)(2,1)S(1)} %multiply_convert_fusion.1.refs_1_), channel_id=1, source_target_pairs={{0,8},{8,16},{16,24},{24,0},{1,9},{9,17},{17,25},{25,1},{2,10},{10... | collective-permute-start | bytes 344072 | tf_op jit(solution)/shard_map/ppermute | solution.py:22
  109.3 7.1 %collective-permute-start.10 = (bf16[112,512]{1,0:T(8,128)(2,1)S(1)}, bf16[112,512]{1,0:T(8,128)(2,1)S(1)}, u32[]{:S(2)}, u32[]{:S(2)}) collective-permute-start(bf16[112,512]{1,0:T(8,128)(2,1)S(1)} %multiply_convert_fusion.1.refs_1_), channel_id=1, source_target_pairs={{0,16},{8,24},{16,0},{24,8},{1,17},{9,25},{17,1},{25,9},{2,18},{10... | collective-permute-start | bytes 344072 | tf_op jit(solution)/shard_map/ppermute | solution.py:22
  112.3 5.0 %collective-permute-start.11 = (bf16[112,512]{1,0:T(8,128)(2,1)S(1)}, bf16[112,512]{1,0:T(8,128)(2,1)S(1)}, u32[]{:S(2)}, u32[]{:S(2)}) collective-permute-start(bf16[112,512]{1,0:T(8,128)(2,1)S(1)} %multiply_convert_fusion.1.refs_1_), channel_id=1, source_target_pairs={{0,24},{8,0},{16,8},{24,16},{1,25},{9,1},{17,9},{25,17},{2,26},{10... | collective-permute-start | bytes 344072 | tf_op jit(solution)/shard_map/ppermute | solution.py:22
  113.0 1.2 copy-start.1
  114.3 3.1 %copy-start.2 = (bf16[32,128,128]{2,1,0:T(8,128)(2,1)S(1)}, bf16[32,128,128]{2,1,0:T(8,128)(2,1)}, u32[]{:S(2)}) copy-start(bf16[32,128,128]{2,1,0:T(8,128)(2,1)} %all-gather.3.cloned.1.call-done) | copy-start | bytes 3145732
Sparse Core Ops, SparseCore 0:
  74.4 36.8 all-gather.2

commit v5 on v4

--- a/solution.py
+++ b/solution.py
@@ -22,18 +22,29 @@
     return lax.ppermute(value, axis, [(i, (i + step) % size) for i in range(size)])
 
 
-def act_kernel(place, gain, hidden_at, basis_at, out_at, hidden, basis, out, sems):
+def first_kernel(place, gain, gate_at, grad_at, hidden_at, basis_at, out_at, up_at,
+                 gate, grad, hidden, basis, out, up, sems):
     tokens, features = hidden.shape
     depth = basis.shape[0]
     strip = tokens // 4
+    load_gate = pltpu.make_async_copy(gate_at, gate, sems.at[9])
+    load_grad = pltpu.make_async_copy(grad_at, grad, sems.at[10])
     loads = [
         pltpu.make_async_copy(hidden_at.at[here], hidden.at[here], sems.at[i])
         for i, here in enumerate(pl.ds(at, strip) for at in range(0, tokens, strip))
     ]
     load_basis = pltpu.make_async_copy(basis_at, basis, sems.at[4])
-    for load in loads:
+    for load in (load_gate, load_grad, *loads, load_basis):
         load.start()
-    load_basis.start()
+    load_gate.wait()
+    load_grad.wait()
+    for at in range(0, tokens, 32):
+        here = slice(at, at + 32)
+        wide = gate[here, :].astype(jnp.float32)
+        wide = grad[here, :].astype(jnp.float32) * (wide / (1.0 + jnp.exp(-wide)))
+        up[here, :] = wide.astype(jnp.bfloat16)
+    store_up = pltpu.make_async_copy(up, up_at, sems.at[11])
+    store_up.start()
     stats = []
     for i, load in enumerate(loads):
         load.wait()
@@ -48,7 +59,7 @@
     normed = (scaled * gain[:, mine]).astype(jnp.bfloat16)
     load_basis.wait()
     block = basis.shape[1] // 32
-    stores = []
+    stores = [store_up]
     for x in range(4):
         for z_hi in range(2):
             at = (z_hi * 16 + x * 4) * block
@@ -66,32 +77,38 @@
         store.wait()
 
 
-def act_partials(hidden, norm_gain, act_basis):
+def first_partials(hidden, norm_gain, gate_pre, out_grad, act_basis):
     tokens = hidden.shape[0]
     shape = (16, tokens, act_basis.shape[1] // 16)
     place = lax.axis_index(DP).astype(jnp.int32).reshape(1)
     return pl.pallas_call(
-        act_kernel,
-        out_shape=pltpu.HBM(shape, jnp.bfloat16),
-        in_specs=[SMEM, VMEM, ANY, ANY],
-        out_specs=ANY,
+        first_kernel,
+        out_shape=(pltpu.HBM(shape, jnp.bfloat16), pltpu.HBM(out_grad.shape, jnp.bfloat16)),
+        in_specs=[SMEM, VMEM, ANY, ANY, ANY, ANY],
+        out_specs=(ANY, ANY),
         scratch_shapes=[
+            pltpu.VMEM(gate_pre.shape, jnp.bfloat16),
+            pltpu.VMEM(out_grad.shape, jnp.bfloat16),
             pltpu.VMEM(hidden.shape, jnp.bfloat16),
             pltpu.VMEM(act_basis.shape, jnp.bfloat16),
             pltpu.VMEM(shape, jnp.bfloat16),
-            pltpu.SemaphoreType.DMA((9,)),
+            pltpu.VMEM(out_grad.shape, jnp.bfloat16),
+            pltpu.SemaphoreType.DMA((12,)),
         ],
         compiler_params=WHOLE,
-        name="act",
-    )(place, norm_gain.reshape(1, -1), hidden, act_basis)
-
-
-def grad_kernel(count, *refs):
-    parts, basis, out_at, rows, out, sem = refs[:count], refs[count], *refs[-4:]
-    at = 0
-    for part in parts:
-        rows[at : at + part.shape[0], :] = part[...]
-        at += part.shape[0]
+        name="first",
+    )(place, norm_gain.reshape(1, -1), gate_pre, out_grad, hidden, act_basis)
+
+
+def grad_kernel(picks, *refs):
+    place, *parts, basis, out_at, rows, out, sem = refs
+    tokens = parts[0].shape[-2]
+    if picks:
+        chips = [lax.rem(place[0] + 4 - step, 4) for step in picks]
+        cores = [lax.rem(place[1] + flip, 2) for flip in range(2)]
+        parts = [parts[0].at[chip, core] for chip in chips for core in cores]
+    for at, part in enumerate(parts):
+        rows[at * tokens : (at + 1) * tokens, :] = part[...]
     stores = []
     for at in range(0, basis.shape[1], 256):
         here = pl.ds(at, 256)
@@ -105,14 +122,14 @@
         store.wait()
 
 
-def grad_partials(parts, basis, *after):
+def grad_partials(place, parts, basis, picks=()):
     depth, columns = basis.shape
-    tokens = sum(part.shape[0] for part in parts)
+    tokens = parts[0].shape[-2] * (2 * len(picks) if picks else len(parts))
     shape = (columns, tokens)
     return pl.pallas_call(
-        lambda *refs: grad_kernel(len(parts), *refs),
+        lambda *refs: grad_kernel(picks, *refs),
         out_shape=pltpu.HBM(shape, jnp.bfloat16),
-        in_specs=[VMEM] * (len(parts) + 1) + [ANY] * len(after),
+        in_specs=[SMEM] + [VMEM] * (len(parts) + 1),
         out_specs=ANY,
         scratch_shapes=[
             pltpu.VMEM((tokens, depth), jnp.bfloat16),
@@ -121,7 +138,7 @@
         ],
         compiler_params=PARAMS,
         name="grad",
-    )(*parts, basis, *after)
+    )(place, *parts, basis)
 
 
 def act_sum_kernel(place, got, kept, given):
@@ -207,10 +224,9 @@
             out[x, at, :] = here
 
 
-def corrected(steps, grad_sq, act_sq, *before):
+def corrected(steps, place, grad_sq, act_sq, *before):
     rows, tokens = grad_sq.shape
     block = act_sq.shape[4]
-    place = jnp.stack([lax.axis_index(a) for a in ("z_lo", "core", "x", "y")]).astype(jnp.int32)
     pieces = [grad_sq] + [shifted(grad_sq, "y", step) for step in (1, 2, 3)]
     return pl.pallas_call(
         lambda *refs: correct_kernel(steps, *refs),
@@ -223,26 +239,20 @@
     )(place, *pieces, *before, act_sq)
 
 
-CHUNKS = ((0, 1), (2, 3))
-
-
 def per_device(hidden, norm_gain, gate_pre, out_grad, grad_basis, act_basis):
-    up_grad = (out_grad.astype(jnp.float32) * jax.nn.silu(gate_pre.astype(jnp.float32))).astype(
-        jnp.bfloat16
-    )
-    moved = [up_grad] + [shifted(up_grad, "z_lo", step) for step in (1, 2, 3)]
-    both = [(own, shifted(own, "core", 1)) for own in moved]
-    act_row, act_sq = act_squares(act_partials(hidden, norm_gain, act_basis))
-    grad_got = []
-    for chunk, steps in enumerate(CHUNKS):
-        partial = grad_partials([part for step in steps for part in both[step]], grad_basis)
-        if chunk:
-            partial = gated(partial, *act_row)
-        grad_got.append(exchanged(partial))
-    out = []
-    for steps, got in zip(CHUNKS, grad_got):
-        out = [corrected(steps, squared(got), act_sq, *out)]
-    out = lax.all_to_all(out[0], "x", 0, 0, tiled=True)
+    place = jnp.stack([lax.axis_index(a) for a in ("z_lo", "core", "x", "y")]).astype(jnp.int32)
+    act_parts, up_grad = first_partials(hidden, norm_gain, gate_pre, out_grad, act_basis)
+    near = shifted(up_grad, "z_lo", 1)
+    parts = [up_grad, shifted(up_grad, "core", 1), near, shifted(near, "core", 1)]
+    every = lax.all_gather(up_grad, TENSOR, axis=0, tiled=False)
+    every = every.reshape((4, 2) + up_grad.shape)
+    act_row, act_sq = act_squares(act_parts)
+    near_got = exchanged(grad_partials(place, parts, grad_basis))
+    far_partial = grad_partials(place, [every], grad_basis, (2, 3))
+    far_got = exchanged(gated(far_partial, *act_row))
+    out = corrected((0, 1), place, squared(near_got), act_sq)
+    out = corrected((2, 3), place, squared(far_got), act_sq, out)
+    out = lax.all_to_all(out, "x", 0, 0, tiled=True)
     return out.reshape(grad_basis.shape[1], -1)
 
 

time: 144 us -> 148 us (1.028)
  blocking collectives: 15.5 us -> 19.9 us
  starting transfers between devices: 51.5 us -> 47.9 us
  Pallas kernels: 14.1 us -> 16.2 us
  local copies, waits for them, and re-layouts: 2.15 us -> 3.77 us
    all_gather x1, waiting for transfers between devices: 0.02 us -> 4.64 us  [act_squares(): spread = lax.all_gather(jnp.stack(row), TENSOR, axis=0, tiled=False)]
    all_to_all x1, blocking collectives: 15.5 us -> 19.9 us  [per_device(): out = lax.all_to_all(out, 'x', 0, 0, tiled=True)]
    ppermute x19 -> x15, waiting for transfers between devices: 18.6 us -> 14.2 us  [shifted(): lax.ppermute(value, axis, [(i, (i + step) % size) for i in range(size)])]
    all_to_all x2, starting transfers between devices: 10.2 us -> 8.14 us  [exchanged(): lax.all_to_all(partial.reshape(16, columns // 16, tokens), ('x', 'y'), 0,...]
    pallas_call x3, Pallas kernels: 10.6 us -> 12.6 us  [the longest x2 7.78 us: grad_partials(): pl.pallas_call(lambda *refs: grad_kernel(picks, *refs), out_shape=pltpu.H...]
    ppermute x19 -> x15, starting transfers between devices: 34.2 us -> 32.5 us  [shifted(): lax.ppermute(value, axis, [(i, (i + step) % size) for i in range(size)])]
    unnamed x7 -> x11, local copies, waits for them, and re-layouts: 2.15 us -> 3.77 us
  transfers between devices with their start and end apart: 23 -> 20, of which waited for: 10 -> 10; matrix products, arithmetic and copies ran while one was open for 3% -> 2% of each run, Pallas kernels for 6% -> 7%
where the time goes in v5:
time: 148 us; the launch traced here: 146 us
  starting transfers between devices  47.9 us (32%)
  waiting for transfers between devices  41.3 us (28%)
  blocking collectives  19.9 us (13%)
  Pallas kernels  16.2 us (11%)
  between operations  13.6 us (9%)
  local copies, waits for them, and re-layouts  3.77 us (3%)
  other arithmetic  2.9 us (2%)
    ppermute x15, starting transfers between devices, shifted(): lax.ppermute(value, axis, [(i, (i + step) % size) for i in range(size)])  32.5 us
    all_to_all x1, blocking collectives, per_device(): out = lax.all_to_all(out, 'x', 0, 0, tiled=True)  19.9 us
    all_to_all x2, waiting for transfers between devices, exchanged(): lax.all_to_all(partial.reshape(16, columns // 16, tokens), ('x', 'y'), 0,...  18 us
    ppermute x15, waiting for transfers between devices, shifted(): lax.ppermute(value, axis, [(i, (i + step) % size) for i in range(size)])  14.2 us
    all_to_all x2, starting transfers between devices, exchanged(): lax.all_to_all(partial.reshape(16, columns // 16, tokens), ('x', 'y'), 0,...  8.14 us
    pallas_call x2, Pallas kernels, grad_partials(): pl.pallas_call(lambda *refs: grad_kernel(picks, *refs), out_shape=pltpu.H...  7.78 us
    all_to_all x1, starting transfers between devices, act_squares(): got = lax.all_to_all(partials, ('x', 'y'), 0, 0, tiled=True)  7.22 us
    pallas_call x1, Pallas kernels, first_partials(): pl.pallas_call(first_kernel, out_shape=(pltpu.HBM(shape, jnp.bfloat16), p...  4.84 us
  transfers between devices with their start and end apart: 20, of which 10 were waited for; matrix products, arithmetic and copies ran while one was open for 2% of the time, Pallas kernels for 7%

profile of v5, /device:TPU:64, one launch (start us, length us, event | category | flops | bytes accessed | tf_op | source)
XLA Modules:
  0.0 145.5 jit_solution(2487827571226022804)
XLA Ops:
  6.5 4.8 %first.1 = (bf16[16,128,256]{2,1,0:T(8,128)(2,1)}, bf16[128,896]{1,0:T(8,128)(2,1)}) custom-call(s32[1]{0:T(128)} %bitcast.4.place, f32[1,8192]{1,0:T(1,128)} %bitcast.26, bf16[128,896]{1,0:T(8,128)(2,1)} %gate_at.1, bf16[128,896]{1,0:T(8,128)(2,1)} %grad_at.1, bf16[128,8192]{1,0:T(8,128)(2,1)} %hidden_at.1, bf16[256,4096]{1,0:T(8,128)(2,1)} %basis_at.1), custom_call_target="tpu_custom_call" | custom-call | tf_op jit(solution)/shard_map/first/pallas_call | solution.py:84
  11.4 7.2 %all-to-all-start = ((bf16[16,128,256]{2,1,0:T(8,128)(2,1)}), bf16[16,128,256]{2,1,0:T(8,128)(2,1)}, u32[]{:S(2)}, u32[]{:S(2)}) async-start(bf16[16,128,256]{2,1,0:T(8,128)(2,1)} %get-tuple-element.10), calls=%async_computation | async-start | bytes 2097152 | tf_op jit(solution)/shard_map/all_to_all | solution.py:155
  18.7 2.0 %collective-permute-start.9 = (bf16[128,896]{1,0:T(8,128)(2,1)S(1)}, bf16[128,896]{1,0:T(8,128)(2,1)}, u32[]{:S(2)}, u32[]{:S(2)}) collective-permute-start(bf16[128,896]{1,0:T(8,128)(2,1)S(1)} %copy-done.4), channel_id=1, source_target_pairs={{0,2},{2,4},{4,6},{6,0},{1,3},{3,5},{5,7},{7,1},{8,10},{10,12},{12... | collective-permute-start | bytes 688136 | tf_op jit(solution)/shard_map/ppermute | solution.py:22
  20.7 5.2 %collective-permute-done.9.refs_3_ = bf16[128,896]{1,0:T(8,128)(2,1)} collective-permute-done((bf16[128,896]{1,0:T(8,128)(2,1)S(1)}, bf16[128,896]{1,0:T(8,128)(2,1)}, u32[]{:S(2)}, u32[]{:S(2)}) %collective-permute-start.9) | collective-permute-done | bytes 229408 | tf_op jit(solution)/shard_map/ppermute | solution.py:22
  26.0 1.7 %collective-permute-done.10.refs_4_ = bf16[128,896]{1,0:T(8,128)(2,1)} collective-permute-done((bf16[128,896]{1,0:T(8,128)(2,1)}, bf16[128,896]{1,0:T(8,128)(2,1)}, u32[]{:S(2)}, u32[]{:S(2)}) %collective-permute-start.10) | collective-permute-done | bytes 229408 | tf_op jit(solution)/shard_map/ppermute | solution.py:22
  27.8 4.2 %grad.3 = bf16[1792,512]{1,0:T(8,128)(2,1)} custom-call(s32[4]{0:T(128)S(1)} %pad_add_fusion.refs_0_, bf16[128,896]{1,0:T(8,128)(2,1)S(1)} %copy-done.4, bf16[128,896]{1,0:T(8,128)(2,1)} %collective-permute-done.8.refs_2_, bf16[128,896]{1,0:T(8,128)(2,1)} %collective-permute-done.9.refs_3_, bf16[128,896]{1,0:T(8,128)(2,1)} %collective-permute-done.10.refs_4_, ...), custom_call_target="tpu_custom_call" | custom-call | tf_op jit(solution)/shard_map/grad/pallas_call | solution.py:129
  32.0 4.4 %all-to-all-done.got = bf16[16,128,256]{2,1,0:T(8,128)(2,1)} async-done(((bf16[16,128,256]{2,1,0:T(8,128)(2,1)}), bf16[16,128,256]{2,1,0:T(8,128)(2,1)}, u32[]{:S(2)}, u32[]{:S(2)}) %all-to-all-start) | async-done | bytes 1048608 | tf_op jit(solution)/shard_map/all_to_all | solution.py:155
  36.4 4.4 %all-to-all-start.2 = ((bf16[16,112,512]{2,1,0:T(8,128)(2,1)}), bf16[16,112,512]{2,1,0:T(8,128)(2,1)}, u32[]{:S(2)}, u32[]{:S(2)}) async-start(bf16[16,112,512]{2,1,0:T(8,128)(2,1)} %bitcast.24), calls=%async_computation.2 | async-start | bytes 3670016 | tf_op jit(solution)/shard_map/all_to_all | solution.py:192
  40.9 1.4 act_sum.1
  42.2 5.5 %collective-permute-start = (f32[128,128]{1,0:T(8,128)S(1)}, f32[128,128]{1,0:T(8,128)S(1)}, u32[]{:S(2)}, u32[]{:S(2)}) collective-permute-start(f32[128,128]{1,0:T(8,128)S(1)} %get-tuple-element.12), channel_id=1, source_target_pairs={{0,128},{128,0},{1,129},{129,1},{2,130},{130,2},{3,131},{131,3},{4... | collective-permute-start | bytes 196616 | tf_op jit(solution)/shard_map/ppermute | solution.py:22
  47.7 4.0 %collective-permute-done = f32[128,128]{1,0:T(8,128)S(1)} collective-permute-done((f32[128,128]{1,0:T(8,128)S(1)}, f32[128,128]{1,0:T(8,128)S(1)}, u32[]{:S(2)}, u32[]{:S(2)}) %collective-permute-start) | collective-permute-done | bytes 65568 | tf_op jit(solution)/shard_map/ppermute | solution.py:22
  51.8 1.7 %collective-permute-start.1 = (bf16[128,128]{1,0:T(8,128)(2,1)S(1)}, bf16[128,128]{1,0:T(8,128)(2,1)S(1)}, u32[]{:S(2)}, u32[]{:S(2)}) collective-permute-start(bf16[128,128]{1,0:T(8,128)(2,1)S(1)} %multiply_convert_fusion.2.refs_1_), channel_id=1, source_target_pairs={{0,32},{32,64},{64,96},{96,0},{1,33},{33,65},{65,97},{97,1},{2,34}... | collective-permute-start | bytes 98312 | tf_op jit(solution)/shard_map/ppermute | solution.py:22
  53.5 2.7 %collective-permute-start.2 = (bf16[128,128]{1,0:T(8,128)(2,1)S(1)}, bf16[128,128]{1,0:T(8,128)(2,1)S(1)}, u32[]{:S(2)}, u32[]{:S(2)}) collective-permute-start(bf16[128,128]{1,0:T(8,128)(2,1)S(1)} %multiply_convert_fusion.2.refs_1_), channel_id=1, source_target_pairs={{0,64},{32,96},{64,0},{96,32},{1,65},{33,97},{65,1},{97,33},{2,66}... | collective-permute-start | bytes 98312 | tf_op jit(solution)/shard_map/ppermute | solution.py:22
  56.2 1.5 %collective-permute-start.3 = (bf16[128,128]{1,0:T(8,128)(2,1)S(1)}, bf16[128,128]{1,0:T(8,128)(2,1)S(1)}, u32[]{:S(2)}, u32[]{:S(2)}) collective-permute-start(bf16[128,128]{1,0:T(8,128)(2,1)S(1)} %multiply_convert_fusion.2.refs_1_), channel_id=1, source_target_pairs={{0,96},{32,0},{64,32},{96,64},{1,97},{33,1},{65,33},{97,65},{2,98}... | collective-permute-start | bytes 98312 | tf_op jit(solution)/shard_map/ppermute | solution.py:22
  57.6 1.5 %copy-done.3 = bf16[1024,896]{1,0:T(8,128)(2,1)S(1)} copy-done((bf16[1024,896]{1,0:T(8,128)(2,1)S(1)}, bf16[1024,896]{1,0:T(8,128)(2,1)}, u32[]{:S(2)}) %copy-start.3) | copy-done | bytes 1835032
  59.1 3.6 %grad.2.refs_0_ = bf16[1792,512]{1,0:T(8,128)(2,1)} custom-call(s32[4]{0:T(128)S(1)} %pad_add_fusion.refs_0_, bf16[4,2,128,896]{3,2,1,0:T(8,128)(2,1)S(1)} %bitcast.18, bf16[896,1792]{1,0:T(8,128)(2,1)S(1)} %copy-done), custom_call_target="tpu_custom_call" | custom-call | tf_op jit(solution)/shard_map/grad/pallas_call | solution.py:129
  62.7 1.3 collective-permute-done.1.refs_2_
  64.3 2.2 %all-to-all-done.2 = bf16[16,112,512]{2,1,0:T(8,128)(2,1)} async-done(((bf16[16,112,512]{2,1,0:T(8,128)(2,1)}), bf16[16,112,512]{2,1,0:T(8,128)(2,1)}, u32[]{:S(2)}, u32[]{:S(2)}) %all-to-all-start.2) | async-done | bytes 1835040 | tf_op jit(solution)/shard_map/all_to_all | solution.py:192
  66.6 3.7 %all-to-all-start.1 = ((bf16[16,112,512]{2,1,0:T(8,128)(2,1)}), bf16[16,112,512]{2,1,0:T(8,128)(2,1)S(1)}, u32[]{:S(2)}, u32[]{:S(2)}) async-start(bf16[16,112,512]{2,1,0:T(8,128)(2,1)} %bitcast.23), calls=%async_computation.1 | async-start | bytes 3670016 | tf_op jit(solution)/shard_map/all_to_all | solution.py:192
  71.0 1.8 %convert_reduce_fusion = f32[112,512]{1,0:T(8,128)S(1)} fusion(bf16[16,112,512]{2,1,0:T(8,128)(2,1)} %all-to-all-done.2), kind=kLoop, calls=%fused_computation | loop fusion | flops 1777664 | bytes 2064384 | tf_op jit(solution)/shard_map/reduce_sum | solution.py:196
  72.8 5.8 %collective-permute-start.11 = (bf16[112,512]{1,0:T(8,128)(2,1)S(1)}, bf16[112,512]{1,0:T(8,128)(2,1)S(1)}, u32[]{:S(2)}, u32[]{:S(2)}) collective-permute-start(bf16[112,512]{1,0:T(8,128)(2,1)S(1)} %convert_element_type.33), channel_id=1, source_target_pairs={{0,128},{128,0},{1,129},{129,1},{2,130},{130,2},{3,131},{131,3},{4... | collective-permute-start | bytes 344072 | tf_op jit(solution)/shard_map/ppermute | solution.py:22
  78.7 15.8 %all-to-all-done.1 = bf16[16,112,512]{2,1,0:T(8,128)(2,1)S(1)} async-done(((bf16[16,112,512]{2,1,0:T(8,128)(2,1)}), bf16[16,112,512]{2,1,0:T(8,128)(2,1)S(1)}, u32[]{:S(2)}, u32[]{:S(2)}) %all-to-all-start.1) | async-done | bytes 1835040 | tf_op jit(solution)/shard_map/all_to_all | solution.py:192
  94.7 5.7 %collective-permute-start.4 = (bf16[112,512]{1,0:T(8,128)(2,1)S(1)}, bf16[112,512]{1,0:T(8,128)(2,1)S(1)}, u32[]{:S(2)}, u32[]{:S(2)}) collective-permute-start(bf16[112,512]{1,0:T(8,128)(2,1)S(1)} %convert_element_type.29), channel_id=1, source_target_pairs={{0,128},{128,0},{1,129},{129,1},{2,130},{130,2},{3,131},{131,3},{4... | collective-permute-start | bytes 344072 | tf_op jit(solution)/shard_map/ppermute | solution.py:22
  101.2 2.1 %collective-permute-start.13 = (bf16[112,512]{1,0:T(8,128)(2,1)S(1)}, bf16[112,512]{1,0:T(8,128)(2,1)S(1)}, u32[]{:S(2)}, u32[]{:S(2)}) collective-permute-start(bf16[112,512]{1,0:T(8,128)(2,1)S(1)} %multiply_convert_fusion.refs_1_), channel_id=1, source_target_pairs={{0,16},{8,24},{16,0},{24,8},{1,17},{9,25},{17,1},{25,9},{2,18},{10... | collective-permute-start | bytes 344072 | tf_op jit(solution)/shard_map/ppermute | solution.py:22
  104.3 1.1 collective-permute-start.5
  105.4 1.7 %collective-permute-start.6 = (bf16[112,512]{1,0:T(8,128)(2,1)S(1)}, bf16[112,512]{1,0:T(8,128)(2,1)S(1)}, u32[]{:S(2)}, u32[]{:S(2)}) collective-permute-start(bf16[112,512]{1,0:T(8,128)(2,1)S(1)} %multiply_convert_fusion.1.refs_1_), channel_id=1, source_target_pairs={{0,16},{8,24},{16,0},{24,8},{1,17},{9,25},{17,1},{25,9},{2,18},{10... | collective-permute-start | bytes 344072 | tf_op jit(solution)/shard_map/ppermute | solution.py:22
  107.1 1.6 %collective-permute-done.12.refs_2_ = bf16[112,512]{1,0:T(8,128)(2,1)S(1)} collective-permute-done((bf16[112,512]{1,0:T(8,128)(2,1)S(1)}, bf16[112,512]{1,0:T(8,128)(2,1)S(1)}, u32[]{:S(2)}, u32[]{:S(2)}) %collective-permute-start.12) | collective-permute-done | bytes 114720 | tf_op jit(solution)/shard_map/ppermute | solution.py:22
  109.7 4.6 %all-gather.7.cloned.1.call-done = bf16[32,128,128]{2,1,0:T(8,128)(2,1)} async-done(((bf16[4,128,128]{2,1,0:T(8,128)(2,1)}), bf16[32,128,128]{2,1,0:T(8,128)(2,1)}) %all-gather.7.cloned.1.call-update) | async-done | bytes 1048592 | tf_op jit(solution)/shard_map/all_gather | solution.py:170
  114.3 1.2 copy-done.1
  115.5 1.1 correct.2.refs_5_
  116.8 1.1 correct.3
  117.9 19.9 %all_to_all.20 = f32[4,448,128]{2,1,0:T(8,128)S(1)} all-to-all(f32[4,448,128]{2,1,0:T(8,128)S(1)} %correct.3), channel_id=1, replica_groups=mesh['z_hi'=2,'x'=4,'y'=4,'z_lo'=4,'core'=2] {'x'}, dimensions={0} | all-to-all | bytes 1835008 | tf_op jit(solution)/shard_map/all_to_all | solution.py:255
  (38 shorter events, 5.3 us)
Async XLA Ops:
  6.5 51.1 %all-gather.5.cloned.1.call-start = ((), (), s32[]{:S(2)}) async-start(), calls=%async_computation.4 | async-start | bytes 2064384 | tf_op jit(solution)/shard_map/all_gather | solution.py:247
  6.5 21.2 %copy-start = (bf16[896,1792]{1,0:T(8,128)(2,1)S(1)}, bf16[896,1792]{1,0:T(8,128)(2,1)}, u32[]{:S(2)}) copy-start(bf16[896,1792]{1,0:T(8,128)(2,1)} %refs_5_.1) | copy-start | bytes 9633796
  11.4 7.3 %copy-start.4 = (bf16[128,896]{1,0:T(8,128)(2,1)S(1)}, bf16[128,896]{1,0:T(8,128)(2,1)}, u32[]{:S(2)}) copy-start(bf16[128,896]{1,0:T(8,128)(2,1)} %get-tuple-element.9.refs_1_) | copy-start | bytes 688132
  11.4 25.0 %all-to-all-start = ((bf16[16,128,256]{2,1,0:T(8,128)(2,1)}), bf16[16,128,256]{2,1,0:T(8,128)(2,1)}, u32[]{:S(2)}, u32[]{:S(2)}) async-start(bf16[16,128,256]{2,1,0:T(8,128)(2,1)} %get-tuple-element.10), calls=%async_computation | async-start | bytes 2097152 | tf_op jit(solution)/shard_map/all_to_all | solution.py:155
  18.7 7.3 %collective-permute-start.9 = (bf16[128,896]{1,0:T(8,128)(2,1)S(1)}, bf16[128,896]{1,0:T(8,128)(2,1)}, u32[]{:S(2)}, u32[]{:S(2)}) collective-permute-start(bf16[128,896]{1,0:T(8,128)(2,1)S(1)} %copy-done.4), channel_id=1, source_target_pairs={{0,2},{2,4},{4,6},{6,0},{1,3},{3,5},{5,7},{7,1},{8,10},{10,12},{12... | collective-permute-start | bytes 688136 | tf_op jit(solution)/shard_map/ppermute | solution.py:22
  20.7 5.3 %collective-permute-start.8 = (bf16[128,896]{1,0:T(8,128)(2,1)S(1)}, bf16[128,896]{1,0:T(8,128)(2,1)}, u32[]{:S(2)}, u32[]{:S(2)}) collective-permute-start(bf16[128,896]{1,0:T(8,128)(2,1)S(1)} %copy-done.4), channel_id=1, source_target_pairs={{0,1},{1,0},{2,3},{3,2},{4,5},{5,4},{6,7},{7,6},{8,9},{9,8},{10,11... | collective-permute-start | bytes 688136 | tf_op jit(solution)/shard_map/ppermute | solution.py:22
  25.9 1.8 %collective-permute-start.10 = (bf16[128,896]{1,0:T(8,128)(2,1)}, bf16[128,896]{1,0:T(8,128)(2,1)}, u32[]{:S(2)}, u32[]{:S(2)}) collective-permute-start(bf16[128,896]{1,0:T(8,128)(2,1)} %collective-permute-done.9.refs_3_), channel_id=1, source_target_pairs={{0,1},{1,0},{2,3},{3,2},{4,5},{5,4},{6,7},{7,6},{8,9},{9,8},{10,11... | collective-permute-start | bytes 688136 | tf_op jit(solution)/shard_map/ppermute | solution.py:22
  36.4 30.1 %all-to-all-start.2 = ((bf16[16,112,512]{2,1,0:T(8,128)(2,1)}), bf16[16,112,512]{2,1,0:T(8,128)(2,1)}, u32[]{:S(2)}, u32[]{:S(2)}) async-start(bf16[16,112,512]{2,1,0:T(8,128)(2,1)} %bitcast.24), calls=%async_computation.2 | async-start | bytes 3670016 | tf_op jit(solution)/shard_map/all_to_all | solution.py:192
  42.2 9.5 %collective-permute-start = (f32[128,128]{1,0:T(8,128)S(1)}, f32[128,128]{1,0:T(8,128)S(1)}, u32[]{:S(2)}, u32[]{:S(2)}) collective-permute-start(f32[128,128]{1,0:T(8,128)S(1)} %get-tuple-element.12), channel_id=1, source_target_pairs={{0,128},{128,0},{1,129},{129,1},{2,130},{130,2},{3,131},{131,3},{4... | collective-permute-start | bytes 196616 | tf_op jit(solution)/shard_map/ppermute | solution.py:22
  51.8 12.2 %collective-permute-start.1 = (bf16[128,128]{1,0:T(8,128)(2,1)S(1)}, bf16[128,128]{1,0:T(8,128)(2,1)S(1)}, u32[]{:S(2)}, u32[]{:S(2)}) collective-permute-start(bf16[128,128]{1,0:T(8,128)(2,1)S(1)} %multiply_convert_fusion.2.refs_1_), channel_id=1, source_target_pairs={{0,32},{32,64},{64,96},{96,0},{1,33},{33,65},{65,97},{97,1},{2,34}... | collective-permute-start | bytes 98312 | tf_op jit(solution)/shard_map/ppermute | solution.py:22
  53.5 10.8 %collective-permute-start.2 = (bf16[128,128]{1,0:T(8,128)(2,1)S(1)}, bf16[128,128]{1,0:T(8,128)(2,1)S(1)}, u32[]{:S(2)}, u32[]{:S(2)}) collective-permute-start(bf16[128,128]{1,0:T(8,128)(2,1)S(1)} %multiply_convert_fusion.2.refs_1_), channel_id=1, source_target_pairs={{0,64},{32,96},{64,0},{96,32},{1,65},{33,97},{65,1},{97,33},{2,66}... | collective-permute-start | bytes 98312 | tf_op jit(solution)/shard_map/ppermute | solution.py:22
  56.2 8.2 %collective-permute-start.3 = (bf16[128,128]{1,0:T(8,128)(2,1)S(1)}, bf16[128,128]{1,0:T(8,128)(2,1)S(1)}, u32[]{:S(2)}, u32[]{:S(2)}) collective-permute-start(bf16[128,128]{1,0:T(8,128)(2,1)S(1)} %multiply_convert_fusion.2.refs_1_), channel_id=1, source_target_pairs={{0,96},{32,0},{64,32},{96,64},{1,97},{33,1},{65,33},{97,65},{2,98}... | collective-permute-start | bytes 98312 | tf_op jit(solution)/shard_map/ppermute | solution.py:22
  57.6 1.5 %copy-start.3 = (bf16[1024,896]{1,0:T(8,128)(2,1)S(1)}, bf16[1024,896]{1,0:T(8,128)(2,1)}, u32[]{:S(2)}) copy-start(bf16[1024,896]{1,0:T(8,128)(2,1)} %all-gather.5.cloned.1.call-done) | copy-start | bytes 5505028
  66.6 27.9 %all-to-all-start.1 = ((bf16[16,112,512]{2,1,0:T(8,128)(2,1)}), bf16[16,112,512]{2,1,0:T(8,128)(2,1)S(1)}, u32[]{:S(2)}, u32[]{:S(2)}) async-start(bf16[16,112,512]{2,1,0:T(8,128)(2,1)} %bitcast.23), calls=%async_computation.1 | async-start | bytes 3670016 | tf_op jit(solution)/shard_map/all_to_all | solution.py:192
  70.3 44.0 %all-gather.7.cloned.1.call-start = ((), (), s32[]{:S(2)}) async-start(), calls=%async_computation.5 | async-start | bytes 1179648 | tf_op jit(solution)/shard_map/all_gather | solution.py:170
  72.8 27.6 %collective-permute-start.11 = (bf16[112,512]{1,0:T(8,128)(2,1)S(1)}, bf16[112,512]{1,0:T(8,128)(2,1)S(1)}, u32[]{:S(2)}, u32[]{:S(2)}) collective-permute-start(bf16[112,512]{1,0:T(8,128)(2,1)S(1)} %convert_element_type.33), channel_id=1, source_target_pairs={{0,128},{128,0},{1,129},{129,1},{2,130},{130,2},{3,131},{131,3},{4... | collective-permute-start | bytes 344072 | tf_op jit(solution)/shard_map/ppermute | solution.py:22
  94.7 9.6 %collective-permute-start.4 = (bf16[112,512]{1,0:T(8,128)(2,1)S(1)}, bf16[112,512]{1,0:T(8,128)(2,1)S(1)}, u32[]{:S(2)}, u32[]{:S(2)}) collective-permute-start(bf16[112,512]{1,0:T(8,128)(2,1)S(1)} %convert_element_type.29), channel_id=1, source_target_pairs={{0,128},{128,0},{1,129},{129,1},{2,130},{130,2},{3,131},{131,3},{4... | collective-permute-start | bytes 344072 | tf_op jit(solution)/shard_map/ppermute | solution.py:22
  100.5 8.2 %collective-permute-start.12 = (bf16[112,512]{1,0:T(8,128)(2,1)S(1)}, bf16[112,512]{1,0:T(8,128)(2,1)S(1)}, u32[]{:S(2)}, u32[]{:S(2)}) collective-permute-start(bf16[112,512]{1,0:T(8,128)(2,1)S(1)} %multiply_convert_fusion.refs_1_), channel_id=1, source_target_pairs={{0,8},{8,16},{16,24},{24,0},{1,9},{9,17},{17,25},{25,1},{2,10},{10... | collective-permute-start | bytes 344072 | tf_op jit(solution)/shard_map/ppermute | solution.py:22
  101.2 8.5 %collective-permute-start.13 = (bf16[112,512]{1,0:T(8,128)(2,1)S(1)}, bf16[112,512]{1,0:T(8,128)(2,1)S(1)}, u32[]{:S(2)}, u32[]{:S(2)}) collective-permute-start(bf16[112,512]{1,0:T(8,128)(2,1)S(1)} %multiply_convert_fusion.refs_1_), channel_id=1, source_target_pairs={{0,16},{8,24},{16,0},{24,8},{1,17},{9,25},{17,1},{25,9},{2,18},{10... | collective-permute-start | bytes 344072 | tf_op jit(solution)/shard_map/ppermute | solution.py:22
  103.3 6.4 %collective-permute-start.14 = (bf16[112,512]{1,0:T(8,128)(2,1)S(1)}, bf16[112,512]{1,0:T(8,128)(2,1)S(1)}, u32[]{:S(2)}, u32[]{:S(2)}) collective-permute-start(bf16[112,512]{1,0:T(8,128)(2,1)S(1)} %multiply_convert_fusion.refs_1_), channel_id=1, source_target_pairs={{0,24},{8,0},{16,8},{24,16},{1,25},{9,1},{17,9},{25,17},{2,26},{10... | collective-permute-start | bytes 344072 | tf_op jit(solution)/shard_map/ppermute | solution.py:22
  104.3 12.3 %collective-permute-start.5 = (bf16[112,512]{1,0:T(8,128)(2,1)S(1)}, bf16[112,512]{1,0:T(8,128)(2,1)S(1)}, u32[]{:S(2)}, u32[]{:S(2)}) collective-permute-start(bf16[112,512]{1,0:T(8,128)(2,1)S(1)} %multiply_convert_fusion.1.refs_1_), channel_id=1, source_target_pairs={{0,8},{8,16},{16,24},{24,0},{1,9},{9,17},{17,25},{25,1},{2,10},{10... | collective-permute-start | bytes 344072 | tf_op jit(solution)/shard_map/ppermute | solution.py:22
  105.4 11.2 %collective-permute-start.6 = (bf16[112,512]{1,0:T(8,128)(2,1)S(1)}, bf16[112,512]{1,0:T(8,128)(2,1)S(1)}, u32[]{:S(2)}, u32[]{:S(2)}) collective-permute-start(bf16[112,512]{1,0:T(8,128)(2,1)S(1)} %multiply_convert_fusion.1.refs_1_), channel_id=1, source_target_pairs={{0,16},{8,24},{16,0},{24,8},{1,17},{9,25},{17,1},{25,9},{2,18},{10... | collective-permute-start | bytes 344072 | tf_op jit(solution)/shard_map/ppermute | solution.py:22
  108.7 8.0 %collective-permute-start.7 = (bf16[112,512]{1,0:T(8,128)(2,1)S(1)}, bf16[112,512]{1,0:T(8,128)(2,1)S(1)}, u32[]{:S(2)}, u32[]{:S(2)}) collective-permute-start(bf16[112,512]{1,0:T(8,128)(2,1)S(1)} %multiply_convert_fusion.1.refs_1_), channel_id=1, source_target_pairs={{0,24},{8,0},{16,8},{24,16},{1,25},{9,1},{17,9},{25,17},{2,26},{10... | collective-permute-start | bytes 344072 | tf_op jit(solution)/shard_map/ppermute | solution.py:22
  114.3 1.2 copy-start.1
  115.5 1.2 copy-start.2
Sparse Core Ops, SparseCore 0:
  11.5 36.1 all-gather.4
  72.9 41.3 all-gather.6

commit v6 on v5

--- a/solution.py
+++ b/solution.py
@@ -100,15 +100,12 @@
     )(place, norm_gain.reshape(1, -1), gate_pre, out_grad, hidden, act_basis)
 
 
-def grad_kernel(picks, *refs):
-    place, *parts, basis, out_at, rows, out, sem = refs
-    tokens = parts[0].shape[-2]
-    if picks:
-        chips = [lax.rem(place[0] + 4 - step, 4) for step in picks]
-        cores = [lax.rem(place[1] + flip, 2) for flip in range(2)]
-        parts = [parts[0].at[chip, core] for chip in chips for core in cores]
-    for at, part in enumerate(parts):
-        rows[at * tokens : (at + 1) * tokens, :] = part[...]
+def grad_kernel(count, *refs):
+    parts, basis, out_at, rows, out, sem = refs[:count], refs[count], *refs[-4:]
+    at = 0
+    for part in parts:
+        rows[at : at + part.shape[0], :] = part[...]
+        at += part.shape[0]
     stores = []
     for at in range(0, basis.shape[1], 256):
         here = pl.ds(at, 256)
@@ -122,14 +119,14 @@
         store.wait()
 
 
-def grad_partials(place, parts, basis, picks=()):
+def grad_partials(parts, basis, *after):
     depth, columns = basis.shape
-    tokens = parts[0].shape[-2] * (2 * len(picks) if picks else len(parts))
+    tokens = sum(part.shape[0] for part in parts)
     shape = (columns, tokens)
     return pl.pallas_call(
-        lambda *refs: grad_kernel(picks, *refs),
+        lambda *refs: grad_kernel(len(parts), *refs),
         out_shape=pltpu.HBM(shape, jnp.bfloat16),
-        in_specs=[SMEM] + [VMEM] * (len(parts) + 1),
+        in_specs=[VMEM] * (len(parts) + 1) + [ANY] * len(after),
         out_specs=ANY,
         scratch_shapes=[
             pltpu.VMEM((tokens, depth), jnp.bfloat16),
@@ -138,7 +135,7 @@
         ],
         compiler_params=PARAMS,
         name="grad",
-    )(place, *parts, basis)
+    )(*parts, basis, *after)
 
 
 def act_sum_kernel(place, got, kept, given):
@@ -166,9 +163,7 @@
     )(place, got)
     total = kept + shifted(given, "z_hi", 1)
     square = (total * total).astype(jnp.bfloat16)
-    row = [square] + [shifted(square, "x", step) for step in (1, 2, 3)]
-    spread = lax.all_gather(jnp.stack(row), TENSOR, axis=0, tiled=False)
-    return row, spread.reshape(4, 2, 4, tokens, wide // 2)
+    return [square] + [shifted(square, "x", step) for step in (1, 2, 3)]
 
 
 def gate_kernel(*refs):
@@ -198,60 +193,58 @@
     return (total * total).astype(jnp.bfloat16)
 
 
-def correct_kernel(steps, *refs):
-    place, *pieces, act_sq, out, act = refs
-    pieces, before = pieces[:4], pieces[4:]
-    tokens, block = act_sq.shape[3:]
-    at = 0
-    for step in steps:
-        chip = lax.rem(place[0] + 4 - step, 4)
-        for flip in range(2):
-            core = lax.rem(place[1] + flip, 2)
-            for behind in range(4):
-                to = slice(behind * block, (behind + 1) * block)
-                act[at : at + tokens, to] = act_sq[chip, core, behind]
-            at += tokens
+def correct_kernel(place, *refs):
+    pieces, acts, before, (out, act) = refs[:4], refs[4:8], refs[8:-2], refs[-2:]
+    _, tokens, block = acts[0].shape
+    for i, part in enumerate(acts):
+        for behind in range(4):
+            here = slice(i * tokens, (i + 1) * tokens), slice(behind * block, (behind + 1) * block)
+            act[here] = part[behind]
     rows = pieces[0].shape[0]
     for y_behind, piece in enumerate(pieces):
         part = jnp.dot(piece[...], act[...], preferred_element_type=jnp.float32)
         part = part * (1.0 / (8 * tokens))
-        at = pl.ds(pl.multiple_of(lax.rem(place[3] + 4 - y_behind, 4) * rows, rows), rows)
+        at = pl.ds(pl.multiple_of(lax.rem(place[1] + 4 - y_behind, 4) * rows, rows), rows)
         for behind in range(4):
-            x = lax.rem(place[2] + 4 - behind, 4)
+            x = lax.rem(place[0] + 4 - behind, 4)
             here = part[:, behind * block : (behind + 1) * block]
             if before:
                 here = before[0][x, at, :] + here
             out[x, at, :] = here
 
 
-def corrected(steps, place, grad_sq, act_sq, *before):
-    rows, tokens = grad_sq.shape
-    block = act_sq.shape[4]
-    pieces = [grad_sq] + [shifted(grad_sq, "y", step) for step in (1, 2, 3)]
-    return pl.pallas_call(
-        lambda *refs: correct_kernel(steps, *refs),
+def corrected(pieces, acts, *before):
+    rows, tokens = pieces[0].shape
+    block = acts[0].shape[2]
+    place = jnp.stack([lax.axis_index("x"), lax.axis_index("y")]).astype(jnp.int32)
+    return pl.pallas_call(
+        correct_kernel,
         out_shape=jax.ShapeDtypeStruct((4, 4 * rows, block), jnp.float32),
-        in_specs=[SMEM] + [VMEM] * (5 + len(before)),
+        in_specs=[SMEM] + [VMEM] * (8 + len(before)),
         out_specs=VMEM,
         scratch_shapes=[pltpu.VMEM((tokens, 4 * block), jnp.bfloat16)],
         compiler_params=PARAMS,
         name="correct",
-    )(place, *pieces, *before, act_sq)
+    )(place, *pieces, *acts, *before)
 
 
 def per_device(hidden, norm_gain, gate_pre, out_grad, grad_basis, act_basis):
-    place = jnp.stack([lax.axis_index(a) for a in ("z_lo", "core", "x", "y")]).astype(jnp.int32)
     act_parts, up_grad = first_partials(hidden, norm_gain, gate_pre, out_grad, act_basis)
-    near = shifted(up_grad, "z_lo", 1)
-    parts = [up_grad, shifted(up_grad, "core", 1), near, shifted(near, "core", 1)]
-    every = lax.all_gather(up_grad, TENSOR, axis=0, tiled=False)
-    every = every.reshape((4, 2) + up_grad.shape)
-    act_row, act_sq = act_squares(act_parts)
-    near_got = exchanged(grad_partials(place, parts, grad_basis))
-    far_partial = grad_partials(place, [every], grad_basis, (2, 3))
-    far_got = exchanged(gated(far_partial, *act_row))
-    out = corrected((0, 1), place, squared(near_got), act_sq)
-    out = corrected((2, 3), place, squared(far_got), act_sq, out)
+    rows = []
+    for own in [up_grad] + [shifted(up_grad, "z_lo", step) for step in (1, 2, 3)]:
+        rows += [own, shifted(own, "core", 1)]
+    act_row = act_squares(act_parts)
+    near_got = exchanged(grad_partials(rows[:4], grad_basis))
+    far_got = exchanged(gated(grad_partials(rows[4:], grad_basis), *act_row))
+    act_own = jnp.stack(act_row)
+    acts = []
+    for own in [act_own] + [shifted(act_own, "z_lo", step) for step in (1, 2, 3)]:
+        acts += [own, shifted(own, "core", 1)]
+    near_sq = squared(near_got)
+    near_pieces = [near_sq] + [shifted(near_sq, "y", step) for step in (1, 2, 3)]
+    far_sq = squared(gated(far_got, *near_pieces, *acts))
+    far_pieces = [far_sq] + [shifted(far_sq, "y", step) for step in (1, 2, 3)]
+    out = corrected(far_pieces, acts[4:], corrected(near_pieces, acts[:4]))
     out = lax.all_to_all(out, "x", 0, 0, tiled=True)
     return out.reshape(grad_basis.shape[1], -1)
 

time: 148 us -> 139 us (0.939)
  the two profiles are of different devices: /device:TPU:64 before, /device:TPU:56 now
where the time goes in v6:
time: 139 us; the launch traced here: 138 us
  starting transfers between devices  59.8 us (43%)
  waiting for transfers between devices  43.6 us (31%)
  blocking collectives  15.8 us (11%)
  Pallas kernels  14.4 us (10%)
  other arithmetic  3.76 us (3%)
    ppermute x26, waiting for transfers between devices, shifted(): lax.ppermute(value, axis, [(i, (i + step) % size) for i in range(size)])  40.1 us
    ppermute x26, starting transfers between devices, shifted(): lax.ppermute(value, axis, [(i, (i + step) % size) for i in range(size)])  38.9 us
    all_to_all x1, blocking collectives, per_device(): out = lax.all_to_all(out, 'x', 0, 0, tiled=True)  15.8 us
    all_to_all x2, starting transfers between devices, exchanged(): lax.all_to_all(partial.reshape(16, columns // 16, tokens), ('x', 'y'), 0,...  13.5 us
    all_to_all x1, starting transfers between devices, act_squares(): got = lax.all_to_all(partials, ('x', 'y'), 0, 0, tiled=True)  7.32 us
    pallas_call x2, Pallas kernels, grad_partials(): pl.pallas_call(lambda *refs: grad_kernel(len(parts), *refs), out_shape=pl...  6.04 us
    pallas_call x1, Pallas kernels, first_partials(): pl.pallas_call(first_kernel, out_shape=(pltpu.HBM(shape, jnp.bfloat16), p...  4.85 us
    reduce_sum x2, other arithmetic, squared(): summed = jnp.sum(got.astype(jnp.float32), axis=0)  3.55 us
  transfers between devices with their start and end apart: 29, of which 15 were waited for; matrix products, arithmetic and copies ran while one was open for 1% of the time, Pallas kernels for 6%

profile of v6, /device:TPU:56, one launch (start us, length us, event | category | flops | bytes accessed | tf_op | source)
XLA Modules:
  0.0 138.4 jit_solution(1126450843473477395)
XLA Ops:
  0.0 4.8 %first.1 = (bf16[16,128,256]{2,1,0:T(8,128)(2,1)}, bf16[128,896]{1,0:T(8,128)(2,1)}) custom-call(s32[1]{0:T(128)} %bitcast.2.place, f32[1,8192]{1,0:T(1,128)} %bitcast.19, bf16[128,896]{1,0:T(8,128)(2,1)} %gate_at.1, bf16[128,896]{1,0:T(8,128)(2,1)} %grad_at.1, bf16[128,8192]{1,0:T(8,128)(2,1)} %hidden_at.1, bf16[256,4096]{1,0:T(8,128)(2,1)} %basis_at.1), custom_call_target="tpu_custom_call" | custom-call | tf_op jit(solution)/shard_map/first/pallas_call | solution.py:84
  4.9 7.3 %all-to-all-start = ((bf16[16,128,256]{2,1,0:T(8,128)(2,1)}), bf16[16,128,256]{2,1,0:T(8,128)(2,1)}, u32[]{:S(2)}, u32[]{:S(2)}) async-start(bf16[16,128,256]{2,1,0:T(8,128)(2,1)} %get-tuple-element.10), calls=%async_computation | async-start | bytes 2097152 | tf_op jit(solution)/shard_map/all_to_all | solution.py:152
  12.2 2.0 %collective-permute-start.9 = (bf16[128,896]{1,0:T(8,128)(2,1)S(1)}, bf16[128,896]{1,0:T(8,128)(2,1)S(1)}, u32[]{:S(2)}, u32[]{:S(2)}) collective-permute-start(bf16[128,896]{1,0:T(8,128)(2,1)S(1)} %copy-done.1), channel_id=1, source_target_pairs={{0,2},{2,4},{4,6},{6,0},{1,3},{3,5},{5,7},{7,1},{8,10},{10,12},{12... | collective-permute-start | bytes 688136 | tf_op jit(solution)/shard_map/ppermute | solution.py:22
  14.2 4.9 %collective-permute-done.9.refs_2_ = bf16[128,896]{1,0:T(8,128)(2,1)S(1)} collective-permute-done((bf16[128,896]{1,0:T(8,128)(2,1)S(1)}, bf16[128,896]{1,0:T(8,128)(2,1)S(1)}, u32[]{:S(2)}, u32[]{:S(2)}) %collective-permute-start.9) | collective-permute-done | bytes 229408 | tf_op jit(solution)/shard_map/ppermute | solution.py:22
  19.1 1.5 %collective-permute-done.10.refs_3_ = bf16[128,896]{1,0:T(8,128)(2,1)S(1)} collective-permute-done((bf16[128,896]{1,0:T(8,128)(2,1)S(1)}, bf16[128,896]{1,0:T(8,128)(2,1)S(1)}, u32[]{:S(2)}, u32[]{:S(2)}) %collective-permute-start.10) | collective-permute-done | bytes 229408 | tf_op jit(solution)/shard_map/ppermute | solution.py:22
  20.5 3.0 %grad.3 = bf16[1792,512]{1,0:T(8,128)(2,1)} custom-call(bf16[128,896]{1,0:T(8,128)(2,1)S(1)} %copy-done.1, bf16[128,896]{1,0:T(8,128)(2,1)S(1)} %collective-permute-done.8.refs_1_, bf16[128,896]{1,0:T(8,128)(2,1)S(1)} %collective-permute-done.9.refs_2_, bf16[128,896]{1,0:T(8,128)(2,1)S(1)} %collective-permute-done.10.refs_3_, bf16[896,1792]{1,0:T(8,128)(2,1)S(1)} %copy-done), custom_call_target="tpu_custom_call" | custom-call | tf_op jit(solution)/shard_map/grad/pallas_call | solution.py:126
  23.6 3.4 %all-to-all-done.got = bf16[16,128,256]{2,1,0:T(8,128)(2,1)} async-done(((bf16[16,128,256]{2,1,0:T(8,128)(2,1)}), bf16[16,128,256]{2,1,0:T(8,128)(2,1)}, u32[]{:S(2)}, u32[]{:S(2)}) %all-to-all-start) | async-done | bytes 1048608 | tf_op jit(solution)/shard_map/all_to_all | solution.py:152
  27.0 7.2 %all-to-all-start.2 = ((bf16[16,112,512]{2,1,0:T(8,128)(2,1)}), bf16[16,112,512]{2,1,0:T(8,128)(2,1)}, u32[]{:S(2)}, u32[]{:S(2)}) async-start(bf16[16,112,512]{2,1,0:T(8,128)(2,1)} %bitcast.17), calls=%async_computation.2 | async-start | bytes 3670016 | tf_op jit(solution)/shard_map/all_to_all | solution.py:187
  34.2 3.3 %collective-permute-start = (bf16[128,896]{1,0:T(8,128)(2,1)S(1)}, bf16[128,896]{1,0:T(8,128)(2,1)S(1)}, u32[]{:S(2)}, u32[]{:S(2)}) collective-permute-start(bf16[128,896]{1,0:T(8,128)(2,1)S(1)} %copy-done.1), channel_id=1, source_target_pairs={{0,4},{2,6},{4,0},{6,2},{1,5},{3,7},{5,1},{7,3},{8,12},{10,14},{12... | collective-permute-start | bytes 688136 | tf_op jit(solution)/shard_map/ppermute | solution.py:22
  39.0 5.5 %collective-permute-start.4 = (f32[128,128]{1,0:T(8,128)S(1)}, f32[128,128]{1,0:T(8,128)S(1)}, u32[]{:S(2)}, u32[]{:S(2)}) collective-permute-start(f32[128,128]{1,0:T(8,128)S(1)} %get-tuple-element.12), channel_id=1, source_target_pairs={{0,128},{128,0},{1,129},{129,1},{2,130},{130,2},{3,131},{131,3},{4... | collective-permute-start | bytes 196616 | tf_op jit(solution)/shard_map/ppermute | solution.py:22
  44.5 7.3 %collective-permute-done.refs_0_ = bf16[128,896]{1,0:T(8,128)(2,1)S(1)} collective-permute-done((bf16[128,896]{1,0:T(8,128)(2,1)S(1)}, bf16[128,896]{1,0:T(8,128)(2,1)S(1)}, u32[]{:S(2)}, u32[]{:S(2)}) %collective-permute-start) | collective-permute-done | bytes 229408 | tf_op jit(solution)/shard_map/ppermute | solution.py:22
  53.0 1.6 %collective-permute-start.5 = (bf16[128,128]{1,0:T(8,128)(2,1)S(1)}, bf16[128,128]{1,0:T(8,128)(2,1)S(1)}, u32[]{:S(2)}, u32[]{:S(2)}) collective-permute-start(bf16[128,128]{1,0:T(8,128)(2,1)S(1)} %multiply_convert_fusion.2.refs_1_), channel_id=1, source_target_pairs={{0,32},{32,64},{64,96},{96,0},{1,33},{33,65},{65,97},{97,1},{2,34}... | collective-permute-start | bytes 98312 | tf_op jit(solution)/shard_map/ppermute | solution.py:22
  54.6 2.6 %collective-permute-start.6 = (bf16[128,128]{1,0:T(8,128)(2,1)S(1)}, bf16[128,128]{1,0:T(8,128)(2,1)S(1)}, u32[]{:S(2)}, u32[]{:S(2)}) collective-permute-start(bf16[128,128]{1,0:T(8,128)(2,1)S(1)} %multiply_convert_fusion.2.refs_1_), channel_id=1, source_target_pairs={{0,64},{32,96},{64,0},{96,32},{1,65},{33,97},{65,1},{97,33},{2,66}... | collective-permute-start | bytes 98312 | tf_op jit(solution)/shard_map/ppermute | solution.py:22
  57.3 1.5 %collective-permute-start.7 = (bf16[128,128]{1,0:T(8,128)(2,1)S(1)}, bf16[128,128]{1,0:T(8,128)(2,1)S(1)}, u32[]{:S(2)}, u32[]{:S(2)}) collective-permute-start(bf16[128,128]{1,0:T(8,128)(2,1)S(1)} %multiply_convert_fusion.2.refs_1_), channel_id=1, source_target_pairs={{0,96},{32,0},{64,32},{96,64},{1,97},{33,1},{65,33},{97,65},{2,98}... | collective-permute-start | bytes 98312 | tf_op jit(solution)/shard_map/ppermute | solution.py:22
  58.7 3.0 %grad.2.refs_0_ = bf16[1792,512]{1,0:T(8,128)(2,1)} custom-call(bf16[128,896]{1,0:T(8,128)(2,1)S(1)} %collective-permute-done.refs_0_, bf16[128,896]{1,0:T(8,128)(2,1)S(1)} %collective-permute-done.1.refs_1_, bf16[128,896]{1,0:T(8,128)(2,1)S(1)} %collective-permute-done.2.refs_2_, bf16[128,896]{1,0:T(8,128)(2,1)S(1)} %collective-permute-done.3.refs_3_, ...), custom_call_target="tpu_custom_call" | custom-call | tf_op jit(solution)/shard_map/grad/pallas_call | solution.py:126
  61.8 6.3 %all-to-all-start.1 = ((bf16[16,112,512]{2,1,0:T(8,128)(2,1)}), bf16[16,112,512]{2,1,0:T(8,128)(2,1)}, u32[]{:S(2)}, u32[]{:S(2)}) async-start(bf16[16,112,512]{2,1,0:T(8,128)(2,1)} %bitcast.16), calls=%async_computation.1 | async-start | bytes 3670016 | tf_op jit(solution)/shard_map/all_to_all | solution.py:187
  68.2 2.8 %collective-permute-start.18 = (bf16[4,128,128]{2,1,0:T(8,128)(2,1)S(1)}, bf16[4,128,128]{2,1,0:T(8,128)(2,1)S(1)}, u32[]{:S(2)}, u32[]{:S(2)}) collective-permute-start(bf16[4,128,128]{2,1,0:T(8,128)(2,1)S(1)} %pad_maximum_fusion.refs_5_.refs_4_), channel_id=1, source_target_pairs={{0,4},{2,6},{4,0},{6,2},{1,5},{3,7},{5,1},{7,3},{8,12},{10,14},{12... | collective-permute-start | bytes 393224 | tf_op jit(solution)/shard_map/ppermute | solution.py:22
  71.0 1.9 %collective-permute-start.20 = (bf16[4,128,128]{2,1,0:T(8,128)(2,1)S(1)}, bf16[4,128,128]{2,1,0:T(8,128)(2,1)S(1)}, u32[]{:S(2)}, u32[]{:S(2)}) collective-permute-start(bf16[4,128,128]{2,1,0:T(8,128)(2,1)S(1)} %pad_maximum_fusion.refs_5_.refs_4_), channel_id=1, source_target_pairs={{0,6},{2,0},{4,2},{6,4},{1,7},{3,1},{5,3},{7,5},{8,14},{10,8},{12,... | collective-permute-start | bytes 393224 | tf_op jit(solution)/shard_map/ppermute | solution.py:22
  73.0 1.8 %convert_reduce_fusion.1 = f32[112,512]{1,0:T(8,128)S(1)} fusion(bf16[16,112,512]{2,1,0:T(8,128)(2,1)} %all-to-all-done.2), kind=kLoop, calls=%fused_computation.1 | loop fusion | flops 1777664 | bytes 2064384 | tf_op jit(solution)/shard_map/reduce_sum | solution.py:191
  74.8 5.1 %collective-permute-start.11 = (bf16[112,512]{1,0:T(8,128)(2,1)S(1)}, bf16[112,512]{1,0:T(8,128)(2,1)S(1)}, u32[]{:S(2)}, u32[]{:S(2)}) collective-permute-start(bf16[112,512]{1,0:T(8,128)(2,1)S(1)} %convert_element_type.29), channel_id=1, source_target_pairs={{0,128},{128,0},{1,129},{129,1},{2,130},{130,2},{3,131},{131,3},{4... | collective-permute-start | bytes 344072 | tf_op jit(solution)/shard_map/ppermute | solution.py:22
  80.4 3.4 %collective-permute-done.18.refs_9_.refs_4_ = bf16[4,128,128]{2,1,0:T(8,128)(2,1)S(1)} collective-permute-done((bf16[4,128,128]{2,1,0:T(8,128)(2,1)S(1)}, bf16[4,128,128]{2,1,0:T(8,128)(2,1)S(1)}, u32[]{:S(2)}, u32[]{:S(2)}) %collective-permute-start.18) | collective-permute-done | bytes 131104 | tf_op jit(solution)/shard_map/ppermute | solution.py:22
  84.4 3.2 %collective-permute-done.11 = bf16[112,512]{1,0:T(8,128)(2,1)S(1)} collective-permute-done((bf16[112,512]{1,0:T(8,128)(2,1)S(1)}, bf16[112,512]{1,0:T(8,128)(2,1)S(1)}, u32[]{:S(2)}, u32[]{:S(2)}) %collective-permute-start.11) | collective-permute-done | bytes 114720 | tf_op jit(solution)/shard_map/ppermute | solution.py:22
  88.2 2.5 %collective-permute-start.13 = (bf16[112,512]{1,0:T(8,128)(2,1)S(1)}, bf16[112,512]{1,0:T(8,128)(2,1)S(1)}, u32[]{:S(2)}, u32[]{:S(2)}) collective-permute-start(bf16[112,512]{1,0:T(8,128)(2,1)S(1)} %multiply_convert_fusion.1.refs_1_.refs_0_), channel_id=1, source_target_pairs={{0,16},{8,24},{16,0},{24,8},{1,17},{9,25},{17,1},{25,9},{2,18},{10... | collective-permute-start | bytes 344072 | tf_op jit(solution)/shard_map/ppermute | solution.py:22
  90.7 3.1 %collective-permute-done.12.refs_2_.refs_1_ = bf16[112,512]{1,0:T(8,128)(2,1)S(1)} collective-permute-done((bf16[112,512]{1,0:T(8,128)(2,1)S(1)}, bf16[112,512]{1,0:T(8,128)(2,1)S(1)}, u32[]{:S(2)}, u32[]{:S(2)}) %collective-permute-start.12) | collective-permute-done | bytes 114720 | tf_op jit(solution)/shard_map/ppermute | solution.py:22
  94.5 2.2 %collective-permute-done.14.refs_4_.refs_3_ = bf16[112,512]{1,0:T(8,128)(2,1)S(1)} collective-permute-done((bf16[112,512]{1,0:T(8,128)(2,1)S(1)}, bf16[112,512]{1,0:T(8,128)(2,1)S(1)}, u32[]{:S(2)}, u32[]{:S(2)}) %collective-permute-start.14) | collective-permute-done | bytes 114720 | tf_op jit(solution)/shard_map/ppermute | solution.py:22
  96.7 1.8 %convert_reduce_fusion = f32[112,512]{1,0:T(8,128)S(1)} fusion(bf16[16,112,512]{2,1,0:T(8,128)(2,1)} %gate.3), kind=kLoop, calls=%fused_computation | loop fusion | flops 1777664 | bytes 2064384 | tf_op jit(solution)/shard_map/reduce_sum | solution.py:191
  98.5 4.6 %collective-permute-start.22 = (bf16[112,512]{1,0:T(8,128)(2,1)S(1)}, bf16[112,512]{1,0:T(8,128)(2,1)S(1)}, u32[]{:S(2)}, u32[]{:S(2)}) collective-permute-start(bf16[112,512]{1,0:T(8,128)(2,1)S(1)} %convert_element_type.33), channel_id=1, source_target_pairs={{0,128},{128,0},{1,129},{129,1},{2,130},{130,2},{3,131},{131,3},{4... | collective-permute-start | bytes 344072 | tf_op jit(solution)/shard_map/ppermute | solution.py:22
  103.0 6.0 %collective-permute-done.22 = bf16[112,512]{1,0:T(8,128)(2,1)S(1)} collective-permute-done((bf16[112,512]{1,0:T(8,128)(2,1)S(1)}, bf16[112,512]{1,0:T(8,128)(2,1)S(1)}, u32[]{:S(2)}, u32[]{:S(2)}) %collective-permute-start.22) | collective-permute-done | bytes 114720 | tf_op jit(solution)/shard_map/ppermute | solution.py:22
  109.1 3.4 %collective-permute-start.23 = (bf16[112,512]{1,0:T(8,128)(2,1)S(1)}, bf16[112,512]{1,0:T(8,128)(2,1)S(1)}, u32[]{:S(2)}, u32[]{:S(2)}) collective-permute-start(bf16[112,512]{1,0:T(8,128)(2,1)S(1)} %multiply_convert_fusion.refs_0_), channel_id=1, source_target_pairs={{0,8},{8,16},{16,24},{24,0},{1,9},{9,17},{17,25},{25,1},{2,10},{10... | collective-permute-start | bytes 344072 | tf_op jit(solution)/shard_map/ppermute | solution.py:22
  114.6 2.3 %collective-permute-done.23.refs_1_ = bf16[112,512]{1,0:T(8,128)(2,1)S(1)} collective-permute-done((bf16[112,512]{1,0:T(8,128)(2,1)S(1)}, bf16[112,512]{1,0:T(8,128)(2,1)S(1)}, u32[]{:S(2)}, u32[]{:S(2)}) %collective-permute-start.23) | collective-permute-done | bytes 114720 | tf_op jit(solution)/shard_map/ppermute | solution.py:22
  116.9 2.6 %collective-permute-done.24.refs_2_ = bf16[112,512]{1,0:T(8,128)(2,1)S(1)} collective-permute-done((bf16[112,512]{1,0:T(8,128)(2,1)S(1)}, bf16[112,512]{1,0:T(8,128)(2,1)S(1)}, u32[]{:S(2)}, u32[]{:S(2)}) %collective-permute-start.24) | collective-permute-done | bytes 114720 | tf_op jit(solution)/shard_map/ppermute | solution.py:22
  121.7 15.8 %all_to_all.20 = f32[4,448,128]{2,1,0:T(8,128)S(1)} all-to-all(f32[4,448,128]{2,1,0:T(8,128)S(1)} %correct.3), channel_id=1, replica_groups=mesh['z_hi'=2,'x'=4,'y'=4,'z_lo'=4,'core'=2] {'x'}, dimensions={0} | all-to-all | bytes 1835008 | tf_op jit(solution)/shard_map/all_to_all | solution.py:248
  (49 shorter events, 10.5 us)
Async XLA Ops:
  0.0 20.5 %copy-start = (bf16[896,1792]{1,0:T(8,128)(2,1)S(1)}, bf16[896,1792]{1,0:T(8,128)(2,1)}, u32[]{:S(2)}) copy-start(bf16[896,1792]{1,0:T(8,128)(2,1)} %refs_4_.3) | copy-start | bytes 9633796
  4.9 7.3 %copy-start.1 = (bf16[128,896]{1,0:T(8,128)(2,1)S(1)}, bf16[128,896]{1,0:T(8,128)(2,1)}, u32[]{:S(2)}) copy-start(bf16[128,896]{1,0:T(8,128)(2,1)} %get-tuple-element.9.refs_0_) | copy-start | bytes 688132
  4.9 22.1 %all-to-all-start = ((bf16[16,128,256]{2,1,0:T(8,128)(2,1)}), bf16[16,128,256]{2,1,0:T(8,128)(2,1)}, u32[]{:S(2)}, u32[]{:S(2)}) async-start(bf16[16,128,256]{2,1,0:T(8,128)(2,1)} %get-tuple-element.10), calls=%async_computation | async-start | bytes 2097152 | tf_op jit(solution)/shard_map/all_to_all | solution.py:152
  12.2 6.9 %collective-permute-start.9 = (bf16[128,896]{1,0:T(8,128)(2,1)S(1)}, bf16[128,896]{1,0:T(8,128)(2,1)S(1)}, u32[]{:S(2)}, u32[]{:S(2)}) collective-permute-start(bf16[128,896]{1,0:T(8,128)(2,1)S(1)} %copy-done.1), channel_id=1, source_target_pairs={{0,2},{2,4},{4,6},{6,0},{1,3},{3,5},{5,7},{7,1},{8,10},{10,12},{12... | collective-permute-start | bytes 688136 | tf_op jit(solution)/shard_map/ppermute | solution.py:22
  14.2 4.9 %collective-permute-start.8 = (bf16[128,896]{1,0:T(8,128)(2,1)S(1)}, bf16[128,896]{1,0:T(8,128)(2,1)S(1)}, u32[]{:S(2)}, u32[]{:S(2)}) collective-permute-start(bf16[128,896]{1,0:T(8,128)(2,1)S(1)} %copy-done.1), channel_id=1, source_target_pairs={{0,1},{1,0},{2,3},{3,2},{4,5},{5,4},{6,7},{7,6},{8,9},{9,8},{10,11... | collective-permute-start | bytes 688136 | tf_op jit(solution)/shard_map/ppermute | solution.py:22
  19.0 1.5 %collective-permute-start.10 = (bf16[128,896]{1,0:T(8,128)(2,1)S(1)}, bf16[128,896]{1,0:T(8,128)(2,1)S(1)}, u32[]{:S(2)}, u32[]{:S(2)}) collective-permute-start(bf16[128,896]{1,0:T(8,128)(2,1)S(1)} %collective-permute-done.9.refs_2_), channel_id=1, source_target_pairs={{0,1},{1,0},{2,3},{3,2},{4,5},{5,4},{6,7},{7,6},{8,9},{9,8},{10,11... | collective-permute-start | bytes 688136 | tf_op jit(solution)/shard_map/ppermute | solution.py:22
  27.0 34.8 %all-to-all-start.2 = ((bf16[16,112,512]{2,1,0:T(8,128)(2,1)}), bf16[16,112,512]{2,1,0:T(8,128)(2,1)}, u32[]{:S(2)}, u32[]{:S(2)}) async-start(bf16[16,112,512]{2,1,0:T(8,128)(2,1)} %bitcast.17), calls=%async_computation.2 | async-start | bytes 3670016 | tf_op jit(solution)/shard_map/all_to_all | solution.py:187
  34.2 17.6 %collective-permute-start = (bf16[128,896]{1,0:T(8,128)(2,1)S(1)}, bf16[128,896]{1,0:T(8,128)(2,1)S(1)}, u32[]{:S(2)}, u32[]{:S(2)}) collective-permute-start(bf16[128,896]{1,0:T(8,128)(2,1)S(1)} %copy-done.1), channel_id=1, source_target_pairs={{0,4},{2,6},{4,0},{6,2},{1,5},{3,7},{5,1},{7,3},{8,12},{10,14},{12... | collective-permute-start | bytes 688136 | tf_op jit(solution)/shard_map/ppermute | solution.py:22
  37.5 15.5 %collective-permute-start.2 = (bf16[128,896]{1,0:T(8,128)(2,1)S(1)}, bf16[128,896]{1,0:T(8,128)(2,1)S(1)}, u32[]{:S(2)}, u32[]{:S(2)}) collective-permute-start(bf16[128,896]{1,0:T(8,128)(2,1)S(1)} %copy-done.1), channel_id=1, source_target_pairs={{0,6},{2,0},{4,2},{6,4},{1,7},{3,1},{5,3},{7,5},{8,14},{10,8},{12,... | collective-permute-start | bytes 688136 | tf_op jit(solution)/shard_map/ppermute | solution.py:22
  39.0 14.0 %collective-permute-start.4 = (f32[128,128]{1,0:T(8,128)S(1)}, f32[128,128]{1,0:T(8,128)S(1)}, u32[]{:S(2)}, u32[]{:S(2)}) collective-permute-start(f32[128,128]{1,0:T(8,128)S(1)} %get-tuple-element.12), channel_id=1, source_target_pairs={{0,128},{128,0},{1,129},{129,1},{2,130},{130,2},{3,131},{131,3},{4... | collective-permute-start | bytes 196616 | tf_op jit(solution)/shard_map/ppermute | solution.py:22
  51.8 6.9 %collective-permute-start.1 = (bf16[128,896]{1,0:T(8,128)(2,1)S(1)}, bf16[128,896]{1,0:T(8,128)(2,1)S(1)}, u32[]{:S(2)}, u32[]{:S(2)}) collective-permute-start(bf16[128,896]{1,0:T(8,128)(2,1)S(1)} %collective-permute-done.refs_0_), channel_id=1, source_target_pairs={{0,1},{1,0},{2,3},{3,2},{4,5},{5,4},{6,7},{7,6},{8,9},{9,8},{10,11... | collective-permute-start | bytes 688136 | tf_op jit(solution)/shard_map/ppermute | solution.py:22
  53.0 5.7 %collective-permute-start.3 = (bf16[128,896]{1,0:T(8,128)(2,1)S(1)}, bf16[128,896]{1,0:T(8,128)(2,1)S(1)}, u32[]{:S(2)}, u32[]{:S(2)}) collective-permute-start(bf16[128,896]{1,0:T(8,128)(2,1)S(1)} %collective-permute-done.2.refs_2_), channel_id=1, source_target_pairs={{0,1},{1,0},{2,3},{3,2},{4,5},{5,4},{6,7},{7,6},{8,9},{9,8},{10,11... | collective-permute-start | bytes 688136 | tf_op jit(solution)/shard_map/ppermute | solution.py:22
  53.0 8.7 %collective-permute-start.5 = (bf16[128,128]{1,0:T(8,128)(2,1)S(1)}, bf16[128,128]{1,0:T(8,128)(2,1)S(1)}, u32[]{:S(2)}, u32[]{:S(2)}) collective-permute-start(bf16[128,128]{1,0:T(8,128)(2,1)S(1)} %multiply_convert_fusion.2.refs_1_), channel_id=1, source_target_pairs={{0,32},{32,64},{64,96},{96,0},{1,33},{33,65},{65,97},{97,1},{2,34}... | collective-permute-start | bytes 98312 | tf_op jit(solution)/shard_map/ppermute | solution.py:22
  54.6 7.2 %collective-permute-start.6 = (bf16[128,128]{1,0:T(8,128)(2,1)S(1)}, bf16[128,128]{1,0:T(8,128)(2,1)S(1)}, u32[]{:S(2)}, u32[]{:S(2)}) collective-permute-start(bf16[128,128]{1,0:T(8,128)(2,1)S(1)} %multiply_convert_fusion.2.refs_1_), channel_id=1, source_target_pairs={{0,64},{32,96},{64,0},{96,32},{1,65},{33,97},{65,1},{97,33},{2,66}... | collective-permute-start | bytes 98312 | tf_op jit(solution)/shard_map/ppermute | solution.py:22
  57.3 4.5 %collective-permute-start.7 = (bf16[128,128]{1,0:T(8,128)(2,1)S(1)}, bf16[128,128]{1,0:T(8,128)(2,1)S(1)}, u32[]{:S(2)}, u32[]{:S(2)}) collective-permute-start(bf16[128,128]{1,0:T(8,128)(2,1)S(1)} %multiply_convert_fusion.2.refs_1_), channel_id=1, source_target_pairs={{0,96},{32,0},{64,32},{96,64},{1,97},{33,1},{65,33},{97,65},{2,98}... | collective-permute-start | bytes 98312 | tf_op jit(solution)/shard_map/ppermute | solution.py:22
  61.8 34.8 %all-to-all-start.1 = ((bf16[16,112,512]{2,1,0:T(8,128)(2,1)}), bf16[16,112,512]{2,1,0:T(8,128)(2,1)}, u32[]{:S(2)}, u32[]{:S(2)}) async-start(bf16[16,112,512]{2,1,0:T(8,128)(2,1)} %bitcast.16), calls=%async_computation.1 | async-start | bytes 3670016 | tf_op jit(solution)/shard_map/all_to_all | solution.py:187
  68.1 11.7 %collective-permute-start.16 = (bf16[4,128,128]{2,1,0:T(8,128)(2,1)S(1)}, bf16[4,128,128]{2,1,0:T(8,128)(2,1)S(1)}, u32[]{:S(2)}, u32[]{:S(2)}) collective-permute-start(bf16[4,128,128]{2,1,0:T(8,128)(2,1)S(1)} %pad_maximum_fusion.refs_5_.refs_4_), channel_id=1, source_target_pairs={{0,2},{2,4},{4,6},{6,0},{1,3},{3,5},{5,7},{7,1},{8,10},{10,12},{12... | collective-permute-start | bytes 393224 | tf_op jit(solution)/shard_map/ppermute | solution.py:22
  68.2 15.6 %collective-permute-start.18 = (bf16[4,128,128]{2,1,0:T(8,128)(2,1)S(1)}, bf16[4,128,128]{2,1,0:T(8,128)(2,1)S(1)}, u32[]{:S(2)}, u32[]{:S(2)}) collective-permute-start(bf16[4,128,128]{2,1,0:T(8,128)(2,1)S(1)} %pad_maximum_fusion.refs_5_.refs_4_), channel_id=1, source_target_pairs={{0,4},{2,6},{4,0},{6,2},{1,5},{3,7},{5,1},{7,3},{8,12},{10,14},{12... | collective-permute-start | bytes 393224 | tf_op jit(solution)/shard_map/ppermute | solution.py:22
  71.0 13.3 %collective-permute-start.20 = (bf16[4,128,128]{2,1,0:T(8,128)(2,1)S(1)}, bf16[4,128,128]{2,1,0:T(8,128)(2,1)S(1)}, u32[]{:S(2)}, u32[]{:S(2)}) collective-permute-start(bf16[4,128,128]{2,1,0:T(8,128)(2,1)S(1)} %pad_maximum_fusion.refs_5_.refs_4_), channel_id=1, source_target_pairs={{0,6},{2,0},{4,2},{6,4},{1,7},{3,1},{5,3},{7,5},{8,14},{10,8},{12,... | collective-permute-start | bytes 393224 | tf_op jit(solution)/shard_map/ppermute | solution.py:22
  74.8 12.8 %collective-permute-start.11 = (bf16[112,512]{1,0:T(8,128)(2,1)S(1)}, bf16[112,512]{1,0:T(8,128)(2,1)S(1)}, u32[]{:S(2)}, u32[]{:S(2)}) collective-permute-start(bf16[112,512]{1,0:T(8,128)(2,1)S(1)} %convert_element_type.29), channel_id=1, source_target_pairs={{0,128},{128,0},{1,129},{129,1},{2,130},{130,2},{3,131},{131,3},{4... | collective-permute-start | bytes 344072 | tf_op jit(solution)/shard_map/ppermute | solution.py:22
  79.8 8.3 %collective-permute-start.15 = (bf16[4,128,128]{2,1,0:T(8,128)(2,1)S(1)}, bf16[4,128,128]{2,1,0:T(8,128)(2,1)S(1)}, u32[]{:S(2)}, u32[]{:S(2)}) collective-permute-start(bf16[4,128,128]{2,1,0:T(8,128)(2,1)S(1)} %pad_maximum_fusion.refs_5_.refs_4_), channel_id=1, source_target_pairs={{0,1},{1,0},{2,3},{3,2},{4,5},{5,4},{6,7},{7,6},{8,9},{9,8},{10,11... | collective-permute-start | bytes 393224 | tf_op jit(solution)/shard_map/ppermute | solution.py:22
  79.9 10.8 %collective-permute-start.17 = (bf16[4,128,128]{2,1,0:T(8,128)(2,1)S(1)}, bf16[4,128,128]{2,1,0:T(8,128)(2,1)S(1)}, u32[]{:S(2)}, u32[]{:S(2)}) collective-permute-start(bf16[4,128,128]{2,1,0:T(8,128)(2,1)S(1)} %collective-permute-done.16.refs_7_.refs_6_), channel_id=1, source_target_pairs={{0,1},{1,0},{2,3},{3,2},{4,5},{5,4},{6,7},{7,6},{8,9},{9,8},{10,11... | collective-permute-start | bytes 393224 | tf_op jit(solution)/shard_map/ppermute | solution.py:22
  83.8 6.9 %collective-permute-start.19 = (bf16[4,128,128]{2,1,0:T(8,128)(2,1)S(1)}, bf16[4,128,128]{2,1,0:T(8,128)(2,1)S(1)}, u32[]{:S(2)}, u32[]{:S(2)}) collective-permute-start(bf16[4,128,128]{2,1,0:T(8,128)(2,1)S(1)} %collective-permute-done.18.refs_9_.refs_4_), channel_id=1, source_target_pairs={{0,1},{1,0},{2,3},{3,2},{4,5},{5,4},{6,7},{7,6},{8,9},{9,8},{10,11... | collective-permute-start | bytes 393224 | tf_op jit(solution)/shard_map/ppermute | solution.py:22
  84.4 6.3 %collective-permute-start.21 = (bf16[4,128,128]{2,1,0:T(8,128)(2,1)S(1)}, bf16[4,128,128]{2,1,0:T(8,128)(2,1)S(1)}, u32[]{:S(2)}, u32[]{:S(2)}) collective-permute-start(bf16[4,128,128]{2,1,0:T(8,128)(2,1)S(1)} %collective-permute-done.20.refs_11_.refs_6_), channel_id=1, source_target_pairs={{0,1},{1,0},{2,3},{3,2},{4,5},{5,4},{6,7},{7,6},{8,9},{9,8},{10,11... | collective-permute-start | bytes 393224 | tf_op jit(solution)/shard_map/ppermute | solution.py:22
  87.7 6.1 %collective-permute-start.12 = (bf16[112,512]{1,0:T(8,128)(2,1)S(1)}, bf16[112,512]{1,0:T(8,128)(2,1)S(1)}, u32[]{:S(2)}, u32[]{:S(2)}) collective-permute-start(bf16[112,512]{1,0:T(8,128)(2,1)S(1)} %multiply_convert_fusion.1.refs_1_.refs_0_), channel_id=1, source_target_pairs={{0,8},{8,16},{16,24},{24,0},{1,9},{9,17},{17,25},{25,1},{2,10},{10... | collective-permute-start | bytes 344072 | tf_op jit(solution)/shard_map/ppermute | solution.py:22
  88.2 6.3 %collective-permute-start.13 = (bf16[112,512]{1,0:T(8,128)(2,1)S(1)}, bf16[112,512]{1,0:T(8,128)(2,1)S(1)}, u32[]{:S(2)}, u32[]{:S(2)}) collective-permute-start(bf16[112,512]{1,0:T(8,128)(2,1)S(1)} %multiply_convert_fusion.1.refs_1_.refs_0_), channel_id=1, source_target_pairs={{0,16},{8,24},{16,0},{24,8},{1,17},{9,25},{17,1},{25,9},{2,18},{10... | collective-permute-start | bytes 344072 | tf_op jit(solution)/shard_map/ppermute | solution.py:22
  90.7 6.0 %collective-permute-start.14 = (bf16[112,512]{1,0:T(8,128)(2,1)S(1)}, bf16[112,512]{1,0:T(8,128)(2,1)S(1)}, u32[]{:S(2)}, u32[]{:S(2)}) collective-permute-start(bf16[112,512]{1,0:T(8,128)(2,1)S(1)} %multiply_convert_fusion.1.refs_1_.refs_0_), channel_id=1, source_target_pairs={{0,24},{8,0},{16,8},{24,16},{1,25},{9,1},{17,9},{25,17},{2,26},{10... | collective-permute-start | bytes 344072 | tf_op jit(solution)/shard_map/ppermute | solution.py:22
  98.5 10.6 %collective-permute-start.22 = (bf16[112,512]{1,0:T(8,128)(2,1)S(1)}, bf16[112,512]{1,0:T(8,128)(2,1)S(1)}, u32[]{:S(2)}, u32[]{:S(2)}) collective-permute-start(bf16[112,512]{1,0:T(8,128)(2,1)S(1)} %convert_element_type.33), channel_id=1, source_target_pairs={{0,128},{128,0},{1,129},{129,1},{2,130},{130,2},{3,131},{131,3},{4... | collective-permute-start | bytes 344072 | tf_op jit(solution)/shard_map/ppermute | solution.py:22
  109.1 7.8 %collective-permute-start.23 = (bf16[112,512]{1,0:T(8,128)(2,1)S(1)}, bf16[112,512]{1,0:T(8,128)(2,1)S(1)}, u32[]{:S(2)}, u32[]{:S(2)}) collective-permute-start(bf16[112,512]{1,0:T(8,128)(2,1)S(1)} %multiply_convert_fusion.refs_0_), channel_id=1, source_target_pairs={{0,8},{8,16},{16,24},{24,0},{1,9},{9,17},{17,25},{25,1},{2,10},{10... | collective-permute-start | bytes 344072 | tf_op jit(solution)/shard_map/ppermute | solution.py:22
  112.5 7.0 %collective-permute-start.24 = (bf16[112,512]{1,0:T(8,128)(2,1)S(1)}, bf16[112,512]{1,0:T(8,128)(2,1)S(1)}, u32[]{:S(2)}, u32[]{:S(2)}) collective-permute-start(bf16[112,512]{1,0:T(8,128)(2,1)S(1)} %multiply_convert_fusion.refs_0_), channel_id=1, source_target_pairs={{0,16},{8,24},{16,0},{24,8},{1,17},{9,25},{17,1},{25,9},{2,18},{10... | collective-permute-start | bytes 344072 | tf_op jit(solution)/shard_map/ppermute | solution.py:22
  113.1 7.5 %collective-permute-start.25 = (bf16[112,512]{1,0:T(8,128)(2,1)S(1)}, bf16[112,512]{1,0:T(8,128)(2,1)S(1)}, u32[]{:S(2)}, u32[]{:S(2)}) collective-permute-start(bf16[112,512]{1,0:T(8,128)(2,1)S(1)} %multiply_convert_fusion.refs_0_), channel_id=1, source_target_pairs={{0,24},{8,0},{16,8},{24,16},{1,25},{9,1},{17,9},{25,17},{2,26},{10... | collective-permute-start | bytes 344072 | tf_op jit(solution)/shard_map/ppermute | solution.py:22

commit v7 on v6

--- a/solution.py
+++ b/solution.py
@@ -170,10 +170,10 @@
     del refs
 
 
-def gated(value, *after):
+def gated(value, after, place=pltpu.HBM):
     return pl.pallas_call(
         gate_kernel,
-        out_shape=pltpu.HBM(value.shape, value.dtype),
+        out_shape=place(value.shape, value.dtype),
         in_specs=[ANY] * (1 + len(after)),
         out_specs=ANY,
         input_output_aliases={0: 0},
@@ -230,19 +230,20 @@
 
 def per_device(hidden, norm_gain, gate_pre, out_grad, grad_basis, act_basis):
     act_parts, up_grad = first_partials(hidden, norm_gain, gate_pre, out_grad, act_basis)
-    rows = []
-    for own in [up_grad] + [shifted(up_grad, "z_lo", step) for step in (1, 2, 3)]:
-        rows += [own, shifted(own, "core", 1)]
+    near, far, farthest = [shifted(up_grad, "z_lo", step) for step in (1, 2, 3)]
+    near = gated(near, [far], jax.ShapeDtypeStruct)
+    near_rows = [up_grad, shifted(up_grad, "core", 1), near, shifted(near, "core", 1)]
+    far_rows = [far, shifted(far, "core", 1), farthest, shifted(farthest, "core", 1)]
     act_row = act_squares(act_parts)
-    near_got = exchanged(grad_partials(rows[:4], grad_basis))
-    far_got = exchanged(gated(grad_partials(rows[4:], grad_basis), *act_row))
+    near_got = exchanged(grad_partials(near_rows, grad_basis))
+    far_got = exchanged(gated(grad_partials(far_rows, grad_basis), act_row))
     act_own = jnp.stack(act_row)
     acts = []
     for own in [act_own] + [shifted(act_own, "z_lo", step) for step in (1, 2, 3)]:
         acts += [own, shifted(own, "core", 1)]
     near_sq = squared(near_got)
     near_pieces = [near_sq] + [shifted(near_sq, "y", step) for step in (1, 2, 3)]
-    far_sq = squared(gated(far_got, *near_pieces, *acts))
+    far_sq = squared(gated(far_got, acts, jax.ShapeDtypeStruct))
     far_pieces = [far_sq] + [shifted(far_sq, "y", step) for step in (1, 2, 3)]
     out = corrected(far_pieces, acts[4:], corrected(near_pieces, acts[:4]))
     out = lax.all_to_all(out, "x", 0, 0, tiled=True)

time: 139 us -> 136 us (0.978)
  the two profiles are of different devices: /device:TPU:56 before, /device:TPU:64 now
where the time goes in v7:
time: 136 us; the launch traced here: 133 us
  waiting for transfers between devices  50.6 us (37%)
  starting transfers between devices  50.4 us (37%)
  Pallas kernels  14.4 us (11%)
  blocking collectives  13 us (10%)
  local copies, waits for them, and re-layouts  2.48 us (2%)
  other arithmetic  2.24 us (2%)
    ppermute x26, waiting for transfers between devices, shifted(): lax.ppermute(value, axis, [(i, (i + step) % size) for i in range(size)])  42.2 us
    ppermute x26, starting transfers between devices, shifted(): lax.ppermute(value, axis, [(i, (i + step) % size) for i in range(size)])  32.6 us
    all_to_all x1, blocking collectives, per_device(): out = lax.all_to_all(out, 'x', 0, 0, tiled=True)  13 us
    all_to_all x2, starting transfers between devices, exchanged(): lax.all_to_all(partial.reshape(16, columns // 16, tokens), ('x', 'y'), 0,...  10.7 us
    all_to_all x2, waiting for transfers between devices, exchanged(): lax.all_to_all(partial.reshape(16, columns // 16, tokens), ('x', 'y'), 0,...  8.42 us
    all_to_all x1, starting transfers between devices, act_squares(): got = lax.all_to_all(partials, ('x', 'y'), 0, 0, tiled=True)  7.1 us
    pallas_call x2, Pallas kernels, grad_partials(): pl.pallas_call(lambda *refs: grad_kernel(len(parts), *refs), out_shape=pl...  6.05 us
    pallas_call x1, Pallas kernels, first_partials(): pl.pallas_call(first_kernel, out_shape=(pltpu.HBM(shape, jnp.bfloat16), p...  4.83 us
  transfers between devices with their start and end apart: 29, of which 13 were waited for; matrix products, arithmetic and copies ran while one was open for 2% of the time, Pallas kernels for 6%

profile of v7, /device:TPU:64, one launch (start us, length us, event | category | flops | bytes accessed | tf_op | source)
XLA Modules:
  0.0 133.2 jit_solution(12527627704892781989)
XLA Ops:
  0.0 4.8 %first.1 = (bf16[16,128,256]{2,1,0:T(8,128)(2,1)}, bf16[128,896]{1,0:T(8,128)(2,1)}) custom-call(s32[1]{0:T(128)} %bitcast.2.place, f32[1,8192]{1,0:T(1,128)} %bitcast.19, bf16[128,896]{1,0:T(8,128)(2,1)} %gate_at.1, bf16[128,896]{1,0:T(8,128)(2,1)} %grad_at.1, bf16[128,8192]{1,0:T(8,128)(2,1)} %hidden_at.1, bf16[256,4096]{1,0:T(8,128)(2,1)} %basis_at.1), custom_call_target="tpu_custom_call" | custom-call | tf_op jit(solution)/shard_map/first/pallas_call | solution.py:84
  4.8 7.1 %all-to-all-start = ((bf16[16,128,256]{2,1,0:T(8,128)(2,1)}), bf16[16,128,256]{2,1,0:T(8,128)(2,1)}, u32[]{:S(2)}, u32[]{:S(2)}) async-start(bf16[16,128,256]{2,1,0:T(8,128)(2,1)} %get-tuple-element.10), calls=%async_computation | async-start | bytes 2097152 | tf_op jit(solution)/shard_map/all_to_all | solution.py:152
  12.1 2.0 %collective-permute-start.20 = (bf16[128,896]{1,0:T(8,128)(2,1)}, bf16[128,896]{1,0:T(8,128)(2,1)S(1)}, u32[]{:S(2)}, u32[]{:S(2)}) collective-permute-start(bf16[128,896]{1,0:T(8,128)(2,1)} %get-tuple-element.9.refs_0_), channel_id=1, source_target_pairs={{0,2},{2,4},{4,6},{6,0},{1,3},{3,5},{5,7},{7,1},{8,10},{10,12},{12... | collective-permute-start | bytes 688136 | tf_op jit(solution)/shard_map/ppermute | solution.py:22
  14.0 13.0 %collective-permute-done.refs_0_.refs_1_ = bf16[128,896]{1,0:T(8,128)(2,1)S(1)} collective-permute-done((bf16[128,896]{1,0:T(8,128)(2,1)}, bf16[128,896]{1,0:T(8,128)(2,1)S(1)}, u32[]{:S(2)}, u32[]{:S(2)}) %collective-permute-start) | collective-permute-done | bytes 229408 | tf_op jit(solution)/shard_map/ppermute | solution.py:22
  27.0 3.0 %collective-permute-done.20.refs_0_ = bf16[128,896]{1,0:T(8,128)(2,1)S(1)} collective-permute-done((bf16[128,896]{1,0:T(8,128)(2,1)}, bf16[128,896]{1,0:T(8,128)(2,1)S(1)}, u32[]{:S(2)}, u32[]{:S(2)}) %collective-permute-start.20) | collective-permute-done | bytes 229408 | tf_op jit(solution)/shard_map/ppermute | solution.py:22
  30.1 1.5 %collective-permute-done.21.refs_3_ = bf16[128,896]{1,0:T(8,128)(2,1)S(1)} collective-permute-done((bf16[128,896]{1,0:T(8,128)(2,1)S(1)}, bf16[128,896]{1,0:T(8,128)(2,1)S(1)}, u32[]{:S(2)}, u32[]{:S(2)}) %collective-permute-start.21) | collective-permute-done | bytes 229408 | tf_op jit(solution)/shard_map/ppermute | solution.py:22
  32.5 3.0 %grad.3 = bf16[1792,512]{1,0:T(8,128)(2,1)} custom-call(bf16[128,896]{1,0:T(8,128)(2,1)S(1)} %copy-done.1, bf16[128,896]{1,0:T(8,128)(2,1)S(1)} %collective-permute-done.19.refs_1_, bf16[128,896]{1,0:T(8,128)(2,1)S(1)} %gate.5.refs_2_, bf16[128,896]{1,0:T(8,128)(2,1)S(1)} %collective-permute-done.21.refs_3_, bf16[896,1792]{1,0:T(8,128)(2,1)S(1)} %copy-done), custom_call_target="tpu_custom_call" | custom-call | tf_op jit(solution)/shard_map/grad/pallas_call | solution.py:126
  35.5 6.9 %all-to-all-start.2 = ((bf16[16,112,512]{2,1,0:T(8,128)(2,1)}), bf16[16,112,512]{2,1,0:T(8,128)(2,1)}, u32[]{:S(2)}, u32[]{:S(2)}) async-start(bf16[16,112,512]{2,1,0:T(8,128)(2,1)} %bitcast.17), calls=%async_computation.2 | async-start | bytes 3670016 | tf_op jit(solution)/shard_map/all_to_all | solution.py:187
  42.5 1.4 %act_sum.1 = (f32[128,128]{1,0:T(8,128)S(1)}, f32[128,128]{1,0:T(8,128)S(1)}) custom-call(s32[1]{0:T(128)} %bitcast.4.place, bf16[16,128,256]{2,1,0:T(8,128)(2,1)} %all-to-all-done.got), custom_call_target="tpu_custom_call" | custom-call | tf_op jit(solution)/shard_map/act_sum/pallas_call | solution.py:156
  43.8 5.0 %collective-permute-start.4 = (f32[128,128]{1,0:T(8,128)S(1)}, f32[128,128]{1,0:T(8,128)S(1)}, u32[]{:S(2)}, u32[]{:S(2)}) collective-permute-start(f32[128,128]{1,0:T(8,128)S(1)} %get-tuple-element.12), channel_id=1, source_target_pairs={{0,128},{128,0},{1,129},{129,1},{2,130},{130,2},{3,131},{131,3},{4... | collective-permute-start | bytes 196616 | tf_op jit(solution)/shard_map/ppermute | solution.py:22
  48.9 1.2 collective-permute-done.2.refs_2_
  50.0 7.3 %collective-permute-done.4 = f32[128,128]{1,0:T(8,128)S(1)} collective-permute-done((f32[128,128]{1,0:T(8,128)S(1)}, f32[128,128]{1,0:T(8,128)S(1)}, u32[]{:S(2)}, u32[]{:S(2)}) %collective-permute-start.4) | collective-permute-done | bytes 65568 | tf_op jit(solution)/shard_map/ppermute | solution.py:22
  57.4 1.6 %collective-permute-start.5 = (bf16[128,128]{1,0:T(8,128)(2,1)S(1)}, bf16[128,128]{1,0:T(8,128)(2,1)S(1)}, u32[]{:S(2)}, u32[]{:S(2)}) collective-permute-start(bf16[128,128]{1,0:T(8,128)(2,1)S(1)} %multiply_convert_fusion.2.refs_1_), channel_id=1, source_target_pairs={{0,32},{32,64},{64,96},{96,0},{1,33},{33,65},{65,97},{97,1},{2,34}... | collective-permute-start | bytes 98312 | tf_op jit(solution)/shard_map/ppermute | solution.py:22
  59.0 2.7 %collective-permute-start.6 = (bf16[128,128]{1,0:T(8,128)(2,1)S(1)}, bf16[128,128]{1,0:T(8,128)(2,1)S(1)}, u32[]{:S(2)}, u32[]{:S(2)}) collective-permute-start(bf16[128,128]{1,0:T(8,128)(2,1)S(1)} %multiply_convert_fusion.2.refs_1_), channel_id=1, source_target_pairs={{0,64},{32,96},{64,0},{96,32},{1,65},{33,97},{65,1},{97,33},{2,66}... | collective-permute-start | bytes 98312 | tf_op jit(solution)/shard_map/ppermute | solution.py:22
  61.7 1.5 %collective-permute-start.7 = (bf16[128,128]{1,0:T(8,128)(2,1)S(1)}, bf16[128,128]{1,0:T(8,128)(2,1)S(1)}, u32[]{:S(2)}, u32[]{:S(2)}) collective-permute-start(bf16[128,128]{1,0:T(8,128)(2,1)S(1)} %multiply_convert_fusion.2.refs_1_), channel_id=1, source_target_pairs={{0,96},{32,0},{64,32},{96,64},{1,97},{33,1},{65,33},{97,65},{2,98}... | collective-permute-start | bytes 98312 | tf_op jit(solution)/shard_map/ppermute | solution.py:22
  63.1 3.0 %grad.2.refs_0_ = bf16[1792,512]{1,0:T(8,128)(2,1)} custom-call(bf16[128,896]{1,0:T(8,128)(2,1)S(1)} %collective-permute-done.refs_0_.refs_1_, bf16[128,896]{1,0:T(8,128)(2,1)S(1)} %collective-permute-done.1.refs_1_, bf16[128,896]{1,0:T(8,128)(2,1)S(1)} %collective-permute-done.2.refs_2_, bf16[128,896]{1,0:T(8,128)(2,1)S(1)} %collective-permute-done.3.refs_3_, ...), custom_call_target="tpu_custom_call" | custom-call | tf_op jit(solution)/shard_map/grad/pallas_call | solution.py:126
  66.2 1.7 %collective-permute-done.6.refs_3_ = bf16[128,128]{1,0:T(8,128)(2,1)S(1)} collective-permute-done((bf16[128,128]{1,0:T(8,128)(2,1)S(1)}, bf16[128,128]{1,0:T(8,128)(2,1)S(1)}, u32[]{:S(2)}, u32[]{:S(2)}) %collective-permute-start.6) | collective-permute-done | bytes 32800 | tf_op jit(solution)/shard_map/ppermute | solution.py:22
  68.5 1.6 %all-to-all-done.2 = bf16[16,112,512]{2,1,0:T(8,128)(2,1)} async-done(((bf16[16,112,512]{2,1,0:T(8,128)(2,1)}), bf16[16,112,512]{2,1,0:T(8,128)(2,1)}, u32[]{:S(2)}, u32[]{:S(2)}) %all-to-all-start.2) | async-done | bytes 1835040 | tf_op jit(solution)/shard_map/all_to_all | solution.py:187
  70.1 3.8 %all-to-all-start.1 = ((bf16[16,112,512]{2,1,0:T(8,128)(2,1)}), bf16[16,112,512]{2,1,0:T(8,128)(2,1)S(1)}, u32[]{:S(2)}, u32[]{:S(2)}) async-start(bf16[16,112,512]{2,1,0:T(8,128)(2,1)} %bitcast.16), calls=%async_computation.1 | async-start | bytes 3670016 | tf_op jit(solution)/shard_map/all_to_all | solution.py:187
  74.1 1.2 collective-permute-start.11
  75.2 2.1 %collective-permute-start.13 = (bf16[4,128,128]{2,1,0:T(8,128)(2,1)S(1)}, bf16[4,128,128]{2,1,0:T(8,128)(2,1)S(1)}, u32[]{:S(2)}, u32[]{:S(2)}) collective-permute-start(bf16[4,128,128]{2,1,0:T(8,128)(2,1)S(1)} %pad_maximum_fusion.refs_1_.refs_4_), channel_id=1, source_target_pairs={{0,6},{2,0},{4,2},{6,4},{1,7},{3,1},{5,3},{7,5},{8,14},{10,8},{12,... | collective-permute-start | bytes 393224 | tf_op jit(solution)/shard_map/ppermute | solution.py:22
  77.3 7.5 %collective-permute-done.9.refs_3_.refs_6_ = bf16[4,128,128]{2,1,0:T(8,128)(2,1)S(1)} collective-permute-done((bf16[4,128,128]{2,1,0:T(8,128)(2,1)S(1)}, bf16[4,128,128]{2,1,0:T(8,128)(2,1)S(1)}, u32[]{:S(2)}, u32[]{:S(2)}) %collective-permute-start.9) | collective-permute-done | bytes 131104 | tf_op jit(solution)/shard_map/ppermute | solution.py:22
  85.5 1.8 %convert_reduce_fusion = f32[112,512]{1,0:T(8,128)S(1)} fusion(bf16[16,112,512]{2,1,0:T(8,128)(2,1)} %all-to-all-done.2), kind=kLoop, calls=%fused_computation | loop fusion | flops 1777664 | bytes 2064384 | tf_op jit(solution)/shard_map/reduce_sum | solution.py:191
  87.3 5.4 %collective-permute-start.22 = (bf16[112,512]{1,0:T(8,128)(2,1)S(1)}, bf16[112,512]{1,0:T(8,128)(2,1)S(1)}, u32[]{:S(2)}, u32[]{:S(2)}) collective-permute-start(bf16[112,512]{1,0:T(8,128)(2,1)S(1)} %convert_element_type.33), channel_id=1, source_target_pairs={{0,128},{128,0},{1,129},{129,1},{2,130},{130,2},{3,131},{131,3},{4... | collective-permute-start | bytes 344072 | tf_op jit(solution)/shard_map/ppermute | solution.py:22
  92.7 6.8 %all-to-all-done.1.refs_0_ = bf16[16,112,512]{2,1,0:T(8,128)(2,1)S(1)} async-done(((bf16[16,112,512]{2,1,0:T(8,128)(2,1)}), bf16[16,112,512]{2,1,0:T(8,128)(2,1)S(1)}, u32[]{:S(2)}, u32[]{:S(2)}) %all-to-all-start.1) | async-done | bytes 1835040 | tf_op jit(solution)/shard_map/all_to_all | solution.py:187
  99.8 5.0 %collective-permute-start.15 = (bf16[112,512]{1,0:T(8,128)(2,1)S(1)}, bf16[112,512]{1,0:T(8,128)(2,1)S(1)}, u32[]{:S(2)}, u32[]{:S(2)}) collective-permute-start(bf16[112,512]{1,0:T(8,128)(2,1)S(1)} %convert_element_type.29), channel_id=1, source_target_pairs={{0,128},{128,0},{1,129},{129,1},{2,130},{130,2},{3,131},{131,3},{4... | collective-permute-start | bytes 344072 | tf_op jit(solution)/shard_map/ppermute | solution.py:22
  106.3 2.0 %collective-permute-start.25 = (bf16[112,512]{1,0:T(8,128)(2,1)S(1)}, bf16[112,512]{1,0:T(8,128)(2,1)S(1)}, u32[]{:S(2)}, u32[]{:S(2)}) collective-permute-start(bf16[112,512]{1,0:T(8,128)(2,1)S(1)} %multiply_convert_fusion.refs_0_), channel_id=1, source_target_pairs={{0,24},{8,0},{16,8},{24,16},{1,25},{9,1},{17,9},{25,17},{2,26},{10... | collective-permute-start | bytes 344072 | tf_op jit(solution)/shard_map/ppermute | solution.py:22
  108.3 1.6 %collective-permute-done.15 = bf16[112,512]{1,0:T(8,128)(2,1)S(1)} collective-permute-done((bf16[112,512]{1,0:T(8,128)(2,1)S(1)}, bf16[112,512]{1,0:T(8,128)(2,1)S(1)}, u32[]{:S(2)}, u32[]{:S(2)}) %collective-permute-start.15) | collective-permute-done | bytes 114720 | tf_op jit(solution)/shard_map/ppermute | solution.py:22
  111.3 2.1 %collective-permute-done.23.refs_1_ = bf16[112,512]{1,0:T(8,128)(2,1)S(1)} collective-permute-done((bf16[112,512]{1,0:T(8,128)(2,1)S(1)}, bf16[112,512]{1,0:T(8,128)(2,1)S(1)}, u32[]{:S(2)}, u32[]{:S(2)}) %collective-permute-start.23) | collective-permute-done | bytes 114720 | tf_op jit(solution)/shard_map/ppermute | solution.py:22
  115.0 2.3 %collective-permute-done.16.refs_1_ = bf16[112,512]{1,0:T(8,128)(2,1)S(1)} collective-permute-done((bf16[112,512]{1,0:T(8,128)(2,1)S(1)}, bf16[112,512]{1,0:T(8,128)(2,1)S(1)}, u32[]{:S(2)}, u32[]{:S(2)}) %collective-permute-start.16) | collective-permute-done | bytes 114720 | tf_op jit(solution)/shard_map/ppermute | solution.py:22
  118.2 1.1 correct.3
  119.3 13.0 %all_to_all.20 = f32[4,448,128]{2,1,0:T(8,128)S(1)} all-to-all(f32[4,448,128]{2,1,0:T(8,128)S(1)} %correct.3), channel_id=1, replica_groups=mesh['z_hi'=2,'x'=4,'y'=4,'z_lo'=4,'core'=2] {'x'}, dimensions={0} | all-to-all | bytes 1835008 | tf_op jit(solution)/shard_map/all_to_all | solution.py:249
  (54 shorter events, 9.1 us)
Async XLA Ops:
  0.0 31.5 %copy-start = (bf16[896,1792]{1,0:T(8,128)(2,1)S(1)}, bf16[896,1792]{1,0:T(8,128)(2,1)}, u32[]{:S(2)}) copy-start(bf16[896,1792]{1,0:T(8,128)(2,1)} %refs_4_.3) | copy-start | bytes 9633796
  4.8 30.7 %all-to-all-start = ((bf16[16,128,256]{2,1,0:T(8,128)(2,1)}), bf16[16,128,256]{2,1,0:T(8,128)(2,1)}, u32[]{:S(2)}, u32[]{:S(2)}) async-start(bf16[16,128,256]{2,1,0:T(8,128)(2,1)} %get-tuple-element.10), calls=%async_computation | async-start | bytes 2097152 | tf_op jit(solution)/shard_map/all_to_all | solution.py:152
  12.0 15.1 %collective-permute-start = (bf16[128,896]{1,0:T(8,128)(2,1)}, bf16[128,896]{1,0:T(8,128)(2,1)S(1)}, u32[]{:S(2)}, u32[]{:S(2)}) collective-permute-start(bf16[128,896]{1,0:T(8,128)(2,1)} %get-tuple-element.9.refs_0_), channel_id=1, source_target_pairs={{0,4},{2,6},{4,0},{6,2},{1,5},{3,7},{5,1},{7,3},{8,12},{10,14},{12... | collective-permute-start | bytes 688136 | tf_op jit(solution)/shard_map/ppermute | solution.py:22
  12.1 18.0 %collective-permute-start.20 = (bf16[128,896]{1,0:T(8,128)(2,1)}, bf16[128,896]{1,0:T(8,128)(2,1)S(1)}, u32[]{:S(2)}, u32[]{:S(2)}) collective-permute-start(bf16[128,896]{1,0:T(8,128)(2,1)} %get-tuple-element.9.refs_0_), channel_id=1, source_target_pairs={{0,2},{2,4},{4,6},{6,0},{1,3},{3,5},{5,7},{7,1},{8,10},{10,12},{12... | collective-permute-start | bytes 688136 | tf_op jit(solution)/shard_map/ppermute | solution.py:22
  14.0 16.0 %collective-permute-start.19 = (bf16[128,896]{1,0:T(8,128)(2,1)}, bf16[128,896]{1,0:T(8,128)(2,1)S(1)}, u32[]{:S(2)}, u32[]{:S(2)}) collective-permute-start(bf16[128,896]{1,0:T(8,128)(2,1)} %get-tuple-element.9.refs_0_), channel_id=1, source_target_pairs={{0,1},{1,0},{2,3},{3,2},{4,5},{5,4},{6,7},{7,6},{8,9},{9,8},{10,11... | collective-permute-start | bytes 688136 | tf_op jit(solution)/shard_map/ppermute | solution.py:22
  30.0 1.5 %collective-permute-start.21 = (bf16[128,896]{1,0:T(8,128)(2,1)S(1)}, bf16[128,896]{1,0:T(8,128)(2,1)S(1)}, u32[]{:S(2)}, u32[]{:S(2)}) collective-permute-start(bf16[128,896]{1,0:T(8,128)(2,1)S(1)} %gate.5.refs_2_), channel_id=1, source_target_pairs={{0,1},{1,0},{2,3},{3,2},{4,5},{5,4},{6,7},{7,6},{8,9},{9,8},{10,11... | collective-permute-start | bytes 688136 | tf_op jit(solution)/shard_map/ppermute | solution.py:22
  31.5 0.9 copy-start.1
  35.5 34.6 %all-to-all-start.2 = ((bf16[16,112,512]{2,1,0:T(8,128)(2,1)}), bf16[16,112,512]{2,1,0:T(8,128)(2,1)}, u32[]{:S(2)}, u32[]{:S(2)}) async-start(bf16[16,112,512]{2,1,0:T(8,128)(2,1)} %bitcast.17), calls=%async_computation.2 | async-start | bytes 3670016 | tf_op jit(solution)/shard_map/all_to_all | solution.py:187
  42.4 7.7 %collective-permute-start.2 = (bf16[128,896]{1,0:T(8,128)(2,1)}, bf16[128,896]{1,0:T(8,128)(2,1)S(1)}, u32[]{:S(2)}, u32[]{:S(2)}) collective-permute-start(bf16[128,896]{1,0:T(8,128)(2,1)} %get-tuple-element.9.refs_0_), channel_id=1, source_target_pairs={{0,6},{2,0},{4,2},{6,4},{1,7},{3,1},{5,3},{7,5},{8,14},{10,8},{12,... | collective-permute-start | bytes 688136 | tf_op jit(solution)/shard_map/ppermute | solution.py:22
  43.8 13.5 %collective-permute-start.4 = (f32[128,128]{1,0:T(8,128)S(1)}, f32[128,128]{1,0:T(8,128)S(1)}, u32[]{:S(2)}, u32[]{:S(2)}) collective-permute-start(f32[128,128]{1,0:T(8,128)S(1)} %get-tuple-element.12), channel_id=1, source_target_pairs={{0,128},{128,0},{1,129},{129,1},{2,130},{130,2},{3,131},{131,3},{4... | collective-permute-start | bytes 196616 | tf_op jit(solution)/shard_map/ppermute | solution.py:22
  48.9 14.3 %collective-permute-start.1 = (bf16[128,896]{1,0:T(8,128)(2,1)S(1)}, bf16[128,896]{1,0:T(8,128)(2,1)S(1)}, u32[]{:S(2)}, u32[]{:S(2)}) collective-permute-start(bf16[128,896]{1,0:T(8,128)(2,1)S(1)} %collective-permute-done.refs_0_.refs_1_), channel_id=1, source_target_pairs={{0,1},{1,0},{2,3},{3,2},{4,5},{5,4},{6,7},{7,6},{8,9},{9,8},{10,11... | collective-permute-start | bytes 688136 | tf_op jit(solution)/shard_map/ppermute | solution.py:22
  50.0 13.1 %collective-permute-start.3 = (bf16[128,896]{1,0:T(8,128)(2,1)S(1)}, bf16[128,896]{1,0:T(8,128)(2,1)S(1)}, u32[]{:S(2)}, u32[]{:S(2)}) collective-permute-start(bf16[128,896]{1,0:T(8,128)(2,1)S(1)} %collective-permute-done.2.refs_2_), channel_id=1, source_target_pairs={{0,1},{1,0},{2,3},{3,2},{4,5},{5,4},{6,7},{7,6},{8,9},{9,8},{10,11... | collective-permute-start | bytes 688136 | tf_op jit(solution)/shard_map/ppermute | solution.py:22
  57.4 8.8 %collective-permute-start.5 = (bf16[128,128]{1,0:T(8,128)(2,1)S(1)}, bf16[128,128]{1,0:T(8,128)(2,1)S(1)}, u32[]{:S(2)}, u32[]{:S(2)}) collective-permute-start(bf16[128,128]{1,0:T(8,128)(2,1)S(1)} %multiply_convert_fusion.2.refs_1_), channel_id=1, source_target_pairs={{0,32},{32,64},{64,96},{96,0},{1,33},{33,65},{65,97},{97,1},{2,34}... | collective-permute-start | bytes 98312 | tf_op jit(solution)/shard_map/ppermute | solution.py:22
  59.0 8.9 %collective-permute-start.6 = (bf16[128,128]{1,0:T(8,128)(2,1)S(1)}, bf16[128,128]{1,0:T(8,128)(2,1)S(1)}, u32[]{:S(2)}, u32[]{:S(2)}) collective-permute-start(bf16[128,128]{1,0:T(8,128)(2,1)S(1)} %multiply_convert_fusion.2.refs_1_), channel_id=1, source_target_pairs={{0,64},{32,96},{64,0},{96,32},{1,65},{33,97},{65,1},{97,33},{2,66}... | collective-permute-start | bytes 98312 | tf_op jit(solution)/shard_map/ppermute | solution.py:22
  61.7 6.2 %collective-permute-start.7 = (bf16[128,128]{1,0:T(8,128)(2,1)S(1)}, bf16[128,128]{1,0:T(8,128)(2,1)S(1)}, u32[]{:S(2)}, u32[]{:S(2)}) collective-permute-start(bf16[128,128]{1,0:T(8,128)(2,1)S(1)} %multiply_convert_fusion.2.refs_1_), channel_id=1, source_target_pairs={{0,96},{32,0},{64,32},{96,64},{1,97},{33,1},{65,33},{97,65},{2,98}... | collective-permute-start | bytes 98312 | tf_op jit(solution)/shard_map/ppermute | solution.py:22
  70.1 3.9 %copy-start.3 = (bf16[128,128]{1,0:T(8,128)(2,1)S(1)}, bf16[128,128]{1,0:T(8,128)(2,1)}, u32[]{:S(2)}) copy-start(bf16[128,128]{1,0:T(8,128)(2,1)} %copy-done.2) | copy-start | bytes 98308
  70.1 29.4 %all-to-all-start.1 = ((bf16[16,112,512]{2,1,0:T(8,128)(2,1)}), bf16[16,112,512]{2,1,0:T(8,128)(2,1)S(1)}, u32[]{:S(2)}, u32[]{:S(2)}) async-start(bf16[16,112,512]{2,1,0:T(8,128)(2,1)} %bitcast.16), calls=%async_computation.1 | async-start | bytes 3670016 | tf_op jit(solution)/shard_map/all_to_all | solution.py:187
  74.0 10.9 %collective-permute-start.9 = (bf16[4,128,128]{2,1,0:T(8,128)(2,1)S(1)}, bf16[4,128,128]{2,1,0:T(8,128)(2,1)S(1)}, u32[]{:S(2)}, u32[]{:S(2)}) collective-permute-start(bf16[4,128,128]{2,1,0:T(8,128)(2,1)S(1)} %pad_maximum_fusion.refs_1_.refs_4_), channel_id=1, source_target_pairs={{0,2},{2,4},{4,6},{6,0},{1,3},{3,5},{5,7},{7,1},{8,10},{10,12},{12... | collective-permute-start | bytes 393224 | tf_op jit(solution)/shard_map/ppermute | solution.py:22
  74.1 10.8 %collective-permute-start.11 = (bf16[4,128,128]{2,1,0:T(8,128)(2,1)S(1)}, bf16[4,128,128]{2,1,0:T(8,128)(2,1)S(1)}, u32[]{:S(2)}, u32[]{:S(2)}) collective-permute-start(bf16[4,128,128]{2,1,0:T(8,128)(2,1)S(1)} %pad_maximum_fusion.refs_1_.refs_4_), channel_id=1, source_target_pairs={{0,4},{2,6},{4,0},{6,2},{1,5},{3,7},{5,1},{7,3},{8,12},{10,14},{12... | collective-permute-start | bytes 393224 | tf_op jit(solution)/shard_map/ppermute | solution.py:22
  75.2 10.1 %collective-permute-start.13 = (bf16[4,128,128]{2,1,0:T(8,128)(2,1)S(1)}, bf16[4,128,128]{2,1,0:T(8,128)(2,1)S(1)}, u32[]{:S(2)}, u32[]{:S(2)}) collective-permute-start(bf16[4,128,128]{2,1,0:T(8,128)(2,1)S(1)} %pad_maximum_fusion.refs_1_.refs_4_), channel_id=1, source_target_pairs={{0,6},{2,0},{4,2},{6,4},{1,7},{3,1},{5,3},{7,5},{8,14},{10,8},{12,... | collective-permute-start | bytes 393224 | tf_op jit(solution)/shard_map/ppermute | solution.py:22
  77.3 15.3 %collective-permute-start.8 = (bf16[4,128,128]{2,1,0:T(8,128)(2,1)S(1)}, bf16[4,128,128]{2,1,0:T(8,128)(2,1)S(1)}, u32[]{:S(2)}, u32[]{:S(2)}) collective-permute-start(bf16[4,128,128]{2,1,0:T(8,128)(2,1)S(1)} %pad_maximum_fusion.refs_1_.refs_4_), channel_id=1, source_target_pairs={{0,1},{1,0},{2,3},{3,2},{4,5},{5,4},{6,7},{7,6},{8,9},{9,8},{10,11... | collective-permute-start | bytes 393224 | tf_op jit(solution)/shard_map/ppermute | solution.py:22
  84.9 7.8 %collective-permute-start.10 = (bf16[4,128,128]{2,1,0:T(8,128)(2,1)S(1)}, bf16[4,128,128]{2,1,0:T(8,128)(2,1)S(1)}, u32[]{:S(2)}, u32[]{:S(2)}) collective-permute-start(bf16[4,128,128]{2,1,0:T(8,128)(2,1)S(1)} %collective-permute-done.9.refs_3_.refs_6_), channel_id=1, source_target_pairs={{0,1},{1,0},{2,3},{3,2},{4,5},{5,4},{6,7},{7,6},{8,9},{9,8},{10,11... | collective-permute-start | bytes 393224 | tf_op jit(solution)/shard_map/ppermute | solution.py:22
  84.9 7.8 %collective-permute-start.12 = (bf16[4,128,128]{2,1,0:T(8,128)(2,1)S(1)}, bf16[4,128,128]{2,1,0:T(8,128)(2,1)S(1)}, u32[]{:S(2)}, u32[]{:S(2)}) collective-permute-start(bf16[4,128,128]{2,1,0:T(8,128)(2,1)S(1)} %collective-permute-done.11.refs_5_.refs_4_), channel_id=1, source_target_pairs={{0,1},{1,0},{2,3},{3,2},{4,5},{5,4},{6,7},{7,6},{8,9},{9,8},{10,11... | collective-permute-start | bytes 393224 | tf_op jit(solution)/shard_map/ppermute | solution.py:22
  85.4 7.3 %collective-permute-start.14 = (bf16[4,128,128]{2,1,0:T(8,128)(2,1)S(1)}, bf16[4,128,128]{2,1,0:T(8,128)(2,1)S(1)}, u32[]{:S(2)}, u32[]{:S(2)}) collective-permute-start(bf16[4,128,128]{2,1,0:T(8,128)(2,1)S(1)} %collective-permute-done.13.refs_7_.refs_6_), channel_id=1, source_target_pairs={{0,1},{1,0},{2,3},{3,2},{4,5},{5,4},{6,7},{7,6},{8,9},{9,8},{10,11... | collective-permute-start | bytes 393224 | tf_op jit(solution)/shard_map/ppermute | solution.py:22
  87.3 17.6 %collective-permute-start.22 = (bf16[112,512]{1,0:T(8,128)(2,1)S(1)}, bf16[112,512]{1,0:T(8,128)(2,1)S(1)}, u32[]{:S(2)}, u32[]{:S(2)}) collective-permute-start(bf16[112,512]{1,0:T(8,128)(2,1)S(1)} %convert_element_type.33), channel_id=1, source_target_pairs={{0,128},{128,0},{1,129},{129,1},{2,130},{130,2},{3,131},{131,3},{4... | collective-permute-start | bytes 344072 | tf_op jit(solution)/shard_map/ppermute | solution.py:22
  99.8 10.1 %collective-permute-start.15 = (bf16[112,512]{1,0:T(8,128)(2,1)S(1)}, bf16[112,512]{1,0:T(8,128)(2,1)S(1)}, u32[]{:S(2)}, u32[]{:S(2)}) collective-permute-start(bf16[112,512]{1,0:T(8,128)(2,1)S(1)} %convert_element_type.29), channel_id=1, source_target_pairs={{0,128},{128,0},{1,129},{129,1},{2,130},{130,2},{3,131},{131,3},{4... | collective-permute-start | bytes 344072 | tf_op jit(solution)/shard_map/ppermute | solution.py:22
  104.9 8.5 %collective-permute-start.23 = (bf16[112,512]{1,0:T(8,128)(2,1)S(1)}, bf16[112,512]{1,0:T(8,128)(2,1)S(1)}, u32[]{:S(2)}, u32[]{:S(2)}) collective-permute-start(bf16[112,512]{1,0:T(8,128)(2,1)S(1)} %multiply_convert_fusion.refs_0_), channel_id=1, source_target_pairs={{0,8},{8,16},{16,24},{24,0},{1,9},{9,17},{17,25},{25,1},{2,10},{10... | collective-permute-start | bytes 344072 | tf_op jit(solution)/shard_map/ppermute | solution.py:22
  105.5 8.4 %collective-permute-start.24 = (bf16[112,512]{1,0:T(8,128)(2,1)S(1)}, bf16[112,512]{1,0:T(8,128)(2,1)S(1)}, u32[]{:S(2)}, u32[]{:S(2)}) collective-permute-start(bf16[112,512]{1,0:T(8,128)(2,1)S(1)} %multiply_convert_fusion.refs_0_), channel_id=1, source_target_pairs={{0,16},{8,24},{16,0},{24,8},{1,17},{9,25},{17,1},{25,9},{2,18},{10... | collective-permute-start | bytes 344072 | tf_op jit(solution)/shard_map/ppermute | solution.py:22
  106.3 7.7 %collective-permute-start.25 = (bf16[112,512]{1,0:T(8,128)(2,1)S(1)}, bf16[112,512]{1,0:T(8,128)(2,1)S(1)}, u32[]{:S(2)}, u32[]{:S(2)}) collective-permute-start(bf16[112,512]{1,0:T(8,128)(2,1)S(1)} %multiply_convert_fusion.refs_0_), channel_id=1, source_target_pairs={{0,24},{8,0},{16,8},{24,16},{1,25},{9,1},{17,9},{25,17},{2,26},{10... | collective-permute-start | bytes 344072 | tf_op jit(solution)/shard_map/ppermute | solution.py:22
  110.0 7.3 %collective-permute-start.16 = (bf16[112,512]{1,0:T(8,128)(2,1)S(1)}, bf16[112,512]{1,0:T(8,128)(2,1)S(1)}, u32[]{:S(2)}, u32[]{:S(2)}) collective-permute-start(bf16[112,512]{1,0:T(8,128)(2,1)S(1)} %multiply_convert_fusion.1.refs_0_), channel_id=1, source_target_pairs={{0,8},{8,16},{16,24},{24,0},{1,9},{9,17},{17,25},{25,1},{2,10},{10... | collective-permute-start | bytes 344072 | tf_op jit(solution)/shard_map/ppermute | solution.py:22
  110.6 6.7 %collective-permute-start.17 = (bf16[112,512]{1,0:T(8,128)(2,1)S(1)}, bf16[112,512]{1,0:T(8,128)(2,1)S(1)}, u32[]{:S(2)}, u32[]{:S(2)}) collective-permute-start(bf16[112,512]{1,0:T(8,128)(2,1)S(1)} %multiply_convert_fusion.1.refs_0_), channel_id=1, source_target_pairs={{0,16},{8,24},{16,0},{24,8},{1,17},{9,25},{17,1},{25,9},{2,18},{10... | collective-permute-start | bytes 344072 | tf_op jit(solution)/shard_map/ppermute | solution.py:22
  113.4 4.8 %collective-permute-start.18 = (bf16[112,512]{1,0:T(8,128)(2,1)S(1)}, bf16[112,512]{1,0:T(8,128)(2,1)S(1)}, u32[]{:S(2)}, u32[]{:S(2)}) collective-permute-start(bf16[112,512]{1,0:T(8,128)(2,1)S(1)} %multiply_convert_fusion.1.refs_0_), channel_id=1, source_target_pairs={{0,24},{8,0},{16,8},{24,16},{1,25},{9,1},{17,9},{25,17},{2,26},{10... | collective-permute-start | bytes 344072 | tf_op jit(solution)/shard_map/ppermute | solution.py:22
  (1 other events, 0.6 us)

commit v8 on v4

v8 whole, which is shorter than its diff:
```python
import jax
import jax.numpy as jnp
from jax import lax
from jax.experimental import pallas as pl
from jax.experimental.pallas import tpu as pltpu
from jax.sharding import Mesh
from jax.sharding import PartitionSpec as P

AXES = ("z_hi", "x", "y", "z_lo", "core")
SIZES = (2, 4, 4, 4, 2)
DP = ("z_hi", "x", "y")
TENSOR = ("z_lo", "core")
SMEM = pl.BlockSpec(memory_space=pltpu.SMEM)
VMEM = pl.BlockSpec(memory_space=pltpu.VMEM)
ANY = pl.BlockSpec(memory_space=pl.ANY)
PARAMS = pltpu.CompilerParams(vmem_limit_bytes=32 * 1024 * 1024)
WHOLE = pltpu.CompilerParams(vmem_limit_bytes=60 * 1024 * 1024)


def shifted(value, axis, step):
    size = SIZES[AXES.index(axis)]
    return lax.ppermute(value, axis, [(i, (i + step) % size) for i in range(size)])


def act_kernel(place, gain, hidden_at, basis_at, out_at, hidden, basis, out, sems):
    tokens, features = hidden.shape
    depth = basis.shape[0]
    strip = tokens // 4
    loads = [
        pltpu.make_async_copy(hidden_at.at[here], hidden.at[here], sems.at[i])
        for i, here in enumerate(pl.ds(at, strip) for at in range(0, tokens, strip))
    ]
    load_basis = pltpu.make_async_copy(basis_at, basis, sems.at[4])
    for load in (*loads, load_basis):
        load.start()
    stats = []
    for i, load in enumerate(loads):
        load.wait()
        squares = jnp.zeros((strip, 128), jnp.float32)
        for at in range(0, features, 128):
            wide = hidden[i * strip : (i + 1) * strip, at : at + 128].astype(jnp.float32)
            squares += wide * wide
        stats.append(jnp.sum(squares, axis=-1, keepdims=True) / features)
    stat = jnp.concatenate(stats, axis=0)
    mine = pl.ds(pl.multiple_of(place[0] * depth, depth), depth)
    scaled = hidden[:, mine].astype(jnp.float32) * lax.rsqrt(stat + 1e-05)
    normed = (scaled * gain[:, mine]).astype(jnp.bfloat16)
    load_basis.wait()
    block = basis.shape[1] // 32
    stores = []
    for x in range(4):
        for z_hi in range(2):
            at = (z_hi * 16 + x * 4) * block
            part = jnp.dot(
                normed, basis[:, at : at + 4 * block], preferred_element_type=jnp.float32
            )
            for y in range(4):
                here = part[:, y * block : (y + 1) * block]
                to = slice(z_hi * block, (z_hi + 1) * block)
                out[x * 4 + y, :, to] = here.astype(jnp.bfloat16)
        here = pl.ds(x * 4, 4)
        to = out_at.at[here, pl.ds(0, tokens)]
        stores.append(pltpu.make_async_copy(out.at[here], to, sems.at[5 + x]))
        stores[-1].start()
    for store in stores:
        store.wait()


def act_partials(hidden, norm_gain, act_basis, share):
    tokens = hidden.shape[0]
    wide = act_basis.shape[1] // 16
    place = lax.axis_index(DP).astype(jnp.int32).reshape(1)
    return pl.pallas_call(
        act_kernel,
        out_shape=pltpu.HBM((16, tokens + share, wide), jnp.bfloat16),
        in_specs=[SMEM, VMEM, ANY, ANY],
        out_specs=ANY,
        scratch_shapes=[
            pltpu.VMEM(hidden.shape, jnp.bfloat16),
            pltpu.VMEM(act_basis.shape, jnp.bfloat16),
            pltpu.VMEM((16, tokens, wide), jnp.bfloat16),
            pltpu.SemaphoreType.DMA((9,)),
        ],
        compiler_params=WHOLE,
        name="act",
    )(place, norm_gain.reshape(1, -1), hidden, act_basis)


def own_kernel(own, other, basis, filled, out_at, rows, out, sem):
    del filled
    tokens = own.shape[0]
    rows[:tokens, :] = own[...]
    rows[tokens:, :] = other[...]
    share = out.shape[1]
    for at in range(0, basis.shape[1], 256):
        part = jnp.dot(rows[...], basis[:, at : at + 256], preferred_element_type=jnp.float32)
        part = part.T.astype(jnp.bfloat16)
        for owner in range(at // share, (at + 255) // share + 1):
            low, high = max(at, owner * share), min(at + 256, (owner + 1) * share)
            to = low - owner * share
            out[owner, to : to + high - low, :] = part[low - at : high - at, :]
    store = pltpu.make_async_copy(out, out_at.at[:, pl.ds(tokens, share)], sem)
    store.start()
    store.wait()


def own_partials(filled, own, other, basis):
    tokens, depth = own.shape
    return pl.pallas_call(
        own_kernel,
        out_shape=pltpu.HBM(filled.shape, filled.dtype),
        in_specs=[VMEM, VMEM, VMEM, ANY],
        out_specs=ANY,
        scratch_shapes=[
            pltpu.VMEM((2 * tokens, depth), jnp.bfloat16),
            pltpu.VMEM((16, basis.shape[1] // 16, 2 * tokens), jnp.bfloat16),
            pltpu.SemaphoreType.DMA,
        ],
        input_output_aliases={3: 0},
        compiler_params=PARAMS,
        name="own",
    )(own, other, basis, filled)


def grad_kernel(count, *refs):
    parts, basis, out_at, rows, out, sem = refs[:count], refs[count], *refs[-4:]
    at = 0
    for part in parts:
        rows[at : at + part.shape[0], :] = part[...]
        at += part.shape[0]
    stores = []
    for at in range(0, basis.shape[1], 256):
        here = pl.ds(at, 256)
        part = jnp.dot(rows[...], basis[:, here], preferred_element_type=jnp.float32)
        out[here, :] = part.T.astype(jnp.bfloat16)
        stores.append(
            pltpu.make_async_copy(out.at[here], out_at.at[here], sem.at[at // 256])
        )
        stores[-1].start()
    for store in stores:
        store.wait()


def grad_partials(parts, basis):
    depth, columns = basis.shape
    tokens = sum(part.shape[0] for part in parts)
    shape = (columns, tokens)
    return pl.pallas_call(
        lambda *refs: grad_kernel(len(parts), *refs),
        out_shape=pltpu.HBM(shape, jnp.bfloat16),
        in_specs=[VMEM] * (len(parts) + 1),
        out_specs=ANY,
        scratch_shapes=[
            pltpu.VMEM((tokens, depth), jnp.bfloat16),
            pltpu.VMEM(shape, jnp.bfloat16),
            pltpu.SemaphoreType.DMA((columns // 256,)),
        ],
        compiler_params=PARAMS,
        name="grad",
    )(*parts, basis)


def first_sum_kernel(place, got, kept, grad, given):
    tokens, block = kept.shape
    half = tokens // 2
    act = got[0, :tokens, :].astype(jnp.float32)
    for source in range(1, got.shape[0]):
        act += got[source, :tokens, :].astype(jnp.float32)
    low, high = act[:, :block], act[:, block:]
    first = place[0] == 0
    kept[...] = jnp.where(first, low, high)
    away = jnp.where(first, high, low).astype(jnp.bfloat16)
    given[:half, :block] = away[:half]
    given[:half, block:] = away[half:]
    total = got[0, tokens:, :].astype(jnp.float32)
    for source in range(1, got.shape[0]):
        total += got[source, tokens:, :].astype(jnp.float32)
    grad[...] = total
    given[half:, :] = total.astype(jnp.bfloat16)


def square_kernel(kept, grad, got, act_sq, grad_sq):
    tokens, block = kept.shape
    half = tokens // 2
    for part in range(2):
        rows = slice(part * half, (part + 1) * half)
        total = kept[rows, :] + got[:half, part * block : (part + 1) * block].astype(jnp.float32)
        act_sq[rows, :] = (total * total).astype(jnp.bfloat16)
    total = grad[...] + got[half:, :].astype(jnp.float32)
    grad_sq[...] = (total * total).astype(jnp.bfloat16)


def first_squares(got, tokens):
    share, wide = got.shape[1] - tokens, got.shape[2]
    block = wide // 2
    place = lax.axis_index("z_hi").astype(jnp.int32).reshape(1)
    kept, grad, given = pl.pallas_call(
        first_sum_kernel,
        out_shape=(
            jax.ShapeDtypeStruct((tokens, block), jnp.float32),
            jax.ShapeDtypeStruct((share, wide), jnp.float32),
            jax.ShapeDtypeStruct((tokens // 2 + share, wide), jnp.bfloat16),
        ),
        in_specs=[SMEM, VMEM],
        out_specs=(VMEM, VMEM, VMEM),
        compiler_params=PARAMS,
        name="first_sum",
    )(place, got)
    return pl.pallas_call(
        square_kernel,
        out_shape=(
            jax.ShapeDtypeStruct((tokens, block), jnp.bfloat16),
            jax.ShapeDtypeStruct((share, wide), jnp.bfloat16),
        ),
        in_specs=[VMEM] * 3,
        out_specs=(VMEM, VMEM),
        compiler_params=PARAMS,
        name="square",
    )(kept, grad, shifted(given, "z_hi", 1))


def gate_kernel(*refs):
    del refs


def gated(value, after, place=pltpu.HBM):
    return pl.pallas_call(
        gate_kernel,
        out_shape=place(value.shape, value.dtype),
        in_specs=[ANY] * (1 + len(after)),
        out_specs=ANY,
        input_output_aliases={0: 0},
        compiler_params=PARAMS,
        name="gate",
    )(value, *after)


def exchanged(partial):
    columns, tokens = partial.shape
    return lax.all_to_all(partial.reshape(16, columns // 16, tokens), ("x", "y"), 0, 0, tiled=True)


def squared(got):
    summed = jnp.sum(got.astype(jnp.float32), axis=0)
    total = summed + shifted(summed.astype(jnp.bfloat16), "z_hi", 1).astype(jnp.float32)
    return (total * total).astype(jnp.bfloat16)


def correct_kernel(steps, place, *refs):
    pieces, acts, before, (out, act) = refs[:4], refs[4:8], refs[8:-2], refs[-2:]
    chips, cores, tokens, block = acts[0].shape
    for behind, part in enumerate(acts):
        to = slice(behind * block, (behind + 1) * block)
        for i, step in enumerate(steps):
            for core in range(cores):
                at = (i * cores + core) * tokens
                act[at : at + tokens, to] = part[step, core]
    rows = pieces[0].shape[0]
    for y_behind, piece in enumerate(pieces):
        part = jnp.dot(piece[...], act[...], preferred_element_type=jnp.float32)
        part = part * (1.0 / (chips * cores * tokens))
        at = pl.ds(pl.multiple_of(lax.rem(place[1] + 4 - y_behind, 4) * rows, rows), rows)
        for behind in range(4):
            x = lax.rem(place[0] + 4 - behind, 4)
            here = part[:, behind * block : (behind + 1) * block]
            if before:
                here = before[0][x, at, :] + here
            out[x, at, :] = here


def spread(grad_sq):
    return [grad_sq] + [shifted(grad_sq, "y", step) for step in (1, 2, 3)]


def corrected(steps, pieces, acts, *before):
    rows, tokens = pieces[0].shape
    block = acts[0].shape[3]
    place = jnp.stack([lax.axis_index("x"), lax.axis_index("y")]).astype(jnp.int32)
    return pl.pallas_call(
        lambda *refs: correct_kernel(steps, *refs),
        out_shape=jax.ShapeDtypeStruct((4, 4 * rows, block), jnp.float32),
        in_specs=[SMEM] + [VMEM] * (8 + len(before)),
        out_specs=VMEM,
        scratch_shapes=[pltpu.VMEM((tokens, 4 * block), jnp.bfloat16)],
        compiler_params=PARAMS,
        name="correct",
    )(place, *pieces, *acts, *before)


def per_device(hidden, norm_gain, gate_pre, out_grad, grad_basis, act_basis):
    tokens = hidden.shape[0]
    up_grad = (out_grad.astype(jnp.float32) * jax.nn.silu(gate_pre.astype(jnp.float32))).astype(
        jnp.bfloat16
    )
    first = act_partials(hidden, norm_gain, act_basis, grad_basis.shape[1] // 16)
    first = own_partials(first, up_grad, shifted(up_grad, "core", 1), grad_basis)
    first_got = lax.all_to_all(first, ("x", "y"), 0, 0, tiled=True)
    rows = []
    for step in (1, 2, 3):
        own = shifted(up_grad, "z_lo", step)
        rows += [own, shifted(own, "core", 1)]
    rest_got = exchanged(grad_partials(rows, grad_basis))
    act_own, first_sq = first_squares(first_got, tokens)
    act_chip = jnp.stack([act_own, shifted(act_own, "core", 1)])
    act_all = [act_chip] + [shifted(act_chip, "z_lo", step) for step in (1, 2, 3)]
    first_pieces = spread(first_sq)
    rest_sq = squared(gated(rest_got, act_all + first_pieces, jax.ShapeDtypeStruct))
    act_all = jnp.stack(act_all)
    acts = [act_all] + [shifted(act_all, "x", step) for step in (1, 2, 3)]
    out = corrected((0,), first_pieces, acts)
    out = corrected((1, 2, 3), spread(rest_sq), acts, out)
    out = lax.all_to_all(out, "x", 0, 0, tiled=True)
    return out.reshape(grad_basis.shape[1], -1)


def solution(mesh):
    fine = Mesh(mesh.devices.reshape(SIZES), AXES)
    placed = (
        P(TENSOR, None),
        P(),
        P(TENSOR, DP),
        P(TENSOR, DP),
        P(DP, TENSOR),
        P(DP, None),
    )
    return jax.shard_map(
        per_device, mesh=fine, in_specs=placed, out_specs=P(TENSOR, DP), check_vma=False
    )
```

time: 144 us -> 139 us (0.965); the launches traced: 142 us -> 138 us
  between operations: 13.6 us -> 0.19 us
  waiting for transfers between devices: 40.7 us -> 49.2 us
  blocking collectives: 15.5 us -> 18.5 us
  other arithmetic: 4.09 us -> 1.79 us
  Pallas kernels: 14.1 us -> 15.7 us
    ppermute x19 -> x22, waiting for transfers between devices: 18.6 us -> 45.8 us  [shifted(): lax.ppermute(value, axis, [(i, (i + step) % size) for i in range(size)])]
    all_to_all x2 -> x1, waiting for transfers between devices: 17.2 us -> 3.35 us  [exchanged(): lax.all_to_all(partial.reshape(16, columns // 16, tokens), ('x', 'y'), 0,...]
    all_to_all x1, waiting for transfers between devices: 4.91 us -> 0.01 us  [per_device(): first_got = lax.all_to_all(first, ('x', 'y'), 0, 0, tiled=True)]
    ppermute x19 -> x22, starting transfers between devices: 34.2 us -> 38.1 us  [shifted(): lax.ppermute(value, axis, [(i, (i + step) % size) for i in range(size)])]
    pallas_call x3 -> x5, Pallas kernels: 5.91 us -> 9.49 us  [the longest x1 4.51 us: act_partials(): pl.pallas_call(act_kernel, out_shape=pltpu.HBM((16, tokens + share, wide)...]
    all_to_all x2 -> x1, starting transfers between devices: 10.2 us -> 6.83 us  [exchanged(): lax.all_to_all(partial.reshape(16, columns // 16, tokens), ('x', 'y'), 0,...]
    all_to_all x1, blocking collectives: 15.5 us -> 18.5 us  [per_device(): out = lax.all_to_all(out, 'x', 0, 0, tiled=True)]
    pallas_call x2 -> x1, Pallas kernels: 6.03 us -> 4.06 us  [grad_partials(): pl.pallas_call(lambda *refs: grad_kernel(len(parts), *refs), out_shape=pl...]
  transfers between devices with their start and end apart: 23 -> 24, of which waited for: 10 -> 13; matrix products, arithmetic and copies ran while one was open for 3% -> 0% of each run, Pallas kernels for 6% -> 8%
where the time goes in v8:
time: 139 us; the launch traced here: 138 us
  starting transfers between devices  52.1 us (37%)
  waiting for transfers between devices  49.2 us (35%)
  blocking collectives  18.5 us (13%)
  Pallas kernels  15.7 us (11%)
  other arithmetic  1.79 us (1%)
    ppermute x22, waiting for transfers between devices, shifted(): lax.ppermute(value, axis, [(i, (i + step) % size) for i in range(size)])  45.8 us
    ppermute x22, starting transfers between devices, shifted(): lax.ppermute(value, axis, [(i, (i + step) % size) for i in range(size)])  38.1 us
    all_to_all x1, blocking collectives, per_device(): out = lax.all_to_all(out, 'x', 0, 0, tiled=True)  18.5 us
    all_to_all x1, starting transfers between devices, per_device(): first_got = lax.all_to_all(first, ('x', 'y'), 0, 0, tiled=True)  7.1 us
    all_to_all x1, starting transfers between devices, exchanged(): lax.all_to_all(partial.reshape(16, columns // 16, tokens), ('x', 'y'), 0,...  6.83 us
    pallas_call x1, Pallas kernels, act_partials(): pl.pallas_call(act_kernel, out_shape=pltpu.HBM((16, tokens + share, wide)...  4.51 us
    pallas_call x1, Pallas kernels, grad_partials(): pl.pallas_call(lambda *refs: grad_kernel(len(parts), *refs), out_shape=pl...  4.06 us
    all_to_all x1, waiting for transfers between devices, exchanged(): lax.all_to_all(partial.reshape(16, columns // 16, tokens), ('x', 'y'), 0,...  3.35 us
  transfers between devices with their start and end apart: 24, of which 13 were waited for; matrix products, arithmetic and copies ran while one was open for 0% of the time, Pallas kernels for 8%

profile of v8, /device:TPU:64, one launch (start us, length us, event | category | flops | bytes accessed | tf_op | source)
XLA Modules:
  0.0 138.3 jit_solution(1891787377816241666)
XLA Ops:
  0.0 1.2 fusion.4.own
  1.3 4.5 %act.1.filled = bf16[16,240,256]{2,1,0:T(8,128)(2,1)} custom-call(s32[1]{0:T(128)} %bitcast.4.place, f32[1,8192]{1,0:T(1,128)} %bitcast.20, bf16[128,8192]{1,0:T(8,128)(2,1)} %hidden_at.1, bf16[256,4096]{1,0:T(8,128)(2,1)} %basis_at.1), custom_call_target="tpu_custom_call" | custom-call | tf_op jit(solution)/shard_map/act/pallas_call | solution.py:73
  5.9 3.1 %own.1 = bf16[16,240,256]{2,1,0:T(8,128)(2,1)} custom-call(bf16[128,896]{1,0:T(8,128)(2,1)S(1)} %fusion.4.own, bf16[128,896]{1,0:T(8,128)(2,1)} %collective-permute-done.6.other, bf16[896,1792]{1,0:T(8,128)(2,1)S(1)} %copy-done, bf16[16,240,256]{2,1,0:T(8,128)(2,1)} %act.1.filled), custom_call_target="tpu_custom_call", output_to_operand_aliasing={{}: (3, {})} | custom-call | tf_op jit(solution)/shard_map/own/pallas_call | solution.py:109
  9.0 7.1 %all-to-all-start.1 = ((bf16[16,240,256]{2,1,0:T(8,128)(2,1)}), bf16[16,240,256]{2,1,0:T(8,128)(2,1)}, u32[]{:S(2)}, u32[]{:S(2)}) async-start(bf16[16,240,256]{2,1,0:T(8,128)(2,1)} %own.1), calls=%async_computation.1 | async-start | bytes 3932160 | tf_op jit(solution)/shard_map/all_to_all | solution.py:297
  16.3 4.2 %collective-permute-start.2 = (bf16[128,896]{1,0:T(8,128)(2,1)S(1)}, bf16[128,896]{1,0:T(8,128)(2,1)S(1)}, u32[]{:S(2)}, u32[]{:S(2)}) collective-permute-start(bf16[128,896]{1,0:T(8,128)(2,1)S(1)} %fusion.4.own), channel_id=1, source_target_pairs={{0,4},{2,6},{4,0},{6,2},{1,5},{3,7},{5,1},{7,3},{8,12},{10,14},{12... | collective-permute-start | bytes 688136 | tf_op jit(solution)/shard_map/ppermute | solution.py:22
  20.5 4.1 %collective-permute-done.4.refs_4_ = bf16[128,896]{1,0:T(8,128)(2,1)S(1)} collective-permute-done((bf16[128,896]{1,0:T(8,128)(2,1)S(1)}, bf16[128,896]{1,0:T(8,128)(2,1)S(1)}, u32[]{:S(2)}, u32[]{:S(2)}) %collective-permute-start.4) | collective-permute-done | bytes 229408 | tf_op jit(solution)/shard_map/ppermute | solution.py:22
  24.6 11.8 %collective-permute-done.2.refs_2_ = bf16[128,896]{1,0:T(8,128)(2,1)S(1)} collective-permute-done((bf16[128,896]{1,0:T(8,128)(2,1)S(1)}, bf16[128,896]{1,0:T(8,128)(2,1)S(1)}, u32[]{:S(2)}, u32[]{:S(2)}) %collective-permute-start.2) | collective-permute-done | bytes 229408 | tf_op jit(solution)/shard_map/ppermute | solution.py:22
  36.5 3.7 %collective-permute-done.refs_0_ = bf16[128,896]{1,0:T(8,128)(2,1)S(1)} collective-permute-done((bf16[128,896]{1,0:T(8,128)(2,1)S(1)}, bf16[128,896]{1,0:T(8,128)(2,1)S(1)}, u32[]{:S(2)}, u32[]{:S(2)}) %collective-permute-start) | collective-permute-done | bytes 229408 | tf_op jit(solution)/shard_map/ppermute | solution.py:22
  40.2 1.5 %collective-permute-done.1.refs_1_ = bf16[128,896]{1,0:T(8,128)(2,1)S(1)} collective-permute-done((bf16[128,896]{1,0:T(8,128)(2,1)S(1)}, bf16[128,896]{1,0:T(8,128)(2,1)S(1)}, u32[]{:S(2)}, u32[]{:S(2)}) %collective-permute-start.1) | collective-permute-done | bytes 229408 | tf_op jit(solution)/shard_map/ppermute | solution.py:22
  41.6 4.1 %grad.1 = bf16[1792,768]{1,0:T(8,128)(2,1)} custom-call(bf16[128,896]{1,0:T(8,128)(2,1)S(1)} %collective-permute-done.refs_0_, bf16[128,896]{1,0:T(8,128)(2,1)S(1)} %collective-permute-done.1.refs_1_, bf16[128,896]{1,0:T(8,128)(2,1)S(1)} %collective-permute-done.2.refs_2_, bf16[128,896]{1,0:T(8,128)(2,1)S(1)} %collective-permute-done.3.refs_3_, ...), custom_call_target="tpu_custom_call" | custom-call | tf_op jit(solution)/shard_map/grad/pallas_call | solution.py:148
  45.7 6.8 %all-to-all-start = ((bf16[16,112,768]{2,1,0:T(8,128)(2,1)}), bf16[16,112,768]{2,1,0:T(8,128)(2,1)S(1)}, u32[]{:S(2)}, u32[]{:S(2)}) async-start(bf16[16,112,768]{2,1,0:T(8,128)(2,1)} %bitcast.18), calls=%async_computation | async-start | bytes 5505024 | tf_op jit(solution)/shard_map/all_to_all | solution.py:240
  52.5 1.8 %first_sum.1 = (f32[128,128]{1,0:T(8,128)S(1)}, f32[112,256]{1,0:T(8,128)S(1)}, bf16[176,256]{1,0:T(8,128)(2,1)S(1)}) custom-call(s32[1]{0:T(128)} %bitcast.3.place, bf16[16,240,256]{2,1,0:T(8,128)(2,1)} %all-to-all-done.1.got), custom_call_target="tpu_custom_call" | custom-call | tf_op jit(solution)/shard_map/first_sum/pallas_call | solution.py:197
  54.4 5.2 %collective-permute-start.7 = (bf16[176,256]{1,0:T(8,128)(2,1)S(1)}, bf16[176,256]{1,0:T(8,128)(2,1)S(1)}, u32[]{:S(2)}, u32[]{:S(2)}) collective-permute-start(bf16[176,256]{1,0:T(8,128)(2,1)S(1)} %get-tuple-element.12), channel_id=1, source_target_pairs={{0,128},{128,0},{1,129},{129,1},{2,130},{130,2},{3,131},{131,3},{4... | collective-permute-start | bytes 270344 | tf_op jit(solution)/shard_map/ppermute | solution.py:22
  59.6 5.2 %collective-permute-done.7.got = bf16[176,256]{1,0:T(8,128)(2,1)S(1)} collective-permute-done((bf16[176,256]{1,0:T(8,128)(2,1)S(1)}, bf16[176,256]{1,0:T(8,128)(2,1)S(1)}, u32[]{:S(2)}, u32[]{:S(2)}) %collective-permute-start.7) | collective-permute-done | bytes 90144 | tf_op jit(solution)/shard_map/ppermute | solution.py:22
  64.9 2.9 %collective-permute-start.14 = (bf16[112,256]{1,0:T(8,128)(2,1)S(1)}, bf16[112,256]{1,0:T(8,128)(2,1)S(1)}, u32[]{:S(2)}, u32[]{:S(2)}) collective-permute-start(bf16[112,256]{1,0:T(8,128)(2,1)S(1)} %get-tuple-element.14.refs_5_.refs_1_), channel_id=1, source_target_pairs={{0,24},{8,0},{16,8},{24,16},{1,25},{9,1},{17,9},{25,17},{2,26},{10... | collective-permute-start | bytes 172040 | tf_op jit(solution)/shard_map/ppermute | solution.py:22
  68.8 1.4 collective-permute-start.9
  70.1 1.4 %collective-permute-start.13 = (bf16[112,256]{1,0:T(8,128)(2,1)S(1)}, bf16[112,256]{1,0:T(8,128)(2,1)S(1)}, u32[]{:S(2)}, u32[]{:S(2)}) collective-permute-start(bf16[112,256]{1,0:T(8,128)(2,1)S(1)} %get-tuple-element.14.refs_5_.refs_1_), channel_id=1, source_target_pairs={{0,16},{8,24},{16,0},{24,8},{1,17},{9,25},{17,1},{25,9},{2,18},{10... | collective-permute-start | bytes 172040 | tf_op jit(solution)/shard_map/ppermute | solution.py:22
  71.5 7.6 %collective-permute-done.14.refs_8_.refs_4_ = bf16[112,256]{1,0:T(8,128)(2,1)S(1)} collective-permute-done((bf16[112,256]{1,0:T(8,128)(2,1)S(1)}, bf16[112,256]{1,0:T(8,128)(2,1)S(1)}, u32[]{:S(2)}, u32[]{:S(2)}) %collective-permute-start.14) | collective-permute-done | bytes 57376 | tf_op jit(solution)/shard_map/ppermute | solution.py:22
  79.2 5.9 %collective-permute-start.12 = (bf16[112,256]{1,0:T(8,128)(2,1)S(1)}, bf16[112,256]{1,0:T(8,128)(2,1)S(1)}, u32[]{:S(2)}, u32[]{:S(2)}) collective-permute-start(bf16[112,256]{1,0:T(8,128)(2,1)S(1)} %get-tuple-element.14.refs_5_.refs_1_), channel_id=1, source_target_pairs={{0,8},{8,16},{16,24},{24,0},{1,9},{9,17},{17,25},{25,1},{2,10},{10... | collective-permute-start | bytes 172040 | tf_op jit(solution)/shard_map/ppermute | solution.py:22
  85.0 2.2 %collective-permute-done.12.refs_6_.refs_2_ = bf16[112,256]{1,0:T(8,128)(2,1)S(1)} collective-permute-done((bf16[112,256]{1,0:T(8,128)(2,1)S(1)}, bf16[112,256]{1,0:T(8,128)(2,1)S(1)}, u32[]{:S(2)}, u32[]{:S(2)}) %collective-permute-start.12) | collective-permute-done | bytes 57376 | tf_op jit(solution)/shard_map/ppermute | solution.py:22
  87.3 3.3 %all-to-all-done.refs_0_ = bf16[16,112,768]{2,1,0:T(8,128)(2,1)S(1)} async-done(((bf16[16,112,768]{2,1,0:T(8,128)(2,1)}), bf16[16,112,768]{2,1,0:T(8,128)(2,1)S(1)}, u32[]{:S(2)}, u32[]{:S(2)}) %all-to-all-start) | async-done | bytes 2752544 | tf_op jit(solution)/shard_map/all_to_all | solution.py:240
  91.1 4.9 %collective-permute-start.15 = (bf16[112,768]{1,0:T(8,128)(2,1)S(1)}, bf16[112,768]{1,0:T(8,128)(2,1)S(1)}, u32[]{:S(2)}, u32[]{:S(2)}) collective-permute-start(bf16[112,768]{1,0:T(8,128)(2,1)S(1)} %convert_element_type.25), channel_id=1, source_target_pairs={{0,128},{128,0},{1,129},{129,1},{2,130},{130,2},{3,131},{131,3},{4... | collective-permute-start | bytes 516104 | tf_op jit(solution)/shard_map/ppermute | solution.py:22
  96.0 7.4 %collective-permute-start.21 = (bf16[4,2,128,128]{3,2,1,0:T(8,128)(2,1)S(1)}, bf16[4,2,128,128]{3,2,1,0:T(8,128)(2,1)S(1)}, u32[]{:S(2)}, u32[]{:S(2)}) collective-permute-start(bf16[4,2,128,128]{3,2,1,0:T(8,128)(2,1)S(1)} %pad_maximum_fusion.refs_5_), channel_id=1, source_target_pairs={{0,96},{32,0},{64,32},{96,64},{1,97},{33,1},{65,33},{97,65},{2,98}... | collective-permute-start | bytes 786440 | tf_op jit(solution)/shard_map/ppermute | solution.py:22
  103.4 1.1 collective-permute-start.20
  104.6 2.2 %collective-permute-start.18 = (bf16[112,768]{1,0:T(8,128)(2,1)S(1)}, bf16[112,768]{1,0:T(8,128)(2,1)S(1)}, u32[]{:S(2)}, u32[]{:S(2)}) collective-permute-start(bf16[112,768]{1,0:T(8,128)(2,1)S(1)} %multiply_convert_fusion.refs_1_), channel_id=1, source_target_pairs={{0,24},{8,0},{16,8},{24,16},{1,25},{9,1},{17,9},{25,17},{2,26},{10... | collective-permute-start | bytes 516104 | tf_op jit(solution)/shard_map/ppermute | solution.py:22
  107.0 3.7 %collective-permute-done.21.refs_8_ = bf16[4,2,128,128]{3,2,1,0:T(8,128)(2,1)S(1)} collective-permute-done((bf16[4,2,128,128]{3,2,1,0:T(8,128)(2,1)S(1)}, bf16[4,2,128,128]{3,2,1,0:T(8,128)(2,1)S(1)}, u32[]{:S(2)}, u32[]{:S(2)}) %collective-permute-start.21) | collective-permute-done | bytes 262176 | tf_op jit(solution)/shard_map/ppermute | solution.py:22
  110.8 0.9 collective-permute-done.20.refs_7_
  111.7 2.7 %collective-permute-done.19.refs_6_ = bf16[4,2,128,128]{3,2,1,0:T(8,128)(2,1)S(1)} collective-permute-done((bf16[4,2,128,128]{3,2,1,0:T(8,128)(2,1)S(1)}, bf16[4,2,128,128]{3,2,1,0:T(8,128)(2,1)S(1)}, u32[]{:S(2)}, u32[]{:S(2)}) %collective-permute-start.19) | collective-permute-done | bytes 262176 | tf_op jit(solution)/shard_map/ppermute | solution.py:22
  115.6 2.0 %collective-permute-done.16.refs_2_ = bf16[112,768]{1,0:T(8,128)(2,1)S(1)} collective-permute-done((bf16[112,768]{1,0:T(8,128)(2,1)S(1)}, bf16[112,768]{1,0:T(8,128)(2,1)S(1)}, u32[]{:S(2)}, u32[]{:S(2)}) %collective-permute-start.16) | collective-permute-done | bytes 172064 | tf_op jit(solution)/shard_map/ppermute | solution.py:22
  117.7 1.3 correct.3
  118.9 18.5 %all_to_all.15 = f32[4,448,128]{2,1,0:T(8,128)S(1)} all-to-all(f32[4,448,128]{2,1,0:T(8,128)S(1)} %correct.3), channel_id=1, replica_groups=mesh['z_hi'=2,'x'=4,'y'=4,'z_lo'=4,'core'=2] {'x'}, dimensions={0} | all-to-all | bytes 1835008 | tf_op jit(solution)/shard_map/all_to_all | solution.py:312
  137.4 0.9 copy.12
  (35 shorter events, 3.3 us)
Async XLA Ops:
  1.2 4.6 %collective-permute-start.6 = (bf16[128,896]{1,0:T(8,128)(2,1)S(1)}, bf16[128,896]{1,0:T(8,128)(2,1)}, u32[]{:S(2)}, u32[]{:S(2)}) collective-permute-start(bf16[128,896]{1,0:T(8,128)(2,1)S(1)} %fusion.4.own), channel_id=1, source_target_pairs={{0,1},{1,0},{2,3},{3,2},{4,5},{5,4},{6,7},{7,6},{8,9},{9,8},{10,11... | collective-permute-start | bytes 688136 | tf_op jit(solution)/shard_map/ppermute | solution.py:22
  1.3 4.5 %copy-start = (bf16[896,1792]{1,0:T(8,128)(2,1)S(1)}, bf16[896,1792]{1,0:T(8,128)(2,1)}, u32[]{:S(2)}) copy-start(bf16[896,1792]{1,0:T(8,128)(2,1)} %basis.1) | copy-start | bytes 9633796
  9.0 36.7 %all-to-all-start.1 = ((bf16[16,240,256]{2,1,0:T(8,128)(2,1)}), bf16[16,240,256]{2,1,0:T(8,128)(2,1)}, u32[]{:S(2)}, u32[]{:S(2)}) async-start(bf16[16,240,256]{2,1,0:T(8,128)(2,1)} %own.1), calls=%async_computation.1 | async-start | bytes 3932160 | tf_op jit(solution)/shard_map/all_to_all | solution.py:297
  16.1 8.5 %collective-permute-start.4 = (bf16[128,896]{1,0:T(8,128)(2,1)S(1)}, bf16[128,896]{1,0:T(8,128)(2,1)S(1)}, u32[]{:S(2)}, u32[]{:S(2)}) collective-permute-start(bf16[128,896]{1,0:T(8,128)(2,1)S(1)} %fusion.4.own), channel_id=1, source_target_pairs={{0,6},{2,0},{4,2},{6,4},{1,7},{3,1},{5,3},{7,5},{8,14},{10,8},{12,... | collective-permute-start | bytes 688136 | tf_op jit(solution)/shard_map/ppermute | solution.py:22
  16.3 20.1 %collective-permute-start.2 = (bf16[128,896]{1,0:T(8,128)(2,1)S(1)}, bf16[128,896]{1,0:T(8,128)(2,1)S(1)}, u32[]{:S(2)}, u32[]{:S(2)}) collective-permute-start(bf16[128,896]{1,0:T(8,128)(2,1)S(1)} %fusion.4.own), channel_id=1, source_target_pairs={{0,4},{2,6},{4,0},{6,2},{1,5},{3,7},{5,1},{7,3},{8,12},{10,14},{12... | collective-permute-start | bytes 688136 | tf_op jit(solution)/shard_map/ppermute | solution.py:22
  20.5 19.7 %collective-permute-start = (bf16[128,896]{1,0:T(8,128)(2,1)S(1)}, bf16[128,896]{1,0:T(8,128)(2,1)S(1)}, u32[]{:S(2)}, u32[]{:S(2)}) collective-permute-start(bf16[128,896]{1,0:T(8,128)(2,1)S(1)} %fusion.4.own), channel_id=1, source_target_pairs={{0,2},{2,4},{4,6},{6,0},{1,3},{3,5},{5,7},{7,1},{8,10},{10,12},{12... | collective-permute-start | bytes 688136 | tf_op jit(solution)/shard_map/ppermute | solution.py:22
  24.6 15.5 %collective-permute-start.5 = (bf16[128,896]{1,0:T(8,128)(2,1)S(1)}, bf16[128,896]{1,0:T(8,128)(2,1)S(1)}, u32[]{:S(2)}, u32[]{:S(2)}) collective-permute-start(bf16[128,896]{1,0:T(8,128)(2,1)S(1)} %collective-permute-done.4.refs_4_), channel_id=1, source_target_pairs={{0,1},{1,0},{2,3},{3,2},{4,5},{5,4},{6,7},{7,6},{8,9},{9,8},{10,11... | collective-permute-start | bytes 688136 | tf_op jit(solution)/shard_map/ppermute | solution.py:22
  36.5 3.7 %collective-permute-start.3 = (bf16[128,896]{1,0:T(8,128)(2,1)S(1)}, bf16[128,896]{1,0:T(8,128)(2,1)S(1)}, u32[]{:S(2)}, u32[]{:S(2)}) collective-permute-start(bf16[128,896]{1,0:T(8,128)(2,1)S(1)} %collective-permute-done.2.refs_2_), channel_id=1, source_target_pairs={{0,1},{1,0},{2,3},{3,2},{4,5},{5,4},{6,7},{7,6},{8,9},{9,8},{10,11... | collective-permute-start | bytes 688136 | tf_op jit(solution)/shard_map/ppermute | solution.py:22
  40.1 1.5 %collective-permute-start.1 = (bf16[128,896]{1,0:T(8,128)(2,1)S(1)}, bf16[128,896]{1,0:T(8,128)(2,1)S(1)}, u32[]{:S(2)}, u32[]{:S(2)}) collective-permute-start(bf16[128,896]{1,0:T(8,128)(2,1)S(1)} %collective-permute-done.refs_0_), channel_id=1, source_target_pairs={{0,1},{1,0},{2,3},{3,2},{4,5},{5,4},{6,7},{7,6},{8,9},{9,8},{10,11... | collective-permute-start | bytes 688136 | tf_op jit(solution)/shard_map/ppermute | solution.py:22
  45.7 44.9 %all-to-all-start = ((bf16[16,112,768]{2,1,0:T(8,128)(2,1)}), bf16[16,112,768]{2,1,0:T(8,128)(2,1)S(1)}, u32[]{:S(2)}, u32[]{:S(2)}) async-start(bf16[16,112,768]{2,1,0:T(8,128)(2,1)} %bitcast.18), calls=%async_computation | async-start | bytes 5505024 | tf_op jit(solution)/shard_map/all_to_all | solution.py:240
  54.4 10.4 %collective-permute-start.7 = (bf16[176,256]{1,0:T(8,128)(2,1)S(1)}, bf16[176,256]{1,0:T(8,128)(2,1)S(1)}, u32[]{:S(2)}, u32[]{:S(2)}) collective-permute-start(bf16[176,256]{1,0:T(8,128)(2,1)S(1)} %get-tuple-element.12), channel_id=1, source_target_pairs={{0,128},{128,0},{1,129},{129,1},{2,130},{130,2},{3,131},{131,3},{4... | collective-permute-start | bytes 270344 | tf_op jit(solution)/shard_map/ppermute | solution.py:22
  64.8 3.0 %collective-permute-start.8 = (bf16[128,128]{1,0:T(8,128)(2,1)S(1)}, bf16[128,128]{1,0:T(8,128)(2,1)S(1)}, u32[]{:S(2)}, u32[]{:S(2)}) collective-permute-start(bf16[128,128]{1,0:T(8,128)(2,1)S(1)} %get-tuple-element.13), channel_id=1, source_target_pairs={{0,1},{1,0},{2,3},{3,2},{4,5},{5,4},{6,7},{7,6},{8,9},{9,8},{10,11... | collective-permute-start | bytes 98312 | tf_op jit(solution)/shard_map/ppermute | solution.py:22
  64.9 14.3 %collective-permute-start.14 = (bf16[112,256]{1,0:T(8,128)(2,1)S(1)}, bf16[112,256]{1,0:T(8,128)(2,1)S(1)}, u32[]{:S(2)}, u32[]{:S(2)}) collective-permute-start(bf16[112,256]{1,0:T(8,128)(2,1)S(1)} %get-tuple-element.14.refs_5_.refs_1_), channel_id=1, source_target_pairs={{0,24},{8,0},{16,8},{24,16},{1,25},{9,1},{17,9},{25,17},{2,26},{10... | collective-permute-start | bytes 172040 | tf_op jit(solution)/shard_map/ppermute | solution.py:22
  67.8 19.5 %collective-permute-start.11 = (bf16[2,128,128]{2,1,0:T(8,128)(2,1)S(1)}, bf16[2,128,128]{2,1,0:T(8,128)(2,1)S(1)}, u32[]{:S(2)}, u32[]{:S(2)}) collective-permute-start(bf16[2,128,128]{2,1,0:T(8,128)(2,1)S(1)} %get-tuple-element.16.refs_1_), channel_id=1, source_target_pairs={{0,6},{2,0},{4,2},{6,4},{1,7},{3,1},{5,3},{7,5},{8,14},{10,8},{12,... | collective-permute-start | bytes 196616 | tf_op jit(solution)/shard_map/ppermute | solution.py:22
  68.1 19.2 %collective-permute-start.10 = (bf16[2,128,128]{2,1,0:T(8,128)(2,1)S(1)}, bf16[2,128,128]{2,1,0:T(8,128)(2,1)S(1)}, u32[]{:S(2)}, u32[]{:S(2)}) collective-permute-start(bf16[2,128,128]{2,1,0:T(8,128)(2,1)S(1)} %get-tuple-element.16.refs_1_), channel_id=1, source_target_pairs={{0,4},{2,6},{4,0},{6,2},{1,5},{3,7},{5,1},{7,3},{8,12},{10,14},{12... | collective-permute-start | bytes 196616 | tf_op jit(solution)/shard_map/ppermute | solution.py:22
  68.8 18.5 %collective-permute-start.9 = (bf16[2,128,128]{2,1,0:T(8,128)(2,1)S(1)}, bf16[2,128,128]{2,1,0:T(8,128)(2,1)S(1)}, u32[]{:S(2)}, u32[]{:S(2)}) collective-permute-start(bf16[2,128,128]{2,1,0:T(8,128)(2,1)S(1)} %get-tuple-element.16.refs_1_), channel_id=1, source_target_pairs={{0,2},{2,4},{4,6},{6,0},{1,3},{3,5},{5,7},{7,1},{8,10},{10,12},{12... | collective-permute-start | bytes 196616 | tf_op jit(solution)/shard_map/ppermute | solution.py:22
  70.1 14.9 %collective-permute-start.13 = (bf16[112,256]{1,0:T(8,128)(2,1)S(1)}, bf16[112,256]{1,0:T(8,128)(2,1)S(1)}, u32[]{:S(2)}, u32[]{:S(2)}) collective-permute-start(bf16[112,256]{1,0:T(8,128)(2,1)S(1)} %get-tuple-element.14.refs_5_.refs_1_), channel_id=1, source_target_pairs={{0,16},{8,24},{16,0},{24,8},{1,17},{9,25},{17,1},{25,9},{2,18},{10... | collective-permute-start | bytes 172040 | tf_op jit(solution)/shard_map/ppermute | solution.py:22
  79.2 8.1 %collective-permute-start.12 = (bf16[112,256]{1,0:T(8,128)(2,1)S(1)}, bf16[112,256]{1,0:T(8,128)(2,1)S(1)}, u32[]{:S(2)}, u32[]{:S(2)}) collective-permute-start(bf16[112,256]{1,0:T(8,128)(2,1)S(1)} %get-tuple-element.14.refs_5_.refs_1_), channel_id=1, source_target_pairs={{0,8},{8,16},{16,24},{24,0},{1,9},{9,17},{17,25},{25,1},{2,10},{10... | collective-permute-start | bytes 172040 | tf_op jit(solution)/shard_map/ppermute | solution.py:22
  91.1 13.5 %collective-permute-start.15 = (bf16[112,768]{1,0:T(8,128)(2,1)S(1)}, bf16[112,768]{1,0:T(8,128)(2,1)S(1)}, u32[]{:S(2)}, u32[]{:S(2)}) collective-permute-start(bf16[112,768]{1,0:T(8,128)(2,1)S(1)} %convert_element_type.25), channel_id=1, source_target_pairs={{0,128},{128,0},{1,129},{129,1},{2,130},{130,2},{3,131},{131,3},{4... | collective-permute-start | bytes 516104 | tf_op jit(solution)/shard_map/ppermute | solution.py:22
  96.0 14.7 %collective-permute-start.21 = (bf16[4,2,128,128]{3,2,1,0:T(8,128)(2,1)S(1)}, bf16[4,2,128,128]{3,2,1,0:T(8,128)(2,1)S(1)}, u32[]{:S(2)}, u32[]{:S(2)}) collective-permute-start(bf16[4,2,128,128]{3,2,1,0:T(8,128)(2,1)S(1)} %pad_maximum_fusion.refs_5_), channel_id=1, source_target_pairs={{0,96},{32,0},{64,32},{96,64},{1,97},{33,1},{65,33},{97,65},{2,98}... | collective-permute-start | bytes 786440 | tf_op jit(solution)/shard_map/ppermute | solution.py:22
  103.4 8.3 %collective-permute-start.20 = (bf16[4,2,128,128]{3,2,1,0:T(8,128)(2,1)S(1)}, bf16[4,2,128,128]{3,2,1,0:T(8,128)(2,1)S(1)}, u32[]{:S(2)}, u32[]{:S(2)}) collective-permute-start(bf16[4,2,128,128]{3,2,1,0:T(8,128)(2,1)S(1)} %pad_maximum_fusion.refs_5_), channel_id=1, source_target_pairs={{0,64},{32,96},{64,0},{96,32},{1,65},{33,97},{65,1},{97,33},{2,66}... | collective-permute-start | bytes 786440 | tf_op jit(solution)/shard_map/ppermute | solution.py:22
  104.6 9.9 %collective-permute-start.19 = (bf16[4,2,128,128]{3,2,1,0:T(8,128)(2,1)S(1)}, bf16[4,2,128,128]{3,2,1,0:T(8,128)(2,1)S(1)}, u32[]{:S(2)}, u32[]{:S(2)}) collective-permute-start(bf16[4,2,128,128]{3,2,1,0:T(8,128)(2,1)S(1)} %pad_maximum_fusion.refs_5_), channel_id=1, source_target_pairs={{0,32},{32,64},{64,96},{96,0},{1,33},{33,65},{65,97},{97,1},{2,34}... | collective-permute-start | bytes 786440 | tf_op jit(solution)/shard_map/ppermute | solution.py:22
  104.6 10.7 %collective-permute-start.18 = (bf16[112,768]{1,0:T(8,128)(2,1)S(1)}, bf16[112,768]{1,0:T(8,128)(2,1)S(1)}, u32[]{:S(2)}, u32[]{:S(2)}) collective-permute-start(bf16[112,768]{1,0:T(8,128)(2,1)S(1)} %multiply_convert_fusion.refs_1_), channel_id=1, source_target_pairs={{0,24},{8,0},{16,8},{24,16},{1,25},{9,1},{17,9},{25,17},{2,26},{10... | collective-permute-start | bytes 516104 | tf_op jit(solution)/shard_map/ppermute | solution.py:22
  106.8 8.8 %collective-permute-start.17 = (bf16[112,768]{1,0:T(8,128)(2,1)S(1)}, bf16[112,768]{1,0:T(8,128)(2,1)S(1)}, u32[]{:S(2)}, u32[]{:S(2)}) collective-permute-start(bf16[112,768]{1,0:T(8,128)(2,1)S(1)} %multiply_convert_fusion.refs_1_), channel_id=1, source_target_pairs={{0,16},{8,24},{16,0},{24,8},{1,17},{9,25},{17,1},{25,9},{2,18},{10... | collective-permute-start | bytes 516104 | tf_op jit(solution)/shard_map/ppermute | solution.py:22
  110.7 7.0 %collective-permute-start.16 = (bf16[112,768]{1,0:T(8,128)(2,1)S(1)}, bf16[112,768]{1,0:T(8,128)(2,1)S(1)}, u32[]{:S(2)}, u32[]{:S(2)}) collective-permute-start(bf16[112,768]{1,0:T(8,128)(2,1)S(1)} %multiply_convert_fusion.refs_1_), channel_id=1, source_target_pairs={{0,8},{8,16},{16,24},{24,0},{1,9},{9,17},{17,25},{25,1},{2,10},{10... | collective-permute-start | bytes 516104 | tf_op jit(solution)/shard_map/ppermute | solution.py:22

commit v9 on v8

--- a/solution.py
+++ b/solution.py
@@ -86,78 +86,53 @@
     )(place, norm_gain.reshape(1, -1), hidden, act_basis)
 
 
-def own_kernel(own, other, basis, filled, out_at, rows, out, sem):
-    del filled
-    tokens = own.shape[0]
-    rows[:tokens, :] = own[...]
-    rows[tokens:, :] = other[...]
-    share = out.shape[1]
-    for at in range(0, basis.shape[1], 256):
+def grad_kernel(count, start, *refs):
+    parts, basis, (out_at, mark, rows, out, sems) = refs[:count], refs[count], refs[-5:]
+    mark[...] = jnp.zeros_like(mark)
+    tokens = parts[0].shape[0]
+    for i, part in enumerate(parts):
+        rows[i * tokens : (i + 1) * tokens, :] = part[...]
+    columns = basis.shape[1]
+    share = columns // 16
+    stores = []
+    for at in range(0, columns, 256):
         part = jnp.dot(rows[...], basis[:, at : at + 256], preferred_element_type=jnp.float32)
         part = part.T.astype(jnp.bfloat16)
         for owner in range(at // share, (at + 255) // share + 1):
             low, high = max(at, owner * share), min(at + 256, (owner + 1) * share)
-            to = low - owner * share
-            out[owner, to : to + high - low, :] = part[low - at : high - at, :]
-    store = pltpu.make_async_copy(out, out_at.at[:, pl.ds(tokens, share)], sem)
-    store.start()
-    store.wait()
-
-
-def own_partials(filled, own, other, basis):
-    tokens, depth = own.shape
-    return pl.pallas_call(
-        own_kernel,
-        out_shape=pltpu.HBM(filled.shape, filled.dtype),
-        in_specs=[VMEM, VMEM, VMEM, ANY],
-        out_specs=ANY,
-        scratch_shapes=[
-            pltpu.VMEM((2 * tokens, depth), jnp.bfloat16),
-            pltpu.VMEM((16, basis.shape[1] // 16, 2 * tokens), jnp.bfloat16),
-            pltpu.SemaphoreType.DMA,
-        ],
-        input_output_aliases={3: 0},
-        compiler_params=PARAMS,
-        name="own",
-    )(own, other, basis, filled)
-
-
-def grad_kernel(count, *refs):
-    parts, basis, out_at, rows, out, sem = refs[:count], refs[count], *refs[-4:]
-    at = 0
-    for part in parts:
-        rows[at : at + part.shape[0], :] = part[...]
-        at += part.shape[0]
-    stores = []
-    for at in range(0, basis.shape[1], 256):
-        here = pl.ds(at, 256)
-        part = jnp.dot(rows[...], basis[:, here], preferred_element_type=jnp.float32)
-        out[here, :] = part.T.astype(jnp.bfloat16)
-        stores.append(
-            pltpu.make_async_copy(out.at[here], out_at.at[here], sem.at[at // 256])
-        )
-        stores[-1].start()
+            for chip in range(count // 2):
+                to = chip * share + low - owner * share
+                here = slice(2 * chip * tokens, 2 * (chip + 1) * tokens)
+                out[owner, to : to + high - low, :] = part[low - at : high - at, here]
+        while 4 * (len(stores) + 1) * share <= at + 256:
+            here = pl.ds(4 * len(stores), 4)
+            to = out_at.at[here, pl.ds(start, out.shape[1])]
+            stores.append(pltpu.make_async_copy(out.at[here], to, sems.at[len(stores)]))
+            stores[-1].start()
     for store in stores:
         store.wait()
 
 
-def grad_partials(parts, basis):
-    depth, columns = basis.shape
-    tokens = sum(part.shape[0] for part in parts)
-    shape = (columns, tokens)
-    return pl.pallas_call(
-        lambda *refs: grad_kernel(len(parts), *refs),
-        out_shape=pltpu.HBM(shape, jnp.bfloat16),
-        in_specs=[VMEM] * (len(parts) + 1),
-        out_specs=ANY,
+def grad_partials(parts, basis, height, start=0, *filled):
+    tokens, depth = parts[0].shape
+    share = basis.shape[1] // 16
+    return pl.pallas_call(
+        lambda *refs: grad_kernel(len(parts), start, *refs),
+        out_shape=(
+            pltpu.HBM((16, height, 2 * tokens), jnp.bfloat16),
+            jax.ShapeDtypeStruct((8, 128), jnp.float32),
+        ),
+        in_specs=[VMEM] * (len(parts) + 1) + [ANY] * len(filled),
+        out_specs=(ANY, VMEM),
         scratch_shapes=[
-            pltpu.VMEM((tokens, depth), jnp.bfloat16),
-            pltpu.VMEM(shape, jnp.bfloat16),
-            pltpu.SemaphoreType.DMA((columns // 256,)),
+            pltpu.VMEM((len(parts) * tokens, depth), jnp.bfloat16),
+            pltpu.VMEM((16, len(parts) // 2 * share, 2 * tokens), jnp.bfloat16),
+            pltpu.SemaphoreType.DMA((4,)),
         ],
+        input_output_aliases={len(parts) + 1: 0} if filled else {},
         compiler_params=PARAMS,
         name="grad",
-    )(*parts, basis)
+    )(*parts, basis, *filled)
 
 
 def first_sum_kernel(place, got, kept, grad, given):
@@ -235,11 +210,6 @@
     )(value, *after)
 
 
-def exchanged(partial):
-    columns, tokens = partial.shape
-    return lax.all_to_all(partial.reshape(16, columns // 16, tokens), ("x", "y"), 0, 0, tiled=True)
-
-
 def squared(got):
     summed = jnp.sum(got.astype(jnp.float32), axis=0)
     total = summed + shifted(summed.astype(jnp.bfloat16), "z_hi", 1).astype(jnp.float32)
@@ -255,9 +225,17 @@
             for core in range(cores):
                 at = (i * cores + core) * tokens
                 act[at : at + tokens, to] = part[step, core]
-    rows = pieces[0].shape[0]
+    rows = pieces[0].shape[0] // len(steps)
+    wide = cores * tokens
     for y_behind, piece in enumerate(pieces):
-        part = jnp.dot(piece[...], act[...], preferred_element_type=jnp.float32)
+        part = sum(
+            jnp.dot(
+                piece[i * rows : (i + 1) * rows, :],
+                act[i * wide : (i + 1) * wide, :],
+                preferred_element_type=jnp.float32,
+            )
+            for i in range(len(steps))
+        )
         part = part * (1.0 / (chips * cores * tokens))
         at = pl.ds(pl.multiple_of(lax.rem(place[1] + 4 - y_behind, 4) * rows, rows), rows)
         for behind in range(4):
@@ -273,42 +251,47 @@
 
 
 def corrected(steps, pieces, acts, *before):
-    rows, tokens = pieces[0].shape
-    block = acts[0].shape[3]
+    rows = pieces[0].shape[0] // len(steps)
+    _, cores, tokens, block = acts[0].shape
     place = jnp.stack([lax.axis_index("x"), lax.axis_index("y")]).astype(jnp.int32)
     return pl.pallas_call(
         lambda *refs: correct_kernel(steps, *refs),
         out_shape=jax.ShapeDtypeStruct((4, 4 * rows, block), jnp.float32),
         in_specs=[SMEM] + [VMEM] * (8 + len(before)),
         out_specs=VMEM,
-        scratch_shapes=[pltpu.VMEM((tokens, 4 * block), jnp.bfloat16)],
+        scratch_shapes=[pltpu.VMEM((len(steps) * cores * tokens, 4 * block), jnp.bfloat16)],
         compiler_params=PARAMS,
         name="correct",
     )(place, *pieces, *acts, *before)
 
 
+def chip_rows(own):
+    return [own, shifted(own, "core", 1)]
+
+
 def per_device(hidden, norm_gain, gate_pre, out_grad, grad_basis, act_basis):
     tokens = hidden.shape[0]
+    share = grad_basis.shape[1] // 16
     up_grad = (out_grad.astype(jnp.float32) * jax.nn.silu(gate_pre.astype(jnp.float32))).astype(
         jnp.bfloat16
     )
-    first = act_partials(hidden, norm_gain, act_basis, grad_basis.shape[1] // 16)
-    first = own_partials(first, up_grad, shifted(up_grad, "core", 1), grad_basis)
+    near, *far = [shifted(up_grad, "z_lo", step) for step in (1, 2, 3)]
+    height = tokens + 2 * share
+    first = act_partials(hidden, norm_gain, act_basis, 2 * share)
+    first, mark = grad_partials(chip_rows(up_grad), grad_basis, height, tokens, first)
+    near = gated(near, [mark], jax.ShapeDtypeStruct)
+    first, _ = grad_partials(chip_rows(near), grad_basis, height, tokens + share, first)
     first_got = lax.all_to_all(first, ("x", "y"), 0, 0, tiled=True)
-    rows = []
-    for step in (1, 2, 3):
-        own = shifted(up_grad, "z_lo", step)
-        rows += [own, shifted(own, "core", 1)]
-    rest_got = exchanged(grad_partials(rows, grad_basis))
+    rest, _ = grad_partials(chip_rows(far[0]) + chip_rows(far[1]), grad_basis, 2 * share)
+    rest_got = lax.all_to_all(rest, ("x", "y"), 0, 0, tiled=True)
     act_own, first_sq = first_squares(first_got, tokens)
     act_chip = jnp.stack([act_own, shifted(act_own, "core", 1)])
     act_all = [act_chip] + [shifted(act_chip, "z_lo", step) for step in (1, 2, 3)]
-    first_pieces = spread(first_sq)
-    rest_sq = squared(gated(rest_got, act_all + first_pieces, jax.ShapeDtypeStruct))
+    rest_sq = squared(gated(rest_got, act_all, jax.ShapeDtypeStruct))
     act_all = jnp.stack(act_all)
     acts = [act_all] + [shifted(act_all, "x", step) for step in (1, 2, 3)]
-    out = corrected((0,), first_pieces, acts)
-    out = corrected((1, 2, 3), spread(rest_sq), acts, out)
+    out = corrected((0, 1), spread(first_sq), acts)
+    out = corrected((2, 3), spread(rest_sq), acts, out)
     out = lax.all_to_all(out, "x", 0, 0, tiled=True)
     return out.reshape(grad_basis.shape[1], -1)
 

time: 139 us -> 141 us (1.014)
  the two profiles are of different devices: /device:TPU:64 before, /device:TPU:8 now
where the time goes in v9:
time: 141 us
  starting transfers between devices  52.7 us (37%)
  waiting for transfers between devices  49.4 us (35%)
  Pallas kernels  18.2 us (13%)
  blocking collectives  17 us (12%)
  other arithmetic  2.3 us (2%)
    ppermute x22, starting transfers between devices, shifted(): lax.ppermute(value, axis, [(i, (i + step) % size) for i in range(size)])  36.6 us
    ppermute x22, waiting for transfers between devices, shifted(): lax.ppermute(value, axis, [(i, (i + step) % size) for i in range(size)])  26.7 us
    all_to_all x1, waiting for transfers between devices, per_device(): first_got = lax.all_to_all(first, ('x', 'y'), 0, 0, tiled=True)  19.4 us
    all_to_all x1, blocking collectives, per_device(): out = lax.all_to_all(out, 'x', 0, 0, tiled=True)  17 us
    pallas_call x3, Pallas kernels, grad_partials(): pl.pallas_call(lambda *refs: grad_kernel(len(parts), start, *refs), out_s...  9.36 us
    all_to_all x1, starting transfers between devices, per_device(): rest_got = lax.all_to_all(rest, ('x', 'y'), 0, 0, tiled=True)  8.67 us
    all_to_all x1, starting transfers between devices, per_device(): first_got = lax.all_to_all(first, ('x', 'y'), 0, 0, tiled=True)  7.4 us
    pallas_call x1, Pallas kernels, act_partials(): pl.pallas_call(act_kernel, out_shape=pltpu.HBM((16, tokens + share, wide)...  4.53 us
  transfers between devices with their start and end apart: 24, of which 13 were waited for; matrix products, arithmetic and copies ran while one was open for 0% of the time, Pallas kernels for 10%

profile of v9, /device:TPU:8, one launch (start us, length us, event | category | flops | bytes accessed | tf_op | source)
XLA Modules:
  0.0 140.7 jit_solution(2575502404767269555)
XLA Ops:
  0.0 1.9 %fusion.4.refs_0_ = bf16[128,896]{1,0:T(8,128)(2,1)} fusion(bf16[128,896]{1,0:T(8,128)(2,1)} %param.8, bf16[128,896]{1,0:T(8,128)(2,1)} %param.9), kind=kLoop, calls=%fused_computation.7 | loop fusion | flops 917504 | bytes 688128 | tf_op jit(solution)/shard_map/convert_element_type | solution.py:275
  1.9 1.9 %collective-permute-start.4 = (bf16[128,896]{1,0:T(8,128)(2,1)}, bf16[128,896]{1,0:T(8,128)(2,1)S(1)}, u32[]{:S(2)}, u32[]{:S(2)}) collective-permute-start(bf16[128,896]{1,0:T(8,128)(2,1)} %fusion.4.refs_0_), channel_id=1, source_target_pairs={{0,2},{2,4},{4,6},{6,0},{1,3},{3,5},{5,7},{7,1},{8,10},{10,12},{12... | collective-permute-start | bytes 688136 | tf_op jit(solution)/shard_map/ppermute | solution.py:22
  3.8 4.5 %act.1.refs_3_ = bf16[16,352,256]{2,1,0:T(8,128)(2,1)} custom-call(s32[1]{0:T(128)} %bitcast.3.place, f32[1,8192]{1,0:T(1,128)} %bitcast.18, bf16[128,8192]{1,0:T(8,128)(2,1)} %hidden_at.1, bf16[256,4096]{1,0:T(8,128)(2,1)} %basis_at.1), custom_call_target="tpu_custom_call" | custom-call | tf_op jit(solution)/shard_map/act/pallas_call | solution.py:73
  8.4 3.1 %grad.4 = (bf16[16,352,256]{2,1,0:T(8,128)(2,1)}, f32[8,128]{1,0:T(8,128)S(1)}) custom-call(bf16[128,896]{1,0:T(8,128)(2,1)} %fusion.4.refs_0_, bf16[128,896]{1,0:T(8,128)(2,1)} %collective-permute-done.5.refs_1_, bf16[896,1792]{1,0:T(8,128)(2,1)S(1)} %copy-done, bf16[16,352,256]{2,1,0:T(8,128)(2,1)} %act.1.refs_3_), custom_call_target="tpu_custom_call", output_to_operand_aliasing={{0}: (3, {})} | custom-call | tf_op jit(solution)/shard_map/grad/pallas_call | solution.py:119
  11.4 1.6 %collective-permute-done.4.refs_0_ = bf16[128,896]{1,0:T(8,128)(2,1)S(1)} collective-permute-done((bf16[128,896]{1,0:T(8,128)(2,1)}, bf16[128,896]{1,0:T(8,128)(2,1)S(1)}, u32[]{:S(2)}, u32[]{:S(2)}) %collective-permute-start.4) | collective-permute-done | bytes 229408 | tf_op jit(solution)/shard_map/ppermute | solution.py:22
  13.0 1.5 %collective-permute-done.6.refs_1_ = bf16[128,896]{1,0:T(8,128)(2,1)S(1)} collective-permute-done((bf16[128,896]{1,0:T(8,128)(2,1)S(1)}, bf16[128,896]{1,0:T(8,128)(2,1)S(1)}, u32[]{:S(2)}, u32[]{:S(2)}) %collective-permute-start.6) | collective-permute-done | bytes 229408 | tf_op jit(solution)/shard_map/ppermute | solution.py:22
  14.5 2.6 %grad.5 = (bf16[16,352,256]{2,1,0:T(8,128)(2,1)}, f32[8,128]{1,0:T(8,128)}) custom-call(bf16[128,896]{1,0:T(8,128)(2,1)S(1)} %gate.2.refs_0_, bf16[128,896]{1,0:T(8,128)(2,1)S(1)} %collective-permute-done.6.refs_1_, bf16[896,1792]{1,0:T(8,128)(2,1)S(1)} %copy-done, bf16[16,352,256]{2,1,0:T(8,128)(2,1)} %get-tuple-element.16.refs_3_), custom_call_target="tpu_custom_call", output_to_operand_aliasing={{0}: (3, {})} | custom-call | tf_op jit(solution)/shard_map/grad/pallas_call | solution.py:119
  17.1 7.4 %all-to-all-start.1 = ((bf16[16,352,256]{2,1,0:T(8,128)(2,1)}), bf16[16,352,256]{2,1,0:T(8,128)(2,1)}, u32[]{:S(2)}, u32[]{:S(2)}) async-start(bf16[16,352,256]{2,1,0:T(8,128)(2,1)} %get-tuple-element.17), calls=%async_computation.1 | async-start | bytes 5767168 | tf_op jit(solution)/shard_map/all_to_all | solution.py:284
  24.5 1.8 %collective-permute-start = (bf16[128,896]{1,0:T(8,128)(2,1)}, bf16[128,896]{1,0:T(8,128)(2,1)S(1)}, u32[]{:S(2)}, u32[]{:S(2)}) collective-permute-start(bf16[128,896]{1,0:T(8,128)(2,1)} %fusion.4.refs_0_), channel_id=1, source_target_pairs={{0,4},{2,6},{4,0},{6,2},{1,5},{3,7},{5,1},{7,3},{8,12},{10,14},{12... | collective-permute-start | bytes 688136 | tf_op jit(solution)/shard_map/ppermute | solution.py:22
  27.3 10.4 %collective-permute-done.refs_0_ = bf16[128,896]{1,0:T(8,128)(2,1)S(1)} collective-permute-done((bf16[128,896]{1,0:T(8,128)(2,1)}, bf16[128,896]{1,0:T(8,128)(2,1)S(1)}, u32[]{:S(2)}, u32[]{:S(2)}) %collective-permute-start) | collective-permute-done | bytes 229408 | tf_op jit(solution)/shard_map/ppermute | solution.py:22
  39.8 3.7 %grad.3 = (bf16[16,224,256]{2,1,0:T(8,128)(2,1)}, f32[8,128]{1,0:T(8,128)}) custom-call(bf16[128,896]{1,0:T(8,128)(2,1)S(1)} %collective-permute-done.refs_0_, bf16[128,896]{1,0:T(8,128)(2,1)S(1)} %collective-permute-done.1.refs_1_, bf16[128,896]{1,0:T(8,128)(2,1)S(1)} %collective-permute-done.2.refs_2_, ...), custom_call_target="tpu_custom_call" | custom-call | tf_op jit(solution)/shard_map/grad/pallas_call | solution.py:119
  43.5 19.4 %all-to-all-done.1.got = bf16[16,352,256]{2,1,0:T(8,128)(2,1)} async-done(((bf16[16,352,256]{2,1,0:T(8,128)(2,1)}), bf16[16,352,256]{2,1,0:T(8,128)(2,1)}, u32[]{:S(2)}, u32[]{:S(2)}) %all-to-all-start.1) | async-done | bytes 2883616 | tf_op jit(solution)/shard_map/all_to_all | solution.py:284
  62.9 8.7 %all-to-all-start = ((bf16[16,224,256]{2,1,0:T(8,128)(2,1)}), bf16[16,224,256]{2,1,0:T(8,128)(2,1)S(1)}, u32[]{:S(2)}, u32[]{:S(2)}) async-start(bf16[16,224,256]{2,1,0:T(8,128)(2,1)} %get-tuple-element.14), calls=%async_computation | async-start | bytes 3670016 | tf_op jit(solution)/shard_map/all_to_all | solution.py:286
  71.6 2.2 %first_sum.1 = (f32[128,128]{1,0:T(8,128)S(1)}, f32[224,256]{1,0:T(8,128)S(1)}, bf16[288,256]{1,0:T(8,128)(2,1)S(1)}) custom-call(s32[1]{0:T(128)} %bitcast.2.place, bf16[16,352,256]{2,1,0:T(8,128)(2,1)} %all-to-all-done.1.got), custom_call_target="tpu_custom_call" | custom-call | tf_op jit(solution)/shard_map/first_sum/pallas_call | solution.py:172
  73.8 6.3 %collective-permute-start.7 = (bf16[288,256]{1,0:T(8,128)(2,1)S(1)}, bf16[288,256]{1,0:T(8,128)(2,1)S(1)}, u32[]{:S(2)}, u32[]{:S(2)}) collective-permute-start(bf16[288,256]{1,0:T(8,128)(2,1)S(1)} %get-tuple-element.20), channel_id=1, source_target_pairs={{0,128},{128,0},{1,129},{129,1},{2,130},{130,2},{3,131},{131,3},{4... | collective-permute-start | bytes 442376 | tf_op jit(solution)/shard_map/ppermute | solution.py:22
  80.0 5.0 %collective-permute-done.7.got = bf16[288,256]{1,0:T(8,128)(2,1)S(1)} collective-permute-done((bf16[288,256]{1,0:T(8,128)(2,1)S(1)}, bf16[288,256]{1,0:T(8,128)(2,1)S(1)}, u32[]{:S(2)}, u32[]{:S(2)}) %collective-permute-start.7) | collective-permute-done | bytes 147488 | tf_op jit(solution)/shard_map/ppermute | solution.py:22
  85.2 1.2 collective-permute-done.8
  86.4 2.2 %collective-permute-start.11 = (bf16[2,128,128]{2,1,0:T(8,128)(2,1)S(1)}, bf16[2,128,128]{2,1,0:T(8,128)(2,1)S(1)}, u32[]{:S(2)}, u32[]{:S(2)}) collective-permute-start(bf16[2,128,128]{2,1,0:T(8,128)(2,1)S(1)} %get-tuple-element.24.refs_1_), channel_id=1, source_target_pairs={{0,6},{2,0},{4,2},{6,4},{1,7},{3,1},{5,3},{7,5},{8,14},{10,8},{12,... | collective-permute-start | bytes 196616 | tf_op jit(solution)/shard_map/ppermute | solution.py:22
  88.6 2.9 %collective-permute-start.10 = (bf16[2,128,128]{2,1,0:T(8,128)(2,1)S(1)}, bf16[2,128,128]{2,1,0:T(8,128)(2,1)S(1)}, u32[]{:S(2)}, u32[]{:S(2)}) collective-permute-start(bf16[2,128,128]{2,1,0:T(8,128)(2,1)S(1)} %get-tuple-element.24.refs_1_), channel_id=1, source_target_pairs={{0,4},{2,6},{4,0},{6,2},{1,5},{3,7},{5,1},{7,3},{8,12},{10,14},{12... | collective-permute-start | bytes 196616 | tf_op jit(solution)/shard_map/ppermute | solution.py:22
  91.5 1.5 %collective-permute-start.19 = (bf16[224,256]{1,0:T(8,128)(2,1)S(1)}, bf16[224,256]{1,0:T(8,128)(2,1)S(1)}, u32[]{:S(2)}, u32[]{:S(2)}) collective-permute-start(bf16[224,256]{1,0:T(8,128)(2,1)S(1)} %get-tuple-element.22.refs_1_), channel_id=1, source_target_pairs={{0,8},{8,16},{16,24},{24,0},{1,9},{9,17},{17,25},{25,1},{2,10},{10... | collective-permute-start | bytes 344072 | tf_op jit(solution)/shard_map/ppermute | solution.py:22
  92.9 3.2 %all-to-all-done.refs_0_ = bf16[16,224,256]{2,1,0:T(8,128)(2,1)S(1)} async-done(((bf16[16,224,256]{2,1,0:T(8,128)(2,1)}), bf16[16,224,256]{2,1,0:T(8,128)(2,1)S(1)}, u32[]{:S(2)}, u32[]{:S(2)}) %all-to-all-start) | async-done | bytes 1835040 | tf_op jit(solution)/shard_map/all_to_all | solution.py:286
  96.7 6.0 %collective-permute-start.12 = (bf16[224,256]{1,0:T(8,128)(2,1)S(1)}, bf16[224,256]{1,0:T(8,128)(2,1)S(1)}, u32[]{:S(2)}, u32[]{:S(2)}) collective-permute-start(bf16[224,256]{1,0:T(8,128)(2,1)S(1)} %convert_element_type.25), channel_id=1, source_target_pairs={{0,128},{128,0},{1,129},{129,1},{2,130},{130,2},{3,131},{131,3},{4... | collective-permute-start | bytes 344072 | tf_op jit(solution)/shard_map/ppermute | solution.py:22
  102.7 1.4 collective-permute-start.16
  104.1 2.1 %collective-permute-start.20 = (bf16[224,256]{1,0:T(8,128)(2,1)S(1)}, bf16[224,256]{1,0:T(8,128)(2,1)S(1)}, u32[]{:S(2)}, u32[]{:S(2)}) collective-permute-start(bf16[224,256]{1,0:T(8,128)(2,1)S(1)} %get-tuple-element.22.refs_1_), channel_id=1, source_target_pairs={{0,16},{8,24},{16,0},{24,8},{1,17},{9,25},{17,1},{25,9},{2,18},{10... | collective-permute-start | bytes 344072 | tf_op jit(solution)/shard_map/ppermute | solution.py:22
  106.2 1.5 %collective-permute-start.21 = (bf16[224,256]{1,0:T(8,128)(2,1)S(1)}, bf16[224,256]{1,0:T(8,128)(2,1)S(1)}, u32[]{:S(2)}, u32[]{:S(2)}) collective-permute-start(bf16[224,256]{1,0:T(8,128)(2,1)S(1)} %get-tuple-element.22.refs_1_), channel_id=1, source_target_pairs={{0,24},{8,0},{16,8},{24,16},{1,25},{9,1},{17,9},{25,17},{2,26},{10... | collective-permute-start | bytes 344072 | tf_op jit(solution)/shard_map/ppermute | solution.py:22
  107.6 2.7 %collective-permute-start.17 = (bf16[4,2,128,128]{3,2,1,0:T(8,128)(2,1)S(1)}, bf16[4,2,128,128]{3,2,1,0:T(8,128)(2,1)S(1)}, u32[]{:S(2)}, u32[]{:S(2)}) collective-permute-start(bf16[4,2,128,128]{3,2,1,0:T(8,128)(2,1)S(1)} %pad_maximum_fusion.refs_5_), channel_id=1, source_target_pairs={{0,64},{32,96},{64,0},{96,32},{1,65},{33,97},{65,1},{97,33},{2,66}... | collective-permute-start | bytes 786440 | tf_op jit(solution)/shard_map/ppermute | solution.py:22
  110.3 1.5 %collective-permute-start.18 = (bf16[4,2,128,128]{3,2,1,0:T(8,128)(2,1)S(1)}, bf16[4,2,128,128]{3,2,1,0:T(8,128)(2,1)S(1)}, u32[]{:S(2)}, u32[]{:S(2)}) collective-permute-start(bf16[4,2,128,128]{3,2,1,0:T(8,128)(2,1)S(1)} %pad_maximum_fusion.refs_5_), channel_id=1, source_target_pairs={{0,96},{32,0},{64,32},{96,64},{1,97},{33,1},{65,33},{97,65},{2,98}... | collective-permute-start | bytes 786440 | tf_op jit(solution)/shard_map/ppermute | solution.py:22
  112.5 2.7 %collective-permute-start.14 = (bf16[224,256]{1,0:T(8,128)(2,1)S(1)}, bf16[224,256]{1,0:T(8,128)(2,1)S(1)}, u32[]{:S(2)}, u32[]{:S(2)}) collective-permute-start(bf16[224,256]{1,0:T(8,128)(2,1)S(1)} %multiply_convert_fusion.refs_1_), channel_id=1, source_target_pairs={{0,16},{8,24},{16,0},{24,8},{1,17},{9,25},{17,1},{25,9},{2,18},{10... | collective-permute-start | bytes 344072 | tf_op jit(solution)/shard_map/ppermute | solution.py:22
  115.8 2.1 %collective-permute-done.17.refs_7_ = bf16[4,2,128,128]{3,2,1,0:T(8,128)(2,1)S(1)} collective-permute-done((bf16[4,2,128,128]{3,2,1,0:T(8,128)(2,1)S(1)}, bf16[4,2,128,128]{3,2,1,0:T(8,128)(2,1)S(1)}, u32[]{:S(2)}, u32[]{:S(2)}) %collective-permute-start.17) | collective-permute-done | bytes 262176 | tf_op jit(solution)/shard_map/ppermute | solution.py:22
  118.0 2.6 %collective-permute-done.18.refs_8_ = bf16[4,2,128,128]{3,2,1,0:T(8,128)(2,1)S(1)} collective-permute-done((bf16[4,2,128,128]{3,2,1,0:T(8,128)(2,1)S(1)}, bf16[4,2,128,128]{3,2,1,0:T(8,128)(2,1)S(1)}, u32[]{:S(2)}, u32[]{:S(2)}) %collective-permute-start.18) | collective-permute-done | bytes 262176 | tf_op jit(solution)/shard_map/ppermute | solution.py:22
  121.7 1.1 correct.3
  122.8 17.0 %all_to_all.15 = f32[4,448,128]{2,1,0:T(8,128)S(1)} all-to-all(f32[4,448,128]{2,1,0:T(8,128)S(1)} %correct.3), channel_id=1, replica_groups=mesh['z_hi'=2,'x'=4,'y'=4,'z_lo'=4,'core'=2] {'x'}, dimensions={0} | all-to-all | bytes 1835008 | tf_op jit(solution)/shard_map/all_to_all | solution.py:295
  (37 shorter events, 7.1 us)
Async XLA Ops:
  1.9 6.5 %collective-permute-start.5 = (bf16[128,896]{1,0:T(8,128)(2,1)}, bf16[128,896]{1,0:T(8,128)(2,1)}, u32[]{:S(2)}, u32[]{:S(2)}) collective-permute-start(bf16[128,896]{1,0:T(8,128)(2,1)} %fusion.4.refs_0_), channel_id=1, source_target_pairs={{0,1},{1,0},{2,3},{3,2},{4,5},{5,4},{6,7},{7,6},{8,9},{9,8},{10,11... | collective-permute-start | bytes 688136 | tf_op jit(solution)/shard_map/ppermute | solution.py:22
  1.9 11.1 %collective-permute-start.4 = (bf16[128,896]{1,0:T(8,128)(2,1)}, bf16[128,896]{1,0:T(8,128)(2,1)S(1)}, u32[]{:S(2)}, u32[]{:S(2)}) collective-permute-start(bf16[128,896]{1,0:T(8,128)(2,1)} %fusion.4.refs_0_), channel_id=1, source_target_pairs={{0,2},{2,4},{4,6},{6,0},{1,3},{3,5},{5,7},{7,1},{8,10},{10,12},{12... | collective-permute-start | bytes 688136 | tf_op jit(solution)/shard_map/ppermute | solution.py:22
  3.8 4.5 %copy-start = (bf16[896,1792]{1,0:T(8,128)(2,1)S(1)}, bf16[896,1792]{1,0:T(8,128)(2,1)}, u32[]{:S(2)}) copy-start(bf16[896,1792]{1,0:T(8,128)(2,1)} %refs_2_.3) | copy-start | bytes 9633796
  13.0 1.5 %collective-permute-start.6 = (bf16[128,896]{1,0:T(8,128)(2,1)S(1)}, bf16[128,896]{1,0:T(8,128)(2,1)S(1)}, u32[]{:S(2)}, u32[]{:S(2)}) collective-permute-start(bf16[128,896]{1,0:T(8,128)(2,1)S(1)} %gate.2.refs_0_), channel_id=1, source_target_pairs={{0,1},{1,0},{2,3},{3,2},{4,5},{5,4},{6,7},{7,6},{8,9},{9,8},{10,11... | collective-permute-start | bytes 688136 | tf_op jit(solution)/shard_map/ppermute | solution.py:22
  17.1 45.8 %all-to-all-start.1 = ((bf16[16,352,256]{2,1,0:T(8,128)(2,1)}), bf16[16,352,256]{2,1,0:T(8,128)(2,1)}, u32[]{:S(2)}, u32[]{:S(2)}) async-start(bf16[16,352,256]{2,1,0:T(8,128)(2,1)} %get-tuple-element.17), calls=%async_computation.1 | async-start | bytes 5767168 | tf_op jit(solution)/shard_map/all_to_all | solution.py:284
  24.5 13.2 %collective-permute-start = (bf16[128,896]{1,0:T(8,128)(2,1)}, bf16[128,896]{1,0:T(8,128)(2,1)S(1)}, u32[]{:S(2)}, u32[]{:S(2)}) collective-permute-start(bf16[128,896]{1,0:T(8,128)(2,1)} %fusion.4.refs_0_), channel_id=1, source_target_pairs={{0,4},{2,6},{4,0},{6,2},{1,5},{3,7},{5,1},{7,3},{8,12},{10,14},{12... | collective-permute-start | bytes 688136 | tf_op jit(solution)/shard_map/ppermute | solution.py:22
  26.3 12.0 %collective-permute-start.2 = (bf16[128,896]{1,0:T(8,128)(2,1)}, bf16[128,896]{1,0:T(8,128)(2,1)S(1)}, u32[]{:S(2)}, u32[]{:S(2)}) collective-permute-start(bf16[128,896]{1,0:T(8,128)(2,1)} %fusion.4.refs_0_), channel_id=1, source_target_pairs={{0,6},{2,0},{4,2},{6,4},{1,7},{3,1},{5,3},{7,5},{8,14},{10,8},{12,... | collective-permute-start | bytes 688136 | tf_op jit(solution)/shard_map/ppermute | solution.py:22
  37.7 1.5 %collective-permute-start.1 = (bf16[128,896]{1,0:T(8,128)(2,1)S(1)}, bf16[128,896]{1,0:T(8,128)(2,1)S(1)}, u32[]{:S(2)}, u32[]{:S(2)}) collective-permute-start(bf16[128,896]{1,0:T(8,128)(2,1)S(1)} %collective-permute-done.refs_0_), channel_id=1, source_target_pairs={{0,1},{1,0},{2,3},{3,2},{4,5},{5,4},{6,7},{7,6},{8,9},{9,8},{10,11... | collective-permute-start | bytes 688136 | tf_op jit(solution)/shard_map/ppermute | solution.py:22
  38.3 1.5 %collective-permute-start.3 = (bf16[128,896]{1,0:T(8,128)(2,1)S(1)}, bf16[128,896]{1,0:T(8,128)(2,1)S(1)}, u32[]{:S(2)}, u32[]{:S(2)}) collective-permute-start(bf16[128,896]{1,0:T(8,128)(2,1)S(1)} %collective-permute-done.2.refs_2_), channel_id=1, source_target_pairs={{0,1},{1,0},{2,3},{3,2},{4,5},{5,4},{6,7},{7,6},{8,9},{9,8},{10,11... | collective-permute-start | bytes 688136 | tf_op jit(solution)/shard_map/ppermute | solution.py:22
  62.9 33.2 %all-to-all-start = ((bf16[16,224,256]{2,1,0:T(8,128)(2,1)}), bf16[16,224,256]{2,1,0:T(8,128)(2,1)S(1)}, u32[]{:S(2)}, u32[]{:S(2)}) async-start(bf16[16,224,256]{2,1,0:T(8,128)(2,1)} %get-tuple-element.14), calls=%async_computation | async-start | bytes 3670016 | tf_op jit(solution)/shard_map/all_to_all | solution.py:286
  73.8 11.3 %collective-permute-start.7 = (bf16[288,256]{1,0:T(8,128)(2,1)S(1)}, bf16[288,256]{1,0:T(8,128)(2,1)S(1)}, u32[]{:S(2)}, u32[]{:S(2)}) collective-permute-start(bf16[288,256]{1,0:T(8,128)(2,1)S(1)} %get-tuple-element.20), channel_id=1, source_target_pairs={{0,128},{128,0},{1,129},{129,1},{2,130},{130,2},{3,131},{131,3},{4... | collective-permute-start | bytes 442376 | tf_op jit(solution)/shard_map/ppermute | solution.py:22
  85.1 1.3 collective-permute-start.8
  86.4 9.7 %collective-permute-start.11 = (bf16[2,128,128]{2,1,0:T(8,128)(2,1)S(1)}, bf16[2,128,128]{2,1,0:T(8,128)(2,1)S(1)}, u32[]{:S(2)}, u32[]{:S(2)}) collective-permute-start(bf16[2,128,128]{2,1,0:T(8,128)(2,1)S(1)} %get-tuple-element.24.refs_1_), channel_id=1, source_target_pairs={{0,6},{2,0},{4,2},{6,4},{1,7},{3,1},{5,3},{7,5},{8,14},{10,8},{12,... | collective-permute-start | bytes 196616 | tf_op jit(solution)/shard_map/ppermute | solution.py:22
  88.6 7.6 %collective-permute-start.9 = (bf16[2,128,128]{2,1,0:T(8,128)(2,1)S(1)}, bf16[2,128,128]{2,1,0:T(8,128)(2,1)S(1)}, u32[]{:S(2)}, u32[]{:S(2)}) collective-permute-start(bf16[2,128,128]{2,1,0:T(8,128)(2,1)S(1)} %get-tuple-element.24.refs_1_), channel_id=1, source_target_pairs={{0,2},{2,4},{4,6},{6,0},{1,3},{3,5},{5,7},{7,1},{8,10},{10,12},{12... | collective-permute-start | bytes 196616 | tf_op jit(solution)/shard_map/ppermute | solution.py:22
  88.6 7.8 %collective-permute-start.10 = (bf16[2,128,128]{2,1,0:T(8,128)(2,1)S(1)}, bf16[2,128,128]{2,1,0:T(8,128)(2,1)S(1)}, u32[]{:S(2)}, u32[]{:S(2)}) collective-permute-start(bf16[2,128,128]{2,1,0:T(8,128)(2,1)S(1)} %get-tuple-element.24.refs_1_), channel_id=1, source_target_pairs={{0,4},{2,6},{4,0},{6,2},{1,5},{3,7},{5,1},{7,3},{8,12},{10,14},{12... | collective-permute-start | bytes 196616 | tf_op jit(solution)/shard_map/ppermute | solution.py:22
  91.5 16.2 %collective-permute-start.19 = (bf16[224,256]{1,0:T(8,128)(2,1)S(1)}, bf16[224,256]{1,0:T(8,128)(2,1)S(1)}, u32[]{:S(2)}, u32[]{:S(2)}) collective-permute-start(bf16[224,256]{1,0:T(8,128)(2,1)S(1)} %get-tuple-element.22.refs_1_), channel_id=1, source_target_pairs={{0,8},{8,16},{16,24},{24,0},{1,9},{9,17},{17,25},{25,1},{2,10},{10... | collective-permute-start | bytes 344072 | tf_op jit(solution)/shard_map/ppermute | solution.py:22
  96.7 13.6 %collective-permute-start.12 = (bf16[224,256]{1,0:T(8,128)(2,1)S(1)}, bf16[224,256]{1,0:T(8,128)(2,1)S(1)}, u32[]{:S(2)}, u32[]{:S(2)}) collective-permute-start(bf16[224,256]{1,0:T(8,128)(2,1)S(1)} %convert_element_type.25), channel_id=1, source_target_pairs={{0,128},{128,0},{1,129},{129,1},{2,130},{130,2},{3,131},{131,3},{4... | collective-permute-start | bytes 344072 | tf_op jit(solution)/shard_map/ppermute | solution.py:22
  102.7 12.4 %collective-permute-start.16 = (bf16[4,2,128,128]{3,2,1,0:T(8,128)(2,1)S(1)}, bf16[4,2,128,128]{3,2,1,0:T(8,128)(2,1)S(1)}, u32[]{:S(2)}, u32[]{:S(2)}) collective-permute-start(bf16[4,2,128,128]{3,2,1,0:T(8,128)(2,1)S(1)} %pad_maximum_fusion.refs_5_), channel_id=1, source_target_pairs={{0,32},{32,64},{64,96},{96,0},{1,33},{33,65},{65,97},{97,1},{2,34}... | collective-permute-start | bytes 786440 | tf_op jit(solution)/shard_map/ppermute | solution.py:22
  104.1 7.7 %collective-permute-start.20 = (bf16[224,256]{1,0:T(8,128)(2,1)S(1)}, bf16[224,256]{1,0:T(8,128)(2,1)S(1)}, u32[]{:S(2)}, u32[]{:S(2)}) collective-permute-start(bf16[224,256]{1,0:T(8,128)(2,1)S(1)} %get-tuple-element.22.refs_1_), channel_id=1, source_target_pairs={{0,16},{8,24},{16,0},{24,8},{1,17},{9,25},{17,1},{25,9},{2,18},{10... | collective-permute-start | bytes 344072 | tf_op jit(solution)/shard_map/ppermute | solution.py:22
  106.2 6.3 %collective-permute-start.21 = (bf16[224,256]{1,0:T(8,128)(2,1)S(1)}, bf16[224,256]{1,0:T(8,128)(2,1)S(1)}, u32[]{:S(2)}, u32[]{:S(2)}) collective-permute-start(bf16[224,256]{1,0:T(8,128)(2,1)S(1)} %get-tuple-element.22.refs_1_), channel_id=1, source_target_pairs={{0,24},{8,0},{16,8},{24,16},{1,25},{9,1},{17,9},{25,17},{2,26},{10... | collective-permute-start | bytes 344072 | tf_op jit(solution)/shard_map/ppermute | solution.py:22
  107.6 10.3 %collective-permute-start.17 = (bf16[4,2,128,128]{3,2,1,0:T(8,128)(2,1)S(1)}, bf16[4,2,128,128]{3,2,1,0:T(8,128)(2,1)S(1)}, u32[]{:S(2)}, u32[]{:S(2)}) collective-permute-start(bf16[4,2,128,128]{3,2,1,0:T(8,128)(2,1)S(1)} %pad_maximum_fusion.refs_5_), channel_id=1, source_target_pairs={{0,64},{32,96},{64,0},{96,32},{1,65},{33,97},{65,1},{97,33},{2,66}... | collective-permute-start | bytes 786440 | tf_op jit(solution)/shard_map/ppermute | solution.py:22
  110.3 10.3 %collective-permute-start.18 = (bf16[4,2,128,128]{3,2,1,0:T(8,128)(2,1)S(1)}, bf16[4,2,128,128]{3,2,1,0:T(8,128)(2,1)S(1)}, u32[]{:S(2)}, u32[]{:S(2)}) collective-permute-start(bf16[4,2,128,128]{3,2,1,0:T(8,128)(2,1)S(1)} %pad_maximum_fusion.refs_5_), channel_id=1, source_target_pairs={{0,96},{32,0},{64,32},{96,64},{1,97},{33,1},{65,33},{97,65},{2,98}... | collective-permute-start | bytes 786440 | tf_op jit(solution)/shard_map/ppermute | solution.py:22
  111.8 9.8 %collective-permute-start.13 = (bf16[224,256]{1,0:T(8,128)(2,1)S(1)}, bf16[224,256]{1,0:T(8,128)(2,1)S(1)}, u32[]{:S(2)}, u32[]{:S(2)}) collective-permute-start(bf16[224,256]{1,0:T(8,128)(2,1)S(1)} %multiply_convert_fusion.refs_1_), channel_id=1, source_target_pairs={{0,8},{8,16},{16,24},{24,0},{1,9},{9,17},{17,25},{25,1},{2,10},{10... | collective-permute-start | bytes 344072 | tf_op jit(solution)/shard_map/ppermute | solution.py:22
  112.5 9.2 %collective-permute-start.14 = (bf16[224,256]{1,0:T(8,128)(2,1)S(1)}, bf16[224,256]{1,0:T(8,128)(2,1)S(1)}, u32[]{:S(2)}, u32[]{:S(2)}) collective-permute-start(bf16[224,256]{1,0:T(8,128)(2,1)S(1)} %multiply_convert_fusion.refs_1_), channel_id=1, source_target_pairs={{0,16},{8,24},{16,0},{24,8},{1,17},{9,25},{17,1},{25,9},{2,18},{10... | collective-permute-start | bytes 344072 | tf_op jit(solution)/shard_map/ppermute | solution.py:22
  115.1 6.5 %collective-permute-start.15 = (bf16[224,256]{1,0:T(8,128)(2,1)S(1)}, bf16[224,256]{1,0:T(8,128)(2,1)S(1)}, u32[]{:S(2)}, u32[]{:S(2)}) collective-permute-start(bf16[224,256]{1,0:T(8,128)(2,1)S(1)} %multiply_convert_fusion.refs_1_), channel_id=1, source_target_pairs={{0,24},{8,0},{16,8},{24,16},{1,25},{9,1},{17,9},{25,17},{2,26},{10... | collective-permute-start | bytes 344072 | tf_op jit(solution)/shard_map/ppermute | solution.py:22

commit v10 on v7

--- a/solution.py
+++ b/solution.py
@@ -119,7 +119,7 @@
         store.wait()
 
 
-def grad_partials(parts, basis, *after):
+def grad_partials(parts, basis, after=(), cost=None):
     depth, columns = basis.shape
     tokens = sum(part.shape[0] for part in parts)
     shape = (columns, tokens)
@@ -134,6 +134,7 @@
             pltpu.SemaphoreType.DMA((columns // 256,)),
         ],
         compiler_params=PARAMS,
+        cost_estimate=cost,
         name="grad",
     )(*parts, basis, *after)
 
@@ -231,11 +232,12 @@
 def per_device(hidden, norm_gain, gate_pre, out_grad, grad_basis, act_basis):
     act_parts, up_grad = first_partials(hidden, norm_gain, gate_pre, out_grad, act_basis)
     near, far, farthest = [shifted(up_grad, "z_lo", step) for step in (1, 2, 3)]
-    near = gated(near, [far], jax.ShapeDtypeStruct)
+    near = gated(near, [far, farthest], jax.ShapeDtypeStruct)
     near_rows = [up_grad, shifted(up_grad, "core", 1), near, shifted(near, "core", 1)]
     far_rows = [far, shifted(far, "core", 1), farthest, shifted(farthest, "core", 1)]
     act_row = act_squares(act_parts)
-    near_got = exchanged(grad_partials(near_rows, grad_basis))
+    cost = pl.CostEstimate(flops=8*10**9, bytes_accessed=10**7, transcendentals=0)
+    near_got = exchanged(grad_partials(near_rows, grad_basis, (), cost))
     far_got = exchanged(gated(grad_partials(far_rows, grad_basis), act_row))
     act_own = jnp.stack(act_row)
     acts = []
@@ -243,7 +245,7 @@
         acts += [own, shifted(own, "core", 1)]
     near_sq = squared(near_got)
     near_pieces = [near_sq] + [shifted(near_sq, "y", step) for step in (1, 2, 3)]
-    far_sq = squared(gated(far_got, acts, jax.ShapeDtypeStruct))
+    far_sq = squared(gated(far_got, acts + [near_sq], jax.ShapeDtypeStruct))
     far_pieces = [far_sq] + [shifted(far_sq, "y", step) for step in (1, 2, 3)]
     out = corrected(far_pieces, acts[4:], corrected(near_pieces, acts[:4]))
     out = lax.all_to_all(out, "x", 0, 0, tiled=True)

time: 136 us -> 134 us (0.985); the launches traced: 133 us -> 133 us
  waiting for transfers between devices: 50.6 us -> 45.8 us
  local copies, waits for them, and re-layouts: 2.48 us -> 5.99 us
  starting transfers between devices: 50.4 us -> 52.4 us
  Pallas kernels: 14.4 us -> 12.9 us
    ppermute x26, waiting for transfers between devices: 42.2 us -> 34.4 us  [shifted(): lax.ppermute(value, axis, [(i, (i + step) % size) for i in range(size)])]
    unnamed x9, local copies, waits for them, and re-layouts: 2.48 us -> 5.99 us
    all_to_all x2, waiting for transfers between devices: 8.42 us -> 11.4 us  [exchanged(): lax.all_to_all(partial.reshape(16, columns // 16, tokens), ('x', 'y'), 0,...]
    ppermute x26, starting transfers between devices: 32.6 us -> 34.6 us  [shifted(): lax.ppermute(value, axis, [(i, (i + step) % size) for i in range(size)])]
  transfers between devices with their start and end apart: 29 -> 29, of which waited for: 13 -> 17; matrix products, arithmetic and copies ran while one was open for 2% -> 1% of each run, Pallas kernels for 6% -> 5%
where the time goes in v10:
time: 134 us; the launch traced here: 133 us
  starting transfers between devices  52.4 us (39%)
  waiting for transfers between devices  45.8 us (34%)
  blocking collectives  13.3 us (10%)
  Pallas kernels  12.9 us (10%)
  local copies, waits for them, and re-layouts  5.99 us (4%)
  other arithmetic  2.24 us (2%)
    ppermute x26, starting transfers between devices, shifted(): lax.ppermute(value, axis, [(i, (i + step) % size) for i in range(size)])  34.6 us
    ppermute x26, waiting for transfers between devices, shifted(): lax.ppermute(value, axis, [(i, (i + step) % size) for i in range(size)])  34.4 us
    all_to_all x1, blocking collectives, per_device(): out = lax.all_to_all(out, 'x', 0, 0, tiled=True)  13.3 us
    all_to_all x2, waiting for transfers between devices, exchanged(): lax.all_to_all(partial.reshape(16, columns // 16, tokens), ('x', 'y'), 0,...  11.4 us
    all_to_all x2, starting transfers between devices, exchanged(): lax.all_to_all(partial.reshape(16, columns // 16, tokens), ('x', 'y'), 0,...  10.8 us
    all_to_all x1, starting transfers between devices, act_squares(): got = lax.all_to_all(partials, ('x', 'y'), 0, 0, tiled=True)  7 us
    pallas_call x2, Pallas kernels, grad_partials(): pl.pallas_call(lambda *refs: grad_kernel(len(parts), *refs), out_shape=pl...  6.03 us
    unnamed x9, local copies, waits for them, and re-layouts  5.99 us
  transfers between devices with their start and end apart: 29, of which 17 were waited for; matrix products, arithmetic and copies ran while one was open for 1% of the time, Pallas kernels for 5%

profile of v10, /device:TPU:64, one launch (start us, length us, event | category | flops | bytes accessed | tf_op | source)
XLA Modules:
  0.0 132.9 jit_solution(8777204220865656031)
XLA Ops:
  0.0 4.6 %first.1 = (bf16[16,128,256]{2,1,0:T(8,128)(2,1)}, bf16[128,896]{1,0:T(8,128)(2,1)}) custom-call(s32[1]{0:T(128)} %bitcast.2.place, f32[1,8192]{1,0:T(1,128)} %bitcast.19, bf16[128,896]{1,0:T(8,128)(2,1)} %gate_at.1, bf16[128,896]{1,0:T(8,128)(2,1)} %grad_at.1, bf16[128,8192]{1,0:T(8,128)(2,1)} %hidden_at.1, bf16[256,4096]{1,0:T(8,128)(2,1)} %basis_at.1), custom_call_target="tpu_custom_call" | custom-call | tf_op jit(solution)/shard_map/first/pallas_call | solution.py:84
  4.6 1.5 %collective-permute-start = (bf16[128,896]{1,0:T(8,128)(2,1)}, bf16[128,896]{1,0:T(8,128)(2,1)S(1)}, u32[]{:S(2)}, u32[]{:S(2)}) collective-permute-start(bf16[128,896]{1,0:T(8,128)(2,1)} %get-tuple-element.9.refs_0_), channel_id=1, source_target_pairs={{0,4},{2,6},{4,0},{6,2},{1,5},{3,7},{5,1},{7,3},{8,12},{10,14},{12... | collective-permute-start | bytes 688136 | tf_op jit(solution)/shard_map/ppermute | solution.py:22
  6.1 2.0 %collective-permute-start.2 = (bf16[128,896]{1,0:T(8,128)(2,1)}, bf16[128,896]{1,0:T(8,128)(2,1)S(1)}, u32[]{:S(2)}, u32[]{:S(2)}) collective-permute-start(bf16[128,896]{1,0:T(8,128)(2,1)} %get-tuple-element.9.refs_0_), channel_id=1, source_target_pairs={{0,6},{2,0},{4,2},{6,4},{1,7},{3,1},{5,3},{7,5},{8,14},{10,8},{12,... | collective-permute-start | bytes 688136 | tf_op jit(solution)/shard_map/ppermute | solution.py:22
  8.1 7.0 %all-to-all-start = ((bf16[16,128,256]{2,1,0:T(8,128)(2,1)}), bf16[16,128,256]{2,1,0:T(8,128)(2,1)S(1)}, u32[]{:S(2)}, u32[]{:S(2)}) async-start(bf16[16,128,256]{2,1,0:T(8,128)(2,1)} %get-tuple-element.10), calls=%async_computation | async-start | bytes 2097152 | tf_op jit(solution)/shard_map/all_to_all | solution.py:153
  15.3 1.9 %collective-permute-done.refs_0_.refs_1_ = bf16[128,896]{1,0:T(8,128)(2,1)S(1)} collective-permute-done((bf16[128,896]{1,0:T(8,128)(2,1)}, bf16[128,896]{1,0:T(8,128)(2,1)S(1)}, u32[]{:S(2)}, u32[]{:S(2)}) %collective-permute-start) | collective-permute-done | bytes 229408 | tf_op jit(solution)/shard_map/ppermute | solution.py:22
  17.2 7.8 %collective-permute-done.2.refs_2_ = bf16[128,896]{1,0:T(8,128)(2,1)S(1)} collective-permute-done((bf16[128,896]{1,0:T(8,128)(2,1)}, bf16[128,896]{1,0:T(8,128)(2,1)S(1)}, u32[]{:S(2)}, u32[]{:S(2)}) %collective-permute-start.2) | collective-permute-done | bytes 229408 | tf_op jit(solution)/shard_map/ppermute | solution.py:22
  25.0 3.0 %collective-permute-done.16.refs_0_ = bf16[128,896]{1,0:T(8,128)(2,1)S(1)} collective-permute-done((bf16[128,896]{1,0:T(8,128)(2,1)}, bf16[128,896]{1,0:T(8,128)(2,1)S(1)}, u32[]{:S(2)}, u32[]{:S(2)}) %collective-permute-start.16) | collective-permute-done | bytes 229408 | tf_op jit(solution)/shard_map/ppermute | solution.py:22
  28.0 1.5 %collective-permute-done.17.refs_3_ = bf16[128,896]{1,0:T(8,128)(2,1)S(1)} collective-permute-done((bf16[128,896]{1,0:T(8,128)(2,1)S(1)}, bf16[128,896]{1,0:T(8,128)(2,1)S(1)}, u32[]{:S(2)}, u32[]{:S(2)}) %collective-permute-start.17) | collective-permute-done | bytes 229408 | tf_op jit(solution)/shard_map/ppermute | solution.py:22
  29.5 1.9 %copy-done = bf16[896,1792]{1,0:T(8,128)(2,1)S(1)} copy-done((bf16[896,1792]{1,0:T(8,128)(2,1)S(1)}, bf16[896,1792]{1,0:T(8,128)(2,1)}, u32[]{:S(2)}) %copy-start) | copy-done | bytes 3211288
  31.4 3.0 %grad.3 = bf16[1792,512]{1,0:T(8,128)(2,1)} custom-call(bf16[128,896]{1,0:T(8,128)(2,1)S(1)} %copy-done.2, bf16[128,896]{1,0:T(8,128)(2,1)S(1)} %collective-permute-done.15.refs_1_, bf16[128,896]{1,0:T(8,128)(2,1)S(1)} %gate.4.refs_2_, bf16[128,896]{1,0:T(8,128)(2,1)S(1)} %collective-permute-done.17.refs_3_, bf16[896,1792]{1,0:T(8,128)(2,1)S(1)} %copy-done), custom_call_target="tpu_custom_call" | custom-call | flops 8000000000 | bytes 10000000 | tf_op jit(solution)/shard_map/grad/pallas_call | solution.py:126
  34.4 7.0 %all-to-all-start.2 = ((bf16[16,112,512]{2,1,0:T(8,128)(2,1)}), bf16[16,112,512]{2,1,0:T(8,128)(2,1)S(1)}, u32[]{:S(2)}, u32[]{:S(2)}) async-start(bf16[16,112,512]{2,1,0:T(8,128)(2,1)} %bitcast.18), calls=%async_computation.2 | async-start | bytes 3670016 | tf_op jit(solution)/shard_map/all_to_all | solution.py:188
  41.6 5.0 %collective-permute-start.4 = (f32[128,128]{1,0:T(8,128)S(1)}, f32[128,128]{1,0:T(8,128)S(1)}, u32[]{:S(2)}, u32[]{:S(2)}) collective-permute-start(f32[128,128]{1,0:T(8,128)S(1)} %get-tuple-element.12), channel_id=1, source_target_pairs={{0,128},{128,0},{1,129},{129,1},{2,130},{130,2},{3,131},{131,3},{4... | collective-permute-start | bytes 196616 | tf_op jit(solution)/shard_map/ppermute | solution.py:22
  47.2 2.7 %collective-permute-done.4 = f32[128,128]{1,0:T(8,128)S(1)} collective-permute-done((f32[128,128]{1,0:T(8,128)S(1)}, f32[128,128]{1,0:T(8,128)S(1)}, u32[]{:S(2)}, u32[]{:S(2)}) %collective-permute-start.4) | collective-permute-done | bytes 65568 | tf_op jit(solution)/shard_map/ppermute | solution.py:22
  49.9 2.0 %collective-permute-start.5 = (bf16[128,128]{1,0:T(8,128)(2,1)S(1)}, bf16[128,128]{1,0:T(8,128)(2,1)S(1)}, u32[]{:S(2)}, u32[]{:S(2)}) collective-permute-start(bf16[128,128]{1,0:T(8,128)(2,1)S(1)} %multiply_convert_fusion.2.refs_1_), channel_id=1, source_target_pairs={{0,32},{32,64},{64,96},{96,0},{1,33},{33,65},{65,97},{97,1},{2,34}... | collective-permute-start | bytes 98312 | tf_op jit(solution)/shard_map/ppermute | solution.py:22
  51.9 2.7 %collective-permute-start.6 = (bf16[128,128]{1,0:T(8,128)(2,1)S(1)}, bf16[128,128]{1,0:T(8,128)(2,1)S(1)}, u32[]{:S(2)}, u32[]{:S(2)}) collective-permute-start(bf16[128,128]{1,0:T(8,128)(2,1)S(1)} %multiply_convert_fusion.2.refs_1_), channel_id=1, source_target_pairs={{0,64},{32,96},{64,0},{96,32},{1,65},{33,97},{65,1},{97,33},{2,66}... | collective-permute-start | bytes 98312 | tf_op jit(solution)/shard_map/ppermute | solution.py:22
  54.6 1.5 %collective-permute-start.7 = (bf16[128,128]{1,0:T(8,128)(2,1)S(1)}, bf16[128,128]{1,0:T(8,128)(2,1)S(1)}, u32[]{:S(2)}, u32[]{:S(2)}) collective-permute-start(bf16[128,128]{1,0:T(8,128)(2,1)S(1)} %multiply_convert_fusion.2.refs_1_), channel_id=1, source_target_pairs={{0,96},{32,0},{64,32},{96,64},{1,97},{33,1},{65,33},{97,65},{2,98}... | collective-permute-start | bytes 98312 | tf_op jit(solution)/shard_map/ppermute | solution.py:22
  56.0 1.9 %copy-done.1 = bf16[896,1792]{1,0:T(8,128)(2,1)S(1)} copy-done((bf16[896,1792]{1,0:T(8,128)(2,1)S(1)}, bf16[896,1792]{1,0:T(8,128)(2,1)}, u32[]{:S(2)}) %copy-start.1) | copy-done | bytes 3211288
  58.0 3.0 %grad.2.refs_0_ = bf16[1792,512]{1,0:T(8,128)(2,1)} custom-call(bf16[128,896]{1,0:T(8,128)(2,1)S(1)} %collective-permute-done.refs_0_.refs_1_, bf16[128,896]{1,0:T(8,128)(2,1)S(1)} %collective-permute-done.1.refs_1_, bf16[128,896]{1,0:T(8,128)(2,1)S(1)} %collective-permute-done.2.refs_2_, bf16[128,896]{1,0:T(8,128)(2,1)S(1)} %collective-permute-done.3.refs_3_, ...), custom_call_target="tpu_custom_call" | custom-call | tf_op jit(solution)/shard_map/grad/pallas_call | solution.py:126
  61.0 3.8 %collective-permute-done.5.refs_2_ = bf16[128,128]{1,0:T(8,128)(2,1)S(1)} collective-permute-done((bf16[128,128]{1,0:T(8,128)(2,1)S(1)}, bf16[128,128]{1,0:T(8,128)(2,1)S(1)}, u32[]{:S(2)}, u32[]{:S(2)}) %collective-permute-start.5) | collective-permute-done | bytes 32800 | tf_op jit(solution)/shard_map/ppermute | solution.py:22
  64.7 2.3 %collective-permute-done.6.refs_3_ = bf16[128,128]{1,0:T(8,128)(2,1)S(1)} collective-permute-done((bf16[128,128]{1,0:T(8,128)(2,1)S(1)}, bf16[128,128]{1,0:T(8,128)(2,1)S(1)}, u32[]{:S(2)}, u32[]{:S(2)}) %collective-permute-start.6) | collective-permute-done | bytes 32800 | tf_op jit(solution)/shard_map/ppermute | solution.py:22
  67.0 2.1 %all-to-all-done.2 = bf16[16,112,512]{2,1,0:T(8,128)(2,1)S(1)} async-done(((bf16[16,112,512]{2,1,0:T(8,128)(2,1)}), bf16[16,112,512]{2,1,0:T(8,128)(2,1)S(1)}, u32[]{:S(2)}, u32[]{:S(2)}) %all-to-all-start.2) | async-done | bytes 1835040 | tf_op jit(solution)/shard_map/all_to_all | solution.py:188
  70.4 3.8 %all-to-all-start.1 = ((bf16[16,112,512]{2,1,0:T(8,128)(2,1)}), bf16[16,112,512]{2,1,0:T(8,128)(2,1)S(1)}, u32[]{:S(2)}, u32[]{:S(2)}) async-start(bf16[16,112,512]{2,1,0:T(8,128)(2,1)} %bitcast.16), calls=%async_computation.1 | async-start | bytes 3670016 | tf_op jit(solution)/shard_map/all_to_all | solution.py:188
  76.3 1.8 %convert_reduce_fusion.1 = f32[112,512]{1,0:T(8,128)S(1)} fusion(bf16[16,112,512]{2,1,0:T(8,128)(2,1)} %copy-done.3), kind=kLoop, calls=%fused_computation.1 | loop fusion | flops 1777664 | bytes 2064384 | tf_op jit(solution)/shard_map/reduce_sum | solution.py:192
  78.1 5.4 %collective-permute-start.18 = (bf16[112,512]{1,0:T(8,128)(2,1)S(1)}, bf16[112,512]{1,0:T(8,128)(2,1)S(1)}, u32[]{:S(2)}, u32[]{:S(2)}) collective-permute-start(bf16[112,512]{1,0:T(8,128)(2,1)S(1)} %convert_element_type.29), channel_id=1, source_target_pairs={{0,128},{128,0},{1,129},{129,1},{2,130},{130,2},{3,131},{131,3},{4... | collective-permute-start | bytes 344072 | tf_op jit(solution)/shard_map/ppermute | solution.py:22
  83.5 4.4 %collective-permute-done.9.refs_3_.refs_6_ = bf16[4,128,128]{2,1,0:T(8,128)(2,1)S(1)} collective-permute-done((bf16[4,128,128]{2,1,0:T(8,128)(2,1)S(1)}, bf16[4,128,128]{2,1,0:T(8,128)(2,1)S(1)}, u32[]{:S(2)}, u32[]{:S(2)}) %collective-permute-start.9) | collective-permute-done | bytes 131104 | tf_op jit(solution)/shard_map/ppermute | solution.py:22
  89.8 9.3 %all-to-all-done.1.refs_0_ = bf16[16,112,512]{2,1,0:T(8,128)(2,1)S(1)} async-done(((bf16[16,112,512]{2,1,0:T(8,128)(2,1)}), bf16[16,112,512]{2,1,0:T(8,128)(2,1)S(1)}, u32[]{:S(2)}, u32[]{:S(2)}) %all-to-all-start.1) | async-done | bytes 1835040 | tf_op jit(solution)/shard_map/all_to_all | solution.py:188
  99.4 4.9 %collective-permute-start.19 = (bf16[112,512]{1,0:T(8,128)(2,1)S(1)}, bf16[112,512]{1,0:T(8,128)(2,1)S(1)}, u32[]{:S(2)}, u32[]{:S(2)}) collective-permute-start(bf16[112,512]{1,0:T(8,128)(2,1)S(1)} %convert_element_type.33), channel_id=1, source_target_pairs={{0,128},{128,0},{1,129},{129,1},{2,130},{130,2},{3,131},{131,3},{4... | collective-permute-start | bytes 344072 | tf_op jit(solution)/shard_map/ppermute | solution.py:22
  104.9 1.5 %collective-permute-start.24 = (bf16[112,512]{1,0:T(8,128)(2,1)S(1)}, bf16[112,512]{1,0:T(8,128)(2,1)S(1)}, u32[]{:S(2)}, u32[]{:S(2)}) collective-permute-start(bf16[112,512]{1,0:T(8,128)(2,1)S(1)} %multiply_convert_fusion.1.refs_9_.refs_0_), channel_id=1, source_target_pairs={{0,16},{8,24},{16,0},{24,8},{1,17},{9,25},{17,1},{25,9},{2,18},{10... | collective-permute-start | bytes 344072 | tf_op jit(solution)/shard_map/ppermute | solution.py:22
  108.9 1.8 %collective-permute-start.21 = (bf16[112,512]{1,0:T(8,128)(2,1)S(1)}, bf16[112,512]{1,0:T(8,128)(2,1)S(1)}, u32[]{:S(2)}, u32[]{:S(2)}) collective-permute-start(bf16[112,512]{1,0:T(8,128)(2,1)S(1)} %multiply_convert_fusion.refs_0_), channel_id=1, source_target_pairs={{0,16},{8,24},{16,0},{24,8},{1,17},{9,25},{17,1},{25,9},{2,18},{10... | collective-permute-start | bytes 344072 | tf_op jit(solution)/shard_map/ppermute | solution.py:22
  110.7 2.1 %collective-permute-done.23.refs_1_ = bf16[112,512]{1,0:T(8,128)(2,1)S(1)} collective-permute-done((bf16[112,512]{1,0:T(8,128)(2,1)S(1)}, bf16[112,512]{1,0:T(8,128)(2,1)S(1)}, u32[]{:S(2)}, u32[]{:S(2)}) %collective-permute-start.23) | collective-permute-done | bytes 114720 | tf_op jit(solution)/shard_map/ppermute | solution.py:22
  115.5 2.1 %collective-permute-done.22.refs_3_ = bf16[112,512]{1,0:T(8,128)(2,1)S(1)} collective-permute-done((bf16[112,512]{1,0:T(8,128)(2,1)S(1)}, bf16[112,512]{1,0:T(8,128)(2,1)S(1)}, u32[]{:S(2)}, u32[]{:S(2)}) %collective-permute-start.22) | collective-permute-done | bytes 114720 | tf_op jit(solution)/shard_map/ppermute | solution.py:22
  118.6 13.3 %all_to_all.20 = f32[4,448,128]{2,1,0:T(8,128)S(1)} all-to-all(f32[4,448,128]{2,1,0:T(8,128)S(1)} %correct.3), channel_id=1, replica_groups=mesh['z_hi'=2,'x'=4,'y'=4,'z_lo'=4,'core'=2] {'x'}, dimensions={0} | all-to-all | bytes 1835008 | tf_op jit(solution)/shard_map/all_to_all | solution.py:251
  (54 shorter events, 14.1 us)
Async XLA Ops:
  4.6 10.5 %copy-start.2 = (bf16[128,896]{1,0:T(8,128)(2,1)S(1)}, bf16[128,896]{1,0:T(8,128)(2,1)}, u32[]{:S(2)}) copy-start(bf16[128,896]{1,0:T(8,128)(2,1)} %get-tuple-element.9.refs_0_) | copy-start | bytes 688132
  4.6 12.5 %collective-permute-start = (bf16[128,896]{1,0:T(8,128)(2,1)}, bf16[128,896]{1,0:T(8,128)(2,1)S(1)}, u32[]{:S(2)}, u32[]{:S(2)}) collective-permute-start(bf16[128,896]{1,0:T(8,128)(2,1)} %get-tuple-element.9.refs_0_), channel_id=1, source_target_pairs={{0,4},{2,6},{4,0},{6,2},{1,5},{3,7},{5,1},{7,3},{8,12},{10,14},{12... | collective-permute-start | bytes 688136 | tf_op jit(solution)/shard_map/ppermute | solution.py:22
  6.1 18.9 %collective-permute-start.2 = (bf16[128,896]{1,0:T(8,128)(2,1)}, bf16[128,896]{1,0:T(8,128)(2,1)S(1)}, u32[]{:S(2)}, u32[]{:S(2)}) collective-permute-start(bf16[128,896]{1,0:T(8,128)(2,1)} %get-tuple-element.9.refs_0_), channel_id=1, source_target_pairs={{0,6},{2,0},{4,2},{6,4},{1,7},{3,1},{5,3},{7,5},{8,14},{10,8},{12,... | collective-permute-start | bytes 688136 | tf_op jit(solution)/shard_map/ppermute | solution.py:22
  8.1 19.9 %collective-permute-start.16 = (bf16[128,896]{1,0:T(8,128)(2,1)}, bf16[128,896]{1,0:T(8,128)(2,1)S(1)}, u32[]{:S(2)}, u32[]{:S(2)}) collective-permute-start(bf16[128,896]{1,0:T(8,128)(2,1)} %get-tuple-element.9.refs_0_), channel_id=1, source_target_pairs={{0,2},{2,4},{4,6},{6,0},{1,3},{3,5},{5,7},{7,1},{8,10},{10,12},{12... | collective-permute-start | bytes 688136 | tf_op jit(solution)/shard_map/ppermute | solution.py:22
  8.1 26.3 %all-to-all-start = ((bf16[16,128,256]{2,1,0:T(8,128)(2,1)}), bf16[16,128,256]{2,1,0:T(8,128)(2,1)S(1)}, u32[]{:S(2)}, u32[]{:S(2)}) async-start(bf16[16,128,256]{2,1,0:T(8,128)(2,1)} %get-tuple-element.10), calls=%async_computation | async-start | bytes 2097152 | tf_op jit(solution)/shard_map/all_to_all | solution.py:153
  15.2 12.8 %collective-permute-start.15 = (bf16[128,896]{1,0:T(8,128)(2,1)S(1)}, bf16[128,896]{1,0:T(8,128)(2,1)S(1)}, u32[]{:S(2)}, u32[]{:S(2)}) collective-permute-start(bf16[128,896]{1,0:T(8,128)(2,1)S(1)} %copy-done.2), channel_id=1, source_target_pairs={{0,1},{1,0},{2,3},{3,2},{4,5},{5,4},{6,7},{7,6},{8,9},{9,8},{10,11... | collective-permute-start | bytes 688136 | tf_op jit(solution)/shard_map/ppermute | solution.py:22
  28.0 1.5 %collective-permute-start.17 = (bf16[128,896]{1,0:T(8,128)(2,1)S(1)}, bf16[128,896]{1,0:T(8,128)(2,1)S(1)}, u32[]{:S(2)}, u32[]{:S(2)}) collective-permute-start(bf16[128,896]{1,0:T(8,128)(2,1)S(1)} %gate.4.refs_2_), channel_id=1, source_target_pairs={{0,1},{1,0},{2,3},{3,2},{4,5},{5,4},{6,7},{7,6},{8,9},{9,8},{10,11... | collective-permute-start | bytes 688136 | tf_op jit(solution)/shard_map/ppermute | solution.py:22
  29.5 1.9 %copy-start = (bf16[896,1792]{1,0:T(8,128)(2,1)S(1)}, bf16[896,1792]{1,0:T(8,128)(2,1)}, u32[]{:S(2)}) copy-start(bf16[896,1792]{1,0:T(8,128)(2,1)} %refs_4_.3) | copy-start | bytes 9633796
  34.4 34.7 %all-to-all-start.2 = ((bf16[16,112,512]{2,1,0:T(8,128)(2,1)}), bf16[16,112,512]{2,1,0:T(8,128)(2,1)S(1)}, u32[]{:S(2)}, u32[]{:S(2)}) async-start(bf16[16,112,512]{2,1,0:T(8,128)(2,1)} %bitcast.18), calls=%async_computation.2 | async-start | bytes 3670016 | tf_op jit(solution)/shard_map/all_to_all | solution.py:188
  41.6 8.3 %collective-permute-start.4 = (f32[128,128]{1,0:T(8,128)S(1)}, f32[128,128]{1,0:T(8,128)S(1)}, u32[]{:S(2)}, u32[]{:S(2)}) collective-permute-start(f32[128,128]{1,0:T(8,128)S(1)} %get-tuple-element.12), channel_id=1, source_target_pairs={{0,128},{128,0},{1,129},{129,1},{2,130},{130,2},{3,131},{131,3},{4... | collective-permute-start | bytes 196616 | tf_op jit(solution)/shard_map/ppermute | solution.py:22
  46.7 9.4 %collective-permute-start.1 = (bf16[128,896]{1,0:T(8,128)(2,1)S(1)}, bf16[128,896]{1,0:T(8,128)(2,1)S(1)}, u32[]{:S(2)}, u32[]{:S(2)}) collective-permute-start(bf16[128,896]{1,0:T(8,128)(2,1)S(1)} %collective-permute-done.refs_0_.refs_1_), channel_id=1, source_target_pairs={{0,1},{1,0},{2,3},{3,2},{4,5},{5,4},{6,7},{7,6},{8,9},{9,8},{10,11... | collective-permute-start | bytes 688136 | tf_op jit(solution)/shard_map/ppermute | solution.py:22
  46.7 9.4 %collective-permute-start.3 = (bf16[128,896]{1,0:T(8,128)(2,1)S(1)}, bf16[128,896]{1,0:T(8,128)(2,1)S(1)}, u32[]{:S(2)}, u32[]{:S(2)}) collective-permute-start(bf16[128,896]{1,0:T(8,128)(2,1)S(1)} %collective-permute-done.2.refs_2_), channel_id=1, source_target_pairs={{0,1},{1,0},{2,3},{3,2},{4,5},{5,4},{6,7},{7,6},{8,9},{9,8},{10,11... | collective-permute-start | bytes 688136 | tf_op jit(solution)/shard_map/ppermute | solution.py:22
  49.9 14.8 %collective-permute-start.5 = (bf16[128,128]{1,0:T(8,128)(2,1)S(1)}, bf16[128,128]{1,0:T(8,128)(2,1)S(1)}, u32[]{:S(2)}, u32[]{:S(2)}) collective-permute-start(bf16[128,128]{1,0:T(8,128)(2,1)S(1)} %multiply_convert_fusion.2.refs_1_), channel_id=1, source_target_pairs={{0,32},{32,64},{64,96},{96,0},{1,33},{33,65},{65,97},{97,1},{2,34}... | collective-permute-start | bytes 98312 | tf_op jit(solution)/shard_map/ppermute | solution.py:22
  51.9 15.1 %collective-permute-start.6 = (bf16[128,128]{1,0:T(8,128)(2,1)S(1)}, bf16[128,128]{1,0:T(8,128)(2,1)S(1)}, u32[]{:S(2)}, u32[]{:S(2)}) collective-permute-start(bf16[128,128]{1,0:T(8,128)(2,1)S(1)} %multiply_convert_fusion.2.refs_1_), channel_id=1, source_target_pairs={{0,64},{32,96},{64,0},{96,32},{1,65},{33,97},{65,1},{97,33},{2,66}... | collective-permute-start | bytes 98312 | tf_op jit(solution)/shard_map/ppermute | solution.py:22
  54.6 12.5 %collective-permute-start.7 = (bf16[128,128]{1,0:T(8,128)(2,1)S(1)}, bf16[128,128]{1,0:T(8,128)(2,1)S(1)}, u32[]{:S(2)}, u32[]{:S(2)}) collective-permute-start(bf16[128,128]{1,0:T(8,128)(2,1)S(1)} %multiply_convert_fusion.2.refs_1_), channel_id=1, source_target_pairs={{0,96},{32,0},{64,32},{96,64},{1,97},{33,1},{65,33},{97,65},{2,98}... | collective-permute-start | bytes 98312 | tf_op jit(solution)/shard_map/ppermute | solution.py:22
  56.0 1.9 %copy-start.1 = (bf16[896,1792]{1,0:T(8,128)(2,1)S(1)}, bf16[896,1792]{1,0:T(8,128)(2,1)}, u32[]{:S(2)}) copy-start(bf16[896,1792]{1,0:T(8,128)(2,1)} %refs_4_.3) | copy-start | bytes 9633796
  70.4 28.7 %all-to-all-start.1 = ((bf16[16,112,512]{2,1,0:T(8,128)(2,1)}), bf16[16,112,512]{2,1,0:T(8,128)(2,1)S(1)}, u32[]{:S(2)}, u32[]{:S(2)}) async-start(bf16[16,112,512]{2,1,0:T(8,128)(2,1)} %bitcast.16), calls=%async_computation.1 | async-start | bytes 3670016 | tf_op jit(solution)/shard_map/all_to_all | solution.py:188
  74.2 13.7 %collective-permute-start.9 = (bf16[4,128,128]{2,1,0:T(8,128)(2,1)S(1)}, bf16[4,128,128]{2,1,0:T(8,128)(2,1)S(1)}, u32[]{:S(2)}, u32[]{:S(2)}) collective-permute-start(bf16[4,128,128]{2,1,0:T(8,128)(2,1)S(1)} %pad_maximum_fusion.refs_1_.refs_4_), channel_id=1, source_target_pairs={{0,2},{2,4},{4,6},{6,0},{1,3},{3,5},{5,7},{7,1},{8,10},{10,12},{12... | collective-permute-start | bytes 393224 | tf_op jit(solution)/shard_map/ppermute | solution.py:22
  74.3 13.6 %collective-permute-start.11 = (bf16[4,128,128]{2,1,0:T(8,128)(2,1)S(1)}, bf16[4,128,128]{2,1,0:T(8,128)(2,1)S(1)}, u32[]{:S(2)}, u32[]{:S(2)}) collective-permute-start(bf16[4,128,128]{2,1,0:T(8,128)(2,1)S(1)} %pad_maximum_fusion.refs_1_.refs_4_), channel_id=1, source_target_pairs={{0,4},{2,6},{4,0},{6,2},{1,5},{3,7},{5,1},{7,3},{8,12},{10,14},{12... | collective-permute-start | bytes 393224 | tf_op jit(solution)/shard_map/ppermute | solution.py:22
  75.4 13.1 %collective-permute-start.13 = (bf16[4,128,128]{2,1,0:T(8,128)(2,1)S(1)}, bf16[4,128,128]{2,1,0:T(8,128)(2,1)S(1)}, u32[]{:S(2)}, u32[]{:S(2)}) collective-permute-start(bf16[4,128,128]{2,1,0:T(8,128)(2,1)S(1)} %pad_maximum_fusion.refs_1_.refs_4_), channel_id=1, source_target_pairs={{0,6},{2,0},{4,2},{6,4},{1,7},{3,1},{5,3},{7,5},{8,14},{10,8},{12,... | collective-permute-start | bytes 393224 | tf_op jit(solution)/shard_map/ppermute | solution.py:22
  78.1 10.4 %collective-permute-start.18 = (bf16[112,512]{1,0:T(8,128)(2,1)S(1)}, bf16[112,512]{1,0:T(8,128)(2,1)S(1)}, u32[]{:S(2)}, u32[]{:S(2)}) collective-permute-start(bf16[112,512]{1,0:T(8,128)(2,1)S(1)} %convert_element_type.29), channel_id=1, source_target_pairs={{0,128},{128,0},{1,129},{129,1},{2,130},{130,2},{3,131},{131,3},{4... | collective-permute-start | bytes 344072 | tf_op jit(solution)/shard_map/ppermute | solution.py:22
  83.5 5.0 %collective-permute-start.8 = (bf16[4,128,128]{2,1,0:T(8,128)(2,1)S(1)}, bf16[4,128,128]{2,1,0:T(8,128)(2,1)S(1)}, u32[]{:S(2)}, u32[]{:S(2)}) collective-permute-start(bf16[4,128,128]{2,1,0:T(8,128)(2,1)S(1)} %pad_maximum_fusion.refs_1_.refs_4_), channel_id=1, source_target_pairs={{0,1},{1,0},{2,3},{3,2},{4,5},{5,4},{6,7},{7,6},{8,9},{9,8},{10,11... | collective-permute-start | bytes 393224 | tf_op jit(solution)/shard_map/ppermute | solution.py:22
  87.9 1.3 %collective-permute-start.10 = (bf16[4,128,128]{2,1,0:T(8,128)(2,1)S(1)}, bf16[4,128,128]{2,1,0:T(8,128)(2,1)S(1)}, u32[]{:S(2)}, u32[]{:S(2)}) collective-permute-start(bf16[4,128,128]{2,1,0:T(8,128)(2,1)S(1)} %collective-permute-done.9.refs_3_.refs_6_), channel_id=1, source_target_pairs={{0,1},{1,0},{2,3},{3,2},{4,5},{5,4},{6,7},{7,6},{8,9},{9,8},{10,11... | collective-permute-start | bytes 393224 | tf_op jit(solution)/shard_map/ppermute | solution.py:22
  87.9 1.5 %collective-permute-start.12 = (bf16[4,128,128]{2,1,0:T(8,128)(2,1)S(1)}, bf16[4,128,128]{2,1,0:T(8,128)(2,1)S(1)}, u32[]{:S(2)}, u32[]{:S(2)}) collective-permute-start(bf16[4,128,128]{2,1,0:T(8,128)(2,1)S(1)} %collective-permute-done.11.refs_5_.refs_4_), channel_id=1, source_target_pairs={{0,1},{1,0},{2,3},{3,2},{4,5},{5,4},{6,7},{7,6},{8,9},{9,8},{10,11... | collective-permute-start | bytes 393224 | tf_op jit(solution)/shard_map/ppermute | solution.py:22
  88.4 1.3 %collective-permute-start.14 = (bf16[4,128,128]{2,1,0:T(8,128)(2,1)S(1)}, bf16[4,128,128]{2,1,0:T(8,128)(2,1)S(1)}, u32[]{:S(2)}, u32[]{:S(2)}) collective-permute-start(bf16[4,128,128]{2,1,0:T(8,128)(2,1)S(1)} %collective-permute-done.13.refs_7_.refs_6_), channel_id=1, source_target_pairs={{0,1},{1,0},{2,3},{3,2},{4,5},{5,4},{6,7},{7,6},{8,9},{9,8},{10,11... | collective-permute-start | bytes 393224 | tf_op jit(solution)/shard_map/ppermute | solution.py:22
  99.4 8.8 %collective-permute-start.19 = (bf16[112,512]{1,0:T(8,128)(2,1)S(1)}, bf16[112,512]{1,0:T(8,128)(2,1)S(1)}, u32[]{:S(2)}, u32[]{:S(2)}) collective-permute-start(bf16[112,512]{1,0:T(8,128)(2,1)S(1)} %convert_element_type.33), channel_id=1, source_target_pairs={{0,128},{128,0},{1,129},{129,1},{2,130},{130,2},{3,131},{131,3},{4... | collective-permute-start | bytes 344072 | tf_op jit(solution)/shard_map/ppermute | solution.py:22
  104.3 8.5 %collective-permute-start.23 = (bf16[112,512]{1,0:T(8,128)(2,1)S(1)}, bf16[112,512]{1,0:T(8,128)(2,1)S(1)}, u32[]{:S(2)}, u32[]{:S(2)}) collective-permute-start(bf16[112,512]{1,0:T(8,128)(2,1)S(1)} %multiply_convert_fusion.1.refs_9_.refs_0_), channel_id=1, source_target_pairs={{0,8},{8,16},{16,24},{24,0},{1,9},{9,17},{17,25},{25,1},{2,10},{10... | collective-permute-start | bytes 344072 | tf_op jit(solution)/shard_map/ppermute | solution.py:22
  104.9 8.4 %collective-permute-start.24 = (bf16[112,512]{1,0:T(8,128)(2,1)S(1)}, bf16[112,512]{1,0:T(8,128)(2,1)S(1)}, u32[]{:S(2)}, u32[]{:S(2)}) collective-permute-start(bf16[112,512]{1,0:T(8,128)(2,1)S(1)} %multiply_convert_fusion.1.refs_9_.refs_0_), channel_id=1, source_target_pairs={{0,16},{8,24},{16,0},{24,8},{1,17},{9,25},{17,1},{25,9},{2,18},{10... | collective-permute-start | bytes 344072 | tf_op jit(solution)/shard_map/ppermute | solution.py:22
  106.4 6.8 %collective-permute-start.25 = (bf16[112,512]{1,0:T(8,128)(2,1)S(1)}, bf16[112,512]{1,0:T(8,128)(2,1)S(1)}, u32[]{:S(2)}, u32[]{:S(2)}) collective-permute-start(bf16[112,512]{1,0:T(8,128)(2,1)S(1)} %multiply_convert_fusion.1.refs_9_.refs_0_), channel_id=1, source_target_pairs={{0,24},{8,0},{16,8},{24,16},{1,25},{9,1},{17,9},{25,17},{2,26},{10... | collective-permute-start | bytes 344072 | tf_op jit(solution)/shard_map/ppermute | solution.py:22
  108.2 7.3 %collective-permute-start.20 = (bf16[112,512]{1,0:T(8,128)(2,1)S(1)}, bf16[112,512]{1,0:T(8,128)(2,1)S(1)}, u32[]{:S(2)}, u32[]{:S(2)}) collective-permute-start(bf16[112,512]{1,0:T(8,128)(2,1)S(1)} %multiply_convert_fusion.refs_0_), channel_id=1, source_target_pairs={{0,8},{8,16},{16,24},{24,0},{1,9},{9,17},{17,25},{25,1},{2,10},{10... | collective-permute-start | bytes 344072 | tf_op jit(solution)/shard_map/ppermute | solution.py:22
  108.9 6.6 %collective-permute-start.21 = (bf16[112,512]{1,0:T(8,128)(2,1)S(1)}, bf16[112,512]{1,0:T(8,128)(2,1)S(1)}, u32[]{:S(2)}, u32[]{:S(2)}) collective-permute-start(bf16[112,512]{1,0:T(8,128)(2,1)S(1)} %multiply_convert_fusion.refs_0_), channel_id=1, source_target_pairs={{0,16},{8,24},{16,0},{24,8},{1,17},{9,25},{17,1},{25,9},{2,18},{10... | collective-permute-start | bytes 344072 | tf_op jit(solution)/shard_map/ppermute | solution.py:22
  112.8 4.8 %collective-permute-start.22 = (bf16[112,512]{1,0:T(8,128)(2,1)S(1)}, bf16[112,512]{1,0:T(8,128)(2,1)S(1)}, u32[]{:S(2)}, u32[]{:S(2)}) collective-permute-start(bf16[112,512]{1,0:T(8,128)(2,1)S(1)} %multiply_convert_fusion.refs_0_), channel_id=1, source_target_pairs={{0,24},{8,0},{16,8},{24,16},{1,25},{9,1},{17,9},{25,17},{2,26},{10... | collective-permute-start | bytes 344072 | tf_op jit(solution)/shard_map/ppermute | solution.py:22
  (1 other events, 1.3 us)

commit v11 on v10

--- a/solution.py
+++ b/solution.py
@@ -160,6 +160,7 @@
         in_specs=[SMEM, VMEM],
         out_specs=(VMEM, VMEM),
         compiler_params=PARAMS,
+        cost_estimate=pl.CostEstimate(flops=2*10**10, bytes_accessed=10**6, transcendentals=0),
         name="act_sum",
     )(place, got)
     total = kept + shifted(given, "z_hi", 1)
@@ -232,7 +233,6 @@
 def per_device(hidden, norm_gain, gate_pre, out_grad, grad_basis, act_basis):
     act_parts, up_grad = first_partials(hidden, norm_gain, gate_pre, out_grad, act_basis)
     near, far, farthest = [shifted(up_grad, "z_lo", step) for step in (1, 2, 3)]
-    near = gated(near, [far, farthest], jax.ShapeDtypeStruct)
     near_rows = [up_grad, shifted(up_grad, "core", 1), near, shifted(near, "core", 1)]
     far_rows = [far, shifted(far, "core", 1), farthest, shifted(farthest, "core", 1)]
     act_row = act_squares(act_parts)

time: 134 us -> 123 us (0.918)
  waiting for transfers between devices: 45.8 us -> 34.6 us
  local copies, waits for them, and re-layouts: 5.99 us -> 1.55 us
  Pallas kernels: 12.9 us -> 16.4 us
  starting transfers between devices: 52.4 us -> 53.8 us
    ppermute x26, waiting for transfers between devices: 34.4 us -> 17.3 us  [shifted(): lax.ppermute(value, axis, [(i, (i + step) % size) for i in range(size)])]
    all_to_all x1, waiting for transfers between devices: 0.01 us -> 11.1 us  [act_squares(): got = lax.all_to_all(partials, ('x', 'y'), 0, 0, tiled=True)]
    all_to_all x2, waiting for transfers between devices: 11.4 us -> 6.13 us  [exchanged(): lax.all_to_all(partial.reshape(16, columns // 16, tokens), ('x', 'y'), 0,...]
    unnamed x9 -> x7, local copies, waits for them, and re-layouts: 5.99 us -> 1.55 us
    ppermute x26, starting transfers between devices: 34.6 us -> 37.4 us  [shifted(): lax.ppermute(value, axis, [(i, (i + step) % size) for i in range(size)])]
    pallas_call x2, Pallas kernels: 6.03 us -> 8.03 us  [grad_partials(): pl.pallas_call(lambda *refs: grad_kernel(len(parts), *refs), out_shape=pl...]
    all_to_all x2, starting transfers between devices: 10.8 us -> 9.29 us  [exchanged(): lax.all_to_all(partial.reshape(16, columns // 16, tokens), ('x', 'y'), 0,...]
  transfers between devices with their start and end apart: 29 -> 29, of which waited for: 17 -> 11; matrix products, arithmetic and copies ran while one was open for 1% -> 2% of each run, Pallas kernels for 5% -> 9%
where the time goes in v11:
time: 123 us; the launch traced here: 121 us
  starting transfers between devices  53.8 us (44%)
  waiting for transfers between devices  34.6 us (28%)
  Pallas kernels  16.4 us (13%)
  blocking collectives  12.7 us (10%)
  other arithmetic  2.24 us (2%)
  local copies, waits for them, and re-layouts  1.55 us (1%)
    ppermute x26, starting transfers between devices, shifted(): lax.ppermute(value, axis, [(i, (i + step) % size) for i in range(size)])  37.4 us
    ppermute x26, waiting for transfers between devices, shifted(): lax.ppermute(value, axis, [(i, (i + step) % size) for i in range(size)])  17.3 us
    all_to_all x1, blocking collectives, per_device(): out = lax.all_to_all(out, 'x', 0, 0, tiled=True)  12.7 us
    all_to_all x1, waiting for transfers between devices, act_squares(): got = lax.all_to_all(partials, ('x', 'y'), 0, 0, tiled=True)  11.1 us
    all_to_all x2, starting transfers between devices, exchanged(): lax.all_to_all(partial.reshape(16, columns // 16, tokens), ('x', 'y'), 0,...  9.29 us
    pallas_call x2, Pallas kernels, grad_partials(): pl.pallas_call(lambda *refs: grad_kernel(len(parts), *refs), out_shape=pl...  8.03 us
    all_to_all x1, starting transfers between devices, act_squares(): got = lax.all_to_all(partials, ('x', 'y'), 0, 0, tiled=True)  7.09 us
    all_to_all x2, waiting for transfers between devices, exchanged(): lax.all_to_all(partial.reshape(16, columns // 16, tokens), ('x', 'y'), 0,...  6.13 us
  transfers between devices with their start and end apart: 29, of which 11 were waited for; matrix products, arithmetic and copies ran while one was open for 2% of the time, Pallas kernels for 9%

profile of v11, /device:TPU:64, one launch (start us, length us, event | category | flops | bytes accessed | tf_op | source)
XLA Modules:
  0.0 121.4 jit_solution(13229561536173778187)
XLA Ops:
  0.0 4.8 %first.1 = (bf16[16,128,256]{2,1,0:T(8,128)(2,1)}, bf16[128,896]{1,0:T(8,128)(2,1)}) custom-call(s32[1]{0:T(128)} %bitcast.2.place, f32[1,8192]{1,0:T(1,128)} %bitcast.19, bf16[128,896]{1,0:T(8,128)(2,1)} %gate_at.1, bf16[128,896]{1,0:T(8,128)(2,1)} %grad_at.1, bf16[128,8192]{1,0:T(8,128)(2,1)} %hidden_at.1, bf16[256,4096]{1,0:T(8,128)(2,1)} %basis_at.1), custom_call_target="tpu_custom_call" | custom-call | tf_op jit(solution)/shard_map/first/pallas_call | solution.py:84
  4.8 2.0 %collective-permute-start.16 = (bf16[128,896]{1,0:T(8,128)(2,1)}, bf16[128,896]{1,0:T(8,128)(2,1)}, u32[]{:S(2)}, u32[]{:S(2)}) collective-permute-start(bf16[128,896]{1,0:T(8,128)(2,1)} %get-tuple-element.9.refs_0_), channel_id=1, source_target_pairs={{0,2},{2,4},{4,6},{6,0},{1,3},{3,5},{5,7},{7,1},{8,10},{10,12},{12... | collective-permute-start | bytes 688136 | tf_op jit(solution)/shard_map/ppermute | solution.py:22
  6.8 7.1 %all-to-all-start = ((bf16[16,128,256]{2,1,0:T(8,128)(2,1)}), bf16[16,128,256]{2,1,0:T(8,128)(2,1)}, u32[]{:S(2)}, u32[]{:S(2)}) async-start(bf16[16,128,256]{2,1,0:T(8,128)(2,1)} %get-tuple-element.10), calls=%async_computation | async-start | bytes 2097152 | tf_op jit(solution)/shard_map/all_to_all | solution.py:153
  16.0 4.1 %grad.3 = bf16[1792,512]{1,0:T(8,128)(2,1)} custom-call(bf16[128,896]{1,0:T(8,128)(2,1)} %get-tuple-element.9.refs_0_, bf16[128,896]{1,0:T(8,128)(2,1)S(1)} %collective-permute-done.15.refs_1_, bf16[128,896]{1,0:T(8,128)(2,1)} %collective-permute-done.16.refs_2_, bf16[128,896]{1,0:T(8,128)(2,1)S(1)} %collective-permute-done.17.refs_3_, ...), custom_call_target="tpu_custom_call" | custom-call | flops 8000000000 | bytes 10000000 | tf_op jit(solution)/shard_map/grad/pallas_call | solution.py:126
  20.1 11.1 %all-to-all-done.got = bf16[16,128,256]{2,1,0:T(8,128)(2,1)} async-done(((bf16[16,128,256]{2,1,0:T(8,128)(2,1)}), bf16[16,128,256]{2,1,0:T(8,128)(2,1)}, u32[]{:S(2)}, u32[]{:S(2)}) %all-to-all-start) | async-done | bytes 1048608 | tf_op jit(solution)/shard_map/all_to_all | solution.py:153
  31.3 4.4 %all-to-all-start.2 = ((bf16[16,112,512]{2,1,0:T(8,128)(2,1)}), bf16[16,112,512]{2,1,0:T(8,128)(2,1)}, u32[]{:S(2)}, u32[]{:S(2)}) async-start(bf16[16,112,512]{2,1,0:T(8,128)(2,1)} %bitcast.18), calls=%async_computation.2 | async-start | bytes 3670016 | tf_op jit(solution)/shard_map/all_to_all | solution.py:189
  35.7 1.4 %act_sum.1 = (f32[128,128]{1,0:T(8,128)S(1)}, f32[128,128]{1,0:T(8,128)S(1)}) custom-call(s32[1]{0:T(128)} %bitcast.4.place, bf16[16,128,256]{2,1,0:T(8,128)(2,1)} %all-to-all-done.got), custom_call_target="tpu_custom_call" | custom-call | flops 20000000000 | bytes 1000000 | tf_op jit(solution)/shard_map/act_sum/pallas_call | solution.py:157
  37.0 4.6 %collective-permute-start.4 = (f32[128,128]{1,0:T(8,128)S(1)}, f32[128,128]{1,0:T(8,128)S(1)}, u32[]{:S(2)}, u32[]{:S(2)}) collective-permute-start(f32[128,128]{1,0:T(8,128)S(1)} %get-tuple-element.12), channel_id=1, source_target_pairs={{0,128},{128,0},{1,129},{129,1},{2,130},{130,2},{3,131},{131,3},{4... | collective-permute-start | bytes 196616 | tf_op jit(solution)/shard_map/ppermute | solution.py:22
  42.1 3.4 %collective-permute-done.4 = f32[128,128]{1,0:T(8,128)S(1)} collective-permute-done((f32[128,128]{1,0:T(8,128)S(1)}, f32[128,128]{1,0:T(8,128)S(1)}, u32[]{:S(2)}, u32[]{:S(2)}) %collective-permute-start.4) | collective-permute-done | bytes 65568 | tf_op jit(solution)/shard_map/ppermute | solution.py:22
  45.6 1.8 %collective-permute-start.5 = (bf16[128,128]{1,0:T(8,128)(2,1)S(1)}, bf16[128,128]{1,0:T(8,128)(2,1)S(1)}, u32[]{:S(2)}, u32[]{:S(2)}) collective-permute-start(bf16[128,128]{1,0:T(8,128)(2,1)S(1)} %multiply_convert_fusion.2.refs_1_), channel_id=1, source_target_pairs={{0,32},{32,64},{64,96},{96,0},{1,33},{33,65},{65,97},{97,1},{2,34}... | collective-permute-start | bytes 98312 | tf_op jit(solution)/shard_map/ppermute | solution.py:22
  47.3 2.7 %collective-permute-start.6 = (bf16[128,128]{1,0:T(8,128)(2,1)S(1)}, bf16[128,128]{1,0:T(8,128)(2,1)S(1)}, u32[]{:S(2)}, u32[]{:S(2)}) collective-permute-start(bf16[128,128]{1,0:T(8,128)(2,1)S(1)} %multiply_convert_fusion.2.refs_1_), channel_id=1, source_target_pairs={{0,64},{32,96},{64,0},{96,32},{1,65},{33,97},{65,1},{97,33},{2,66}... | collective-permute-start | bytes 98312 | tf_op jit(solution)/shard_map/ppermute | solution.py:22
  50.1 1.4 %collective-permute-start.7 = (bf16[128,128]{1,0:T(8,128)(2,1)S(1)}, bf16[128,128]{1,0:T(8,128)(2,1)S(1)}, u32[]{:S(2)}, u32[]{:S(2)}) collective-permute-start(bf16[128,128]{1,0:T(8,128)(2,1)S(1)} %multiply_convert_fusion.2.refs_1_), channel_id=1, source_target_pairs={{0,96},{32,0},{64,32},{96,64},{1,97},{33,1},{65,33},{97,65},{2,98}... | collective-permute-start | bytes 98312 | tf_op jit(solution)/shard_map/ppermute | solution.py:22
  51.5 4.0 %grad.2.refs_0_ = bf16[1792,512]{1,0:T(8,128)(2,1)} custom-call(bf16[128,896]{1,0:T(8,128)(2,1)S(1)} %collective-permute-done.refs_0_, bf16[128,896]{1,0:T(8,128)(2,1)S(1)} %collective-permute-done.1.refs_1_, bf16[128,896]{1,0:T(8,128)(2,1)} %collective-permute-done.2.refs_2_, bf16[128,896]{1,0:T(8,128)(2,1)S(1)} %collective-permute-done.3.refs_3_, ...), custom_call_target="tpu_custom_call" | custom-call | tf_op jit(solution)/shard_map/grad/pallas_call | solution.py:126
  56.0 3.5 %collective-permute-done.6.refs_3_ = bf16[128,128]{1,0:T(8,128)(2,1)S(1)} collective-permute-done((bf16[128,128]{1,0:T(8,128)(2,1)S(1)}, bf16[128,128]{1,0:T(8,128)(2,1)S(1)}, u32[]{:S(2)}, u32[]{:S(2)}) %collective-permute-start.6) | collective-permute-done | bytes 32800 | tf_op jit(solution)/shard_map/ppermute | solution.py:22
  60.2 4.9 %all-to-all-start.1 = ((bf16[16,112,512]{2,1,0:T(8,128)(2,1)}), bf16[16,112,512]{2,1,0:T(8,128)(2,1)S(1)}, u32[]{:S(2)}, u32[]{:S(2)}) async-start(bf16[16,112,512]{2,1,0:T(8,128)(2,1)} %bitcast.16), calls=%async_computation.1 | async-start | bytes 3670016 | tf_op jit(solution)/shard_map/all_to_all | solution.py:189
  65.8 1.0 collective-permute-start.11
  66.7 1.0 collective-permute-start.13
  67.8 1.8 %convert_reduce_fusion.1 = f32[112,512]{1,0:T(8,128)S(1)} fusion(bf16[16,112,512]{2,1,0:T(8,128)(2,1)} %all-to-all-done.2), kind=kLoop, calls=%fused_computation.1 | loop fusion | flops 1777664 | bytes 2064384 | tf_op jit(solution)/shard_map/reduce_sum | solution.py:193
  69.6 6.5 %collective-permute-start.18 = (bf16[112,512]{1,0:T(8,128)(2,1)S(1)}, bf16[112,512]{1,0:T(8,128)(2,1)S(1)}, u32[]{:S(2)}, u32[]{:S(2)}) collective-permute-start(bf16[112,512]{1,0:T(8,128)(2,1)S(1)} %convert_element_type.29), channel_id=1, source_target_pairs={{0,128},{128,0},{1,129},{129,1},{2,130},{130,2},{3,131},{131,3},{4... | collective-permute-start | bytes 344072 | tf_op jit(solution)/shard_map/ppermute | solution.py:22
  77.1 4.9 %collective-permute-done.18 = bf16[112,512]{1,0:T(8,128)(2,1)S(1)} collective-permute-done((bf16[112,512]{1,0:T(8,128)(2,1)S(1)}, bf16[112,512]{1,0:T(8,128)(2,1)S(1)}, u32[]{:S(2)}, u32[]{:S(2)}) %collective-permute-start.18) | collective-permute-done | bytes 114720 | tf_op jit(solution)/shard_map/ppermute | solution.py:22
  82.1 6.0 %all-to-all-done.1.refs_0_ = bf16[16,112,512]{2,1,0:T(8,128)(2,1)S(1)} async-done(((bf16[16,112,512]{2,1,0:T(8,128)(2,1)}), bf16[16,112,512]{2,1,0:T(8,128)(2,1)S(1)}, u32[]{:S(2)}, u32[]{:S(2)}) %all-to-all-start.1) | async-done | bytes 1835040 | tf_op jit(solution)/shard_map/all_to_all | solution.py:189
  88.4 5.1 %collective-permute-start.19 = (bf16[112,512]{1,0:T(8,128)(2,1)S(1)}, bf16[112,512]{1,0:T(8,128)(2,1)S(1)}, u32[]{:S(2)}, u32[]{:S(2)}) collective-permute-start(bf16[112,512]{1,0:T(8,128)(2,1)S(1)} %convert_element_type.33), channel_id=1, source_target_pairs={{0,128},{128,0},{1,129},{129,1},{2,130},{130,2},{3,131},{131,3},{4... | collective-permute-start | bytes 344072 | tf_op jit(solution)/shard_map/ppermute | solution.py:22
  93.8 1.4 %collective-permute-start.24 = (bf16[112,512]{1,0:T(8,128)(2,1)S(1)}, bf16[112,512]{1,0:T(8,128)(2,1)S(1)}, u32[]{:S(2)}, u32[]{:S(2)}) collective-permute-start(bf16[112,512]{1,0:T(8,128)(2,1)S(1)} %multiply_convert_fusion.1.refs_9_.refs_0_), channel_id=1, source_target_pairs={{0,16},{8,24},{16,0},{24,8},{1,17},{9,25},{17,1},{25,9},{2,18},{10... | collective-permute-start | bytes 344072 | tf_op jit(solution)/shard_map/ppermute | solution.py:22
  95.2 1.9 %collective-permute-start.25 = (bf16[112,512]{1,0:T(8,128)(2,1)S(1)}, bf16[112,512]{1,0:T(8,128)(2,1)S(1)}, u32[]{:S(2)}, u32[]{:S(2)}) collective-permute-start(bf16[112,512]{1,0:T(8,128)(2,1)S(1)} %multiply_convert_fusion.1.refs_9_.refs_0_), channel_id=1, source_target_pairs={{0,24},{8,0},{16,8},{24,16},{1,25},{9,1},{17,9},{25,17},{2,26},{10... | collective-permute-start | bytes 344072 | tf_op jit(solution)/shard_map/ppermute | solution.py:22
  97.1 1.4 %collective-permute-done.19 = bf16[112,512]{1,0:T(8,128)(2,1)S(1)} collective-permute-done((bf16[112,512]{1,0:T(8,128)(2,1)S(1)}, bf16[112,512]{1,0:T(8,128)(2,1)S(1)}, u32[]{:S(2)}, u32[]{:S(2)}) %collective-permute-start.19) | collective-permute-done | bytes 114720 | tf_op jit(solution)/shard_map/ppermute | solution.py:22
  99.0 1.3 %collective-permute-start.21 = (bf16[112,512]{1,0:T(8,128)(2,1)S(1)}, bf16[112,512]{1,0:T(8,128)(2,1)S(1)}, u32[]{:S(2)}, u32[]{:S(2)}) collective-permute-start(bf16[112,512]{1,0:T(8,128)(2,1)S(1)} %multiply_convert_fusion.refs_0_), channel_id=1, source_target_pairs={{0,16},{8,24},{16,0},{24,8},{1,17},{9,25},{17,1},{25,9},{2,18},{10... | collective-permute-start | bytes 344072 | tf_op jit(solution)/shard_map/ppermute | solution.py:22
  100.7 1.8 %collective-permute-start.22 = (bf16[112,512]{1,0:T(8,128)(2,1)S(1)}, bf16[112,512]{1,0:T(8,128)(2,1)S(1)}, u32[]{:S(2)}, u32[]{:S(2)}) collective-permute-start(bf16[112,512]{1,0:T(8,128)(2,1)S(1)} %multiply_convert_fusion.refs_0_), channel_id=1, source_target_pairs={{0,24},{8,0},{16,8},{24,16},{1,25},{9,1},{17,9},{25,17},{2,26},{10... | collective-permute-start | bytes 344072 | tf_op jit(solution)/shard_map/ppermute | solution.py:22
  102.6 1.1 correct.2.refs_8_
  103.7 2.2 %collective-permute-done.20.refs_1_ = bf16[112,512]{1,0:T(8,128)(2,1)S(1)} collective-permute-done((bf16[112,512]{1,0:T(8,128)(2,1)S(1)}, bf16[112,512]{1,0:T(8,128)(2,1)S(1)}, u32[]{:S(2)}, u32[]{:S(2)}) %collective-permute-start.20) | collective-permute-done | bytes 114720 | tf_op jit(solution)/shard_map/ppermute | solution.py:22
  106.7 1.1 correct.3
  107.8 12.7 %all_to_all.20 = f32[4,448,128]{2,1,0:T(8,128)S(1)} all-to-all(f32[4,448,128]{2,1,0:T(8,128)S(1)} %correct.3), channel_id=1, replica_groups=mesh['z_hi'=2,'x'=4,'y'=4,'z_lo'=4,'core'=2] {'x'}, dimensions={0} | all-to-all | bytes 1835008 | tf_op jit(solution)/shard_map/all_to_all | solution.py:251
  120.5 0.9 copy.12
  (51 shorter events, 8.1 us)
Async XLA Ops:
  0.0 16.0 %copy-start = (bf16[896,1792]{1,0:T(8,128)(2,1)S(1)}, bf16[896,1792]{1,0:T(8,128)(2,1)}, u32[]{:S(2)}) copy-start(bf16[896,1792]{1,0:T(8,128)(2,1)} %refs_4_.3) | copy-start | bytes 9633796
  4.8 9.2 %collective-permute-start.16 = (bf16[128,896]{1,0:T(8,128)(2,1)}, bf16[128,896]{1,0:T(8,128)(2,1)}, u32[]{:S(2)}, u32[]{:S(2)}) collective-permute-start(bf16[128,896]{1,0:T(8,128)(2,1)} %get-tuple-element.9.refs_0_), channel_id=1, source_target_pairs={{0,2},{2,4},{4,6},{6,0},{1,3},{3,5},{5,7},{7,1},{8,10},{10,12},{12... | collective-permute-start | bytes 688136 | tf_op jit(solution)/shard_map/ppermute | solution.py:22
  6.8 24.4 %all-to-all-start = ((bf16[16,128,256]{2,1,0:T(8,128)(2,1)}), bf16[16,128,256]{2,1,0:T(8,128)(2,1)}, u32[]{:S(2)}, u32[]{:S(2)}) async-start(bf16[16,128,256]{2,1,0:T(8,128)(2,1)} %get-tuple-element.10), calls=%async_computation | async-start | bytes 2097152 | tf_op jit(solution)/shard_map/all_to_all | solution.py:153
  13.9 2.1 %collective-permute-start.15 = (bf16[128,896]{1,0:T(8,128)(2,1)}, bf16[128,896]{1,0:T(8,128)(2,1)S(1)}, u32[]{:S(2)}, u32[]{:S(2)}) collective-permute-start(bf16[128,896]{1,0:T(8,128)(2,1)} %get-tuple-element.9.refs_0_), channel_id=1, source_target_pairs={{0,1},{1,0},{2,3},{3,2},{4,5},{5,4},{6,7},{7,6},{8,9},{9,8},{10,11... | collective-permute-start | bytes 688136 | tf_op jit(solution)/shard_map/ppermute | solution.py:22
  14.0 2.0 %collective-permute-start.17 = (bf16[128,896]{1,0:T(8,128)(2,1)}, bf16[128,896]{1,0:T(8,128)(2,1)S(1)}, u32[]{:S(2)}, u32[]{:S(2)}) collective-permute-start(bf16[128,896]{1,0:T(8,128)(2,1)} %collective-permute-done.16.refs_2_), channel_id=1, source_target_pairs={{0,1},{1,0},{2,3},{3,2},{4,5},{5,4},{6,7},{7,6},{8,9},{9,8},{10,11... | collective-permute-start | bytes 688136 | tf_op jit(solution)/shard_map/ppermute | solution.py:22
  14.5 27.1 %collective-permute-start = (bf16[128,896]{1,0:T(8,128)(2,1)}, bf16[128,896]{1,0:T(8,128)(2,1)S(1)}, u32[]{:S(2)}, u32[]{:S(2)}) collective-permute-start(bf16[128,896]{1,0:T(8,128)(2,1)} %get-tuple-element.9.refs_0_), channel_id=1, source_target_pairs={{0,4},{2,6},{4,0},{6,2},{1,5},{3,7},{5,1},{7,3},{8,12},{10,14},{12... | collective-permute-start | bytes 688136 | tf_op jit(solution)/shard_map/ppermute | solution.py:22
  15.1 26.5 %collective-permute-start.2 = (bf16[128,896]{1,0:T(8,128)(2,1)}, bf16[128,896]{1,0:T(8,128)(2,1)}, u32[]{:S(2)}, u32[]{:S(2)}) collective-permute-start(bf16[128,896]{1,0:T(8,128)(2,1)} %get-tuple-element.9.refs_0_), channel_id=1, source_target_pairs={{0,6},{2,0},{4,2},{6,4},{1,7},{3,1},{5,3},{7,5},{8,14},{10,8},{12,... | collective-permute-start | bytes 688136 | tf_op jit(solution)/shard_map/ppermute | solution.py:22
  31.3 29.0 %all-to-all-start.2 = ((bf16[16,112,512]{2,1,0:T(8,128)(2,1)}), bf16[16,112,512]{2,1,0:T(8,128)(2,1)}, u32[]{:S(2)}, u32[]{:S(2)}) async-start(bf16[16,112,512]{2,1,0:T(8,128)(2,1)} %bitcast.18), calls=%async_computation.2 | async-start | bytes 3670016 | tf_op jit(solution)/shard_map/all_to_all | solution.py:189
  37.0 8.5 %collective-permute-start.4 = (f32[128,128]{1,0:T(8,128)S(1)}, f32[128,128]{1,0:T(8,128)S(1)}, u32[]{:S(2)}, u32[]{:S(2)}) collective-permute-start(f32[128,128]{1,0:T(8,128)S(1)} %get-tuple-element.12), channel_id=1, source_target_pairs={{0,128},{128,0},{1,129},{129,1},{2,130},{130,2},{3,131},{131,3},{4... | collective-permute-start | bytes 196616 | tf_op jit(solution)/shard_map/ppermute | solution.py:22
  41.6 9.9 %collective-permute-start.1 = (bf16[128,896]{1,0:T(8,128)(2,1)S(1)}, bf16[128,896]{1,0:T(8,128)(2,1)S(1)}, u32[]{:S(2)}, u32[]{:S(2)}) collective-permute-start(bf16[128,896]{1,0:T(8,128)(2,1)S(1)} %collective-permute-done.refs_0_), channel_id=1, source_target_pairs={{0,1},{1,0},{2,3},{3,2},{4,5},{5,4},{6,7},{7,6},{8,9},{9,8},{10,11... | collective-permute-start | bytes 688136 | tf_op jit(solution)/shard_map/ppermute | solution.py:22
  41.6 9.9 %collective-permute-start.3 = (bf16[128,896]{1,0:T(8,128)(2,1)}, bf16[128,896]{1,0:T(8,128)(2,1)S(1)}, u32[]{:S(2)}, u32[]{:S(2)}) collective-permute-start(bf16[128,896]{1,0:T(8,128)(2,1)} %collective-permute-done.2.refs_2_), channel_id=1, source_target_pairs={{0,1},{1,0},{2,3},{3,2},{4,5},{5,4},{6,7},{7,6},{8,9},{9,8},{10,11... | collective-permute-start | bytes 688136 | tf_op jit(solution)/shard_map/ppermute | solution.py:22
  45.6 10.4 %collective-permute-start.5 = (bf16[128,128]{1,0:T(8,128)(2,1)S(1)}, bf16[128,128]{1,0:T(8,128)(2,1)S(1)}, u32[]{:S(2)}, u32[]{:S(2)}) collective-permute-start(bf16[128,128]{1,0:T(8,128)(2,1)S(1)} %multiply_convert_fusion.2.refs_1_), channel_id=1, source_target_pairs={{0,32},{32,64},{64,96},{96,0},{1,33},{33,65},{65,97},{97,1},{2,34}... | collective-permute-start | bytes 98312 | tf_op jit(solution)/shard_map/ppermute | solution.py:22
  47.3 12.1 %collective-permute-start.6 = (bf16[128,128]{1,0:T(8,128)(2,1)S(1)}, bf16[128,128]{1,0:T(8,128)(2,1)S(1)}, u32[]{:S(2)}, u32[]{:S(2)}) collective-permute-start(bf16[128,128]{1,0:T(8,128)(2,1)S(1)} %multiply_convert_fusion.2.refs_1_), channel_id=1, source_target_pairs={{0,64},{32,96},{64,0},{96,32},{1,65},{33,97},{65,1},{97,33},{2,66}... | collective-permute-start | bytes 98312 | tf_op jit(solution)/shard_map/ppermute | solution.py:22
  50.1 9.4 %collective-permute-start.7 = (bf16[128,128]{1,0:T(8,128)(2,1)S(1)}, bf16[128,128]{1,0:T(8,128)(2,1)S(1)}, u32[]{:S(2)}, u32[]{:S(2)}) collective-permute-start(bf16[128,128]{1,0:T(8,128)(2,1)S(1)} %multiply_convert_fusion.2.refs_1_), channel_id=1, source_target_pairs={{0,96},{32,0},{64,32},{96,64},{1,97},{33,1},{65,33},{97,65},{2,98}... | collective-permute-start | bytes 98312 | tf_op jit(solution)/shard_map/ppermute | solution.py:22
  59.5 0.6 copy-start.1
  60.2 4.9 %copy-start.2 = (bf16[128,128]{1,0:T(8,128)(2,1)S(1)}, bf16[128,128]{1,0:T(8,128)(2,1)}, u32[]{:S(2)}) copy-start(bf16[128,128]{1,0:T(8,128)(2,1)} %copy-done.1) | copy-start | bytes 98308
  60.2 27.9 %all-to-all-start.1 = ((bf16[16,112,512]{2,1,0:T(8,128)(2,1)}), bf16[16,112,512]{2,1,0:T(8,128)(2,1)S(1)}, u32[]{:S(2)}, u32[]{:S(2)}) async-start(bf16[16,112,512]{2,1,0:T(8,128)(2,1)} %bitcast.16), calls=%async_computation.1 | async-start | bytes 3670016 | tf_op jit(solution)/shard_map/all_to_all | solution.py:189
  65.1 10.9 %collective-permute-start.9 = (bf16[4,128,128]{2,1,0:T(8,128)(2,1)S(1)}, bf16[4,128,128]{2,1,0:T(8,128)(2,1)S(1)}, u32[]{:S(2)}, u32[]{:S(2)}) collective-permute-start(bf16[4,128,128]{2,1,0:T(8,128)(2,1)S(1)} %pad_maximum_fusion.refs_1_.refs_4_), channel_id=1, source_target_pairs={{0,2},{2,4},{4,6},{6,0},{1,3},{3,5},{5,7},{7,1},{8,10},{10,12},{12... | collective-permute-start | bytes 393224 | tf_op jit(solution)/shard_map/ppermute | solution.py:22
  65.8 10.8 %collective-permute-start.11 = (bf16[4,128,128]{2,1,0:T(8,128)(2,1)S(1)}, bf16[4,128,128]{2,1,0:T(8,128)(2,1)S(1)}, u32[]{:S(2)}, u32[]{:S(2)}) collective-permute-start(bf16[4,128,128]{2,1,0:T(8,128)(2,1)S(1)} %pad_maximum_fusion.refs_1_.refs_4_), channel_id=1, source_target_pairs={{0,4},{2,6},{4,0},{6,2},{1,5},{3,7},{5,1},{7,3},{8,12},{10,14},{12... | collective-permute-start | bytes 393224 | tf_op jit(solution)/shard_map/ppermute | solution.py:22
  66.7 9.9 %collective-permute-start.13 = (bf16[4,128,128]{2,1,0:T(8,128)(2,1)S(1)}, bf16[4,128,128]{2,1,0:T(8,128)(2,1)S(1)}, u32[]{:S(2)}, u32[]{:S(2)}) collective-permute-start(bf16[4,128,128]{2,1,0:T(8,128)(2,1)S(1)} %pad_maximum_fusion.refs_1_.refs_4_), channel_id=1, source_target_pairs={{0,6},{2,0},{4,2},{6,4},{1,7},{3,1},{5,3},{7,5},{8,14},{10,8},{12,... | collective-permute-start | bytes 393224 | tf_op jit(solution)/shard_map/ppermute | solution.py:22
  69.6 12.5 %collective-permute-start.18 = (bf16[112,512]{1,0:T(8,128)(2,1)S(1)}, bf16[112,512]{1,0:T(8,128)(2,1)S(1)}, u32[]{:S(2)}, u32[]{:S(2)}) collective-permute-start(bf16[112,512]{1,0:T(8,128)(2,1)S(1)} %convert_element_type.29), channel_id=1, source_target_pairs={{0,128},{128,0},{1,129},{129,1},{2,130},{130,2},{3,131},{131,3},{4... | collective-permute-start | bytes 344072 | tf_op jit(solution)/shard_map/ppermute | solution.py:22
  76.1 6.0 %collective-permute-start.8 = (bf16[4,128,128]{2,1,0:T(8,128)(2,1)S(1)}, bf16[4,128,128]{2,1,0:T(8,128)(2,1)S(1)}, u32[]{:S(2)}, u32[]{:S(2)}) collective-permute-start(bf16[4,128,128]{2,1,0:T(8,128)(2,1)S(1)} %pad_maximum_fusion.refs_1_.refs_4_), channel_id=1, source_target_pairs={{0,1},{1,0},{2,3},{3,2},{4,5},{5,4},{6,7},{7,6},{8,9},{9,8},{10,11... | collective-permute-start | bytes 393224 | tf_op jit(solution)/shard_map/ppermute | solution.py:22
  76.1 6.0 %collective-permute-start.10 = (bf16[4,128,128]{2,1,0:T(8,128)(2,1)S(1)}, bf16[4,128,128]{2,1,0:T(8,128)(2,1)S(1)}, u32[]{:S(2)}, u32[]{:S(2)}) collective-permute-start(bf16[4,128,128]{2,1,0:T(8,128)(2,1)S(1)} %collective-permute-done.9.refs_3_.refs_6_), channel_id=1, source_target_pairs={{0,1},{1,0},{2,3},{3,2},{4,5},{5,4},{6,7},{7,6},{8,9},{9,8},{10,11... | collective-permute-start | bytes 393224 | tf_op jit(solution)/shard_map/ppermute | solution.py:22
  76.6 5.5 %collective-permute-start.12 = (bf16[4,128,128]{2,1,0:T(8,128)(2,1)S(1)}, bf16[4,128,128]{2,1,0:T(8,128)(2,1)S(1)}, u32[]{:S(2)}, u32[]{:S(2)}) collective-permute-start(bf16[4,128,128]{2,1,0:T(8,128)(2,1)S(1)} %collective-permute-done.11.refs_5_.refs_4_), channel_id=1, source_target_pairs={{0,1},{1,0},{2,3},{3,2},{4,5},{5,4},{6,7},{7,6},{8,9},{9,8},{10,11... | collective-permute-start | bytes 393224 | tf_op jit(solution)/shard_map/ppermute | solution.py:22
  76.7 5.4 %collective-permute-start.14 = (bf16[4,128,128]{2,1,0:T(8,128)(2,1)S(1)}, bf16[4,128,128]{2,1,0:T(8,128)(2,1)S(1)}, u32[]{:S(2)}, u32[]{:S(2)}) collective-permute-start(bf16[4,128,128]{2,1,0:T(8,128)(2,1)S(1)} %collective-permute-done.13.refs_7_.refs_6_), channel_id=1, source_target_pairs={{0,1},{1,0},{2,3},{3,2},{4,5},{5,4},{6,7},{7,6},{8,9},{9,8},{10,11... | collective-permute-start | bytes 393224 | tf_op jit(solution)/shard_map/ppermute | solution.py:22
  88.4 10.1 %collective-permute-start.19 = (bf16[112,512]{1,0:T(8,128)(2,1)S(1)}, bf16[112,512]{1,0:T(8,128)(2,1)S(1)}, u32[]{:S(2)}, u32[]{:S(2)}) collective-permute-start(bf16[112,512]{1,0:T(8,128)(2,1)S(1)} %convert_element_type.33), channel_id=1, source_target_pairs={{0,128},{128,0},{1,129},{129,1},{2,130},{130,2},{3,131},{131,3},{4... | collective-permute-start | bytes 344072 | tf_op jit(solution)/shard_map/ppermute | solution.py:22
  93.5 7.2 %collective-permute-start.23 = (bf16[112,512]{1,0:T(8,128)(2,1)S(1)}, bf16[112,512]{1,0:T(8,128)(2,1)S(1)}, u32[]{:S(2)}, u32[]{:S(2)}) collective-permute-start(bf16[112,512]{1,0:T(8,128)(2,1)S(1)} %multiply_convert_fusion.1.refs_9_.refs_0_), channel_id=1, source_target_pairs={{0,8},{8,16},{16,24},{24,0},{1,9},{9,17},{17,25},{25,1},{2,10},{10... | collective-permute-start | bytes 344072 | tf_op jit(solution)/shard_map/ppermute | solution.py:22
  93.8 8.8 %collective-permute-start.24 = (bf16[112,512]{1,0:T(8,128)(2,1)S(1)}, bf16[112,512]{1,0:T(8,128)(2,1)S(1)}, u32[]{:S(2)}, u32[]{:S(2)}) collective-permute-start(bf16[112,512]{1,0:T(8,128)(2,1)S(1)} %multiply_convert_fusion.1.refs_9_.refs_0_), channel_id=1, source_target_pairs={{0,16},{8,24},{16,0},{24,8},{1,17},{9,25},{17,1},{25,9},{2,18},{10... | collective-permute-start | bytes 344072 | tf_op jit(solution)/shard_map/ppermute | solution.py:22
  95.2 7.5 %collective-permute-start.25 = (bf16[112,512]{1,0:T(8,128)(2,1)S(1)}, bf16[112,512]{1,0:T(8,128)(2,1)S(1)}, u32[]{:S(2)}, u32[]{:S(2)}) collective-permute-start(bf16[112,512]{1,0:T(8,128)(2,1)S(1)} %multiply_convert_fusion.1.refs_9_.refs_0_), channel_id=1, source_target_pairs={{0,24},{8,0},{16,8},{24,16},{1,25},{9,1},{17,9},{25,17},{2,26},{10... | collective-permute-start | bytes 344072 | tf_op jit(solution)/shard_map/ppermute | solution.py:22
  98.5 7.3 %collective-permute-start.20 = (bf16[112,512]{1,0:T(8,128)(2,1)S(1)}, bf16[112,512]{1,0:T(8,128)(2,1)S(1)}, u32[]{:S(2)}, u32[]{:S(2)}) collective-permute-start(bf16[112,512]{1,0:T(8,128)(2,1)S(1)} %multiply_convert_fusion.refs_0_), channel_id=1, source_target_pairs={{0,8},{8,16},{16,24},{24,0},{1,9},{9,17},{17,25},{25,1},{2,10},{10... | collective-permute-start | bytes 344072 | tf_op jit(solution)/shard_map/ppermute | solution.py:22
  99.0 6.8 %collective-permute-start.21 = (bf16[112,512]{1,0:T(8,128)(2,1)S(1)}, bf16[112,512]{1,0:T(8,128)(2,1)S(1)}, u32[]{:S(2)}, u32[]{:S(2)}) collective-permute-start(bf16[112,512]{1,0:T(8,128)(2,1)S(1)} %multiply_convert_fusion.refs_0_), channel_id=1, source_target_pairs={{0,16},{8,24},{16,0},{24,8},{1,17},{9,25},{17,1},{25,9},{2,18},{10... | collective-permute-start | bytes 344072 | tf_op jit(solution)/shard_map/ppermute | solution.py:22
  100.7 6.0 %collective-permute-start.22 = (bf16[112,512]{1,0:T(8,128)(2,1)S(1)}, bf16[112,512]{1,0:T(8,128)(2,1)S(1)}, u32[]{:S(2)}, u32[]{:S(2)}) collective-permute-start(bf16[112,512]{1,0:T(8,128)(2,1)S(1)} %multiply_convert_fusion.refs_0_), channel_id=1, source_target_pairs={{0,24},{8,0},{16,8},{24,16},{1,25},{9,1},{17,9},{25,17},{2,26},{10... | collective-permute-start | bytes 344072 | tf_op jit(solution)/shard_map/ppermute | solution.py:22

commit v12 on v11

--- a/solution.py
+++ b/solution.py
@@ -26,25 +26,20 @@
                  gate, grad, hidden, basis, out, up, sems):
     tokens, features = hidden.shape
     depth = basis.shape[0]
-    strip = tokens // 4
-    load_gate = pltpu.make_async_copy(gate_at, gate, sems.at[9])
-    load_grad = pltpu.make_async_copy(grad_at, grad, sems.at[10])
+    strip = tokens // 2
+    quarter = depth // 4
     loads = [
         pltpu.make_async_copy(hidden_at.at[here], hidden.at[here], sems.at[i])
         for i, here in enumerate(pl.ds(at, strip) for at in range(0, tokens, strip))
     ]
-    load_basis = pltpu.make_async_copy(basis_at, basis, sems.at[4])
-    for load in (load_gate, load_grad, *loads, load_basis):
+    basis_loads = [
+        pltpu.make_async_copy(basis_at.at[here], basis.at[here], sems.at[2 + i])
+        for i, here in enumerate(pl.ds(at, quarter) for at in range(0, depth, quarter))
+    ]
+    load_gate = pltpu.make_async_copy(gate_at, gate, sems.at[10])
+    load_grad = pltpu.make_async_copy(grad_at, grad, sems.at[11])
+    for load in (*loads, *basis_loads, load_gate, load_grad):
         load.start()
-    load_gate.wait()
-    load_grad.wait()
-    for at in range(0, tokens, 32):
-        here = slice(at, at + 32)
-        wide = gate[here, :].astype(jnp.float32)
-        wide = grad[here, :].astype(jnp.float32) * (wide / (1.0 + jnp.exp(-wide)))
-        up[here, :] = wide.astype(jnp.bfloat16)
-    store_up = pltpu.make_async_copy(up, up_at, sems.at[11])
-    store_up.start()
     stats = []
     for i, load in enumerate(loads):
         load.wait()
@@ -57,9 +52,10 @@
     mine = pl.ds(pl.multiple_of(place[0] * depth, depth), depth)
     scaled = hidden[:, mine].astype(jnp.float32) * lax.rsqrt(stat + 1e-05)
     normed = (scaled * gain[:, mine]).astype(jnp.bfloat16)
-    load_basis.wait()
+    for load in basis_loads:
+        load.wait()
     block = basis.shape[1] // 32
-    stores = [store_up]
+    stores = []
     for x in range(4):
         for z_hi in range(2):
             at = (z_hi * 16 + x * 4) * block
@@ -71,8 +67,17 @@
                 to = slice(z_hi * block, (z_hi + 1) * block)
                 out[x * 4 + y, :, to] = here.astype(jnp.bfloat16)
         here = pl.ds(x * 4, 4)
-        stores.append(pltpu.make_async_copy(out.at[here], out_at.at[here], sems.at[5 + x]))
+        stores.append(pltpu.make_async_copy(out.at[here], out_at.at[here], sems.at[6 + x]))
         stores[-1].start()
+    load_gate.wait()
+    load_grad.wait()
+    for at in range(0, tokens, 32):
+        here = slice(at, at + 32)
+        wide = gate[here, :].astype(jnp.float32)
+        wide = grad[here, :].astype(jnp.float32) * (wide / (1.0 + jnp.exp(-wide)))
+        up[here, :] = wide.astype(jnp.bfloat16)
+    stores.append(pltpu.make_async_copy(up, up_at, sems.at[12]))
+    stores[-1].start()
     for store in stores:
         store.wait()
 
@@ -93,7 +98,7 @@
             pltpu.VMEM(act_basis.shape, jnp.bfloat16),
             pltpu.VMEM(shape, jnp.bfloat16),
             pltpu.VMEM(out_grad.shape, jnp.bfloat16),
-            pltpu.SemaphoreType.DMA((12,)),
+            pltpu.SemaphoreType.DMA((13,)),
         ],
         compiler_params=WHOLE,
         name="first",
@@ -160,7 +165,7 @@
         in_specs=[SMEM, VMEM],
         out_specs=(VMEM, VMEM),
         compiler_params=PARAMS,
-        cost_estimate=pl.CostEstimate(flops=2*10**10, bytes_accessed=10**6, transcendentals=0),
+        cost_estimate=pl.CostEstimate(flops=2 * 10**10, bytes_accessed=10**6, transcendentals=0),
         name="act_sum",
     )(place, got)
     total = kept + shifted(given, "z_hi", 1)
@@ -236,10 +241,10 @@
     near_rows = [up_grad, shifted(up_grad, "core", 1), near, shifted(near, "core", 1)]
     far_rows = [far, shifted(far, "core", 1), farthest, shifted(farthest, "core", 1)]
     act_row = act_squares(act_parts)
-    cost = pl.CostEstimate(flops=8*10**9, bytes_accessed=10**7, transcendentals=0)
+    cost = pl.CostEstimate(flops=8 * 10**9, bytes_accessed=10**7, transcendentals=0)
     near_got = exchanged(grad_partials(near_rows, grad_basis, (), cost))
-    far_got = exchanged(gated(grad_partials(far_rows, grad_basis), act_row))
     act_own = jnp.stack(act_row)
+    far_got = exchanged(gated(grad_partials(far_rows, grad_basis), [act_own]))
     acts = []
     for own in [act_own] + [shifted(act_own, "z_lo", step) for step in (1, 2, 3)]:
         acts += [own, shifted(own, "core", 1)]

time: 123 us -> 122 us (level)
  waiting for transfers between devices: 34.6 us -> 32.8 us
    ppermute x26, waiting for transfers between devices: 17.3 us -> 15.6 us  [shifted(): lax.ppermute(value, axis, [(i, (i + step) % size) for i in range(size)])]
  transfers between devices with their start and end apart: 29 -> 29, of which waited for: 11 -> 10; matrix products, arithmetic and copies ran while one was open for 2% -> 2% of each run, Pallas kernels for 9% -> 9%
where the time goes in v12:
time: 122 us; the launch traced here: 120 us
  starting transfers between devices  54.8 us (45%)
  waiting for transfers between devices  32.8 us (27%)
  Pallas kernels  16.1 us (13%)
  blocking collectives  13.3 us (11%)
  other arithmetic  2.24 us (2%)
    ppermute x26, starting transfers between devices, shifted(): lax.ppermute(value, axis, [(i, (i + step) % size) for i in range(size)])  38.6 us
    ppermute x26, waiting for transfers between devices, shifted(): lax.ppermute(value, axis, [(i, (i + step) % size) for i in range(size)])  15.6 us
    all_to_all x1, blocking collectives, per_device(): out = lax.all_to_all(out, 'x', 0, 0, tiled=True)  13.3 us
    all_to_all x1, waiting for transfers between devices, act_squares(): got = lax.all_to_all(partials, ('x', 'y'), 0, 0, tiled=True)  11.1 us
    all_to_all x2, starting transfers between devices, exchanged(): lax.all_to_all(partial.reshape(16, columns // 16, tokens), ('x', 'y'), 0,...  9.16 us
    pallas_call x2, Pallas kernels, grad_partials(): pl.pallas_call(lambda *refs: grad_kernel(len(parts), *refs), out_shape=pl...  8.03 us
    all_to_all x1, starting transfers between devices, act_squares(): got = lax.all_to_all(partials, ('x', 'y'), 0, 0, tiled=True)  7.09 us
    all_to_all x2, waiting for transfers between devices, exchanged(): lax.all_to_all(partial.reshape(16, columns // 16, tokens), ('x', 'y'), 0,...  6.09 us
  transfers between devices with their start and end apart: 29, of which 10 were waited for; matrix products, arithmetic and copies ran while one was open for 2% of the time, Pallas kernels for 9%

profile of v12, /device:TPU:64, one launch (start us, length us, event | category | flops | bytes accessed | tf_op | source)
XLA Modules:
  0.0 120.4 jit_solution(15315431677851199674)
XLA Ops:
  0.0 4.5 %first.1 = (bf16[16,128,256]{2,1,0:T(8,128)(2,1)}, bf16[128,896]{1,0:T(8,128)(2,1)}) custom-call(s32[1]{0:T(128)} %bitcast.2.place, f32[1,8192]{1,0:T(1,128)} %bitcast.16, bf16[128,896]{1,0:T(8,128)(2,1)} %gate_at.1, bf16[128,896]{1,0:T(8,128)(2,1)} %grad_at.1, bf16[128,8192]{1,0:T(8,128)(2,1)} %hidden_at.1, bf16[256,4096]{1,0:T(8,128)(2,1)} %basis_at.1), custom_call_target="tpu_custom_call" | custom-call | tf_op jit(solution)/shard_map/first/pallas_call | solution.py:89
  4.5 2.0 %collective-permute-start.16 = (bf16[128,896]{1,0:T(8,128)(2,1)}, bf16[128,896]{1,0:T(8,128)(2,1)}, u32[]{:S(2)}, u32[]{:S(2)}) collective-permute-start(bf16[128,896]{1,0:T(8,128)(2,1)} %get-tuple-element.9.refs_0_), channel_id=1, source_target_pairs={{0,2},{2,4},{4,6},{6,0},{1,3},{3,5},{5,7},{7,1},{8,10},{10,12},{12... | collective-permute-start | bytes 688136 | tf_op jit(solution)/shard_map/ppermute | solution.py:22
  6.5 7.1 %all-to-all-start = ((bf16[16,128,256]{2,1,0:T(8,128)(2,1)}), bf16[16,128,256]{2,1,0:T(8,128)(2,1)}, u32[]{:S(2)}, u32[]{:S(2)}) async-start(bf16[16,128,256]{2,1,0:T(8,128)(2,1)} %get-tuple-element.10), calls=%async_computation | async-start | bytes 2097152 | tf_op jit(solution)/shard_map/all_to_all | solution.py:158
  14.8 0.9 collective-permute-start.2
  15.7 4.1 %grad.3 = bf16[1792,512]{1,0:T(8,128)(2,1)} custom-call(bf16[128,896]{1,0:T(8,128)(2,1)} %get-tuple-element.9.refs_0_, bf16[128,896]{1,0:T(8,128)(2,1)S(1)} %collective-permute-done.15.refs_1_, bf16[128,896]{1,0:T(8,128)(2,1)} %collective-permute-done.16.refs_2_, bf16[128,896]{1,0:T(8,128)(2,1)S(1)} %collective-permute-done.17.refs_3_, ...), custom_call_target="tpu_custom_call" | custom-call | flops 8000000000 | bytes 10000000 | tf_op jit(solution)/shard_map/grad/pallas_call | solution.py:131
  19.8 11.1 %all-to-all-done.got = bf16[16,128,256]{2,1,0:T(8,128)(2,1)} async-done(((bf16[16,128,256]{2,1,0:T(8,128)(2,1)}), bf16[16,128,256]{2,1,0:T(8,128)(2,1)}, u32[]{:S(2)}, u32[]{:S(2)}) %all-to-all-start) | async-done | bytes 1048608 | tf_op jit(solution)/shard_map/all_to_all | solution.py:158
  30.9 4.4 %all-to-all-start.2 = ((bf16[16,112,512]{2,1,0:T(8,128)(2,1)}), bf16[16,112,512]{2,1,0:T(8,128)(2,1)}, u32[]{:S(2)}, u32[]{:S(2)}) async-start(bf16[16,112,512]{2,1,0:T(8,128)(2,1)} %bitcast.14), calls=%async_computation.2 | async-start | bytes 3670016 | tf_op jit(solution)/shard_map/all_to_all | solution.py:194
  35.4 1.4 %act_sum.1 = (f32[128,128]{1,0:T(8,128)S(1)}, f32[128,128]{1,0:T(8,128)S(1)}) custom-call(s32[1]{0:T(128)} %bitcast.4.place, bf16[16,128,256]{2,1,0:T(8,128)(2,1)} %all-to-all-done.got), custom_call_target="tpu_custom_call" | custom-call | flops 20000000000 | bytes 1000000 | tf_op jit(solution)/shard_map/act_sum/pallas_call | solution.py:162
  36.7 4.6 %collective-permute-start.4 = (f32[128,128]{1,0:T(8,128)S(1)}, f32[128,128]{1,0:T(8,128)S(1)}, u32[]{:S(2)}, u32[]{:S(2)}) collective-permute-start(f32[128,128]{1,0:T(8,128)S(1)} %get-tuple-element.12), channel_id=1, source_target_pairs={{0,128},{128,0},{1,129},{129,1},{2,130},{130,2},{3,131},{131,3},{4... | collective-permute-start | bytes 196616 | tf_op jit(solution)/shard_map/ppermute | solution.py:22
  41.8 3.4 %collective-permute-done.4 = f32[128,128]{1,0:T(8,128)S(1)} collective-permute-done((f32[128,128]{1,0:T(8,128)S(1)}, f32[128,128]{1,0:T(8,128)S(1)}, u32[]{:S(2)}, u32[]{:S(2)}) %collective-permute-start.4) | collective-permute-done | bytes 65568 | tf_op jit(solution)/shard_map/ppermute | solution.py:22
  45.3 1.8 %collective-permute-start.5 = (bf16[128,128]{1,0:T(8,128)(2,1)S(1)}, bf16[128,128]{1,0:T(8,128)(2,1)S(1)}, u32[]{:S(2)}, u32[]{:S(2)}) collective-permute-start(bf16[128,128]{1,0:T(8,128)(2,1)S(1)} %multiply_convert_fusion.2), channel_id=1, source_target_pairs={{0,32},{32,64},{64,96},{96,0},{1,33},{33,65},{65,97},{97,1},{2,34}... | collective-permute-start | bytes 98312 | tf_op jit(solution)/shard_map/ppermute | solution.py:22
  47.0 2.7 %collective-permute-start.6 = (bf16[128,128]{1,0:T(8,128)(2,1)S(1)}, bf16[128,128]{1,0:T(8,128)(2,1)S(1)}, u32[]{:S(2)}, u32[]{:S(2)}) collective-permute-start(bf16[128,128]{1,0:T(8,128)(2,1)S(1)} %multiply_convert_fusion.2), channel_id=1, source_target_pairs={{0,64},{32,96},{64,0},{96,32},{1,65},{33,97},{65,1},{97,33},{2,66}... | collective-permute-start | bytes 98312 | tf_op jit(solution)/shard_map/ppermute | solution.py:22
  49.8 1.4 %collective-permute-start.7 = (bf16[128,128]{1,0:T(8,128)(2,1)S(1)}, bf16[128,128]{1,0:T(8,128)(2,1)S(1)}, u32[]{:S(2)}, u32[]{:S(2)}) collective-permute-start(bf16[128,128]{1,0:T(8,128)(2,1)S(1)} %multiply_convert_fusion.2), channel_id=1, source_target_pairs={{0,96},{32,0},{64,32},{96,64},{1,97},{33,1},{65,33},{97,65},{2,98}... | collective-permute-start | bytes 98312 | tf_op jit(solution)/shard_map/ppermute | solution.py:22
  51.2 4.0 %grad.2.refs_0_ = bf16[1792,512]{1,0:T(8,128)(2,1)} custom-call(bf16[128,896]{1,0:T(8,128)(2,1)S(1)} %collective-permute-done.refs_0_, bf16[128,896]{1,0:T(8,128)(2,1)S(1)} %collective-permute-done.1.refs_1_, bf16[128,896]{1,0:T(8,128)(2,1)} %collective-permute-done.2.refs_2_, bf16[128,896]{1,0:T(8,128)(2,1)S(1)} %collective-permute-done.3.refs_3_, ...), custom_call_target="tpu_custom_call" | custom-call | tf_op jit(solution)/shard_map/grad/pallas_call | solution.py:131
  55.7 3.5 %collective-permute-done.6 = bf16[128,128]{1,0:T(8,128)(2,1)S(1)} collective-permute-done((bf16[128,128]{1,0:T(8,128)(2,1)S(1)}, bf16[128,128]{1,0:T(8,128)(2,1)S(1)}, u32[]{:S(2)}, u32[]{:S(2)}) %collective-permute-start.6) | collective-permute-done | bytes 32800 | tf_op jit(solution)/shard_map/ppermute | solution.py:22
  59.9 4.7 %all-to-all-start.1 = ((bf16[16,112,512]{2,1,0:T(8,128)(2,1)}), bf16[16,112,512]{2,1,0:T(8,128)(2,1)S(1)}, u32[]{:S(2)}, u32[]{:S(2)}) async-start(bf16[16,112,512]{2,1,0:T(8,128)(2,1)} %bitcast.12), calls=%async_computation.1 | async-start | bytes 3670016 | tf_op jit(solution)/shard_map/all_to_all | solution.py:194
  65.3 1.0 collective-permute-start.11
  66.3 1.0 collective-permute-start.13
  67.3 1.8 %convert_reduce_fusion.1 = f32[112,512]{1,0:T(8,128)S(1)} fusion(bf16[16,112,512]{2,1,0:T(8,128)(2,1)} %all-to-all-done.2), kind=kLoop, calls=%fused_computation.1 | loop fusion | flops 1777664 | bytes 2064384 | tf_op jit(solution)/shard_map/reduce_sum | solution.py:198
  69.1 6.5 %collective-permute-start.18 = (bf16[112,512]{1,0:T(8,128)(2,1)S(1)}, bf16[112,512]{1,0:T(8,128)(2,1)S(1)}, u32[]{:S(2)}, u32[]{:S(2)}) collective-permute-start(bf16[112,512]{1,0:T(8,128)(2,1)S(1)} %convert_element_type.29), channel_id=1, source_target_pairs={{0,128},{128,0},{1,129},{129,1},{2,130},{130,2},{3,131},{131,3},{4... | collective-permute-start | bytes 344072 | tf_op jit(solution)/shard_map/ppermute | solution.py:22
  76.6 4.6 %collective-permute-done.18 = bf16[112,512]{1,0:T(8,128)(2,1)S(1)} collective-permute-done((bf16[112,512]{1,0:T(8,128)(2,1)S(1)}, bf16[112,512]{1,0:T(8,128)(2,1)S(1)}, u32[]{:S(2)}, u32[]{:S(2)}) %collective-permute-start.18) | collective-permute-done | bytes 114720 | tf_op jit(solution)/shard_map/ppermute | solution.py:22
  81.3 5.4 %all-to-all-done.1.refs_0_ = bf16[16,112,512]{2,1,0:T(8,128)(2,1)S(1)} async-done(((bf16[16,112,512]{2,1,0:T(8,128)(2,1)}), bf16[16,112,512]{2,1,0:T(8,128)(2,1)S(1)}, u32[]{:S(2)}, u32[]{:S(2)}) %all-to-all-start.1) | async-done | bytes 1835040 | tf_op jit(solution)/shard_map/all_to_all | solution.py:194
  87.0 4.6 %collective-permute-start.19 = (bf16[112,512]{1,0:T(8,128)(2,1)S(1)}, bf16[112,512]{1,0:T(8,128)(2,1)S(1)}, u32[]{:S(2)}, u32[]{:S(2)}) collective-permute-start(bf16[112,512]{1,0:T(8,128)(2,1)S(1)} %convert_element_type.33), channel_id=1, source_target_pairs={{0,128},{128,0},{1,129},{129,1},{2,130},{130,2},{3,131},{131,3},{4... | collective-permute-start | bytes 344072 | tf_op jit(solution)/shard_map/ppermute | solution.py:22
  91.7 2.6 %collective-permute-start.24 = (bf16[112,512]{1,0:T(8,128)(2,1)S(1)}, bf16[112,512]{1,0:T(8,128)(2,1)S(1)}, u32[]{:S(2)}, u32[]{:S(2)}) collective-permute-start(bf16[112,512]{1,0:T(8,128)(2,1)S(1)} %multiply_convert_fusion.1.refs_9_.refs_0_), channel_id=1, source_target_pairs={{0,16},{8,24},{16,0},{24,8},{1,17},{9,25},{17,1},{25,9},{2,18},{10... | collective-permute-start | bytes 344072 | tf_op jit(solution)/shard_map/ppermute | solution.py:22
  94.4 1.7 %collective-permute-start.25 = (bf16[112,512]{1,0:T(8,128)(2,1)S(1)}, bf16[112,512]{1,0:T(8,128)(2,1)S(1)}, u32[]{:S(2)}, u32[]{:S(2)}) collective-permute-start(bf16[112,512]{1,0:T(8,128)(2,1)S(1)} %multiply_convert_fusion.1.refs_9_.refs_0_), channel_id=1, source_target_pairs={{0,24},{8,0},{16,8},{24,16},{1,25},{9,1},{17,9},{25,17},{2,26},{10... | collective-permute-start | bytes 344072 | tf_op jit(solution)/shard_map/ppermute | solution.py:22
  97.0 2.5 %collective-permute-start.21 = (bf16[112,512]{1,0:T(8,128)(2,1)S(1)}, bf16[112,512]{1,0:T(8,128)(2,1)S(1)}, u32[]{:S(2)}, u32[]{:S(2)}) collective-permute-start(bf16[112,512]{1,0:T(8,128)(2,1)S(1)} %multiply_convert_fusion.refs_0_), channel_id=1, source_target_pairs={{0,16},{8,24},{16,0},{24,8},{1,17},{9,25},{17,1},{25,9},{2,18},{10... | collective-permute-start | bytes 344072 | tf_op jit(solution)/shard_map/ppermute | solution.py:22
  99.5 1.8 %collective-permute-start.22 = (bf16[112,512]{1,0:T(8,128)(2,1)S(1)}, bf16[112,512]{1,0:T(8,128)(2,1)S(1)}, u32[]{:S(2)}, u32[]{:S(2)}) collective-permute-start(bf16[112,512]{1,0:T(8,128)(2,1)S(1)} %multiply_convert_fusion.refs_0_), channel_id=1, source_target_pairs={{0,24},{8,0},{16,8},{24,16},{1,25},{9,1},{17,9},{25,17},{2,26},{10... | collective-permute-start | bytes 344072 | tf_op jit(solution)/shard_map/ppermute | solution.py:22
  101.3 1.1 correct.2.refs_8_
  102.4 1.8 %collective-permute-done.20.refs_1_ = bf16[112,512]{1,0:T(8,128)(2,1)S(1)} collective-permute-done((bf16[112,512]{1,0:T(8,128)(2,1)S(1)}, bf16[112,512]{1,0:T(8,128)(2,1)S(1)}, u32[]{:S(2)}, u32[]{:S(2)}) %collective-permute-start.20) | collective-permute-done | bytes 114720 | tf_op jit(solution)/shard_map/ppermute | solution.py:22
  105.1 1.1 correct.3
  106.1 13.3 %all_to_all.20 = f32[4,448,128]{2,1,0:T(8,128)S(1)} all-to-all(f32[4,448,128]{2,1,0:T(8,128)S(1)} %correct.3), channel_id=1, replica_groups=mesh['z_hi'=2,'x'=4,'y'=4,'z_lo'=4,'core'=2] {'x'}, dimensions={0} | all-to-all | bytes 1835008 | tf_op jit(solution)/shard_map/all_to_all | solution.py:256
  119.5 0.9 copy.12
  (47 shorter events, 6.9 us)
Async XLA Ops:
  0.0 15.7 %copy-start = (bf16[896,1792]{1,0:T(8,128)(2,1)S(1)}, bf16[896,1792]{1,0:T(8,128)(2,1)}, u32[]{:S(2)}) copy-start(bf16[896,1792]{1,0:T(8,128)(2,1)} %refs_4_.3) | copy-start | bytes 9633796
  4.5 9.2 %collective-permute-start.16 = (bf16[128,896]{1,0:T(8,128)(2,1)}, bf16[128,896]{1,0:T(8,128)(2,1)}, u32[]{:S(2)}, u32[]{:S(2)}) collective-permute-start(bf16[128,896]{1,0:T(8,128)(2,1)} %get-tuple-element.9.refs_0_), channel_id=1, source_target_pairs={{0,2},{2,4},{4,6},{6,0},{1,3},{3,5},{5,7},{7,1},{8,10},{10,12},{12... | collective-permute-start | bytes 688136 | tf_op jit(solution)/shard_map/ppermute | solution.py:22
  6.5 24.4 %all-to-all-start = ((bf16[16,128,256]{2,1,0:T(8,128)(2,1)}), bf16[16,128,256]{2,1,0:T(8,128)(2,1)}, u32[]{:S(2)}, u32[]{:S(2)}) async-start(bf16[16,128,256]{2,1,0:T(8,128)(2,1)} %get-tuple-element.10), calls=%async_computation | async-start | bytes 2097152 | tf_op jit(solution)/shard_map/all_to_all | solution.py:158
  13.6 2.1 %collective-permute-start.15 = (bf16[128,896]{1,0:T(8,128)(2,1)}, bf16[128,896]{1,0:T(8,128)(2,1)S(1)}, u32[]{:S(2)}, u32[]{:S(2)}) collective-permute-start(bf16[128,896]{1,0:T(8,128)(2,1)} %get-tuple-element.9.refs_0_), channel_id=1, source_target_pairs={{0,1},{1,0},{2,3},{3,2},{4,5},{5,4},{6,7},{7,6},{8,9},{9,8},{10,11... | collective-permute-start | bytes 688136 | tf_op jit(solution)/shard_map/ppermute | solution.py:22
  13.7 2.0 %collective-permute-start.17 = (bf16[128,896]{1,0:T(8,128)(2,1)}, bf16[128,896]{1,0:T(8,128)(2,1)S(1)}, u32[]{:S(2)}, u32[]{:S(2)}) collective-permute-start(bf16[128,896]{1,0:T(8,128)(2,1)} %collective-permute-done.16.refs_2_), channel_id=1, source_target_pairs={{0,1},{1,0},{2,3},{3,2},{4,5},{5,4},{6,7},{7,6},{8,9},{9,8},{10,11... | collective-permute-start | bytes 688136 | tf_op jit(solution)/shard_map/ppermute | solution.py:22
  14.2 27.1 %collective-permute-start = (bf16[128,896]{1,0:T(8,128)(2,1)}, bf16[128,896]{1,0:T(8,128)(2,1)S(1)}, u32[]{:S(2)}, u32[]{:S(2)}) collective-permute-start(bf16[128,896]{1,0:T(8,128)(2,1)} %get-tuple-element.9.refs_0_), channel_id=1, source_target_pairs={{0,4},{2,6},{4,0},{6,2},{1,5},{3,7},{5,1},{7,3},{8,12},{10,14},{12... | collective-permute-start | bytes 688136 | tf_op jit(solution)/shard_map/ppermute | solution.py:22
  14.8 26.5 %collective-permute-start.2 = (bf16[128,896]{1,0:T(8,128)(2,1)}, bf16[128,896]{1,0:T(8,128)(2,1)}, u32[]{:S(2)}, u32[]{:S(2)}) collective-permute-start(bf16[128,896]{1,0:T(8,128)(2,1)} %get-tuple-element.9.refs_0_), channel_id=1, source_target_pairs={{0,6},{2,0},{4,2},{6,4},{1,7},{3,1},{5,3},{7,5},{8,14},{10,8},{12,... | collective-permute-start | bytes 688136 | tf_op jit(solution)/shard_map/ppermute | solution.py:22
  30.9 29.0 %all-to-all-start.2 = ((bf16[16,112,512]{2,1,0:T(8,128)(2,1)}), bf16[16,112,512]{2,1,0:T(8,128)(2,1)}, u32[]{:S(2)}, u32[]{:S(2)}) async-start(bf16[16,112,512]{2,1,0:T(8,128)(2,1)} %bitcast.14), calls=%async_computation.2 | async-start | bytes 3670016 | tf_op jit(solution)/shard_map/all_to_all | solution.py:194
  36.7 8.5 %collective-permute-start.4 = (f32[128,128]{1,0:T(8,128)S(1)}, f32[128,128]{1,0:T(8,128)S(1)}, u32[]{:S(2)}, u32[]{:S(2)}) collective-permute-start(f32[128,128]{1,0:T(8,128)S(1)} %get-tuple-element.12), channel_id=1, source_target_pairs={{0,128},{128,0},{1,129},{129,1},{2,130},{130,2},{3,131},{131,3},{4... | collective-permute-start | bytes 196616 | tf_op jit(solution)/shard_map/ppermute | solution.py:22
  41.3 9.9 %collective-permute-start.1 = (bf16[128,896]{1,0:T(8,128)(2,1)S(1)}, bf16[128,896]{1,0:T(8,128)(2,1)S(1)}, u32[]{:S(2)}, u32[]{:S(2)}) collective-permute-start(bf16[128,896]{1,0:T(8,128)(2,1)S(1)} %collective-permute-done.refs_0_), channel_id=1, source_target_pairs={{0,1},{1,0},{2,3},{3,2},{4,5},{5,4},{6,7},{7,6},{8,9},{9,8},{10,11... | collective-permute-start | bytes 688136 | tf_op jit(solution)/shard_map/ppermute | solution.py:22
  41.3 9.9 %collective-permute-start.3 = (bf16[128,896]{1,0:T(8,128)(2,1)}, bf16[128,896]{1,0:T(8,128)(2,1)S(1)}, u32[]{:S(2)}, u32[]{:S(2)}) collective-permute-start(bf16[128,896]{1,0:T(8,128)(2,1)} %collective-permute-done.2.refs_2_), channel_id=1, source_target_pairs={{0,1},{1,0},{2,3},{3,2},{4,5},{5,4},{6,7},{7,6},{8,9},{9,8},{10,11... | collective-permute-start | bytes 688136 | tf_op jit(solution)/shard_map/ppermute | solution.py:22
  45.3 10.4 %collective-permute-start.5 = (bf16[128,128]{1,0:T(8,128)(2,1)S(1)}, bf16[128,128]{1,0:T(8,128)(2,1)S(1)}, u32[]{:S(2)}, u32[]{:S(2)}) collective-permute-start(bf16[128,128]{1,0:T(8,128)(2,1)S(1)} %multiply_convert_fusion.2), channel_id=1, source_target_pairs={{0,32},{32,64},{64,96},{96,0},{1,33},{33,65},{65,97},{97,1},{2,34}... | collective-permute-start | bytes 98312 | tf_op jit(solution)/shard_map/ppermute | solution.py:22
  47.0 12.1 %collective-permute-start.6 = (bf16[128,128]{1,0:T(8,128)(2,1)S(1)}, bf16[128,128]{1,0:T(8,128)(2,1)S(1)}, u32[]{:S(2)}, u32[]{:S(2)}) collective-permute-start(bf16[128,128]{1,0:T(8,128)(2,1)S(1)} %multiply_convert_fusion.2), channel_id=1, source_target_pairs={{0,64},{32,96},{64,0},{96,32},{1,65},{33,97},{65,1},{97,33},{2,66}... | collective-permute-start | bytes 98312 | tf_op jit(solution)/shard_map/ppermute | solution.py:22
  49.8 9.4 %collective-permute-start.7 = (bf16[128,128]{1,0:T(8,128)(2,1)S(1)}, bf16[128,128]{1,0:T(8,128)(2,1)S(1)}, u32[]{:S(2)}, u32[]{:S(2)}) collective-permute-start(bf16[128,128]{1,0:T(8,128)(2,1)S(1)} %multiply_convert_fusion.2), channel_id=1, source_target_pairs={{0,96},{32,0},{64,32},{96,64},{1,97},{33,1},{65,33},{97,65},{2,98}... | collective-permute-start | bytes 98312 | tf_op jit(solution)/shard_map/ppermute | solution.py:22
  59.9 26.8 %all-to-all-start.1 = ((bf16[16,112,512]{2,1,0:T(8,128)(2,1)}), bf16[16,112,512]{2,1,0:T(8,128)(2,1)S(1)}, u32[]{:S(2)}, u32[]{:S(2)}) async-start(bf16[16,112,512]{2,1,0:T(8,128)(2,1)} %bitcast.12), calls=%async_computation.1 | async-start | bytes 3670016 | tf_op jit(solution)/shard_map/all_to_all | solution.py:194
  64.7 10.9 %collective-permute-start.9 = (bf16[4,128,128]{2,1,0:T(8,128)(2,1)S(1)}, bf16[4,128,128]{2,1,0:T(8,128)(2,1)S(1)}, u32[]{:S(2)}, u32[]{:S(2)}) collective-permute-start(bf16[4,128,128]{2,1,0:T(8,128)(2,1)S(1)} %pad_maximum_fusion.refs_1_.refs_4_), channel_id=1, source_target_pairs={{0,2},{2,4},{4,6},{6,0},{1,3},{3,5},{5,7},{7,1},{8,10},{10,12},{12... | collective-permute-start | bytes 393224 | tf_op jit(solution)/shard_map/ppermute | solution.py:22
  65.3 10.8 %collective-permute-start.11 = (bf16[4,128,128]{2,1,0:T(8,128)(2,1)S(1)}, bf16[4,128,128]{2,1,0:T(8,128)(2,1)S(1)}, u32[]{:S(2)}, u32[]{:S(2)}) collective-permute-start(bf16[4,128,128]{2,1,0:T(8,128)(2,1)S(1)} %pad_maximum_fusion.refs_1_.refs_4_), channel_id=1, source_target_pairs={{0,4},{2,6},{4,0},{6,2},{1,5},{3,7},{5,1},{7,3},{8,12},{10,14},{12... | collective-permute-start | bytes 393224 | tf_op jit(solution)/shard_map/ppermute | solution.py:22
  66.3 9.9 %collective-permute-start.13 = (bf16[4,128,128]{2,1,0:T(8,128)(2,1)S(1)}, bf16[4,128,128]{2,1,0:T(8,128)(2,1)S(1)}, u32[]{:S(2)}, u32[]{:S(2)}) collective-permute-start(bf16[4,128,128]{2,1,0:T(8,128)(2,1)S(1)} %pad_maximum_fusion.refs_1_.refs_4_), channel_id=1, source_target_pairs={{0,6},{2,0},{4,2},{6,4},{1,7},{3,1},{5,3},{7,5},{8,14},{10,8},{12,... | collective-permute-start | bytes 393224 | tf_op jit(solution)/shard_map/ppermute | solution.py:22
  69.1 12.1 %collective-permute-start.18 = (bf16[112,512]{1,0:T(8,128)(2,1)S(1)}, bf16[112,512]{1,0:T(8,128)(2,1)S(1)}, u32[]{:S(2)}, u32[]{:S(2)}) collective-permute-start(bf16[112,512]{1,0:T(8,128)(2,1)S(1)} %convert_element_type.29), channel_id=1, source_target_pairs={{0,128},{128,0},{1,129},{129,1},{2,130},{130,2},{3,131},{131,3},{4... | collective-permute-start | bytes 344072 | tf_op jit(solution)/shard_map/ppermute | solution.py:22
  75.6 5.7 %collective-permute-start.8 = (bf16[4,128,128]{2,1,0:T(8,128)(2,1)S(1)}, bf16[4,128,128]{2,1,0:T(8,128)(2,1)S(1)}, u32[]{:S(2)}, u32[]{:S(2)}) collective-permute-start(bf16[4,128,128]{2,1,0:T(8,128)(2,1)S(1)} %pad_maximum_fusion.refs_1_.refs_4_), channel_id=1, source_target_pairs={{0,1},{1,0},{2,3},{3,2},{4,5},{5,4},{6,7},{7,6},{8,9},{9,8},{10,11... | collective-permute-start | bytes 393224 | tf_op jit(solution)/shard_map/ppermute | solution.py:22
  75.6 5.7 %collective-permute-start.10 = (bf16[4,128,128]{2,1,0:T(8,128)(2,1)S(1)}, bf16[4,128,128]{2,1,0:T(8,128)(2,1)S(1)}, u32[]{:S(2)}, u32[]{:S(2)}) collective-permute-start(bf16[4,128,128]{2,1,0:T(8,128)(2,1)S(1)} %collective-permute-done.9.refs_3_.refs_6_), channel_id=1, source_target_pairs={{0,1},{1,0},{2,3},{3,2},{4,5},{5,4},{6,7},{7,6},{8,9},{9,8},{10,11... | collective-permute-start | bytes 393224 | tf_op jit(solution)/shard_map/ppermute | solution.py:22
  76.1 5.2 %collective-permute-start.12 = (bf16[4,128,128]{2,1,0:T(8,128)(2,1)S(1)}, bf16[4,128,128]{2,1,0:T(8,128)(2,1)S(1)}, u32[]{:S(2)}, u32[]{:S(2)}) collective-permute-start(bf16[4,128,128]{2,1,0:T(8,128)(2,1)S(1)} %collective-permute-done.11.refs_5_.refs_4_), channel_id=1, source_target_pairs={{0,1},{1,0},{2,3},{3,2},{4,5},{5,4},{6,7},{7,6},{8,9},{9,8},{10,11... | collective-permute-start | bytes 393224 | tf_op jit(solution)/shard_map/ppermute | solution.py:22
  76.2 5.1 %collective-permute-start.14 = (bf16[4,128,128]{2,1,0:T(8,128)(2,1)S(1)}, bf16[4,128,128]{2,1,0:T(8,128)(2,1)S(1)}, u32[]{:S(2)}, u32[]{:S(2)}) collective-permute-start(bf16[4,128,128]{2,1,0:T(8,128)(2,1)S(1)} %collective-permute-done.13.refs_7_.refs_6_), channel_id=1, source_target_pairs={{0,1},{1,0},{2,3},{3,2},{4,5},{5,4},{6,7},{7,6},{8,9},{9,8},{10,11... | collective-permute-start | bytes 393224 | tf_op jit(solution)/shard_map/ppermute | solution.py:22
  87.0 9.9 %collective-permute-start.19 = (bf16[112,512]{1,0:T(8,128)(2,1)S(1)}, bf16[112,512]{1,0:T(8,128)(2,1)S(1)}, u32[]{:S(2)}, u32[]{:S(2)}) collective-permute-start(bf16[112,512]{1,0:T(8,128)(2,1)S(1)} %convert_element_type.33), channel_id=1, source_target_pairs={{0,128},{128,0},{1,129},{129,1},{2,130},{130,2},{3,131},{131,3},{4... | collective-permute-start | bytes 344072 | tf_op jit(solution)/shard_map/ppermute | solution.py:22
  91.6 7.8 %collective-permute-start.23 = (bf16[112,512]{1,0:T(8,128)(2,1)S(1)}, bf16[112,512]{1,0:T(8,128)(2,1)S(1)}, u32[]{:S(2)}, u32[]{:S(2)}) collective-permute-start(bf16[112,512]{1,0:T(8,128)(2,1)S(1)} %multiply_convert_fusion.1.refs_9_.refs_0_), channel_id=1, source_target_pairs={{0,8},{8,16},{16,24},{24,0},{1,9},{9,17},{17,25},{25,1},{2,10},{10... | collective-permute-start | bytes 344072 | tf_op jit(solution)/shard_map/ppermute | solution.py:22
  91.7 9.6 %collective-permute-start.24 = (bf16[112,512]{1,0:T(8,128)(2,1)S(1)}, bf16[112,512]{1,0:T(8,128)(2,1)S(1)}, u32[]{:S(2)}, u32[]{:S(2)}) collective-permute-start(bf16[112,512]{1,0:T(8,128)(2,1)S(1)} %multiply_convert_fusion.1.refs_9_.refs_0_), channel_id=1, source_target_pairs={{0,16},{8,24},{16,0},{24,8},{1,17},{9,25},{17,1},{25,9},{2,18},{10... | collective-permute-start | bytes 344072 | tf_op jit(solution)/shard_map/ppermute | solution.py:22
  94.4 6.9 %collective-permute-start.25 = (bf16[112,512]{1,0:T(8,128)(2,1)S(1)}, bf16[112,512]{1,0:T(8,128)(2,1)S(1)}, u32[]{:S(2)}, u32[]{:S(2)}) collective-permute-start(bf16[112,512]{1,0:T(8,128)(2,1)S(1)} %multiply_convert_fusion.1.refs_9_.refs_0_), channel_id=1, source_target_pairs={{0,24},{8,0},{16,8},{24,16},{1,25},{9,1},{17,9},{25,17},{2,26},{10... | collective-permute-start | bytes 344072 | tf_op jit(solution)/shard_map/ppermute | solution.py:22
  96.9 7.3 %collective-permute-start.20 = (bf16[112,512]{1,0:T(8,128)(2,1)S(1)}, bf16[112,512]{1,0:T(8,128)(2,1)S(1)}, u32[]{:S(2)}, u32[]{:S(2)}) collective-permute-start(bf16[112,512]{1,0:T(8,128)(2,1)S(1)} %multiply_convert_fusion.refs_0_), channel_id=1, source_target_pairs={{0,8},{8,16},{16,24},{24,0},{1,9},{9,17},{17,25},{25,1},{2,10},{10... | collective-permute-start | bytes 344072 | tf_op jit(solution)/shard_map/ppermute | solution.py:22
  97.0 7.2 %collective-permute-start.21 = (bf16[112,512]{1,0:T(8,128)(2,1)S(1)}, bf16[112,512]{1,0:T(8,128)(2,1)S(1)}, u32[]{:S(2)}, u32[]{:S(2)}) collective-permute-start(bf16[112,512]{1,0:T(8,128)(2,1)S(1)} %multiply_convert_fusion.refs_0_), channel_id=1, source_target_pairs={{0,16},{8,24},{16,0},{24,8},{1,17},{9,25},{17,1},{25,9},{2,18},{10... | collective-permute-start | bytes 344072 | tf_op jit(solution)/shard_map/ppermute | solution.py:22
  99.5 5.6 %collective-permute-start.22 = (bf16[112,512]{1,0:T(8,128)(2,1)S(1)}, bf16[112,512]{1,0:T(8,128)(2,1)S(1)}, u32[]{:S(2)}, u32[]{:S(2)}) collective-permute-start(bf16[112,512]{1,0:T(8,128)(2,1)S(1)} %multiply_convert_fusion.refs_0_), channel_id=1, source_target_pairs={{0,24},{8,0},{16,8},{24,16},{1,25},{9,1},{17,9},{25,17},{2,26},{10... | collective-permute-start | bytes 344072 | tf_op jit(solution)/shard_map/ppermute | solution.py:22

commit v13 on v12

--- a/solution.py
+++ b/solution.py
@@ -10,6 +10,7 @@
 SIZES = (2, 4, 4, 4, 2)
 DP = ("z_hi", "x", "y")
 TENSOR = ("z_lo", "core")
+Y_STEPS = (2, 1, 3)
 SMEM = pl.BlockSpec(memory_space=pltpu.SMEM)
 VMEM = pl.BlockSpec(memory_space=pltpu.VMEM)
 ANY = pl.BlockSpec(memory_space=pl.ANY)
@@ -201,20 +202,22 @@
 
 
 def correct_kernel(place, *refs):
-    pieces, acts, before, (out, act) = refs[:4], refs[4:8], refs[8:-2], refs[-2:]
+    pieces, acts, before, (out, act, both) = refs[:4], refs[4:8], refs[8:-3], refs[-3:]
     _, tokens, block = acts[0].shape
     for i, part in enumerate(acts):
         for behind in range(4):
             here = slice(i * tokens, (i + 1) * tokens), slice(behind * block, (behind + 1) * block)
             act[here] = part[behind]
     rows = pieces[0].shape[0]
-    for y_behind, piece in enumerate(pieces):
-        part = jnp.dot(piece[...], act[...], preferred_element_type=jnp.float32)
-        part = part * (1.0 / (8 * tokens))
+    for i, piece in enumerate(pieces):
+        both[i * rows : (i + 1) * rows, :] = piece[...]
+    every = jnp.dot(both[...], act[...], preferred_element_type=jnp.float32)
+    every = every * (1.0 / (8 * tokens))
+    for i, y_behind in enumerate((0, *Y_STEPS)):
         at = pl.ds(pl.multiple_of(lax.rem(place[1] + 4 - y_behind, 4) * rows, rows), rows)
         for behind in range(4):
             x = lax.rem(place[0] + 4 - behind, 4)
-            here = part[:, behind * block : (behind + 1) * block]
+            here = every[i * rows : (i + 1) * rows, behind * block : (behind + 1) * block]
             if before:
                 here = before[0][x, at, :] + here
             out[x, at, :] = here
@@ -229,7 +232,10 @@
         out_shape=jax.ShapeDtypeStruct((4, 4 * rows, block), jnp.float32),
         in_specs=[SMEM] + [VMEM] * (8 + len(before)),
         out_specs=VMEM,
-        scratch_shapes=[pltpu.VMEM((tokens, 4 * block), jnp.bfloat16)],
+        scratch_shapes=[
+            pltpu.VMEM((tokens, 4 * block), jnp.bfloat16),
+            pltpu.VMEM((4 * rows, tokens), jnp.bfloat16),
+        ],
         compiler_params=PARAMS,
         name="correct",
     )(place, *pieces, *acts, *before)
@@ -249,9 +255,9 @@
     for own in [act_own] + [shifted(act_own, "z_lo", step) for step in (1, 2, 3)]:
         acts += [own, shifted(own, "core", 1)]
     near_sq = squared(near_got)
-    near_pieces = [near_sq] + [shifted(near_sq, "y", step) for step in (1, 2, 3)]
+    near_pieces = [near_sq] + [shifted(near_sq, "y", step) for step in Y_STEPS]
     far_sq = squared(gated(far_got, acts + [near_sq], jax.ShapeDtypeStruct))
-    far_pieces = [far_sq] + [shifted(far_sq, "y", step) for step in (1, 2, 3)]
+    far_pieces = [far_sq] + [shifted(far_sq, "y", step) for step in Y_STEPS]
     out = corrected(far_pieces, acts[4:], corrected(near_pieces, acts[:4]))
     out = lax.all_to_all(out, "x", 0, 0, tiled=True)
     return out.reshape(grad_basis.shape[1], -1)

time: 122 us -> 122 us (level)
  waiting for transfers between devices: 32.8 us -> 31.1 us
  starting transfers between devices: 54.8 us -> 56.1 us
    ppermute x26, waiting for transfers between devices: 15.6 us -> 13.9 us  [shifted(): lax.ppermute(value, axis, [(i, (i + step) % size) for i in range(size)])]
    ppermute x26, starting transfers between devices: 38.6 us -> 39.9 us  [shifted(): lax.ppermute(value, axis, [(i, (i + step) % size) for i in range(size)])]
where the time goes in v13:
time: 122 us; the launch traced here: 120 us
  starting transfers between devices  56.1 us (46%)
  waiting for transfers between devices  31.1 us (25%)
  Pallas kernels  15.9 us (13%)
  blocking collectives  13.5 us (11%)
  other arithmetic  2.24 us (2%)
    ppermute x26, starting transfers between devices, shifted(): lax.ppermute(value, axis, [(i, (i + step) % size) for i in range(size)])  39.9 us
    ppermute x26, waiting for transfers between devices, shifted(): lax.ppermute(value, axis, [(i, (i + step) % size) for i in range(size)])  13.9 us
    all_to_all x1, blocking collectives, per_device(): out = lax.all_to_all(out, 'x', 0, 0, tiled=True)  13.5 us
    all_to_all x1, waiting for transfers between devices, act_squares(): got = lax.all_to_all(partials, ('x', 'y'), 0, 0, tiled=True)  11.1 us
    all_to_all x2, starting transfers between devices, exchanged(): lax.all_to_all(partial.reshape(16, columns // 16, tokens), ('x', 'y'), 0,...  9.16 us
    pallas_call x2, Pallas kernels, grad_partials(): pl.pallas_call(lambda *refs: grad_kernel(len(parts), *refs), out_shape=pl...  8.03 us
    all_to_all x1, starting transfers between devices, act_squares(): got = lax.all_to_all(partials, ('x', 'y'), 0, 0, tiled=True)  7.09 us
    all_to_all x2, waiting for transfers between devices, exchanged(): lax.all_to_all(partial.reshape(16, columns // 16, tokens), ('x', 'y'), 0,...  6.09 us
  transfers between devices with their start and end apart: 29, of which 10 were waited for; matrix products, arithmetic and copies ran while one was open for 2% of the time, Pallas kernels for 9%

profile of v13, /device:TPU:64, one launch (start us, length us, event | category | flops | bytes accessed | tf_op | source)
XLA Modules:
  0.0 120.1 jit_solution(3496150348642887540)
XLA Ops:
  0.0 4.5 %first.1 = (bf16[16,128,256]{2,1,0:T(8,128)(2,1)}, bf16[128,896]{1,0:T(8,128)(2,1)}) custom-call(s32[1]{0:T(128)} %bitcast.2.place, f32[1,8192]{1,0:T(1,128)} %bitcast.16, bf16[128,896]{1,0:T(8,128)(2,1)} %gate_at.1, bf16[128,896]{1,0:T(8,128)(2,1)} %grad_at.1, bf16[128,8192]{1,0:T(8,128)(2,1)} %hidden_at.1, bf16[256,4096]{1,0:T(8,128)(2,1)} %basis_at.1), custom_call_target="tpu_custom_call" | custom-call | tf_op jit(solution)/shard_map/first/pallas_call | solution.py:90
  4.5 2.0 %collective-permute-start.16 = (bf16[128,896]{1,0:T(8,128)(2,1)}, bf16[128,896]{1,0:T(8,128)(2,1)}, u32[]{:S(2)}, u32[]{:S(2)}) collective-permute-start(bf16[128,896]{1,0:T(8,128)(2,1)} %get-tuple-element.9.refs_0_), channel_id=1, source_target_pairs={{0,2},{2,4},{4,6},{6,0},{1,3},{3,5},{5,7},{7,1},{8,10},{10,12},{12... | collective-permute-start | bytes 688136 | tf_op jit(solution)/shard_map/ppermute | solution.py:23
  6.5 7.1 %all-to-all-start = ((bf16[16,128,256]{2,1,0:T(8,128)(2,1)}), bf16[16,128,256]{2,1,0:T(8,128)(2,1)}, u32[]{:S(2)}, u32[]{:S(2)}) async-start(bf16[16,128,256]{2,1,0:T(8,128)(2,1)} %get-tuple-element.10), calls=%async_computation | async-start | bytes 2097152 | tf_op jit(solution)/shard_map/all_to_all | solution.py:159
  14.8 0.9 collective-permute-start.2
  15.7 4.1 %grad.3 = bf16[1792,512]{1,0:T(8,128)(2,1)} custom-call(bf16[128,896]{1,0:T(8,128)(2,1)} %get-tuple-element.9.refs_0_, bf16[128,896]{1,0:T(8,128)(2,1)S(1)} %collective-permute-done.15.refs_1_, bf16[128,896]{1,0:T(8,128)(2,1)} %collective-permute-done.16.refs_2_, bf16[128,896]{1,0:T(8,128)(2,1)S(1)} %collective-permute-done.17.refs_3_, ...), custom_call_target="tpu_custom_call" | custom-call | flops 8000000000 | bytes 10000000 | tf_op jit(solution)/shard_map/grad/pallas_call | solution.py:132
  19.8 11.1 %all-to-all-done.got = bf16[16,128,256]{2,1,0:T(8,128)(2,1)} async-done(((bf16[16,128,256]{2,1,0:T(8,128)(2,1)}), bf16[16,128,256]{2,1,0:T(8,128)(2,1)}, u32[]{:S(2)}, u32[]{:S(2)}) %all-to-all-start) | async-done | bytes 1048608 | tf_op jit(solution)/shard_map/all_to_all | solution.py:159
  30.9 4.4 %all-to-all-start.2 = ((bf16[16,112,512]{2,1,0:T(8,128)(2,1)}), bf16[16,112,512]{2,1,0:T(8,128)(2,1)}, u32[]{:S(2)}, u32[]{:S(2)}) async-start(bf16[16,112,512]{2,1,0:T(8,128)(2,1)} %bitcast.14), calls=%async_computation.2 | async-start | bytes 3670016 | tf_op jit(solution)/shard_map/all_to_all | solution.py:195
  35.4 1.4 %act_sum.1 = (f32[128,128]{1,0:T(8,128)S(1)}, f32[128,128]{1,0:T(8,128)S(1)}) custom-call(s32[1]{0:T(128)} %bitcast.4.place, bf16[16,128,256]{2,1,0:T(8,128)(2,1)} %all-to-all-done.got), custom_call_target="tpu_custom_call" | custom-call | flops 20000000000 | bytes 1000000 | tf_op jit(solution)/shard_map/act_sum/pallas_call | solution.py:163
  36.7 4.6 %collective-permute-start.4 = (f32[128,128]{1,0:T(8,128)S(1)}, f32[128,128]{1,0:T(8,128)S(1)}, u32[]{:S(2)}, u32[]{:S(2)}) collective-permute-start(f32[128,128]{1,0:T(8,128)S(1)} %get-tuple-element.12), channel_id=1, source_target_pairs={{0,128},{128,0},{1,129},{129,1},{2,130},{130,2},{3,131},{131,3},{4... | collective-permute-start | bytes 196616 | tf_op jit(solution)/shard_map/ppermute | solution.py:23
  41.8 3.4 %collective-permute-done.4 = f32[128,128]{1,0:T(8,128)S(1)} collective-permute-done((f32[128,128]{1,0:T(8,128)S(1)}, f32[128,128]{1,0:T(8,128)S(1)}, u32[]{:S(2)}, u32[]{:S(2)}) %collective-permute-start.4) | collective-permute-done | bytes 65568 | tf_op jit(solution)/shard_map/ppermute | solution.py:23
  45.3 1.8 %collective-permute-start.5 = (bf16[128,128]{1,0:T(8,128)(2,1)S(1)}, bf16[128,128]{1,0:T(8,128)(2,1)S(1)}, u32[]{:S(2)}, u32[]{:S(2)}) collective-permute-start(bf16[128,128]{1,0:T(8,128)(2,1)S(1)} %multiply_convert_fusion.2), channel_id=1, source_target_pairs={{0,32},{32,64},{64,96},{96,0},{1,33},{33,65},{65,97},{97,1},{2,34}... | collective-permute-start | bytes 98312 | tf_op jit(solution)/shard_map/ppermute | solution.py:23
  47.0 2.7 %collective-permute-start.6 = (bf16[128,128]{1,0:T(8,128)(2,1)S(1)}, bf16[128,128]{1,0:T(8,128)(2,1)S(1)}, u32[]{:S(2)}, u32[]{:S(2)}) collective-permute-start(bf16[128,128]{1,0:T(8,128)(2,1)S(1)} %multiply_convert_fusion.2), channel_id=1, source_target_pairs={{0,64},{32,96},{64,0},{96,32},{1,65},{33,97},{65,1},{97,33},{2,66}... | collective-permute-start | bytes 98312 | tf_op jit(solution)/shard_map/ppermute | solution.py:23
  49.8 1.4 %collective-permute-start.7 = (bf16[128,128]{1,0:T(8,128)(2,1)S(1)}, bf16[128,128]{1,0:T(8,128)(2,1)S(1)}, u32[]{:S(2)}, u32[]{:S(2)}) collective-permute-start(bf16[128,128]{1,0:T(8,128)(2,1)S(1)} %multiply_convert_fusion.2), channel_id=1, source_target_pairs={{0,96},{32,0},{64,32},{96,64},{1,97},{33,1},{65,33},{97,65},{2,98}... | collective-permute-start | bytes 98312 | tf_op jit(solution)/shard_map/ppermute | solution.py:23
  51.2 4.0 %grad.2.refs_0_ = bf16[1792,512]{1,0:T(8,128)(2,1)} custom-call(bf16[128,896]{1,0:T(8,128)(2,1)S(1)} %collective-permute-done.refs_0_, bf16[128,896]{1,0:T(8,128)(2,1)S(1)} %collective-permute-done.1.refs_1_, bf16[128,896]{1,0:T(8,128)(2,1)} %collective-permute-done.2.refs_2_, bf16[128,896]{1,0:T(8,128)(2,1)S(1)} %collective-permute-done.3.refs_3_, ...), custom_call_target="tpu_custom_call" | custom-call | tf_op jit(solution)/shard_map/grad/pallas_call | solution.py:132
  55.7 3.5 %collective-permute-done.6 = bf16[128,128]{1,0:T(8,128)(2,1)S(1)} collective-permute-done((bf16[128,128]{1,0:T(8,128)(2,1)S(1)}, bf16[128,128]{1,0:T(8,128)(2,1)S(1)}, u32[]{:S(2)}, u32[]{:S(2)}) %collective-permute-start.6) | collective-permute-done | bytes 32800 | tf_op jit(solution)/shard_map/ppermute | solution.py:23
  59.9 4.7 %all-to-all-start.1 = ((bf16[16,112,512]{2,1,0:T(8,128)(2,1)}), bf16[16,112,512]{2,1,0:T(8,128)(2,1)S(1)}, u32[]{:S(2)}, u32[]{:S(2)}) async-start(bf16[16,112,512]{2,1,0:T(8,128)(2,1)} %bitcast.12), calls=%async_computation.1 | async-start | bytes 3670016 | tf_op jit(solution)/shard_map/all_to_all | solution.py:195
  65.3 1.0 collective-permute-start.11
  66.3 1.0 collective-permute-start.13
  67.3 1.8 %convert_reduce_fusion.1 = f32[112,512]{1,0:T(8,128)S(1)} fusion(bf16[16,112,512]{2,1,0:T(8,128)(2,1)} %all-to-all-done.2), kind=kLoop, calls=%fused_computation.1 | loop fusion | flops 1777664 | bytes 2064384 | tf_op jit(solution)/shard_map/reduce_sum | solution.py:199
  69.1 6.5 %collective-permute-start.18 = (bf16[112,512]{1,0:T(8,128)(2,1)S(1)}, bf16[112,512]{1,0:T(8,128)(2,1)S(1)}, u32[]{:S(2)}, u32[]{:S(2)}) collective-permute-start(bf16[112,512]{1,0:T(8,128)(2,1)S(1)} %convert_element_type.29), channel_id=1, source_target_pairs={{0,128},{128,0},{1,129},{129,1},{2,130},{130,2},{3,131},{131,3},{4... | collective-permute-start | bytes 344072 | tf_op jit(solution)/shard_map/ppermute | solution.py:23
  76.6 4.6 %collective-permute-done.18 = bf16[112,512]{1,0:T(8,128)(2,1)S(1)} collective-permute-done((bf16[112,512]{1,0:T(8,128)(2,1)S(1)}, bf16[112,512]{1,0:T(8,128)(2,1)S(1)}, u32[]{:S(2)}, u32[]{:S(2)}) %collective-permute-start.18) | collective-permute-done | bytes 114720 | tf_op jit(solution)/shard_map/ppermute | solution.py:23
  81.3 5.4 %all-to-all-done.1.refs_0_ = bf16[16,112,512]{2,1,0:T(8,128)(2,1)S(1)} async-done(((bf16[16,112,512]{2,1,0:T(8,128)(2,1)}), bf16[16,112,512]{2,1,0:T(8,128)(2,1)S(1)}, u32[]{:S(2)}, u32[]{:S(2)}) %all-to-all-start.1) | async-done | bytes 1835040 | tf_op jit(solution)/shard_map/all_to_all | solution.py:195
  87.0 4.5 %collective-permute-start.19 = (bf16[112,512]{1,0:T(8,128)(2,1)S(1)}, bf16[112,512]{1,0:T(8,128)(2,1)S(1)}, u32[]{:S(2)}, u32[]{:S(2)}) collective-permute-start(bf16[112,512]{1,0:T(8,128)(2,1)S(1)} %convert_element_type.33), channel_id=1, source_target_pairs={{0,128},{128,0},{1,129},{129,1},{2,130},{130,2},{3,131},{131,3},{4... | collective-permute-start | bytes 344072 | tf_op jit(solution)/shard_map/ppermute | solution.py:23
  91.5 1.9 %collective-permute-start.23 = (bf16[112,512]{1,0:T(8,128)(2,1)S(1)}, bf16[112,512]{1,0:T(8,128)(2,1)S(1)}, u32[]{:S(2)}, u32[]{:S(2)}) collective-permute-start(bf16[112,512]{1,0:T(8,128)(2,1)S(1)} %multiply_convert_fusion.1.refs_9_.refs_0_), channel_id=1, source_target_pairs={{0,16},{8,24},{16,0},{24,8},{1,17},{9,25},{17,1},{25,9},{2,18},{10... | collective-permute-start | bytes 344072 | tf_op jit(solution)/shard_map/ppermute | solution.py:23
  93.7 3.0 %collective-permute-start.25 = (bf16[112,512]{1,0:T(8,128)(2,1)S(1)}, bf16[112,512]{1,0:T(8,128)(2,1)S(1)}, u32[]{:S(2)}, u32[]{:S(2)}) collective-permute-start(bf16[112,512]{1,0:T(8,128)(2,1)S(1)} %multiply_convert_fusion.1.refs_9_.refs_0_), channel_id=1, source_target_pairs={{0,24},{8,0},{16,8},{24,16},{1,25},{9,1},{17,9},{25,17},{2,26},{10... | collective-permute-start | bytes 344072 | tf_op jit(solution)/shard_map/ppermute | solution.py:23
  96.9 1.7 %collective-permute-start.20 = (bf16[112,512]{1,0:T(8,128)(2,1)S(1)}, bf16[112,512]{1,0:T(8,128)(2,1)S(1)}, u32[]{:S(2)}, u32[]{:S(2)}) collective-permute-start(bf16[112,512]{1,0:T(8,128)(2,1)S(1)} %multiply_convert_fusion.refs_0_), channel_id=1, source_target_pairs={{0,16},{8,24},{16,0},{24,8},{1,17},{9,25},{17,1},{25,9},{2,18},{10... | collective-permute-start | bytes 344072 | tf_op jit(solution)/shard_map/ppermute | solution.py:23
  98.9 3.0 %collective-permute-start.22 = (bf16[112,512]{1,0:T(8,128)(2,1)S(1)}, bf16[112,512]{1,0:T(8,128)(2,1)S(1)}, u32[]{:S(2)}, u32[]{:S(2)}) collective-permute-start(bf16[112,512]{1,0:T(8,128)(2,1)S(1)} %multiply_convert_fusion.refs_0_), channel_id=1, source_target_pairs={{0,24},{8,0},{16,8},{24,16},{1,25},{9,1},{17,9},{25,17},{2,26},{10... | collective-permute-start | bytes 344072 | tf_op jit(solution)/shard_map/ppermute | solution.py:23
  101.9 1.0 correct.2.refs_8_
  103.3 1.4 %collective-permute-done.21.refs_2_ = bf16[112,512]{1,0:T(8,128)(2,1)S(1)} collective-permute-done((bf16[112,512]{1,0:T(8,128)(2,1)S(1)}, bf16[112,512]{1,0:T(8,128)(2,1)S(1)}, u32[]{:S(2)}, u32[]{:S(2)}) %collective-permute-start.21) | collective-permute-done | bytes 114720 | tf_op jit(solution)/shard_map/ppermute | solution.py:23
  104.6 1.0 correct.3
  105.6 13.5 %all_to_all.20 = f32[4,448,128]{2,1,0:T(8,128)S(1)} all-to-all(f32[4,448,128]{2,1,0:T(8,128)S(1)} %correct.3), channel_id=1, replica_groups=mesh['z_hi'=2,'x'=4,'y'=4,'z_lo'=4,'core'=2] {'x'}, dimensions={0} | all-to-all | bytes 1835008 | tf_op jit(solution)/shard_map/all_to_all | solution.py:262
  119.2 0.9 copy.12
  (47 shorter events, 6.0 us)
Async XLA Ops:
  0.0 15.7 %copy-start = (bf16[896,1792]{1,0:T(8,128)(2,1)S(1)}, bf16[896,1792]{1,0:T(8,128)(2,1)}, u32[]{:S(2)}) copy-start(bf16[896,1792]{1,0:T(8,128)(2,1)} %refs_4_.3) | copy-start | bytes 9633796
  4.5 9.2 %collective-permute-start.16 = (bf16[128,896]{1,0:T(8,128)(2,1)}, bf16[128,896]{1,0:T(8,128)(2,1)}, u32[]{:S(2)}, u32[]{:S(2)}) collective-permute-start(bf16[128,896]{1,0:T(8,128)(2,1)} %get-tuple-element.9.refs_0_), channel_id=1, source_target_pairs={{0,2},{2,4},{4,6},{6,0},{1,3},{3,5},{5,7},{7,1},{8,10},{10,12},{12... | collective-permute-start | bytes 688136 | tf_op jit(solution)/shard_map/ppermute | solution.py:23
  6.5 24.4 %all-to-all-start = ((bf16[16,128,256]{2,1,0:T(8,128)(2,1)}), bf16[16,128,256]{2,1,0:T(8,128)(2,1)}, u32[]{:S(2)}, u32[]{:S(2)}) async-start(bf16[16,128,256]{2,1,0:T(8,128)(2,1)} %get-tuple-element.10), calls=%async_computation | async-start | bytes 2097152 | tf_op jit(solution)/shard_map/all_to_all | solution.py:159
  13.6 2.1 %collective-permute-start.15 = (bf16[128,896]{1,0:T(8,128)(2,1)}, bf16[128,896]{1,0:T(8,128)(2,1)S(1)}, u32[]{:S(2)}, u32[]{:S(2)}) collective-permute-start(bf16[128,896]{1,0:T(8,128)(2,1)} %get-tuple-element.9.refs_0_), channel_id=1, source_target_pairs={{0,1},{1,0},{2,3},{3,2},{4,5},{5,4},{6,7},{7,6},{8,9},{9,8},{10,11... | collective-permute-start | bytes 688136 | tf_op jit(solution)/shard_map/ppermute | solution.py:23
  13.7 2.0 %collective-permute-start.17 = (bf16[128,896]{1,0:T(8,128)(2,1)}, bf16[128,896]{1,0:T(8,128)(2,1)S(1)}, u32[]{:S(2)}, u32[]{:S(2)}) collective-permute-start(bf16[128,896]{1,0:T(8,128)(2,1)} %collective-permute-done.16.refs_2_), channel_id=1, source_target_pairs={{0,1},{1,0},{2,3},{3,2},{4,5},{5,4},{6,7},{7,6},{8,9},{9,8},{10,11... | collective-permute-start | bytes 688136 | tf_op jit(solution)/shard_map/ppermute | solution.py:23
  14.2 27.1 %collective-permute-start = (bf16[128,896]{1,0:T(8,128)(2,1)}, bf16[128,896]{1,0:T(8,128)(2,1)S(1)}, u32[]{:S(2)}, u32[]{:S(2)}) collective-permute-start(bf16[128,896]{1,0:T(8,128)(2,1)} %get-tuple-element.9.refs_0_), channel_id=1, source_target_pairs={{0,4},{2,6},{4,0},{6,2},{1,5},{3,7},{5,1},{7,3},{8,12},{10,14},{12... | collective-permute-start | bytes 688136 | tf_op jit(solution)/shard_map/ppermute | solution.py:23
  14.8 26.5 %collective-permute-start.2 = (bf16[128,896]{1,0:T(8,128)(2,1)}, bf16[128,896]{1,0:T(8,128)(2,1)}, u32[]{:S(2)}, u32[]{:S(2)}) collective-permute-start(bf16[128,896]{1,0:T(8,128)(2,1)} %get-tuple-element.9.refs_0_), channel_id=1, source_target_pairs={{0,6},{2,0},{4,2},{6,4},{1,7},{3,1},{5,3},{7,5},{8,14},{10,8},{12,... | collective-permute-start | bytes 688136 | tf_op jit(solution)/shard_map/ppermute | solution.py:23
  30.9 29.0 %all-to-all-start.2 = ((bf16[16,112,512]{2,1,0:T(8,128)(2,1)}), bf16[16,112,512]{2,1,0:T(8,128)(2,1)}, u32[]{:S(2)}, u32[]{:S(2)}) async-start(bf16[16,112,512]{2,1,0:T(8,128)(2,1)} %bitcast.14), calls=%async_computation.2 | async-start | bytes 3670016 | tf_op jit(solution)/shard_map/all_to_all | solution.py:195
  36.7 8.5 %collective-permute-start.4 = (f32[128,128]{1,0:T(8,128)S(1)}, f32[128,128]{1,0:T(8,128)S(1)}, u32[]{:S(2)}, u32[]{:S(2)}) collective-permute-start(f32[128,128]{1,0:T(8,128)S(1)} %get-tuple-element.12), channel_id=1, source_target_pairs={{0,128},{128,0},{1,129},{129,1},{2,130},{130,2},{3,131},{131,3},{4... | collective-permute-start | bytes 196616 | tf_op jit(solution)/shard_map/ppermute | solution.py:23
  41.3 9.9 %collective-permute-start.1 = (bf16[128,896]{1,0:T(8,128)(2,1)S(1)}, bf16[128,896]{1,0:T(8,128)(2,1)S(1)}, u32[]{:S(2)}, u32[]{:S(2)}) collective-permute-start(bf16[128,896]{1,0:T(8,128)(2,1)S(1)} %collective-permute-done.refs_0_), channel_id=1, source_target_pairs={{0,1},{1,0},{2,3},{3,2},{4,5},{5,4},{6,7},{7,6},{8,9},{9,8},{10,11... | collective-permute-start | bytes 688136 | tf_op jit(solution)/shard_map/ppermute | solution.py:23
  41.3 9.9 %collective-permute-start.3 = (bf16[128,896]{1,0:T(8,128)(2,1)}, bf16[128,896]{1,0:T(8,128)(2,1)S(1)}, u32[]{:S(2)}, u32[]{:S(2)}) collective-permute-start(bf16[128,896]{1,0:T(8,128)(2,1)} %collective-permute-done.2.refs_2_), channel_id=1, source_target_pairs={{0,1},{1,0},{2,3},{3,2},{4,5},{5,4},{6,7},{7,6},{8,9},{9,8},{10,11... | collective-permute-start | bytes 688136 | tf_op jit(solution)/shard_map/ppermute | solution.py:23
  45.3 10.4 %collective-permute-start.5 = (bf16[128,128]{1,0:T(8,128)(2,1)S(1)}, bf16[128,128]{1,0:T(8,128)(2,1)S(1)}, u32[]{:S(2)}, u32[]{:S(2)}) collective-permute-start(bf16[128,128]{1,0:T(8,128)(2,1)S(1)} %multiply_convert_fusion.2), channel_id=1, source_target_pairs={{0,32},{32,64},{64,96},{96,0},{1,33},{33,65},{65,97},{97,1},{2,34}... | collective-permute-start | bytes 98312 | tf_op jit(solution)/shard_map/ppermute | solution.py:23
  47.0 12.1 %collective-permute-start.6 = (bf16[128,128]{1,0:T(8,128)(2,1)S(1)}, bf16[128,128]{1,0:T(8,128)(2,1)S(1)}, u32[]{:S(2)}, u32[]{:S(2)}) collective-permute-start(bf16[128,128]{1,0:T(8,128)(2,1)S(1)} %multiply_convert_fusion.2), channel_id=1, source_target_pairs={{0,64},{32,96},{64,0},{96,32},{1,65},{33,97},{65,1},{97,33},{2,66}... | collective-permute-start | bytes 98312 | tf_op jit(solution)/shard_map/ppermute | solution.py:23
  49.8 9.4 %collective-permute-start.7 = (bf16[128,128]{1,0:T(8,128)(2,1)S(1)}, bf16[128,128]{1,0:T(8,128)(2,1)S(1)}, u32[]{:S(2)}, u32[]{:S(2)}) collective-permute-start(bf16[128,128]{1,0:T(8,128)(2,1)S(1)} %multiply_convert_fusion.2), channel_id=1, source_target_pairs={{0,96},{32,0},{64,32},{96,64},{1,97},{33,1},{65,33},{97,65},{2,98}... | collective-permute-start | bytes 98312 | tf_op jit(solution)/shard_map/ppermute | solution.py:23
  59.9 26.8 %all-to-all-start.1 = ((bf16[16,112,512]{2,1,0:T(8,128)(2,1)}), bf16[16,112,512]{2,1,0:T(8,128)(2,1)S(1)}, u32[]{:S(2)}, u32[]{:S(2)}) async-start(bf16[16,112,512]{2,1,0:T(8,128)(2,1)} %bitcast.12), calls=%async_computation.1 | async-start | bytes 3670016 | tf_op jit(solution)/shard_map/all_to_all | solution.py:195
  64.7 10.9 %collective-permute-start.9 = (bf16[4,128,128]{2,1,0:T(8,128)(2,1)S(1)}, bf16[4,128,128]{2,1,0:T(8,128)(2,1)S(1)}, u32[]{:S(2)}, u32[]{:S(2)}) collective-permute-start(bf16[4,128,128]{2,1,0:T(8,128)(2,1)S(1)} %pad_maximum_fusion.refs_1_.refs_4_), channel_id=1, source_target_pairs={{0,2},{2,4},{4,6},{6,0},{1,3},{3,5},{5,7},{7,1},{8,10},{10,12},{12... | collective-permute-start | bytes 393224 | tf_op jit(solution)/shard_map/ppermute | solution.py:23
  65.3 10.8 %collective-permute-start.11 = (bf16[4,128,128]{2,1,0:T(8,128)(2,1)S(1)}, bf16[4,128,128]{2,1,0:T(8,128)(2,1)S(1)}, u32[]{:S(2)}, u32[]{:S(2)}) collective-permute-start(bf16[4,128,128]{2,1,0:T(8,128)(2,1)S(1)} %pad_maximum_fusion.refs_1_.refs_4_), channel_id=1, source_target_pairs={{0,4},{2,6},{4,0},{6,2},{1,5},{3,7},{5,1},{7,3},{8,12},{10,14},{12... | collective-permute-start | bytes 393224 | tf_op jit(solution)/shard_map/ppermute | solution.py:23
  66.3 9.9 %collective-permute-start.13 = (bf16[4,128,128]{2,1,0:T(8,128)(2,1)S(1)}, bf16[4,128,128]{2,1,0:T(8,128)(2,1)S(1)}, u32[]{:S(2)}, u32[]{:S(2)}) collective-permute-start(bf16[4,128,128]{2,1,0:T(8,128)(2,1)S(1)} %pad_maximum_fusion.refs_1_.refs_4_), channel_id=1, source_target_pairs={{0,6},{2,0},{4,2},{6,4},{1,7},{3,1},{5,3},{7,5},{8,14},{10,8},{12,... | collective-permute-start | bytes 393224 | tf_op jit(solution)/shard_map/ppermute | solution.py:23
  69.1 12.1 %collective-permute-start.18 = (bf16[112,512]{1,0:T(8,128)(2,1)S(1)}, bf16[112,512]{1,0:T(8,128)(2,1)S(1)}, u32[]{:S(2)}, u32[]{:S(2)}) collective-permute-start(bf16[112,512]{1,0:T(8,128)(2,1)S(1)} %convert_element_type.29), channel_id=1, source_target_pairs={{0,128},{128,0},{1,129},{129,1},{2,130},{130,2},{3,131},{131,3},{4... | collective-permute-start | bytes 344072 | tf_op jit(solution)/shard_map/ppermute | solution.py:23
  75.6 5.7 %collective-permute-start.8 = (bf16[4,128,128]{2,1,0:T(8,128)(2,1)S(1)}, bf16[4,128,128]{2,1,0:T(8,128)(2,1)S(1)}, u32[]{:S(2)}, u32[]{:S(2)}) collective-permute-start(bf16[4,128,128]{2,1,0:T(8,128)(2,1)S(1)} %pad_maximum_fusion.refs_1_.refs_4_), channel_id=1, source_target_pairs={{0,1},{1,0},{2,3},{3,2},{4,5},{5,4},{6,7},{7,6},{8,9},{9,8},{10,11... | collective-permute-start | bytes 393224 | tf_op jit(solution)/shard_map/ppermute | solution.py:23
  75.6 5.7 %collective-permute-start.10 = (bf16[4,128,128]{2,1,0:T(8,128)(2,1)S(1)}, bf16[4,128,128]{2,1,0:T(8,128)(2,1)S(1)}, u32[]{:S(2)}, u32[]{:S(2)}) collective-permute-start(bf16[4,128,128]{2,1,0:T(8,128)(2,1)S(1)} %collective-permute-done.9.refs_3_.refs_6_), channel_id=1, source_target_pairs={{0,1},{1,0},{2,3},{3,2},{4,5},{5,4},{6,7},{7,6},{8,9},{9,8},{10,11... | collective-permute-start | bytes 393224 | tf_op jit(solution)/shard_map/ppermute | solution.py:23
  76.1 5.2 %collective-permute-start.12 = (bf16[4,128,128]{2,1,0:T(8,128)(2,1)S(1)}, bf16[4,128,128]{2,1,0:T(8,128)(2,1)S(1)}, u32[]{:S(2)}, u32[]{:S(2)}) collective-permute-start(bf16[4,128,128]{2,1,0:T(8,128)(2,1)S(1)} %collective-permute-done.11.refs_5_.refs_4_), channel_id=1, source_target_pairs={{0,1},{1,0},{2,3},{3,2},{4,5},{5,4},{6,7},{7,6},{8,9},{9,8},{10,11... | collective-permute-start | bytes 393224 | tf_op jit(solution)/shard_map/ppermute | solution.py:23
  76.2 5.1 %collective-permute-start.14 = (bf16[4,128,128]{2,1,0:T(8,128)(2,1)S(1)}, bf16[4,128,128]{2,1,0:T(8,128)(2,1)S(1)}, u32[]{:S(2)}, u32[]{:S(2)}) collective-permute-start(bf16[4,128,128]{2,1,0:T(8,128)(2,1)S(1)} %collective-permute-done.13.refs_7_.refs_6_), channel_id=1, source_target_pairs={{0,1},{1,0},{2,3},{3,2},{4,5},{5,4},{6,7},{7,6},{8,9},{9,8},{10,11... | collective-permute-start | bytes 393224 | tf_op jit(solution)/shard_map/ppermute | solution.py:23
  87.0 9.8 %collective-permute-start.19 = (bf16[112,512]{1,0:T(8,128)(2,1)S(1)}, bf16[112,512]{1,0:T(8,128)(2,1)S(1)}, u32[]{:S(2)}, u32[]{:S(2)}) collective-permute-start(bf16[112,512]{1,0:T(8,128)(2,1)S(1)} %convert_element_type.33), channel_id=1, source_target_pairs={{0,128},{128,0},{1,129},{129,1},{2,130},{130,2},{3,131},{131,3},{4... | collective-permute-start | bytes 344072 | tf_op jit(solution)/shard_map/ppermute | solution.py:23
  91.5 7.3 %collective-permute-start.23 = (bf16[112,512]{1,0:T(8,128)(2,1)S(1)}, bf16[112,512]{1,0:T(8,128)(2,1)S(1)}, u32[]{:S(2)}, u32[]{:S(2)}) collective-permute-start(bf16[112,512]{1,0:T(8,128)(2,1)S(1)} %multiply_convert_fusion.1.refs_9_.refs_0_), channel_id=1, source_target_pairs={{0,16},{8,24},{16,0},{24,8},{1,17},{9,25},{17,1},{25,9},{2,18},{10... | collective-permute-start | bytes 344072 | tf_op jit(solution)/shard_map/ppermute | solution.py:23
  93.4 8.5 %collective-permute-start.24 = (bf16[112,512]{1,0:T(8,128)(2,1)S(1)}, bf16[112,512]{1,0:T(8,128)(2,1)S(1)}, u32[]{:S(2)}, u32[]{:S(2)}) collective-permute-start(bf16[112,512]{1,0:T(8,128)(2,1)S(1)} %multiply_convert_fusion.1.refs_9_.refs_0_), channel_id=1, source_target_pairs={{0,8},{8,16},{16,24},{24,0},{1,9},{9,17},{17,25},{25,1},{2,10},{10... | collective-permute-start | bytes 344072 | tf_op jit(solution)/shard_map/ppermute | solution.py:23
  93.7 8.2 %collective-permute-start.25 = (bf16[112,512]{1,0:T(8,128)(2,1)S(1)}, bf16[112,512]{1,0:T(8,128)(2,1)S(1)}, u32[]{:S(2)}, u32[]{:S(2)}) collective-permute-start(bf16[112,512]{1,0:T(8,128)(2,1)S(1)} %multiply_convert_fusion.1.refs_9_.refs_0_), channel_id=1, source_target_pairs={{0,24},{8,0},{16,8},{24,16},{1,25},{9,1},{17,9},{25,17},{2,26},{10... | collective-permute-start | bytes 344072 | tf_op jit(solution)/shard_map/ppermute | solution.py:23
  96.9 6.4 %collective-permute-start.20 = (bf16[112,512]{1,0:T(8,128)(2,1)S(1)}, bf16[112,512]{1,0:T(8,128)(2,1)S(1)}, u32[]{:S(2)}, u32[]{:S(2)}) collective-permute-start(bf16[112,512]{1,0:T(8,128)(2,1)S(1)} %multiply_convert_fusion.refs_0_), channel_id=1, source_target_pairs={{0,16},{8,24},{16,0},{24,8},{1,17},{9,25},{17,1},{25,9},{2,18},{10... | collective-permute-start | bytes 344072 | tf_op jit(solution)/shard_map/ppermute | solution.py:23
  98.6 6.0 %collective-permute-start.21 = (bf16[112,512]{1,0:T(8,128)(2,1)S(1)}, bf16[112,512]{1,0:T(8,128)(2,1)S(1)}, u32[]{:S(2)}, u32[]{:S(2)}) collective-permute-start(bf16[112,512]{1,0:T(8,128)(2,1)S(1)} %multiply_convert_fusion.refs_0_), channel_id=1, source_target_pairs={{0,8},{8,16},{16,24},{24,0},{1,9},{9,17},{17,25},{25,1},{2,10},{10... | collective-permute-start | bytes 344072 | tf_op jit(solution)/shard_map/ppermute | solution.py:23
  98.9 5.8 %collective-permute-start.22 = (bf16[112,512]{1,0:T(8,128)(2,1)S(1)}, bf16[112,512]{1,0:T(8,128)(2,1)S(1)}, u32[]{:S(2)}, u32[]{:S(2)}) collective-permute-start(bf16[112,512]{1,0:T(8,128)(2,1)S(1)} %multiply_convert_fusion.refs_0_), channel_id=1, source_target_pairs={{0,24},{8,0},{16,8},{24,16},{1,25},{9,1},{17,9},{25,17},{2,26},{10... | collective-permute-start | bytes 344072 | tf_op jit(solution)/shard_map/ppermute | solution.py:23

commit v14 on v13

--- a/solution.py
+++ b/solution.py
@@ -10,7 +10,7 @@
 SIZES = (2, 4, 4, 4, 2)
 DP = ("z_hi", "x", "y")
 TENSOR = ("z_lo", "core")
-Y_STEPS = (2, 1, 3)
+ROW_STEPS = (2, 1, 3)
 SMEM = pl.BlockSpec(memory_space=pltpu.SMEM)
 VMEM = pl.BlockSpec(memory_space=pltpu.VMEM)
 ANY = pl.BlockSpec(memory_space=pl.ANY)
@@ -21,6 +21,25 @@
 def shifted(value, axis, step):
     size = SIZES[AXES.index(axis)]
     return lax.ppermute(value, axis, [(i, (i + step) % size) for i in range(size)])
+
+
+def shifted_by_core(value, axis, step):
+    pairs = []
+    for x in range(4):
+        for y in range(4):
+            for core in range(2):
+                along_x = (axis == "x") == (core == 0)
+                to_x, to_y = ((x + step) % 4, y) if along_x else (x, (y + step) % 4)
+                pairs.append((x * 8 + y * 2 + core, to_x * 8 + to_y * 2 + core))
+    return lax.ppermute(value, ("x", "y", "core"), pairs)
+
+
+def swapped_by_core(value):
+    groups = [[x * 8 + y * 2 for x in range(4)] for y in range(4)]
+    groups += [[x * 8 + y * 2 + 1 for y in range(4)] for x in range(4)]
+    return lax.all_to_all(
+        value, ("x", "y", "core"), 0, 0, tiled=True, axis_index_groups=groups
+    )
 
 
 def first_kernel(place, gain, gate_at, grad_at, hidden_at, basis_at, out_at, up_at,
@@ -171,7 +190,7 @@
     )(place, got)
     total = kept + shifted(given, "z_hi", 1)
     square = (total * total).astype(jnp.bfloat16)
-    return [square] + [shifted(square, "x", step) for step in (1, 2, 3)]
+    return square
 
 
 def gate_kernel(*refs):
@@ -195,40 +214,48 @@
     return lax.all_to_all(partial.reshape(16, columns // 16, tokens), ("x", "y"), 0, 0, tiled=True)
 
 
-def squared(got):
-    summed = jnp.sum(got.astype(jnp.float32), axis=0)
+def doubled(summed):
     total = summed + shifted(summed.astype(jnp.bfloat16), "z_hi", 1).astype(jnp.float32)
     return (total * total).astype(jnp.bfloat16)
 
 
-def correct_kernel(place, *refs):
+def squared(got):
+    return doubled(jnp.sum(got.astype(jnp.float32), axis=0))
+
+
+def correct_kernel(steps, place, *refs):
     pieces, acts, before, (out, act, both) = refs[:4], refs[4:8], refs[8:-3], refs[-3:]
-    _, tokens, block = acts[0].shape
-    for i, part in enumerate(acts):
-        for behind in range(4):
-            here = slice(i * tokens, (i + 1) * tokens), slice(behind * block, (behind + 1) * block)
-            act[here] = part[behind]
+    chips, cores, tokens, block = acts[0].shape
+    for behind, part in enumerate(acts):
+        to = slice(behind * block, (behind + 1) * block)
+        for i, step in enumerate(steps):
+            for core in range(cores):
+                at = (i * cores + core) * tokens
+                act[at : at + tokens, to] = part[step, core]
     rows = pieces[0].shape[0]
     for i, piece in enumerate(pieces):
         both[i * rows : (i + 1) * rows, :] = piece[...]
     every = jnp.dot(both[...], act[...], preferred_element_type=jnp.float32)
-    every = every * (1.0 / (8 * tokens))
-    for i, y_behind in enumerate((0, *Y_STEPS)):
-        at = pl.ds(pl.multiple_of(lax.rem(place[1] + 4 - y_behind, 4) * rows, rows), rows)
+    every = every * (1.0 / (chips * cores * tokens))
+    for i, row_behind in enumerate((0, *ROW_STEPS)):
+        at = pl.ds(pl.multiple_of(lax.rem(place[1] + 4 - row_behind, 4) * rows, rows), rows)
         for behind in range(4):
-            x = lax.rem(place[0] + 4 - behind, 4)
+            owner = lax.rem(place[0] + 4 - behind, 4)
             here = every[i * rows : (i + 1) * rows, behind * block : (behind + 1) * block]
             if before:
-                here = before[0][x, at, :] + here
-            out[x, at, :] = here
-
-
-def corrected(pieces, acts, *before):
+                here = before[0][owner, at, :] + here
+            out[owner, at, :] = here
+
+
+def spread(grad_sq):
+    return [grad_sq] + [shifted_by_core(grad_sq, "y", step) for step in ROW_STEPS]
+
+
+def corrected(steps, place, pieces, acts, *before):
     rows, tokens = pieces[0].shape
-    block = acts[0].shape[2]
-    place = jnp.stack([lax.axis_index("x"), lax.axis_index("y")]).astype(jnp.int32)
-    return pl.pallas_call(
-        correct_kernel,
+    block = acts[0].shape[3]
+    return pl.pallas_call(
+        lambda *refs: correct_kernel(steps, *refs),
         out_shape=jax.ShapeDtypeStruct((4, 4 * rows, block), jnp.float32),
         in_specs=[SMEM] + [VMEM] * (8 + len(before)),
         out_specs=VMEM,
@@ -241,26 +268,62 @@
     )(place, *pieces, *acts, *before)
 
 
+def order_kernel(place, got, out, sems):
+    rows = got.shape[1] // 4
+    copies = []
+    for sender in range(4):
+        for piece in range(4):
+            to = jnp.where(place[2] == 0, sender * 4 + piece, piece * 4 + sender) * rows
+            copies.append(
+                pltpu.make_async_copy(
+                    got.at[sender, pl.ds(piece * rows, rows)],
+                    out.at[pl.ds(pl.multiple_of(to, rows), rows)],
+                    sems.at[sender * 4 + piece],
+                )
+            )
+            copies[-1].start()
+    for copy in copies:
+        copy.wait()
+
+
+def ordered(place, got):
+    return pl.pallas_call(
+        order_kernel,
+        out_shape=jax.ShapeDtypeStruct((4 * got.shape[1], got.shape[2]), got.dtype),
+        in_specs=[SMEM, ANY],
+        out_specs=ANY,
+        scratch_shapes=[pltpu.SemaphoreType.DMA((16,))],
+        compiler_params=PARAMS,
+        name="order",
+    )(place, got)
+
+
 def per_device(hidden, norm_gain, gate_pre, out_grad, grad_basis, act_basis):
+    x, y, core = [lax.axis_index(axis) for axis in ("x", "y", "core")]
+    on_first = core == 0
+    place = jnp.stack([jnp.where(on_first, x, y), jnp.where(on_first, y, x), core])
+    place = place.astype(jnp.int32)
     act_parts, up_grad = first_partials(hidden, norm_gain, gate_pre, out_grad, act_basis)
     near, far, farthest = [shifted(up_grad, "z_lo", step) for step in (1, 2, 3)]
     near_rows = [up_grad, shifted(up_grad, "core", 1), near, shifted(near, "core", 1)]
     far_rows = [far, shifted(far, "core", 1), farthest, shifted(farthest, "core", 1)]
-    act_row = act_squares(act_parts)
+    act_own = act_squares(act_parts)
     cost = pl.CostEstimate(flops=8 * 10**9, bytes_accessed=10**7, transcendentals=0)
     near_got = exchanged(grad_partials(near_rows, grad_basis, (), cost))
-    act_own = jnp.stack(act_row)
-    far_got = exchanged(gated(grad_partials(far_rows, grad_basis), [act_own]))
-    acts = []
-    for own in [act_own] + [shifted(act_own, "z_lo", step) for step in (1, 2, 3)]:
-        acts += [own, shifted(own, "core", 1)]
+    act_chip = jnp.stack([act_own, shifted(act_own, "core", 1)])
+    act_all = jnp.stack(
+        [act_chip] + [shifted(act_chip, "z_lo", step) for step in (1, 2, 3)]
+    )
+    far_got = exchanged(gated(grad_partials(far_rows, grad_basis), [act_all]))
     near_sq = squared(near_got)
-    near_pieces = [near_sq] + [shifted(near_sq, "y", step) for step in Y_STEPS]
-    far_sq = squared(gated(far_got, acts + [near_sq], jax.ShapeDtypeStruct))
-    far_pieces = [far_sq] + [shifted(far_sq, "y", step) for step in Y_STEPS]
-    out = corrected(far_pieces, acts[4:], corrected(near_pieces, acts[:4]))
-    out = lax.all_to_all(out, "x", 0, 0, tiled=True)
-    return out.reshape(grad_basis.shape[1], -1)
+    far_got = gated(far_got, [near_sq], jax.ShapeDtypeStruct)
+    far_sum = jnp.sum(far_got.astype(jnp.float32), axis=0)
+    far_sq = doubled(far_sum)
+    act_all = gated(act_all, [far_sum], jax.ShapeDtypeStruct)
+    acts = [act_all] + [shifted_by_core(act_all, "x", step) for step in (1, 2, 3)]
+    out = corrected((0, 1), place, spread(near_sq), acts)
+    out = corrected((2, 3), place, spread(far_sq), acts, out)
+    return ordered(place, swapped_by_core(out))
 
 
 def solution(mesh):

time: 122 us -> 130 us (1.066)
  waiting for transfers between devices: 31.1 us -> 45.8 us
  starting transfers between devices: 56.1 us -> 49.7 us
  Pallas kernels: 15.9 us -> 17.5 us
    ppermute x26 -> x14, starting transfers between devices: 39.9 us -> 20.9 us  [shifted(): lax.ppermute(value, axis, [(i, (i + step) % size) for i in range(size)])]
    ppermute x0 -> x9, starting transfers between devices: none -> 12.8 us  [shifted_by_core(): return lax.ppermute(value, ('x', 'y', 'core'), pairs)]
    all_to_all x2, waiting for transfers between devices: 6.09 us -> 15.5 us  [exchanged(): lax.all_to_all(partial.reshape(16, columns // 16, tokens), ('x', 'y'), 0,...]
    ppermute x0 -> x9, waiting for transfers between devices: none -> 7.16 us  [shifted_by_core(): return lax.ppermute(value, ('x', 'y', 'core'), pairs)]
    ppermute x26 -> x14, waiting for transfers between devices: 13.9 us -> 12 us  [shifted(): lax.ppermute(value, axis, [(i, (i + step) % size) for i in range(size)])]
    pallas_call x2 -> x3, Pallas kernels: 2.01 us -> 3.59 us  [the longest x2 2.01 us: corrected(): pl.pallas_call(lambda *refs: correct_kernel(steps, *refs), out_shape=jax....]
  transfers between devices with their start and end apart: 29 -> 26, of which waited for: 10 -> 10; matrix products, arithmetic and copies ran while one was open for 2% -> 2% of each run, Pallas kernels for 9% -> 8%
where the time goes in v14:
time: 130 us; the launch traced here: 128 us
  starting transfers between devices  49.7 us (38%)
  waiting for transfers between devices  45.8 us (35%)
  Pallas kernels  17.5 us (13%)
  blocking collectives  12.6 us (10%)
  other arithmetic  2.26 us (2%)
    ppermute x14, starting transfers between devices, shifted(): lax.ppermute(value, axis, [(i, (i + step) % size) for i in range(size)])  20.9 us
    all_to_all x2, waiting for transfers between devices, exchanged(): lax.all_to_all(partial.reshape(16, columns // 16, tokens), ('x', 'y'), 0,...  15.5 us
    ppermute x9, starting transfers between devices, shifted_by_core(): return lax.ppermute(value, ('x', 'y', 'core'), pairs)  12.8 us
    all_to_all x1, blocking collectives, swapped_by_core(): lax.all_to_all(value, ('x', 'y', 'core'), 0, 0, tiled=True, axis_index_gr...  12.6 us
    ppermute x14, waiting for transfers between devices, shifted(): lax.ppermute(value, axis, [(i, (i + step) % size) for i in range(size)])  12 us
    all_to_all x1, waiting for transfers between devices, act_squares(): got = lax.all_to_all(partials, ('x', 'y'), 0, 0, tiled=True)  11.2 us
    all_to_all x2, starting transfers between devices, exchanged(): lax.all_to_all(partial.reshape(16, columns // 16, tokens), ('x', 'y'), 0,...  8.85 us
    pallas_call x2, Pallas kernels, grad_partials(): pl.pallas_call(lambda *refs: grad_kernel(len(parts), *refs), out_shape=pl...  8.02 us
  transfers between devices with their start and end apart: 26, of which 10 were waited for; matrix products, arithmetic and copies ran while one was open for 2% of the time, Pallas kernels for 8%

profile of v14, /device:TPU:64, one launch (start us, length us, event | category | flops | bytes accessed | tf_op | source)
XLA Modules:
  0.0 128.3 jit_solution(8430617869217228555)
XLA Ops:
  0.0 4.5 %first.1 = (bf16[16,128,256]{2,1,0:T(8,128)(2,1)}, bf16[128,896]{1,0:T(8,128)(2,1)}) custom-call(s32[1]{0:T(128)} %bitcast.3.place, f32[1,8192]{1,0:T(1,128)} %bitcast.21, bf16[128,896]{1,0:T(8,128)(2,1)} %gate_at.1, bf16[128,896]{1,0:T(8,128)(2,1)} %grad_at.1, bf16[128,8192]{1,0:T(8,128)(2,1)} %hidden_at.1, bf16[256,4096]{1,0:T(8,128)(2,1)} %basis_at.1), custom_call_target="tpu_custom_call" | custom-call | tf_op jit(solution)/shard_map/first/pallas_call | solution.py:109
  4.5 2.0 %collective-permute-start.10 = (bf16[128,896]{1,0:T(8,128)(2,1)}, bf16[128,896]{1,0:T(8,128)(2,1)}, u32[]{:S(2)}, u32[]{:S(2)}) collective-permute-start(bf16[128,896]{1,0:T(8,128)(2,1)} %get-tuple-element.9.refs_0_), channel_id=1, source_target_pairs={{0,2},{2,4},{4,6},{6,0},{1,3},{3,5},{5,7},{7,1},{8,10},{10,12},{12... | collective-permute-start | bytes 688136 | tf_op jit(solution)/shard_map/ppermute | solution.py:23
  6.5 7.1 %all-to-all-start = ((bf16[16,128,256]{2,1,0:T(8,128)(2,1)}), bf16[16,128,256]{2,1,0:T(8,128)(2,1)}, u32[]{:S(2)}, u32[]{:S(2)}) async-start(bf16[16,128,256]{2,1,0:T(8,128)(2,1)} %get-tuple-element.10), calls=%async_computation | async-start | bytes 2097152 | tf_op jit(solution)/shard_map/all_to_all | solution.py:178
  15.7 4.0 %grad.3 = bf16[1792,512]{1,0:T(8,128)(2,1)} custom-call(bf16[128,896]{1,0:T(8,128)(2,1)} %get-tuple-element.9.refs_0_, bf16[128,896]{1,0:T(8,128)(2,1)S(1)} %collective-permute-done.9.refs_1_, bf16[128,896]{1,0:T(8,128)(2,1)} %collective-permute-done.10.refs_2_, bf16[128,896]{1,0:T(8,128)(2,1)S(1)} %collective-permute-done.11.refs_3_, ...), custom_call_target="tpu_custom_call" | custom-call | flops 8000000000 | bytes 10000000 | tf_op jit(solution)/shard_map/grad/pallas_call | solution.py:151
  19.8 11.2 %all-to-all-done.got = bf16[16,128,256]{2,1,0:T(8,128)(2,1)} async-done(((bf16[16,128,256]{2,1,0:T(8,128)(2,1)}), bf16[16,128,256]{2,1,0:T(8,128)(2,1)}, u32[]{:S(2)}, u32[]{:S(2)}) %all-to-all-start) | async-done | bytes 1048608 | tf_op jit(solution)/shard_map/all_to_all | solution.py:178
  30.9 4.4 %all-to-all-start.2 = ((bf16[16,112,512]{2,1,0:T(8,128)(2,1)}), bf16[16,112,512]{2,1,0:T(8,128)(2,1)}, u32[]{:S(2)}, u32[]{:S(2)}) async-start(bf16[16,112,512]{2,1,0:T(8,128)(2,1)} %bitcast.16), calls=%async_computation.2 | async-start | bytes 3670016 | tf_op jit(solution)/shard_map/all_to_all | solution.py:214
  35.4 1.4 %act_sum.1 = (f32[128,128]{1,0:T(8,128)S(1)}, f32[128,128]{1,0:T(8,128)S(1)}) custom-call(s32[1]{0:T(128)} %bitcast.5.place, bf16[16,128,256]{2,1,0:T(8,128)(2,1)} %all-to-all-done.got), custom_call_target="tpu_custom_call" | custom-call | flops 20000000000 | bytes 1000000 | tf_op jit(solution)/shard_map/act_sum/pallas_call | solution.py:182
  36.7 4.6 %collective-permute-start.4 = (f32[128,128]{1,0:T(8,128)S(1)}, f32[128,128]{1,0:T(8,128)S(1)}, u32[]{:S(2)}, u32[]{:S(2)}) collective-permute-start(f32[128,128]{1,0:T(8,128)S(1)} %get-tuple-element.12), channel_id=1, source_target_pairs={{0,128},{128,0},{1,129},{129,1},{2,130},{130,2},{3,131},{131,3},{4... | collective-permute-start | bytes 196616 | tf_op jit(solution)/shard_map/ppermute | solution.py:23
  41.8 3.4 %collective-permute-done.4 = f32[128,128]{1,0:T(8,128)S(1)} collective-permute-done((f32[128,128]{1,0:T(8,128)S(1)}, f32[128,128]{1,0:T(8,128)S(1)}, u32[]{:S(2)}, u32[]{:S(2)}) %collective-permute-start.4) | collective-permute-done | bytes 65568 | tf_op jit(solution)/shard_map/ppermute | solution.py:23
  45.4 1.2 collective-permute-done.5
  46.7 2.2 %collective-permute-start.8 = (bf16[2,128,128]{2,1,0:T(8,128)(2,1)S(1)}, bf16[2,128,128]{2,1,0:T(8,128)(2,1)S(1)}, u32[]{:S(2)}, u32[]{:S(2)}) collective-permute-start(bf16[2,128,128]{2,1,0:T(8,128)(2,1)S(1)} %get-tuple-element.14), channel_id=1, source_target_pairs={{0,6},{2,0},{4,2},{6,4},{1,7},{3,1},{5,3},{7,5},{8,14},{10,8},{12,... | collective-permute-start | bytes 196616 | tf_op jit(solution)/shard_map/ppermute | solution.py:23
  48.9 4.0 %grad.2.refs_0_ = bf16[1792,512]{1,0:T(8,128)(2,1)} custom-call(bf16[128,896]{1,0:T(8,128)(2,1)S(1)} %collective-permute-done.refs_0_, bf16[128,896]{1,0:T(8,128)(2,1)S(1)} %collective-permute-done.1.refs_1_, bf16[128,896]{1,0:T(8,128)(2,1)} %collective-permute-done.2.refs_2_, bf16[128,896]{1,0:T(8,128)(2,1)S(1)} %collective-permute-done.3.refs_3_, ...), custom_call_target="tpu_custom_call" | custom-call | tf_op jit(solution)/shard_map/grad/pallas_call | solution.py:151
  52.9 2.3 %collective-permute-done.6 = bf16[2,128,128]{2,1,0:T(8,128)(2,1)S(1)} collective-permute-done((bf16[2,128,128]{2,1,0:T(8,128)(2,1)S(1)}, bf16[2,128,128]{2,1,0:T(8,128)(2,1)S(1)}, u32[]{:S(2)}, u32[]{:S(2)}) %collective-permute-start.6) | collective-permute-done | bytes 65568 | tf_op jit(solution)/shard_map/ppermute | solution.py:23
  55.3 4.3 %all-to-all-done.2 = bf16[16,112,512]{2,1,0:T(8,128)(2,1)} async-done(((bf16[16,112,512]{2,1,0:T(8,128)(2,1)}), bf16[16,112,512]{2,1,0:T(8,128)(2,1)}, u32[]{:S(2)}, u32[]{:S(2)}) %all-to-all-start.2) | async-done | bytes 1835040 | tf_op jit(solution)/shard_map/all_to_all | solution.py:214
  59.6 4.4 %all-to-all-start.1 = ((bf16[16,112,512]{2,1,0:T(8,128)(2,1)}), bf16[16,112,512]{2,1,0:T(8,128)(2,1)S(1)}, u32[]{:S(2)}, u32[]{:S(2)}) async-start(bf16[16,112,512]{2,1,0:T(8,128)(2,1)} %bitcast.15), calls=%async_computation.1 | async-start | bytes 3670016 | tf_op jit(solution)/shard_map/all_to_all | solution.py:214
  64.1 1.8 %convert_reduce_fusion.1 = f32[112,512]{1,0:T(8,128)S(1)} fusion(bf16[16,112,512]{2,1,0:T(8,128)(2,1)} %all-to-all-done.2), kind=kLoop, calls=%fused_computation.1 | loop fusion | flops 1777664 | bytes 2064384 | tf_op jit(solution)/shard_map/reduce_sum | solution.py:223
  65.9 4.6 %collective-permute-start.12 = (bf16[112,512]{1,0:T(8,128)(2,1)S(1)}, bf16[112,512]{1,0:T(8,128)(2,1)S(1)}, u32[]{:S(2)}, u32[]{:S(2)}) collective-permute-start(bf16[112,512]{1,0:T(8,128)(2,1)S(1)} %convert_element_type.29), channel_id=1, source_target_pairs={{0,128},{128,0},{1,129},{129,1},{2,130},{130,2},{3,131},{131,3},{4... | collective-permute-start | bytes 344072 | tf_op jit(solution)/shard_map/ppermute | solution.py:23
  70.5 5.0 %collective-permute-done.12 = bf16[112,512]{1,0:T(8,128)(2,1)S(1)} collective-permute-done((bf16[112,512]{1,0:T(8,128)(2,1)S(1)}, bf16[112,512]{1,0:T(8,128)(2,1)S(1)}, u32[]{:S(2)}, u32[]{:S(2)}) %collective-permute-start.12) | collective-permute-done | bytes 114720 | tf_op jit(solution)/shard_map/ppermute | solution.py:23
  75.5 3.5 %collective-permute-start.20 = (bf16[112,512]{1,0:T(8,128)(2,1)S(1)}, bf16[112,512]{1,0:T(8,128)(2,1)S(1)}, u32[]{:S(2)}, u32[]{:S(2)}) collective-permute-start(bf16[112,512]{1,0:T(8,128)(2,1)S(1)} %multiply_convert_fusion.1.refs_1_), channel_id=1, source_target_pairs={{0,16},{1,65},{8,24},{9,73},{16,0},{17,81},{24,8},{25,89},{32,48},... | collective-permute-start | bytes 344072 | tf_op jit(solution)/shard_map/ppermute | solution.py:34
  79.0 11.2 %all-to-all-done.1.refs_0_ = bf16[16,112,512]{2,1,0:T(8,128)(2,1)S(1)} async-done(((bf16[16,112,512]{2,1,0:T(8,128)(2,1)}), bf16[16,112,512]{2,1,0:T(8,128)(2,1)S(1)}, u32[]{:S(2)}, u32[]{:S(2)}) %all-to-all-start.1) | async-done | bytes 1835040 | tf_op jit(solution)/shard_map/all_to_all | solution.py:214
  90.5 4.8 %collective-permute-start.13 = (bf16[112,512]{1,0:T(8,128)(2,1)S(1)}, bf16[112,512]{1,0:T(8,128)(2,1)S(1)}, u32[]{:S(2)}, u32[]{:S(2)}) collective-permute-start(bf16[112,512]{1,0:T(8,128)(2,1)S(1)} %convert_element_type.33), channel_id=1, source_target_pairs={{0,128},{128,0},{1,129},{129,1},{2,130},{130,2},{3,131},{131,3},{4... | collective-permute-start | bytes 344072 | tf_op jit(solution)/shard_map/ppermute | solution.py:23
  95.7 2.8 %collective-permute-start.22 = (bf16[112,512]{1,0:T(8,128)(2,1)S(1)}, bf16[112,512]{1,0:T(8,128)(2,1)S(1)}, u32[]{:S(2)}, u32[]{:S(2)}) collective-permute-start(bf16[112,512]{1,0:T(8,128)(2,1)S(1)} %multiply_convert_fusion.1.refs_1_), channel_id=1, source_target_pairs={{0,24},{1,97},{8,0},{9,105},{16,8},{17,113},{24,16},{25,121},{32,5... | collective-permute-start | bytes 344072 | tf_op jit(solution)/shard_map/ppermute | solution.py:34
  98.5 2.4 %collective-permute-start.18 = (bf16[4,2,128,128]{3,2,1,0:T(8,128)(2,1)S(1)}, bf16[4,2,128,128]{3,2,1,0:T(8,128)(2,1)S(1)}, u32[]{:S(2)}, u32[]{:S(2)}) collective-permute-start(bf16[4,2,128,128]{3,2,1,0:T(8,128)(2,1)S(1)} %gate.5.refs_5_), channel_id=1, source_target_pairs={{0,64},{1,17},{8,72},{9,25},{16,80},{17,1},{24,88},{25,9},{32,96},... | collective-permute-start | bytes 786440 | tf_op jit(solution)/shard_map/ppermute | solution.py:34
  100.9 1.0 collective-permute-start.19
  102.0 1.9 %collective-permute-start.14 = (bf16[112,512]{1,0:T(8,128)(2,1)S(1)}, bf16[112,512]{1,0:T(8,128)(2,1)S(1)}, u32[]{:S(2)}, u32[]{:S(2)}) collective-permute-start(bf16[112,512]{1,0:T(8,128)(2,1)S(1)} %multiply_convert_fusion.refs_1_), channel_id=1, source_target_pairs={{0,16},{1,65},{8,24},{9,73},{16,0},{17,81},{24,8},{25,89},{32,48},... | collective-permute-start | bytes 344072 | tf_op jit(solution)/shard_map/ppermute | solution.py:34
  104.3 3.8 %collective-permute-done.17.refs_6_ = bf16[4,2,128,128]{3,2,1,0:T(8,128)(2,1)S(1)} collective-permute-done((bf16[4,2,128,128]{3,2,1,0:T(8,128)(2,1)S(1)}, bf16[4,2,128,128]{3,2,1,0:T(8,128)(2,1)S(1)}, u32[]{:S(2)}, u32[]{:S(2)}) %collective-permute-start.17) | collective-permute-done | bytes 262176 | tf_op jit(solution)/shard_map/ppermute | solution.py:34
  108.6 1.2 collective-permute-done.19.refs_8_
  109.8 1.0 correct.2.refs_9_
  110.9 2.1 %collective-permute-done.16.refs_4_ = bf16[112,512]{1,0:T(8,128)(2,1)S(1)} collective-permute-done((bf16[112,512]{1,0:T(8,128)(2,1)S(1)}, bf16[112,512]{1,0:T(8,128)(2,1)S(1)}, u32[]{:S(2)}, u32[]{:S(2)}) %collective-permute-start.16) | collective-permute-done | bytes 114720 | tf_op jit(solution)/shard_map/ppermute | solution.py:34
  112.9 1.0 correct.3
  113.9 12.6 %all_to_all.20.got = f32[4,448,128]{2,1,0:T(8,128)S(1)} all-to-all(f32[4,448,128]{2,1,0:T(8,128)S(1)} %correct.3), channel_id=1, replica_groups={{0,32,64,96},{8,40,72,104},{16,48,80,112},{24,56,88,120},{1,9,17,25},{3..., dimensions={0} | all-to-all | bytes 1835008 | tf_op jit(solution)/shard_map/all_to_all | solution.py:40
  126.5 1.6 %order.1 = f32[1792,128]{1,0:T(8,128)} custom-call(s32[3]{0:T(128)S(1)} %pad_add_fusion.refs_0_.place, f32[4,448,128]{2,1,0:T(8,128)S(1)} %all_to_all.20.got), custom_call_target="tpu_custom_call" | custom-call | tf_op jit(solution)/shard_map/order/pallas_call | solution.py:290
  (43 shorter events, 4.6 us)
Async XLA Ops:
  0.0 15.7 %copy-start = (bf16[896,1792]{1,0:T(8,128)(2,1)S(1)}, bf16[896,1792]{1,0:T(8,128)(2,1)}, u32[]{:S(2)}) copy-start(bf16[896,1792]{1,0:T(8,128)(2,1)} %refs_4_.3) | copy-start | bytes 9633796
  4.5 9.2 %collective-permute-start.10 = (bf16[128,896]{1,0:T(8,128)(2,1)}, bf16[128,896]{1,0:T(8,128)(2,1)}, u32[]{:S(2)}, u32[]{:S(2)}) collective-permute-start(bf16[128,896]{1,0:T(8,128)(2,1)} %get-tuple-element.9.refs_0_), channel_id=1, source_target_pairs={{0,2},{2,4},{4,6},{6,0},{1,3},{3,5},{5,7},{7,1},{8,10},{10,12},{12... | collective-permute-start | bytes 688136 | tf_op jit(solution)/shard_map/ppermute | solution.py:23
  6.5 24.4 %all-to-all-start = ((bf16[16,128,256]{2,1,0:T(8,128)(2,1)}), bf16[16,128,256]{2,1,0:T(8,128)(2,1)}, u32[]{:S(2)}, u32[]{:S(2)}) async-start(bf16[16,128,256]{2,1,0:T(8,128)(2,1)} %get-tuple-element.10), calls=%async_computation | async-start | bytes 2097152 | tf_op jit(solution)/shard_map/all_to_all | solution.py:178
  13.6 2.1 %collective-permute-start.9 = (bf16[128,896]{1,0:T(8,128)(2,1)}, bf16[128,896]{1,0:T(8,128)(2,1)S(1)}, u32[]{:S(2)}, u32[]{:S(2)}) collective-permute-start(bf16[128,896]{1,0:T(8,128)(2,1)} %get-tuple-element.9.refs_0_), channel_id=1, source_target_pairs={{0,1},{1,0},{2,3},{3,2},{4,5},{5,4},{6,7},{7,6},{8,9},{9,8},{10,11... | collective-permute-start | bytes 688136 | tf_op jit(solution)/shard_map/ppermute | solution.py:23
  13.7 2.0 %collective-permute-start.11 = (bf16[128,896]{1,0:T(8,128)(2,1)}, bf16[128,896]{1,0:T(8,128)(2,1)S(1)}, u32[]{:S(2)}, u32[]{:S(2)}) collective-permute-start(bf16[128,896]{1,0:T(8,128)(2,1)} %collective-permute-done.10.refs_2_), channel_id=1, source_target_pairs={{0,1},{1,0},{2,3},{3,2},{4,5},{5,4},{6,7},{7,6},{8,9},{9,8},{10,11... | collective-permute-start | bytes 688136 | tf_op jit(solution)/shard_map/ppermute | solution.py:23
  14.2 27.1 %collective-permute-start = (bf16[128,896]{1,0:T(8,128)(2,1)}, bf16[128,896]{1,0:T(8,128)(2,1)S(1)}, u32[]{:S(2)}, u32[]{:S(2)}) collective-permute-start(bf16[128,896]{1,0:T(8,128)(2,1)} %get-tuple-element.9.refs_0_), channel_id=1, source_target_pairs={{0,4},{2,6},{4,0},{6,2},{1,5},{3,7},{5,1},{7,3},{8,12},{10,14},{12... | collective-permute-start | bytes 688136 | tf_op jit(solution)/shard_map/ppermute | solution.py:23
  14.8 26.5 %collective-permute-start.2 = (bf16[128,896]{1,0:T(8,128)(2,1)}, bf16[128,896]{1,0:T(8,128)(2,1)}, u32[]{:S(2)}, u32[]{:S(2)}) collective-permute-start(bf16[128,896]{1,0:T(8,128)(2,1)} %get-tuple-element.9.refs_0_), channel_id=1, source_target_pairs={{0,6},{2,0},{4,2},{6,4},{1,7},{3,1},{5,3},{7,5},{8,14},{10,8},{12,... | collective-permute-start | bytes 688136 | tf_op jit(solution)/shard_map/ppermute | solution.py:23
  30.9 28.7 %all-to-all-start.2 = ((bf16[16,112,512]{2,1,0:T(8,128)(2,1)}), bf16[16,112,512]{2,1,0:T(8,128)(2,1)}, u32[]{:S(2)}, u32[]{:S(2)}) async-start(bf16[16,112,512]{2,1,0:T(8,128)(2,1)} %bitcast.16), calls=%async_computation.2 | async-start | bytes 3670016 | tf_op jit(solution)/shard_map/all_to_all | solution.py:214
  36.7 8.5 %collective-permute-start.4 = (f32[128,128]{1,0:T(8,128)S(1)}, f32[128,128]{1,0:T(8,128)S(1)}, u32[]{:S(2)}, u32[]{:S(2)}) collective-permute-start(f32[128,128]{1,0:T(8,128)S(1)} %get-tuple-element.12), channel_id=1, source_target_pairs={{0,128},{128,0},{1,129},{129,1},{2,130},{130,2},{3,131},{131,3},{4... | collective-permute-start | bytes 196616 | tf_op jit(solution)/shard_map/ppermute | solution.py:23
  41.3 7.6 %collective-permute-start.1 = (bf16[128,896]{1,0:T(8,128)(2,1)S(1)}, bf16[128,896]{1,0:T(8,128)(2,1)S(1)}, u32[]{:S(2)}, u32[]{:S(2)}) collective-permute-start(bf16[128,896]{1,0:T(8,128)(2,1)S(1)} %collective-permute-done.refs_0_), channel_id=1, source_target_pairs={{0,1},{1,0},{2,3},{3,2},{4,5},{5,4},{6,7},{7,6},{8,9},{9,8},{10,11... | collective-permute-start | bytes 688136 | tf_op jit(solution)/shard_map/ppermute | solution.py:23
  41.3 7.6 %collective-permute-start.3 = (bf16[128,896]{1,0:T(8,128)(2,1)}, bf16[128,896]{1,0:T(8,128)(2,1)S(1)}, u32[]{:S(2)}, u32[]{:S(2)}) collective-permute-start(bf16[128,896]{1,0:T(8,128)(2,1)} %collective-permute-done.2.refs_2_), channel_id=1, source_target_pairs={{0,1},{1,0},{2,3},{3,2},{4,5},{5,4},{6,7},{7,6},{8,9},{9,8},{10,11... | collective-permute-start | bytes 688136 | tf_op jit(solution)/shard_map/ppermute | solution.py:23
  45.3 1.3 %collective-permute-start.5 = (bf16[128,128]{1,0:T(8,128)(2,1)S(1)}, bf16[128,128]{1,0:T(8,128)(2,1)S(1)}, u32[]{:S(2)}, u32[]{:S(2)}) collective-permute-start(bf16[128,128]{1,0:T(8,128)(2,1)S(1)} %multiply_convert_fusion.2), channel_id=1, source_target_pairs={{0,1},{1,0},{2,3},{3,2},{4,5},{5,4},{6,7},{7,6},{8,9},{9,8},{10,11... | collective-permute-start | bytes 98312 | tf_op jit(solution)/shard_map/ppermute | solution.py:23
  46.6 6.3 %collective-permute-start.7 = (bf16[2,128,128]{2,1,0:T(8,128)(2,1)S(1)}, bf16[2,128,128]{2,1,0:T(8,128)(2,1)S(1)}, u32[]{:S(2)}, u32[]{:S(2)}) collective-permute-start(bf16[2,128,128]{2,1,0:T(8,128)(2,1)S(1)} %get-tuple-element.14), channel_id=1, source_target_pairs={{0,4},{2,6},{4,0},{6,2},{1,5},{3,7},{5,1},{7,3},{8,12},{10,14},{12... | collective-permute-start | bytes 196616 | tf_op jit(solution)/shard_map/ppermute | solution.py:23
  46.7 6.2 %collective-permute-start.8 = (bf16[2,128,128]{2,1,0:T(8,128)(2,1)S(1)}, bf16[2,128,128]{2,1,0:T(8,128)(2,1)S(1)}, u32[]{:S(2)}, u32[]{:S(2)}) collective-permute-start(bf16[2,128,128]{2,1,0:T(8,128)(2,1)S(1)} %get-tuple-element.14), channel_id=1, source_target_pairs={{0,6},{2,0},{4,2},{6,4},{1,7},{3,1},{5,3},{7,5},{8,14},{10,8},{12,... | collective-permute-start | bytes 196616 | tf_op jit(solution)/shard_map/ppermute | solution.py:23
  48.9 6.3 %collective-permute-start.6 = (bf16[2,128,128]{2,1,0:T(8,128)(2,1)S(1)}, bf16[2,128,128]{2,1,0:T(8,128)(2,1)S(1)}, u32[]{:S(2)}, u32[]{:S(2)}) collective-permute-start(bf16[2,128,128]{2,1,0:T(8,128)(2,1)S(1)} %get-tuple-element.14), channel_id=1, source_target_pairs={{0,2},{2,4},{4,6},{6,0},{1,3},{3,5},{5,7},{7,1},{8,10},{10,12},{12... | collective-permute-start | bytes 196616 | tf_op jit(solution)/shard_map/ppermute | solution.py:23
  59.6 30.6 %all-to-all-start.1 = ((bf16[16,112,512]{2,1,0:T(8,128)(2,1)}), bf16[16,112,512]{2,1,0:T(8,128)(2,1)S(1)}, u32[]{:S(2)}, u32[]{:S(2)}) async-start(bf16[16,112,512]{2,1,0:T(8,128)(2,1)} %bitcast.15), calls=%async_computation.1 | async-start | bytes 3670016 | tf_op jit(solution)/shard_map/all_to_all | solution.py:214
  65.9 9.6 %collective-permute-start.12 = (bf16[112,512]{1,0:T(8,128)(2,1)S(1)}, bf16[112,512]{1,0:T(8,128)(2,1)S(1)}, u32[]{:S(2)}, u32[]{:S(2)}) collective-permute-start(bf16[112,512]{1,0:T(8,128)(2,1)S(1)} %convert_element_type.29), channel_id=1, source_target_pairs={{0,128},{128,0},{1,129},{129,1},{2,130},{130,2},{3,131},{131,3},{4... | collective-permute-start | bytes 344072 | tf_op jit(solution)/shard_map/ppermute | solution.py:23
  75.5 23.0 %collective-permute-start.20 = (bf16[112,512]{1,0:T(8,128)(2,1)S(1)}, bf16[112,512]{1,0:T(8,128)(2,1)S(1)}, u32[]{:S(2)}, u32[]{:S(2)}) collective-permute-start(bf16[112,512]{1,0:T(8,128)(2,1)S(1)} %multiply_convert_fusion.1.refs_1_), channel_id=1, source_target_pairs={{0,16},{1,65},{8,24},{9,73},{16,0},{17,81},{24,8},{25,89},{32,48},... | collective-permute-start | bytes 344072 | tf_op jit(solution)/shard_map/ppermute | solution.py:34
  90.5 10.4 %collective-permute-start.13 = (bf16[112,512]{1,0:T(8,128)(2,1)S(1)}, bf16[112,512]{1,0:T(8,128)(2,1)S(1)}, u32[]{:S(2)}, u32[]{:S(2)}) collective-permute-start(bf16[112,512]{1,0:T(8,128)(2,1)S(1)} %convert_element_type.33), channel_id=1, source_target_pairs={{0,128},{128,0},{1,129},{129,1},{2,130},{130,2},{3,131},{131,3},{4... | collective-permute-start | bytes 344072 | tf_op jit(solution)/shard_map/ppermute | solution.py:23
  95.3 12.8 %collective-permute-start.17 = (bf16[4,2,128,128]{3,2,1,0:T(8,128)(2,1)S(1)}, bf16[4,2,128,128]{3,2,1,0:T(8,128)(2,1)S(1)}, u32[]{:S(2)}, u32[]{:S(2)}) collective-permute-start(bf16[4,2,128,128]{3,2,1,0:T(8,128)(2,1)S(1)} %gate.5.refs_5_), channel_id=1, source_target_pairs={{0,32},{1,9},{8,40},{9,17},{16,48},{17,25},{24,56},{25,1},{32,64},... | collective-permute-start | bytes 786440 | tf_op jit(solution)/shard_map/ppermute | solution.py:34
  95.3 6.7 %collective-permute-start.21 = (bf16[112,512]{1,0:T(8,128)(2,1)S(1)}, bf16[112,512]{1,0:T(8,128)(2,1)S(1)}, u32[]{:S(2)}, u32[]{:S(2)}) collective-permute-start(bf16[112,512]{1,0:T(8,128)(2,1)S(1)} %multiply_convert_fusion.1.refs_1_), channel_id=1, source_target_pairs={{0,8},{1,33},{8,16},{9,41},{16,24},{17,49},{24,0},{25,57},{32,40},... | collective-permute-start | bytes 344072 | tf_op jit(solution)/shard_map/ppermute | solution.py:34
  95.7 8.2 %collective-permute-start.22 = (bf16[112,512]{1,0:T(8,128)(2,1)S(1)}, bf16[112,512]{1,0:T(8,128)(2,1)S(1)}, u32[]{:S(2)}, u32[]{:S(2)}) collective-permute-start(bf16[112,512]{1,0:T(8,128)(2,1)S(1)} %multiply_convert_fusion.1.refs_1_), channel_id=1, source_target_pairs={{0,24},{1,97},{8,0},{9,105},{16,8},{17,113},{24,16},{25,121},{32,5... | collective-permute-start | bytes 344072 | tf_op jit(solution)/shard_map/ppermute | solution.py:34
  98.5 10.1 %collective-permute-start.18 = (bf16[4,2,128,128]{3,2,1,0:T(8,128)(2,1)S(1)}, bf16[4,2,128,128]{3,2,1,0:T(8,128)(2,1)S(1)}, u32[]{:S(2)}, u32[]{:S(2)}) collective-permute-start(bf16[4,2,128,128]{3,2,1,0:T(8,128)(2,1)S(1)} %gate.5.refs_5_), channel_id=1, source_target_pairs={{0,64},{1,17},{8,72},{9,25},{16,80},{17,1},{24,88},{25,9},{32,96},... | collective-permute-start | bytes 786440 | tf_op jit(solution)/shard_map/ppermute | solution.py:34
  100.9 8.9 %collective-permute-start.19 = (bf16[4,2,128,128]{3,2,1,0:T(8,128)(2,1)S(1)}, bf16[4,2,128,128]{3,2,1,0:T(8,128)(2,1)S(1)}, u32[]{:S(2)}, u32[]{:S(2)}) collective-permute-start(bf16[4,2,128,128]{3,2,1,0:T(8,128)(2,1)S(1)} %gate.5.refs_5_), channel_id=1, source_target_pairs={{0,96},{1,25},{8,104},{9,1},{16,112},{17,9},{24,120},{25,17},{32,0... | collective-permute-start | bytes 786440 | tf_op jit(solution)/shard_map/ppermute | solution.py:34
  102.0 8.9 %collective-permute-start.14 = (bf16[112,512]{1,0:T(8,128)(2,1)S(1)}, bf16[112,512]{1,0:T(8,128)(2,1)S(1)}, u32[]{:S(2)}, u32[]{:S(2)}) collective-permute-start(bf16[112,512]{1,0:T(8,128)(2,1)S(1)} %multiply_convert_fusion.refs_1_), channel_id=1, source_target_pairs={{0,16},{1,65},{8,24},{9,73},{16,0},{17,81},{24,8},{25,89},{32,48},... | collective-permute-start | bytes 344072 | tf_op jit(solution)/shard_map/ppermute | solution.py:34
  103.9 6.9 %collective-permute-start.15 = (bf16[112,512]{1,0:T(8,128)(2,1)S(1)}, bf16[112,512]{1,0:T(8,128)(2,1)S(1)}, u32[]{:S(2)}, u32[]{:S(2)}) collective-permute-start(bf16[112,512]{1,0:T(8,128)(2,1)S(1)} %multiply_convert_fusion.refs_1_), channel_id=1, source_target_pairs={{0,8},{1,33},{8,16},{9,41},{16,24},{17,49},{24,0},{25,57},{32,40},... | collective-permute-start | bytes 344072 | tf_op jit(solution)/shard_map/ppermute | solution.py:34
  108.1 4.8 %collective-permute-start.16 = (bf16[112,512]{1,0:T(8,128)(2,1)S(1)}, bf16[112,512]{1,0:T(8,128)(2,1)S(1)}, u32[]{:S(2)}, u32[]{:S(2)}) collective-permute-start(bf16[112,512]{1,0:T(8,128)(2,1)S(1)} %multiply_convert_fusion.refs_1_), channel_id=1, source_target_pairs={{0,24},{1,97},{8,0},{9,105},{16,8},{17,113},{24,16},{25,121},{32,5... | collective-permute-start | bytes 344072 | tf_op jit(solution)/shard_map/ppermute | solution.py:34

commit v15 on v13

--- a/solution.py
+++ b/solution.py
@@ -247,7 +247,7 @@
     near_rows = [up_grad, shifted(up_grad, "core", 1), near, shifted(near, "core", 1)]
     far_rows = [far, shifted(far, "core", 1), farthest, shifted(farthest, "core", 1)]
     act_row = act_squares(act_parts)
-    cost = pl.CostEstimate(flops=8 * 10**9, bytes_accessed=10**7, transcendentals=0)
+    cost = pl.CostEstimate(flops=5 * 10**9, bytes_accessed=10**7, transcendentals=0)
     near_got = exchanged(grad_partials(near_rows, grad_basis, (), cost))
     act_own = jnp.stack(act_row)
     far_got = exchanged(gated(grad_partials(far_rows, grad_basis), [act_own]))

time: 122 us -> 124 us (1.016)
  waiting for transfers between devices: 31.1 us -> 33.2 us
    all_to_all x1, waiting for transfers between devices: 11.1 us -> 3.04 us  [act_squares(): got = lax.all_to_all(partials, ('x', 'y'), 0, 0, tiled=True)]
    ppermute x26, waiting for transfers between devices: 13.9 us -> 21.1 us  [shifted(): lax.ppermute(value, axis, [(i, (i + step) % size) for i in range(size)])]
    all_to_all x2, waiting for transfers between devices: 6.09 us -> 9.04 us  [exchanged(): lax.all_to_all(partial.reshape(16, columns // 16, tokens), ('x', 'y'), 0,...]
    ppermute x26, starting transfers between devices: 39.9 us -> 41.2 us  [shifted(): lax.ppermute(value, axis, [(i, (i + step) % size) for i in range(size)])]
  transfers between devices with their start and end apart: 29 -> 29, of which waited for: 10 -> 15; matrix products, arithmetic and copies ran while one was open for 2% -> 2% of each run, Pallas kernels for 9% -> 8%
where the time goes in v15:
time: 124 us; the launch traced here: 122 us
  starting transfers between devices  56.4 us (45%)
  waiting for transfers between devices  33.2 us (27%)
  Pallas kernels  15.9 us (13%)
  blocking collectives  13.7 us (11%)
  other arithmetic  2.24 us (2%)
    ppermute x26, starting transfers between devices, shifted(): lax.ppermute(value, axis, [(i, (i + step) % size) for i in range(size)])  41.2 us
    ppermute x26, waiting for transfers between devices, shifted(): lax.ppermute(value, axis, [(i, (i + step) % size) for i in range(size)])  21.1 us
    all_to_all x1, blocking collectives, per_device(): out = lax.all_to_all(out, 'x', 0, 0, tiled=True)  13.7 us
    all_to_all x2, waiting for transfers between devices, exchanged(): lax.all_to_all(partial.reshape(16, columns // 16, tokens), ('x', 'y'), 0,...  9.04 us
    all_to_all x2, starting transfers between devices, exchanged(): lax.all_to_all(partial.reshape(16, columns // 16, tokens), ('x', 'y'), 0,...  8.12 us
    pallas_call x2, Pallas kernels, grad_partials(): pl.pallas_call(lambda *refs: grad_kernel(len(parts), *refs), out_shape=pl...  7.94 us
    all_to_all x1, starting transfers between devices, act_squares(): got = lax.all_to_all(partials, ('x', 'y'), 0, 0, tiled=True)  7.09 us
    pallas_call x1, Pallas kernels, first_partials(): pl.pallas_call(first_kernel, out_shape=(pltpu.HBM(shape, jnp.bfloat16), p...  4.53 us
  transfers between devices with their start and end apart: 29, of which 15 were waited for; matrix products, arithmetic and copies ran while one was open for 2% of the time, Pallas kernels for 8%

profile of v15, /device:TPU:64, one launch (start us, length us, event | category | flops | bytes accessed | tf_op | source)
XLA Modules:
  0.0 122.4 jit_solution(10868021829483794172)
XLA Ops:
  0.0 4.5 %first.1 = (bf16[16,128,256]{2,1,0:T(8,128)(2,1)}, bf16[128,896]{1,0:T(8,128)(2,1)}) custom-call(s32[1]{0:T(128)} %bitcast.2.place, f32[1,8192]{1,0:T(1,128)} %bitcast.16, bf16[128,896]{1,0:T(8,128)(2,1)} %gate_at.1, bf16[128,896]{1,0:T(8,128)(2,1)} %grad_at.1, bf16[128,8192]{1,0:T(8,128)(2,1)} %hidden_at.1, bf16[256,4096]{1,0:T(8,128)(2,1)} %basis_at.1), custom_call_target="tpu_custom_call" | custom-call | tf_op jit(solution)/shard_map/first/pallas_call | solution.py:90
  4.5 7.1 %all-to-all-start = ((bf16[16,128,256]{2,1,0:T(8,128)(2,1)}), bf16[16,128,256]{2,1,0:T(8,128)(2,1)}, u32[]{:S(2)}, u32[]{:S(2)}) async-start(bf16[16,128,256]{2,1,0:T(8,128)(2,1)} %get-tuple-element.10), calls=%async_computation | async-start | bytes 2097152 | tf_op jit(solution)/shard_map/all_to_all | solution.py:159
  11.6 2.0 %collective-permute-start.16 = (bf16[128,896]{1,0:T(8,128)(2,1)}, bf16[128,896]{1,0:T(8,128)(2,1)S(1)}, u32[]{:S(2)}, u32[]{:S(2)}) collective-permute-start(bf16[128,896]{1,0:T(8,128)(2,1)} %get-tuple-element.9.refs_0_), channel_id=1, source_target_pairs={{0,2},{2,4},{4,6},{6,0},{1,3},{3,5},{5,7},{7,1},{8,10},{10,12},{12... | collective-permute-start | bytes 688136 | tf_op jit(solution)/shard_map/ppermute | solution.py:23
  13.6 5.4 %collective-permute-done.16.refs_2_ = bf16[128,896]{1,0:T(8,128)(2,1)S(1)} collective-permute-done((bf16[128,896]{1,0:T(8,128)(2,1)}, bf16[128,896]{1,0:T(8,128)(2,1)S(1)}, u32[]{:S(2)}, u32[]{:S(2)}) %collective-permute-start.16) | collective-permute-done | bytes 229408 | tf_op jit(solution)/shard_map/ppermute | solution.py:23
  19.0 2.5 %collective-permute-start = (bf16[128,896]{1,0:T(8,128)(2,1)}, bf16[128,896]{1,0:T(8,128)(2,1)S(1)}, u32[]{:S(2)}, u32[]{:S(2)}) collective-permute-start(bf16[128,896]{1,0:T(8,128)(2,1)} %get-tuple-element.9.refs_0_), channel_id=1, source_target_pairs={{0,4},{2,6},{4,0},{6,2},{1,5},{3,7},{5,1},{7,3},{8,12},{10,14},{12... | collective-permute-start | bytes 688136 | tf_op jit(solution)/shard_map/ppermute | solution.py:23
  22.4 4.0 %grad.3 = bf16[1792,512]{1,0:T(8,128)(2,1)} custom-call(bf16[128,896]{1,0:T(8,128)(2,1)} %get-tuple-element.9.refs_0_, bf16[128,896]{1,0:T(8,128)(2,1)S(1)} %collective-permute-done.15.refs_1_, bf16[128,896]{1,0:T(8,128)(2,1)S(1)} %collective-permute-done.16.refs_2_, bf16[128,896]{1,0:T(8,128)(2,1)S(1)} %collective-permute-done.17.refs_3_, ...), custom_call_target="tpu_custom_call" | custom-call | flops 5000000000 | bytes 10000000 | tf_op jit(solution)/shard_map/grad/pallas_call | solution.py:132
  26.4 3.0 %all-to-all-done.got = bf16[16,128,256]{2,1,0:T(8,128)(2,1)} async-done(((bf16[16,128,256]{2,1,0:T(8,128)(2,1)}), bf16[16,128,256]{2,1,0:T(8,128)(2,1)}, u32[]{:S(2)}, u32[]{:S(2)}) %all-to-all-start) | async-done | bytes 1048608 | tf_op jit(solution)/shard_map/all_to_all | solution.py:159
  29.4 4.4 %all-to-all-start.2 = ((bf16[16,112,512]{2,1,0:T(8,128)(2,1)}), bf16[16,112,512]{2,1,0:T(8,128)(2,1)}, u32[]{:S(2)}, u32[]{:S(2)}) async-start(bf16[16,112,512]{2,1,0:T(8,128)(2,1)} %bitcast.14), calls=%async_computation.2 | async-start | bytes 3670016 | tf_op jit(solution)/shard_map/all_to_all | solution.py:195
  33.8 1.4 %act_sum.1 = (f32[128,128]{1,0:T(8,128)S(1)}, f32[128,128]{1,0:T(8,128)S(1)}) custom-call(s32[1]{0:T(128)} %bitcast.4.place, bf16[16,128,256]{2,1,0:T(8,128)(2,1)} %all-to-all-done.got), custom_call_target="tpu_custom_call" | custom-call | flops 20000000000 | bytes 1000000 | tf_op jit(solution)/shard_map/act_sum/pallas_call | solution.py:163
  35.2 5.5 %collective-permute-start.4 = (f32[128,128]{1,0:T(8,128)S(1)}, f32[128,128]{1,0:T(8,128)S(1)}, u32[]{:S(2)}, u32[]{:S(2)}) collective-permute-start(f32[128,128]{1,0:T(8,128)S(1)} %get-tuple-element.12), channel_id=1, source_target_pairs={{0,128},{128,0},{1,129},{129,1},{2,130},{130,2},{3,131},{131,3},{4... | collective-permute-start | bytes 196616 | tf_op jit(solution)/shard_map/ppermute | solution.py:23
  41.2 4.1 %collective-permute-done.4 = f32[128,128]{1,0:T(8,128)S(1)} collective-permute-done((f32[128,128]{1,0:T(8,128)S(1)}, f32[128,128]{1,0:T(8,128)S(1)}, u32[]{:S(2)}, u32[]{:S(2)}) %collective-permute-start.4) | collective-permute-done | bytes 65568 | tf_op jit(solution)/shard_map/ppermute | solution.py:23
  45.3 1.6 %collective-permute-start.5 = (bf16[128,128]{1,0:T(8,128)(2,1)S(1)}, bf16[128,128]{1,0:T(8,128)(2,1)S(1)}, u32[]{:S(2)}, u32[]{:S(2)}) collective-permute-start(bf16[128,128]{1,0:T(8,128)(2,1)S(1)} %multiply_convert_fusion.2), channel_id=1, source_target_pairs={{0,32},{32,64},{64,96},{96,0},{1,33},{33,65},{65,97},{97,1},{2,34}... | collective-permute-start | bytes 98312 | tf_op jit(solution)/shard_map/ppermute | solution.py:23
  46.9 2.7 %collective-permute-start.6 = (bf16[128,128]{1,0:T(8,128)(2,1)S(1)}, bf16[128,128]{1,0:T(8,128)(2,1)S(1)}, u32[]{:S(2)}, u32[]{:S(2)}) collective-permute-start(bf16[128,128]{1,0:T(8,128)(2,1)S(1)} %multiply_convert_fusion.2), channel_id=1, source_target_pairs={{0,64},{32,96},{64,0},{96,32},{1,65},{33,97},{65,1},{97,33},{2,66}... | collective-permute-start | bytes 98312 | tf_op jit(solution)/shard_map/ppermute | solution.py:23
  49.5 1.5 %collective-permute-start.7 = (bf16[128,128]{1,0:T(8,128)(2,1)S(1)}, bf16[128,128]{1,0:T(8,128)(2,1)S(1)}, u32[]{:S(2)}, u32[]{:S(2)}) collective-permute-start(bf16[128,128]{1,0:T(8,128)(2,1)S(1)} %multiply_convert_fusion.2), channel_id=1, source_target_pairs={{0,96},{32,0},{64,32},{96,64},{1,97},{33,1},{65,33},{97,65},{2,98}... | collective-permute-start | bytes 98312 | tf_op jit(solution)/shard_map/ppermute | solution.py:23
  51.0 4.0 %grad.2.refs_0_ = bf16[1792,512]{1,0:T(8,128)(2,1)} custom-call(bf16[128,896]{1,0:T(8,128)(2,1)S(1)} %collective-permute-done.refs_0_, bf16[128,896]{1,0:T(8,128)(2,1)S(1)} %collective-permute-done.1.refs_1_, bf16[128,896]{1,0:T(8,128)(2,1)} %collective-permute-done.2.refs_2_, bf16[128,896]{1,0:T(8,128)(2,1)S(1)} %collective-permute-done.3.refs_3_, ...), custom_call_target="tpu_custom_call" | custom-call | tf_op jit(solution)/shard_map/grad/pallas_call | solution.py:132
  55.6 2.6 %collective-permute-done.6 = bf16[128,128]{1,0:T(8,128)(2,1)S(1)} collective-permute-done((bf16[128,128]{1,0:T(8,128)(2,1)S(1)}, bf16[128,128]{1,0:T(8,128)(2,1)S(1)}, u32[]{:S(2)}, u32[]{:S(2)}) %collective-permute-start.6) | collective-permute-done | bytes 32800 | tf_op jit(solution)/shard_map/ppermute | solution.py:23
  58.3 2.2 %all-to-all-done.2 = bf16[16,112,512]{2,1,0:T(8,128)(2,1)} async-done(((bf16[16,112,512]{2,1,0:T(8,128)(2,1)}), bf16[16,112,512]{2,1,0:T(8,128)(2,1)}, u32[]{:S(2)}, u32[]{:S(2)}) %all-to-all-start.2) | async-done | bytes 1835040 | tf_op jit(solution)/shard_map/all_to_all | solution.py:195
  60.5 3.7 %all-to-all-start.1 = ((bf16[16,112,512]{2,1,0:T(8,128)(2,1)}), bf16[16,112,512]{2,1,0:T(8,128)(2,1)S(1)}, u32[]{:S(2)}, u32[]{:S(2)}) async-start(bf16[16,112,512]{2,1,0:T(8,128)(2,1)} %bitcast.12), calls=%async_computation.1 | async-start | bytes 3670016 | tf_op jit(solution)/shard_map/all_to_all | solution.py:195
  64.2 1.3 %collective-permute-start.9 = (bf16[4,128,128]{2,1,0:T(8,128)(2,1)S(1)}, bf16[4,128,128]{2,1,0:T(8,128)(2,1)S(1)}, u32[]{:S(2)}, u32[]{:S(2)}) collective-permute-start(bf16[4,128,128]{2,1,0:T(8,128)(2,1)S(1)} %pad_maximum_fusion.refs_1_.refs_4_), channel_id=1, source_target_pairs={{0,2},{2,4},{4,6},{6,0},{1,3},{3,5},{5,7},{7,1},{8,10},{10,12},{12... | collective-permute-start | bytes 393224 | tf_op jit(solution)/shard_map/ppermute | solution.py:23
  66.2 2.8 %collective-permute-start.13 = (bf16[4,128,128]{2,1,0:T(8,128)(2,1)S(1)}, bf16[4,128,128]{2,1,0:T(8,128)(2,1)S(1)}, u32[]{:S(2)}, u32[]{:S(2)}) collective-permute-start(bf16[4,128,128]{2,1,0:T(8,128)(2,1)S(1)} %pad_maximum_fusion.refs_1_.refs_4_), channel_id=1, source_target_pairs={{0,6},{2,0},{4,2},{6,4},{1,7},{3,1},{5,3},{7,5},{8,14},{10,8},{12,... | collective-permute-start | bytes 393224 | tf_op jit(solution)/shard_map/ppermute | solution.py:23
  69.0 1.8 %convert_reduce_fusion.1 = f32[112,512]{1,0:T(8,128)S(1)} fusion(bf16[16,112,512]{2,1,0:T(8,128)(2,1)} %all-to-all-done.2), kind=kLoop, calls=%fused_computation.1 | loop fusion | flops 1777664 | bytes 2064384 | tf_op jit(solution)/shard_map/reduce_sum | solution.py:199
  70.8 5.2 %collective-permute-start.18 = (bf16[112,512]{1,0:T(8,128)(2,1)S(1)}, bf16[112,512]{1,0:T(8,128)(2,1)S(1)}, u32[]{:S(2)}, u32[]{:S(2)}) collective-permute-start(bf16[112,512]{1,0:T(8,128)(2,1)S(1)} %convert_element_type.29), channel_id=1, source_target_pairs={{0,128},{128,0},{1,129},{129,1},{2,130},{130,2},{3,131},{131,3},{4... | collective-permute-start | bytes 344072 | tf_op jit(solution)/shard_map/ppermute | solution.py:23
  77.1 2.3 %collective-permute-done.13.refs_7_.refs_6_ = bf16[4,128,128]{2,1,0:T(8,128)(2,1)S(1)} collective-permute-done((bf16[4,128,128]{2,1,0:T(8,128)(2,1)S(1)}, bf16[4,128,128]{2,1,0:T(8,128)(2,1)S(1)}, u32[]{:S(2)}, u32[]{:S(2)}) %collective-permute-start.13) | collective-permute-done | bytes 131104 | tf_op jit(solution)/shard_map/ppermute | solution.py:23
  79.4 2.2 %collective-permute-done.18 = bf16[112,512]{1,0:T(8,128)(2,1)S(1)} collective-permute-done((bf16[112,512]{1,0:T(8,128)(2,1)S(1)}, bf16[112,512]{1,0:T(8,128)(2,1)S(1)}, u32[]{:S(2)}, u32[]{:S(2)}) %collective-permute-start.18) | collective-permute-done | bytes 114720 | tf_op jit(solution)/shard_map/ppermute | solution.py:23
  81.6 6.8 %all-to-all-done.1.refs_0_ = bf16[16,112,512]{2,1,0:T(8,128)(2,1)S(1)} async-done(((bf16[16,112,512]{2,1,0:T(8,128)(2,1)}), bf16[16,112,512]{2,1,0:T(8,128)(2,1)S(1)}, u32[]{:S(2)}, u32[]{:S(2)}) %all-to-all-start.1) | async-done | bytes 1835040 | tf_op jit(solution)/shard_map/all_to_all | solution.py:195
  88.7 5.8 %collective-permute-start.19 = (bf16[112,512]{1,0:T(8,128)(2,1)S(1)}, bf16[112,512]{1,0:T(8,128)(2,1)S(1)}, u32[]{:S(2)}, u32[]{:S(2)}) collective-permute-start(bf16[112,512]{1,0:T(8,128)(2,1)S(1)} %convert_element_type.33), channel_id=1, source_target_pairs={{0,128},{128,0},{1,129},{129,1},{2,130},{130,2},{3,131},{131,3},{4... | collective-permute-start | bytes 344072 | tf_op jit(solution)/shard_map/ppermute | solution.py:23
  96.6 2.2 %collective-permute-start.25 = (bf16[112,512]{1,0:T(8,128)(2,1)S(1)}, bf16[112,512]{1,0:T(8,128)(2,1)S(1)}, u32[]{:S(2)}, u32[]{:S(2)}) collective-permute-start(bf16[112,512]{1,0:T(8,128)(2,1)S(1)} %multiply_convert_fusion.1.refs_9_.refs_0_), channel_id=1, source_target_pairs={{0,24},{8,0},{16,8},{24,16},{1,25},{9,1},{17,9},{25,17},{2,26},{10... | collective-permute-start | bytes 344072 | tf_op jit(solution)/shard_map/ppermute | solution.py:23
  98.8 1.4 %collective-permute-start.20 = (bf16[112,512]{1,0:T(8,128)(2,1)S(1)}, bf16[112,512]{1,0:T(8,128)(2,1)S(1)}, u32[]{:S(2)}, u32[]{:S(2)}) collective-permute-start(bf16[112,512]{1,0:T(8,128)(2,1)S(1)} %multiply_convert_fusion.refs_0_), channel_id=1, source_target_pairs={{0,16},{8,24},{16,0},{24,8},{1,17},{9,25},{17,1},{25,9},{2,18},{10... | collective-permute-start | bytes 344072 | tf_op jit(solution)/shard_map/ppermute | solution.py:23
  100.9 1.1 collective-permute-done.23.refs_1_
  102.0 1.5 %collective-permute-start.22 = (bf16[112,512]{1,0:T(8,128)(2,1)S(1)}, bf16[112,512]{1,0:T(8,128)(2,1)S(1)}, u32[]{:S(2)}, u32[]{:S(2)}) collective-permute-start(bf16[112,512]{1,0:T(8,128)(2,1)S(1)} %multiply_convert_fusion.refs_0_), channel_id=1, source_target_pairs={{0,24},{8,0},{16,8},{24,16},{1,25},{9,1},{17,9},{25,17},{2,26},{10... | collective-permute-start | bytes 344072 | tf_op jit(solution)/shard_map/ppermute | solution.py:23
  105.2 1.2 collective-permute-done.21.refs_2_
  107.8 13.7 %all_to_all.20 = f32[4,448,128]{2,1,0:T(8,128)S(1)} all-to-all(f32[4,448,128]{2,1,0:T(8,128)S(1)} %correct.3), channel_id=1, replica_groups=mesh['z_hi'=2,'x'=4,'y'=4,'z_lo'=4,'core'=2] {'x'}, dimensions={0} | all-to-all | bytes 1835008 | tf_op jit(solution)/shard_map/all_to_all | solution.py:262
  (47 shorter events, 10.9 us)
Async XLA Ops:
  0.0 22.4 %copy-start = (bf16[896,1792]{1,0:T(8,128)(2,1)S(1)}, bf16[896,1792]{1,0:T(8,128)(2,1)}, u32[]{:S(2)}) copy-start(bf16[896,1792]{1,0:T(8,128)(2,1)} %refs_4_.3) | copy-start | bytes 9633796
  4.5 24.9 %all-to-all-start = ((bf16[16,128,256]{2,1,0:T(8,128)(2,1)}), bf16[16,128,256]{2,1,0:T(8,128)(2,1)}, u32[]{:S(2)}, u32[]{:S(2)}) async-start(bf16[16,128,256]{2,1,0:T(8,128)(2,1)} %get-tuple-element.10), calls=%async_computation | async-start | bytes 2097152 | tf_op jit(solution)/shard_map/all_to_all | solution.py:159
  11.6 7.4 %collective-permute-start.16 = (bf16[128,896]{1,0:T(8,128)(2,1)}, bf16[128,896]{1,0:T(8,128)(2,1)S(1)}, u32[]{:S(2)}, u32[]{:S(2)}) collective-permute-start(bf16[128,896]{1,0:T(8,128)(2,1)} %get-tuple-element.9.refs_0_), channel_id=1, source_target_pairs={{0,2},{2,4},{4,6},{6,0},{1,3},{3,5},{5,7},{7,1},{8,10},{10,12},{12... | collective-permute-start | bytes 688136 | tf_op jit(solution)/shard_map/ppermute | solution.py:23
  13.6 8.7 %collective-permute-start.15 = (bf16[128,896]{1,0:T(8,128)(2,1)}, bf16[128,896]{1,0:T(8,128)(2,1)S(1)}, u32[]{:S(2)}, u32[]{:S(2)}) collective-permute-start(bf16[128,896]{1,0:T(8,128)(2,1)} %get-tuple-element.9.refs_0_), channel_id=1, source_target_pairs={{0,1},{1,0},{2,3},{3,2},{4,5},{5,4},{6,7},{7,6},{8,9},{9,8},{10,11... | collective-permute-start | bytes 688136 | tf_op jit(solution)/shard_map/ppermute | solution.py:23
  19.0 3.4 %collective-permute-start.17 = (bf16[128,896]{1,0:T(8,128)(2,1)S(1)}, bf16[128,896]{1,0:T(8,128)(2,1)S(1)}, u32[]{:S(2)}, u32[]{:S(2)}) collective-permute-start(bf16[128,896]{1,0:T(8,128)(2,1)S(1)} %collective-permute-done.16.refs_2_), channel_id=1, source_target_pairs={{0,1},{1,0},{2,3},{3,2},{4,5},{5,4},{6,7},{7,6},{8,9},{9,8},{10,11... | collective-permute-start | bytes 688136 | tf_op jit(solution)/shard_map/ppermute | solution.py:23
  19.0 21.7 %collective-permute-start = (bf16[128,896]{1,0:T(8,128)(2,1)}, bf16[128,896]{1,0:T(8,128)(2,1)S(1)}, u32[]{:S(2)}, u32[]{:S(2)}) collective-permute-start(bf16[128,896]{1,0:T(8,128)(2,1)} %get-tuple-element.9.refs_0_), channel_id=1, source_target_pairs={{0,4},{2,6},{4,0},{6,2},{1,5},{3,7},{5,1},{7,3},{8,12},{10,14},{12... | collective-permute-start | bytes 688136 | tf_op jit(solution)/shard_map/ppermute | solution.py:23
  21.5 19.1 %collective-permute-start.2 = (bf16[128,896]{1,0:T(8,128)(2,1)}, bf16[128,896]{1,0:T(8,128)(2,1)}, u32[]{:S(2)}, u32[]{:S(2)}) collective-permute-start(bf16[128,896]{1,0:T(8,128)(2,1)} %get-tuple-element.9.refs_0_), channel_id=1, source_target_pairs={{0,6},{2,0},{4,2},{6,4},{1,7},{3,1},{5,3},{7,5},{8,14},{10,8},{12,... | collective-permute-start | bytes 688136 | tf_op jit(solution)/shard_map/ppermute | solution.py:23
  29.4 31.1 %all-to-all-start.2 = ((bf16[16,112,512]{2,1,0:T(8,128)(2,1)}), bf16[16,112,512]{2,1,0:T(8,128)(2,1)}, u32[]{:S(2)}, u32[]{:S(2)}) async-start(bf16[16,112,512]{2,1,0:T(8,128)(2,1)} %bitcast.14), calls=%async_computation.2 | async-start | bytes 3670016 | tf_op jit(solution)/shard_map/all_to_all | solution.py:195
  35.2 10.1 %collective-permute-start.4 = (f32[128,128]{1,0:T(8,128)S(1)}, f32[128,128]{1,0:T(8,128)S(1)}, u32[]{:S(2)}, u32[]{:S(2)}) collective-permute-start(f32[128,128]{1,0:T(8,128)S(1)} %get-tuple-element.12), channel_id=1, source_target_pairs={{0,128},{128,0},{1,129},{129,1},{2,130},{130,2},{3,131},{131,3},{4... | collective-permute-start | bytes 196616 | tf_op jit(solution)/shard_map/ppermute | solution.py:23
  40.7 10.3 %collective-permute-start.1 = (bf16[128,896]{1,0:T(8,128)(2,1)S(1)}, bf16[128,896]{1,0:T(8,128)(2,1)S(1)}, u32[]{:S(2)}, u32[]{:S(2)}) collective-permute-start(bf16[128,896]{1,0:T(8,128)(2,1)S(1)} %collective-permute-done.refs_0_), channel_id=1, source_target_pairs={{0,1},{1,0},{2,3},{3,2},{4,5},{5,4},{6,7},{7,6},{8,9},{9,8},{10,11... | collective-permute-start | bytes 688136 | tf_op jit(solution)/shard_map/ppermute | solution.py:23
  40.7 10.3 %collective-permute-start.3 = (bf16[128,896]{1,0:T(8,128)(2,1)}, bf16[128,896]{1,0:T(8,128)(2,1)S(1)}, u32[]{:S(2)}, u32[]{:S(2)}) collective-permute-start(bf16[128,896]{1,0:T(8,128)(2,1)} %collective-permute-done.2.refs_2_), channel_id=1, source_target_pairs={{0,1},{1,0},{2,3},{3,2},{4,5},{5,4},{6,7},{7,6},{8,9},{9,8},{10,11... | collective-permute-start | bytes 688136 | tf_op jit(solution)/shard_map/ppermute | solution.py:23
  45.3 10.3 %collective-permute-start.5 = (bf16[128,128]{1,0:T(8,128)(2,1)S(1)}, bf16[128,128]{1,0:T(8,128)(2,1)S(1)}, u32[]{:S(2)}, u32[]{:S(2)}) collective-permute-start(bf16[128,128]{1,0:T(8,128)(2,1)S(1)} %multiply_convert_fusion.2), channel_id=1, source_target_pairs={{0,32},{32,64},{64,96},{96,0},{1,33},{33,65},{65,97},{97,1},{2,34}... | collective-permute-start | bytes 98312 | tf_op jit(solution)/shard_map/ppermute | solution.py:23
  46.9 11.4 %collective-permute-start.6 = (bf16[128,128]{1,0:T(8,128)(2,1)S(1)}, bf16[128,128]{1,0:T(8,128)(2,1)S(1)}, u32[]{:S(2)}, u32[]{:S(2)}) collective-permute-start(bf16[128,128]{1,0:T(8,128)(2,1)S(1)} %multiply_convert_fusion.2), channel_id=1, source_target_pairs={{0,64},{32,96},{64,0},{96,32},{1,65},{33,97},{65,1},{97,33},{2,66}... | collective-permute-start | bytes 98312 | tf_op jit(solution)/shard_map/ppermute | solution.py:23
  49.5 8.7 %collective-permute-start.7 = (bf16[128,128]{1,0:T(8,128)(2,1)S(1)}, bf16[128,128]{1,0:T(8,128)(2,1)S(1)}, u32[]{:S(2)}, u32[]{:S(2)}) collective-permute-start(bf16[128,128]{1,0:T(8,128)(2,1)S(1)} %multiply_convert_fusion.2), channel_id=1, source_target_pairs={{0,96},{32,0},{64,32},{96,64},{1,97},{33,1},{65,33},{97,65},{2,98}... | collective-permute-start | bytes 98312 | tf_op jit(solution)/shard_map/ppermute | solution.py:23
  60.5 27.9 %all-to-all-start.1 = ((bf16[16,112,512]{2,1,0:T(8,128)(2,1)}), bf16[16,112,512]{2,1,0:T(8,128)(2,1)S(1)}, u32[]{:S(2)}, u32[]{:S(2)}) async-start(bf16[16,112,512]{2,1,0:T(8,128)(2,1)} %bitcast.12), calls=%async_computation.1 | async-start | bytes 3670016 | tf_op jit(solution)/shard_map/all_to_all | solution.py:195
  64.2 12.4 %collective-permute-start.9 = (bf16[4,128,128]{2,1,0:T(8,128)(2,1)S(1)}, bf16[4,128,128]{2,1,0:T(8,128)(2,1)S(1)}, u32[]{:S(2)}, u32[]{:S(2)}) collective-permute-start(bf16[4,128,128]{2,1,0:T(8,128)(2,1)S(1)} %pad_maximum_fusion.refs_1_.refs_4_), channel_id=1, source_target_pairs={{0,2},{2,4},{4,6},{6,0},{1,3},{3,5},{5,7},{7,1},{8,10},{10,12},{12... | collective-permute-start | bytes 393224 | tf_op jit(solution)/shard_map/ppermute | solution.py:23
  65.5 11.1 %collective-permute-start.11 = (bf16[4,128,128]{2,1,0:T(8,128)(2,1)S(1)}, bf16[4,128,128]{2,1,0:T(8,128)(2,1)S(1)}, u32[]{:S(2)}, u32[]{:S(2)}) collective-permute-start(bf16[4,128,128]{2,1,0:T(8,128)(2,1)S(1)} %pad_maximum_fusion.refs_1_.refs_4_), channel_id=1, source_target_pairs={{0,4},{2,6},{4,0},{6,2},{1,5},{3,7},{5,1},{7,3},{8,12},{10,14},{12... | collective-permute-start | bytes 393224 | tf_op jit(solution)/shard_map/ppermute | solution.py:23
  66.2 13.2 %collective-permute-start.13 = (bf16[4,128,128]{2,1,0:T(8,128)(2,1)S(1)}, bf16[4,128,128]{2,1,0:T(8,128)(2,1)S(1)}, u32[]{:S(2)}, u32[]{:S(2)}) collective-permute-start(bf16[4,128,128]{2,1,0:T(8,128)(2,1)S(1)} %pad_maximum_fusion.refs_1_.refs_4_), channel_id=1, source_target_pairs={{0,6},{2,0},{4,2},{6,4},{1,7},{3,1},{5,3},{7,5},{8,14},{10,8},{12,... | collective-permute-start | bytes 393224 | tf_op jit(solution)/shard_map/ppermute | solution.py:23
  70.8 10.7 %collective-permute-start.18 = (bf16[112,512]{1,0:T(8,128)(2,1)S(1)}, bf16[112,512]{1,0:T(8,128)(2,1)S(1)}, u32[]{:S(2)}, u32[]{:S(2)}) collective-permute-start(bf16[112,512]{1,0:T(8,128)(2,1)S(1)} %convert_element_type.29), channel_id=1, source_target_pairs={{0,128},{128,0},{1,129},{129,1},{2,130},{130,2},{3,131},{131,3},{4... | collective-permute-start | bytes 344072 | tf_op jit(solution)/shard_map/ppermute | solution.py:23
  76.0 5.6 %collective-permute-start.8 = (bf16[4,128,128]{2,1,0:T(8,128)(2,1)S(1)}, bf16[4,128,128]{2,1,0:T(8,128)(2,1)S(1)}, u32[]{:S(2)}, u32[]{:S(2)}) collective-permute-start(bf16[4,128,128]{2,1,0:T(8,128)(2,1)S(1)} %pad_maximum_fusion.refs_1_.refs_4_), channel_id=1, source_target_pairs={{0,1},{1,0},{2,3},{3,2},{4,5},{5,4},{6,7},{7,6},{8,9},{9,8},{10,11... | collective-permute-start | bytes 393224 | tf_op jit(solution)/shard_map/ppermute | solution.py:23
  76.6 5.0 %collective-permute-start.10 = (bf16[4,128,128]{2,1,0:T(8,128)(2,1)S(1)}, bf16[4,128,128]{2,1,0:T(8,128)(2,1)S(1)}, u32[]{:S(2)}, u32[]{:S(2)}) collective-permute-start(bf16[4,128,128]{2,1,0:T(8,128)(2,1)S(1)} %collective-permute-done.9.refs_3_.refs_6_), channel_id=1, source_target_pairs={{0,1},{1,0},{2,3},{3,2},{4,5},{5,4},{6,7},{7,6},{8,9},{9,8},{10,11... | collective-permute-start | bytes 393224 | tf_op jit(solution)/shard_map/ppermute | solution.py:23
  76.6 5.0 %collective-permute-start.12 = (bf16[4,128,128]{2,1,0:T(8,128)(2,1)S(1)}, bf16[4,128,128]{2,1,0:T(8,128)(2,1)S(1)}, u32[]{:S(2)}, u32[]{:S(2)}) collective-permute-start(bf16[4,128,128]{2,1,0:T(8,128)(2,1)S(1)} %collective-permute-done.11.refs_5_.refs_4_), channel_id=1, source_target_pairs={{0,1},{1,0},{2,3},{3,2},{4,5},{5,4},{6,7},{7,6},{8,9},{9,8},{10,11... | collective-permute-start | bytes 393224 | tf_op jit(solution)/shard_map/ppermute | solution.py:23
  79.4 2.2 %collective-permute-start.14 = (bf16[4,128,128]{2,1,0:T(8,128)(2,1)S(1)}, bf16[4,128,128]{2,1,0:T(8,128)(2,1)S(1)}, u32[]{:S(2)}, u32[]{:S(2)}) collective-permute-start(bf16[4,128,128]{2,1,0:T(8,128)(2,1)S(1)} %collective-permute-done.13.refs_7_.refs_6_), channel_id=1, source_target_pairs={{0,1},{1,0},{2,3},{3,2},{4,5},{5,4},{6,7},{7,6},{8,9},{9,8},{10,11... | collective-permute-start | bytes 393224 | tf_op jit(solution)/shard_map/ppermute | solution.py:23
  88.7 10.0 %collective-permute-start.19 = (bf16[112,512]{1,0:T(8,128)(2,1)S(1)}, bf16[112,512]{1,0:T(8,128)(2,1)S(1)}, u32[]{:S(2)}, u32[]{:S(2)}) collective-permute-start(bf16[112,512]{1,0:T(8,128)(2,1)S(1)} %convert_element_type.33), channel_id=1, source_target_pairs={{0,128},{128,0},{1,129},{129,1},{2,130},{130,2},{3,131},{131,3},{4... | collective-permute-start | bytes 344072 | tf_op jit(solution)/shard_map/ppermute | solution.py:23
  94.6 7.5 %collective-permute-start.23 = (bf16[112,512]{1,0:T(8,128)(2,1)S(1)}, bf16[112,512]{1,0:T(8,128)(2,1)S(1)}, u32[]{:S(2)}, u32[]{:S(2)}) collective-permute-start(bf16[112,512]{1,0:T(8,128)(2,1)S(1)} %multiply_convert_fusion.1.refs_9_.refs_0_), channel_id=1, source_target_pairs={{0,16},{8,24},{16,0},{24,8},{1,17},{9,25},{17,1},{25,9},{2,18},{10... | collective-permute-start | bytes 344072 | tf_op jit(solution)/shard_map/ppermute | solution.py:23
  95.5 8.4 %collective-permute-start.24 = (bf16[112,512]{1,0:T(8,128)(2,1)S(1)}, bf16[112,512]{1,0:T(8,128)(2,1)S(1)}, u32[]{:S(2)}, u32[]{:S(2)}) collective-permute-start(bf16[112,512]{1,0:T(8,128)(2,1)S(1)} %multiply_convert_fusion.1.refs_9_.refs_0_), channel_id=1, source_target_pairs={{0,8},{8,16},{16,24},{24,0},{1,9},{9,17},{17,25},{25,1},{2,10},{10... | collective-permute-start | bytes 344072 | tf_op jit(solution)/shard_map/ppermute | solution.py:23
  96.6 7.3 %collective-permute-start.25 = (bf16[112,512]{1,0:T(8,128)(2,1)S(1)}, bf16[112,512]{1,0:T(8,128)(2,1)S(1)}, u32[]{:S(2)}, u32[]{:S(2)}) collective-permute-start(bf16[112,512]{1,0:T(8,128)(2,1)S(1)} %multiply_convert_fusion.1.refs_9_.refs_0_), channel_id=1, source_target_pairs={{0,24},{8,0},{16,8},{24,16},{1,25},{9,1},{17,9},{25,17},{2,26},{10... | collective-permute-start | bytes 344072 | tf_op jit(solution)/shard_map/ppermute | solution.py:23
  98.8 6.4 %collective-permute-start.20 = (bf16[112,512]{1,0:T(8,128)(2,1)S(1)}, bf16[112,512]{1,0:T(8,128)(2,1)S(1)}, u32[]{:S(2)}, u32[]{:S(2)}) collective-permute-start(bf16[112,512]{1,0:T(8,128)(2,1)S(1)} %multiply_convert_fusion.refs_0_), channel_id=1, source_target_pairs={{0,16},{8,24},{16,0},{24,8},{1,17},{9,25},{17,1},{25,9},{2,18},{10... | collective-permute-start | bytes 344072 | tf_op jit(solution)/shard_map/ppermute | solution.py:23
  100.2 6.2 %collective-permute-start.21 = (bf16[112,512]{1,0:T(8,128)(2,1)S(1)}, bf16[112,512]{1,0:T(8,128)(2,1)S(1)}, u32[]{:S(2)}, u32[]{:S(2)}) collective-permute-start(bf16[112,512]{1,0:T(8,128)(2,1)S(1)} %multiply_convert_fusion.refs_0_), channel_id=1, source_target_pairs={{0,8},{8,16},{16,24},{24,0},{1,9},{9,17},{17,25},{25,1},{2,10},{10... | collective-permute-start | bytes 344072 | tf_op jit(solution)/shard_map/ppermute | solution.py:23
  102.0 4.8 %collective-permute-start.22 = (bf16[112,512]{1,0:T(8,128)(2,1)S(1)}, bf16[112,512]{1,0:T(8,128)(2,1)S(1)}, u32[]{:S(2)}, u32[]{:S(2)}) collective-permute-start(bf16[112,512]{1,0:T(8,128)(2,1)S(1)} %multiply_convert_fusion.refs_0_), channel_id=1, source_target_pairs={{0,24},{8,0},{16,8},{24,16},{1,25},{9,1},{17,9},{25,17},{2,26},{10... | collective-permute-start | bytes 344072 | tf_op jit(solution)/shard_map/ppermute | solution.py:23

commit v16 on v13

--- a/solution.py
+++ b/solution.py
@@ -256,7 +256,11 @@
         acts += [own, shifted(own, "core", 1)]
     near_sq = squared(near_got)
     near_pieces = [near_sq] + [shifted(near_sq, "y", step) for step in Y_STEPS]
-    far_sq = squared(gated(far_got, acts + [near_sq], jax.ShapeDtypeStruct))
+    far_got = gated(far_got, acts + [near_sq], jax.ShapeDtypeStruct)
+    summed = jnp.sum(far_got.astype(jnp.float32), axis=0)
+    other = shifted(summed.astype(jnp.bfloat16), "z_hi", 1)
+    total = summed + gated(other, near_pieces, jax.ShapeDtypeStruct).astype(jnp.float32)
+    far_sq = (total * total).astype(jnp.bfloat16)
     far_pieces = [far_sq] + [shifted(far_sq, "y", step) for step in Y_STEPS]
     out = corrected(far_pieces, acts[4:], corrected(near_pieces, acts[:4]))
     out = lax.all_to_all(out, "x", 0, 0, tiled=True)

time: 122 us -> 122 us (level); the launches traced: 120 us -> 122 us
  waiting for transfers between devices: 31.1 us -> 32.5 us
    ppermute x26, waiting for transfers between devices: 13.9 us -> 20.6 us  [shifted(): lax.ppermute(value, axis, [(i, (i + step) % size) for i in range(size)])]
    all_to_all x2, waiting for transfers between devices: 6.09 us -> 0.72 us  [exchanged(): lax.all_to_all(partial.reshape(16, columns // 16, tokens), ('x', 'y'), 0,...]
  transfers between devices with their start and end apart: 29 -> 29, of which waited for: 10 -> 9; matrix products, arithmetic and copies ran while one was open for 2% -> 2% of each run, Pallas kernels for 9% -> 9%
where the time goes in v16:
time: 122 us
  starting transfers between devices  56.1 us (46%)
  waiting for transfers between devices  32.5 us (27%)
  Pallas kernels  15.9 us (13%)
  blocking collectives  14.2 us (12%)
  other arithmetic  2.24 us (2%)
    ppermute x26, starting transfers between devices, shifted(): lax.ppermute(value, axis, [(i, (i + step) % size) for i in range(size)])  39.8 us
    ppermute x26, waiting for transfers between devices, shifted(): lax.ppermute(value, axis, [(i, (i + step) % size) for i in range(size)])  20.6 us
    all_to_all x1, blocking collectives, per_device(): out = lax.all_to_all(out, 'x', 0, 0, tiled=True)  14.2 us
    all_to_all x1, waiting for transfers between devices, act_squares(): got = lax.all_to_all(partials, ('x', 'y'), 0, 0, tiled=True)  11.1 us
    all_to_all x2, starting transfers between devices, exchanged(): lax.all_to_all(partial.reshape(16, columns // 16, tokens), ('x', 'y'), 0,...  9.16 us
    pallas_call x2, Pallas kernels, grad_partials(): pl.pallas_call(lambda *refs: grad_kernel(len(parts), *refs), out_shape=pl...  8.03 us
    all_to_all x1, starting transfers between devices, act_squares(): got = lax.all_to_all(partials, ('x', 'y'), 0, 0, tiled=True)  7.09 us
    pallas_call x1, Pallas kernels, first_partials(): pl.pallas_call(first_kernel, out_shape=(pltpu.HBM(shape, jnp.bfloat16), p...  4.53 us
  transfers between devices with their start and end apart: 29, of which 9 were waited for; matrix products, arithmetic and copies ran while one was open for 2% of the time, Pallas kernels for 9%

profile of v16, /device:TPU:64, one launch (start us, length us, event | category | flops | bytes accessed | tf_op | source)
XLA Modules:
  0.0 122.0 jit_solution(11478662479571905046)
XLA Ops:
  0.0 4.5 %first.1 = (bf16[16,128,256]{2,1,0:T(8,128)(2,1)}, bf16[128,896]{1,0:T(8,128)(2,1)}) custom-call(s32[1]{0:T(128)} %bitcast.2.place, f32[1,8192]{1,0:T(1,128)} %bitcast.16, bf16[128,896]{1,0:T(8,128)(2,1)} %gate_at.1, bf16[128,896]{1,0:T(8,128)(2,1)} %grad_at.1, bf16[128,8192]{1,0:T(8,128)(2,1)} %hidden_at.1, bf16[256,4096]{1,0:T(8,128)(2,1)} %basis_at.1), custom_call_target="tpu_custom_call" | custom-call | tf_op jit(solution)/shard_map/first/pallas_call | solution.py:90
  4.5 2.0 %collective-permute-start.16 = (bf16[128,896]{1,0:T(8,128)(2,1)}, bf16[128,896]{1,0:T(8,128)(2,1)}, u32[]{:S(2)}, u32[]{:S(2)}) collective-permute-start(bf16[128,896]{1,0:T(8,128)(2,1)} %get-tuple-element.9.refs_0_), channel_id=1, source_target_pairs={{0,2},{2,4},{4,6},{6,0},{1,3},{3,5},{5,7},{7,1},{8,10},{10,12},{12... | collective-permute-start | bytes 688136 | tf_op jit(solution)/shard_map/ppermute | solution.py:23
  6.5 7.1 %all-to-all-start = ((bf16[16,128,256]{2,1,0:T(8,128)(2,1)}), bf16[16,128,256]{2,1,0:T(8,128)(2,1)}, u32[]{:S(2)}, u32[]{:S(2)}) async-start(bf16[16,128,256]{2,1,0:T(8,128)(2,1)} %get-tuple-element.10), calls=%async_computation | async-start | bytes 2097152 | tf_op jit(solution)/shard_map/all_to_all | solution.py:159
  14.8 0.9 collective-permute-start.2
  15.7 4.1 %grad.3 = bf16[1792,512]{1,0:T(8,128)(2,1)} custom-call(bf16[128,896]{1,0:T(8,128)(2,1)} %get-tuple-element.9.refs_0_, bf16[128,896]{1,0:T(8,128)(2,1)S(1)} %collective-permute-done.15.refs_1_, bf16[128,896]{1,0:T(8,128)(2,1)} %collective-permute-done.16.refs_2_, bf16[128,896]{1,0:T(8,128)(2,1)S(1)} %collective-permute-done.17.refs_3_, ...), custom_call_target="tpu_custom_call" | custom-call | flops 8000000000 | bytes 10000000 | tf_op jit(solution)/shard_map/grad/pallas_call | solution.py:132
  19.8 11.1 %all-to-all-done.got = bf16[16,128,256]{2,1,0:T(8,128)(2,1)} async-done(((bf16[16,128,256]{2,1,0:T(8,128)(2,1)}), bf16[16,128,256]{2,1,0:T(8,128)(2,1)}, u32[]{:S(2)}, u32[]{:S(2)}) %all-to-all-start) | async-done | bytes 1048608 | tf_op jit(solution)/shard_map/all_to_all | solution.py:159
  30.9 4.4 %all-to-all-start.2 = ((bf16[16,112,512]{2,1,0:T(8,128)(2,1)}), bf16[16,112,512]{2,1,0:T(8,128)(2,1)}, u32[]{:S(2)}, u32[]{:S(2)}) async-start(bf16[16,112,512]{2,1,0:T(8,128)(2,1)} %bitcast.14), calls=%async_computation.2 | async-start | bytes 3670016 | tf_op jit(solution)/shard_map/all_to_all | solution.py:195
  35.4 1.4 %act_sum.1 = (f32[128,128]{1,0:T(8,128)S(1)}, f32[128,128]{1,0:T(8,128)S(1)}) custom-call(s32[1]{0:T(128)} %bitcast.4.place, bf16[16,128,256]{2,1,0:T(8,128)(2,1)} %all-to-all-done.got), custom_call_target="tpu_custom_call" | custom-call | flops 20000000000 | bytes 1000000 | tf_op jit(solution)/shard_map/act_sum/pallas_call | solution.py:163
  36.7 4.6 %collective-permute-start.4 = (f32[128,128]{1,0:T(8,128)S(1)}, f32[128,128]{1,0:T(8,128)S(1)}, u32[]{:S(2)}, u32[]{:S(2)}) collective-permute-start(f32[128,128]{1,0:T(8,128)S(1)} %get-tuple-element.12), channel_id=1, source_target_pairs={{0,128},{128,0},{1,129},{129,1},{2,130},{130,2},{3,131},{131,3},{4... | collective-permute-start | bytes 196616 | tf_op jit(solution)/shard_map/ppermute | solution.py:23
  41.8 3.4 %collective-permute-done.4 = f32[128,128]{1,0:T(8,128)S(1)} collective-permute-done((f32[128,128]{1,0:T(8,128)S(1)}, f32[128,128]{1,0:T(8,128)S(1)}, u32[]{:S(2)}, u32[]{:S(2)}) %collective-permute-start.4) | collective-permute-done | bytes 65568 | tf_op jit(solution)/shard_map/ppermute | solution.py:23
  45.3 1.8 %collective-permute-start.5 = (bf16[128,128]{1,0:T(8,128)(2,1)S(1)}, bf16[128,128]{1,0:T(8,128)(2,1)S(1)}, u32[]{:S(2)}, u32[]{:S(2)}) collective-permute-start(bf16[128,128]{1,0:T(8,128)(2,1)S(1)} %multiply_convert_fusion.2), channel_id=1, source_target_pairs={{0,32},{32,64},{64,96},{96,0},{1,33},{33,65},{65,97},{97,1},{2,34}... | collective-permute-start | bytes 98312 | tf_op jit(solution)/shard_map/ppermute | solution.py:23
  47.0 2.7 %collective-permute-start.6 = (bf16[128,128]{1,0:T(8,128)(2,1)S(1)}, bf16[128,128]{1,0:T(8,128)(2,1)S(1)}, u32[]{:S(2)}, u32[]{:S(2)}) collective-permute-start(bf16[128,128]{1,0:T(8,128)(2,1)S(1)} %multiply_convert_fusion.2), channel_id=1, source_target_pairs={{0,64},{32,96},{64,0},{96,32},{1,65},{33,97},{65,1},{97,33},{2,66}... | collective-permute-start | bytes 98312 | tf_op jit(solution)/shard_map/ppermute | solution.py:23
  49.8 1.4 %collective-permute-start.7 = (bf16[128,128]{1,0:T(8,128)(2,1)S(1)}, bf16[128,128]{1,0:T(8,128)(2,1)S(1)}, u32[]{:S(2)}, u32[]{:S(2)}) collective-permute-start(bf16[128,128]{1,0:T(8,128)(2,1)S(1)} %multiply_convert_fusion.2), channel_id=1, source_target_pairs={{0,96},{32,0},{64,32},{96,64},{1,97},{33,1},{65,33},{97,65},{2,98}... | collective-permute-start | bytes 98312 | tf_op jit(solution)/shard_map/ppermute | solution.py:23
  51.2 4.0 %grad.2.refs_0_ = bf16[1792,512]{1,0:T(8,128)(2,1)} custom-call(bf16[128,896]{1,0:T(8,128)(2,1)S(1)} %collective-permute-done.refs_0_, bf16[128,896]{1,0:T(8,128)(2,1)S(1)} %collective-permute-done.1.refs_1_, bf16[128,896]{1,0:T(8,128)(2,1)} %collective-permute-done.2.refs_2_, bf16[128,896]{1,0:T(8,128)(2,1)S(1)} %collective-permute-done.3.refs_3_, ...), custom_call_target="tpu_custom_call" | custom-call | tf_op jit(solution)/shard_map/grad/pallas_call | solution.py:132
  55.7 3.5 %collective-permute-done.6 = bf16[128,128]{1,0:T(8,128)(2,1)S(1)} collective-permute-done((bf16[128,128]{1,0:T(8,128)(2,1)S(1)}, bf16[128,128]{1,0:T(8,128)(2,1)S(1)}, u32[]{:S(2)}, u32[]{:S(2)}) %collective-permute-start.6) | collective-permute-done | bytes 32800 | tf_op jit(solution)/shard_map/ppermute | solution.py:23
  59.9 4.7 %all-to-all-start.1 = ((bf16[16,112,512]{2,1,0:T(8,128)(2,1)}), bf16[16,112,512]{2,1,0:T(8,128)(2,1)S(1)}, u32[]{:S(2)}, u32[]{:S(2)}) async-start(bf16[16,112,512]{2,1,0:T(8,128)(2,1)} %bitcast.12), calls=%async_computation.1 | async-start | bytes 3670016 | tf_op jit(solution)/shard_map/all_to_all | solution.py:195
  65.3 1.0 collective-permute-start.11
  66.3 1.0 collective-permute-start.13
  67.3 1.8 %convert_reduce_fusion.1 = f32[112,512]{1,0:T(8,128)S(1)} fusion(bf16[16,112,512]{2,1,0:T(8,128)(2,1)} %all-to-all-done.2), kind=kLoop, calls=%fused_computation.1 | loop fusion | flops 1777664 | bytes 2064384 | tf_op jit(solution)/shard_map/reduce_sum | solution.py:199
  69.1 6.5 %collective-permute-start.18 = (bf16[112,512]{1,0:T(8,128)(2,1)S(1)}, bf16[112,512]{1,0:T(8,128)(2,1)S(1)}, u32[]{:S(2)}, u32[]{:S(2)}) collective-permute-start(bf16[112,512]{1,0:T(8,128)(2,1)S(1)} %convert_element_type.29), channel_id=1, source_target_pairs={{0,128},{128,0},{1,129},{129,1},{2,130},{130,2},{3,131},{131,3},{4... | collective-permute-start | bytes 344072 | tf_op jit(solution)/shard_map/ppermute | solution.py:23
  76.6 4.6 %collective-permute-done.18 = bf16[112,512]{1,0:T(8,128)(2,1)S(1)} collective-permute-done((bf16[112,512]{1,0:T(8,128)(2,1)S(1)}, bf16[112,512]{1,0:T(8,128)(2,1)S(1)}, u32[]{:S(2)}, u32[]{:S(2)}) %collective-permute-start.18) | collective-permute-done | bytes 114720 | tf_op jit(solution)/shard_map/ppermute | solution.py:23
  81.3 4.5 %collective-permute-start.20 = (bf16[112,512]{1,0:T(8,128)(2,1)S(1)}, bf16[112,512]{1,0:T(8,128)(2,1)S(1)}, u32[]{:S(2)}, u32[]{:S(2)}) collective-permute-start(bf16[112,512]{1,0:T(8,128)(2,1)S(1)} %multiply_convert_fusion.1.refs_9_.refs_1_.refs_0_), channel_id=1, source_target_pairs={{0,16},{8,24},{16,0},{24,8},{1,17},{9,25},{17,1},{25,9},{2,18},{10... | collective-permute-start | bytes 344072 | tf_op jit(solution)/shard_map/ppermute | solution.py:23
  86.3 2.7 %collective-permute-start.22 = (bf16[112,512]{1,0:T(8,128)(2,1)S(1)}, bf16[112,512]{1,0:T(8,128)(2,1)S(1)}, u32[]{:S(2)}, u32[]{:S(2)}) collective-permute-start(bf16[112,512]{1,0:T(8,128)(2,1)S(1)} %multiply_convert_fusion.1.refs_9_.refs_1_.refs_0_), channel_id=1, source_target_pairs={{0,24},{8,0},{16,8},{24,16},{1,25},{9,1},{17,9},{25,17},{2,26},{10... | collective-permute-start | bytes 344072 | tf_op jit(solution)/shard_map/ppermute | solution.py:23
  89.3 3.0 %collective-permute-start.19 = (bf16[112,512]{1,0:T(8,128)(2,1)S(1)}, bf16[112,512]{1,0:T(8,128)(2,1)S(1)}, u32[]{:S(2)}, u32[]{:S(2)}) collective-permute-start(bf16[112,512]{1,0:T(8,128)(2,1)S(1)} %convert_element_type.33), channel_id=1, source_target_pairs={{0,128},{128,0},{1,129},{129,1},{2,130},{130,2},{3,131},{131,3},{4... | collective-permute-start | bytes 344072 | tf_op jit(solution)/shard_map/ppermute | solution.py:23
  92.3 5.9 %collective-permute-done.19.refs_0_ = bf16[112,512]{1,0:T(8,128)(2,1)S(1)} collective-permute-done((bf16[112,512]{1,0:T(8,128)(2,1)S(1)}, bf16[112,512]{1,0:T(8,128)(2,1)S(1)}, u32[]{:S(2)}, u32[]{:S(2)}) %collective-permute-start.19) | collective-permute-done | bytes 114720 | tf_op jit(solution)/shard_map/ppermute | solution.py:23
  99.5 2.7 %collective-permute-start.25 = (bf16[112,512]{1,0:T(8,128)(2,1)S(1)}, bf16[112,512]{1,0:T(8,128)(2,1)S(1)}, u32[]{:S(2)}, u32[]{:S(2)}) collective-permute-start(bf16[112,512]{1,0:T(8,128)(2,1)S(1)} %multiply_convert_fusion.refs_0_), channel_id=1, source_target_pairs={{0,24},{8,0},{16,8},{24,16},{1,25},{9,1},{17,9},{25,17},{2,26},{10... | collective-permute-start | bytes 344072 | tf_op jit(solution)/shard_map/ppermute | solution.py:23
  102.2 1.0 correct.2.refs_8_
  103.2 1.5 %collective-permute-done.23.refs_1_ = bf16[112,512]{1,0:T(8,128)(2,1)S(1)} collective-permute-done((bf16[112,512]{1,0:T(8,128)(2,1)S(1)}, bf16[112,512]{1,0:T(8,128)(2,1)S(1)}, u32[]{:S(2)}, u32[]{:S(2)}) %collective-permute-start.23) | collective-permute-done | bytes 114720 | tf_op jit(solution)/shard_map/ppermute | solution.py:23
  104.7 1.1 collective-permute-done.24.refs_2_
  105.9 1.0 correct.3
  106.9 14.2 %all_to_all.20 = f32[4,448,128]{2,1,0:T(8,128)S(1)} all-to-all(f32[4,448,128]{2,1,0:T(8,128)S(1)} %correct.3), channel_id=1, replica_groups=mesh['z_hi'=2,'x'=4,'y'=4,'z_lo'=4,'core'=2] {'x'}, dimensions={0} | all-to-all | bytes 1835008 | tf_op jit(solution)/shard_map/all_to_all | solution.py:266
  121.1 0.9 copy.14
  (48 shorter events, 6.9 us)
Async XLA Ops:
  0.0 15.7 %copy-start = (bf16[896,1792]{1,0:T(8,128)(2,1)S(1)}, bf16[896,1792]{1,0:T(8,128)(2,1)}, u32[]{:S(2)}) copy-start(bf16[896,1792]{1,0:T(8,128)(2,1)} %refs_4_.3) | copy-start | bytes 9633796
  4.5 9.2 %collective-permute-start.16 = (bf16[128,896]{1,0:T(8,128)(2,1)}, bf16[128,896]{1,0:T(8,128)(2,1)}, u32[]{:S(2)}, u32[]{:S(2)}) collective-permute-start(bf16[128,896]{1,0:T(8,128)(2,1)} %get-tuple-element.9.refs_0_), channel_id=1, source_target_pairs={{0,2},{2,4},{4,6},{6,0},{1,3},{3,5},{5,7},{7,1},{8,10},{10,12},{12... | collective-permute-start | bytes 688136 | tf_op jit(solution)/shard_map/ppermute | solution.py:23
  6.5 24.4 %all-to-all-start = ((bf16[16,128,256]{2,1,0:T(8,128)(2,1)}), bf16[16,128,256]{2,1,0:T(8,128)(2,1)}, u32[]{:S(2)}, u32[]{:S(2)}) async-start(bf16[16,128,256]{2,1,0:T(8,128)(2,1)} %get-tuple-element.10), calls=%async_computation | async-start | bytes 2097152 | tf_op jit(solution)/shard_map/all_to_all | solution.py:159
  13.6 2.1 %collective-permute-start.15 = (bf16[128,896]{1,0:T(8,128)(2,1)}, bf16[128,896]{1,0:T(8,128)(2,1)S(1)}, u32[]{:S(2)}, u32[]{:S(2)}) collective-permute-start(bf16[128,896]{1,0:T(8,128)(2,1)} %get-tuple-element.9.refs_0_), channel_id=1, source_target_pairs={{0,1},{1,0},{2,3},{3,2},{4,5},{5,4},{6,7},{7,6},{8,9},{9,8},{10,11... | collective-permute-start | bytes 688136 | tf_op jit(solution)/shard_map/ppermute | solution.py:23
  13.7 2.0 %collective-permute-start.17 = (bf16[128,896]{1,0:T(8,128)(2,1)}, bf16[128,896]{1,0:T(8,128)(2,1)S(1)}, u32[]{:S(2)}, u32[]{:S(2)}) collective-permute-start(bf16[128,896]{1,0:T(8,128)(2,1)} %collective-permute-done.16.refs_2_), channel_id=1, source_target_pairs={{0,1},{1,0},{2,3},{3,2},{4,5},{5,4},{6,7},{7,6},{8,9},{9,8},{10,11... | collective-permute-start | bytes 688136 | tf_op jit(solution)/shard_map/ppermute | solution.py:23
  14.2 27.1 %collective-permute-start = (bf16[128,896]{1,0:T(8,128)(2,1)}, bf16[128,896]{1,0:T(8,128)(2,1)S(1)}, u32[]{:S(2)}, u32[]{:S(2)}) collective-permute-start(bf16[128,896]{1,0:T(8,128)(2,1)} %get-tuple-element.9.refs_0_), channel_id=1, source_target_pairs={{0,4},{2,6},{4,0},{6,2},{1,5},{3,7},{5,1},{7,3},{8,12},{10,14},{12... | collective-permute-start | bytes 688136 | tf_op jit(solution)/shard_map/ppermute | solution.py:23
  14.8 26.5 %collective-permute-start.2 = (bf16[128,896]{1,0:T(8,128)(2,1)}, bf16[128,896]{1,0:T(8,128)(2,1)}, u32[]{:S(2)}, u32[]{:S(2)}) collective-permute-start(bf16[128,896]{1,0:T(8,128)(2,1)} %get-tuple-element.9.refs_0_), channel_id=1, source_target_pairs={{0,6},{2,0},{4,2},{6,4},{1,7},{3,1},{5,3},{7,5},{8,14},{10,8},{12,... | collective-permute-start | bytes 688136 | tf_op jit(solution)/shard_map/ppermute | solution.py:23
  30.9 29.0 %all-to-all-start.2 = ((bf16[16,112,512]{2,1,0:T(8,128)(2,1)}), bf16[16,112,512]{2,1,0:T(8,128)(2,1)}, u32[]{:S(2)}, u32[]{:S(2)}) async-start(bf16[16,112,512]{2,1,0:T(8,128)(2,1)} %bitcast.14), calls=%async_computation.2 | async-start | bytes 3670016 | tf_op jit(solution)/shard_map/all_to_all | solution.py:195
  36.7 8.5 %collective-permute-start.4 = (f32[128,128]{1,0:T(8,128)S(1)}, f32[128,128]{1,0:T(8,128)S(1)}, u32[]{:S(2)}, u32[]{:S(2)}) collective-permute-start(f32[128,128]{1,0:T(8,128)S(1)} %get-tuple-element.12), channel_id=1, source_target_pairs={{0,128},{128,0},{1,129},{129,1},{2,130},{130,2},{3,131},{131,3},{4... | collective-permute-start | bytes 196616 | tf_op jit(solution)/shard_map/ppermute | solution.py:23
  41.3 9.9 %collective-permute-start.1 = (bf16[128,896]{1,0:T(8,128)(2,1)S(1)}, bf16[128,896]{1,0:T(8,128)(2,1)S(1)}, u32[]{:S(2)}, u32[]{:S(2)}) collective-permute-start(bf16[128,896]{1,0:T(8,128)(2,1)S(1)} %collective-permute-done.refs_0_), channel_id=1, source_target_pairs={{0,1},{1,0},{2,3},{3,2},{4,5},{5,4},{6,7},{7,6},{8,9},{9,8},{10,11... | collective-permute-start | bytes 688136 | tf_op jit(solution)/shard_map/ppermute | solution.py:23
  41.3 9.9 %collective-permute-start.3 = (bf16[128,896]{1,0:T(8,128)(2,1)}, bf16[128,896]{1,0:T(8,128)(2,1)S(1)}, u32[]{:S(2)}, u32[]{:S(2)}) collective-permute-start(bf16[128,896]{1,0:T(8,128)(2,1)} %collective-permute-done.2.refs_2_), channel_id=1, source_target_pairs={{0,1},{1,0},{2,3},{3,2},{4,5},{5,4},{6,7},{7,6},{8,9},{9,8},{10,11... | collective-permute-start | bytes 688136 | tf_op jit(solution)/shard_map/ppermute | solution.py:23
  45.3 10.4 %collective-permute-start.5 = (bf16[128,128]{1,0:T(8,128)(2,1)S(1)}, bf16[128,128]{1,0:T(8,128)(2,1)S(1)}, u32[]{:S(2)}, u32[]{:S(2)}) collective-permute-start(bf16[128,128]{1,0:T(8,128)(2,1)S(1)} %multiply_convert_fusion.2), channel_id=1, source_target_pairs={{0,32},{32,64},{64,96},{96,0},{1,33},{33,65},{65,97},{97,1},{2,34}... | collective-permute-start | bytes 98312 | tf_op jit(solution)/shard_map/ppermute | solution.py:23
  47.0 12.1 %collective-permute-start.6 = (bf16[128,128]{1,0:T(8,128)(2,1)S(1)}, bf16[128,128]{1,0:T(8,128)(2,1)S(1)}, u32[]{:S(2)}, u32[]{:S(2)}) collective-permute-start(bf16[128,128]{1,0:T(8,128)(2,1)S(1)} %multiply_convert_fusion.2), channel_id=1, source_target_pairs={{0,64},{32,96},{64,0},{96,32},{1,65},{33,97},{65,1},{97,33},{2,66}... | collective-permute-start | bytes 98312 | tf_op jit(solution)/shard_map/ppermute | solution.py:23
  49.8 9.4 %collective-permute-start.7 = (bf16[128,128]{1,0:T(8,128)(2,1)S(1)}, bf16[128,128]{1,0:T(8,128)(2,1)S(1)}, u32[]{:S(2)}, u32[]{:S(2)}) collective-permute-start(bf16[128,128]{1,0:T(8,128)(2,1)S(1)} %multiply_convert_fusion.2), channel_id=1, source_target_pairs={{0,96},{32,0},{64,32},{96,64},{1,97},{33,1},{65,33},{97,65},{2,98}... | collective-permute-start | bytes 98312 | tf_op jit(solution)/shard_map/ppermute | solution.py:23
  59.9 29.1 %all-to-all-start.1 = ((bf16[16,112,512]{2,1,0:T(8,128)(2,1)}), bf16[16,112,512]{2,1,0:T(8,128)(2,1)S(1)}, u32[]{:S(2)}, u32[]{:S(2)}) async-start(bf16[16,112,512]{2,1,0:T(8,128)(2,1)} %bitcast.12), calls=%async_computation.1 | async-start | bytes 3670016 | tf_op jit(solution)/shard_map/all_to_all | solution.py:195
  64.7 10.9 %collective-permute-start.9 = (bf16[4,128,128]{2,1,0:T(8,128)(2,1)S(1)}, bf16[4,128,128]{2,1,0:T(8,128)(2,1)S(1)}, u32[]{:S(2)}, u32[]{:S(2)}) collective-permute-start(bf16[4,128,128]{2,1,0:T(8,128)(2,1)S(1)} %pad_maximum_fusion.refs_1_.refs_4_), channel_id=1, source_target_pairs={{0,2},{2,4},{4,6},{6,0},{1,3},{3,5},{5,7},{7,1},{8,10},{10,12},{12... | collective-permute-start | bytes 393224 | tf_op jit(solution)/shard_map/ppermute | solution.py:23
  65.3 10.8 %collective-permute-start.11 = (bf16[4,128,128]{2,1,0:T(8,128)(2,1)S(1)}, bf16[4,128,128]{2,1,0:T(8,128)(2,1)S(1)}, u32[]{:S(2)}, u32[]{:S(2)}) collective-permute-start(bf16[4,128,128]{2,1,0:T(8,128)(2,1)S(1)} %pad_maximum_fusion.refs_1_.refs_4_), channel_id=1, source_target_pairs={{0,4},{2,6},{4,0},{6,2},{1,5},{3,7},{5,1},{7,3},{8,12},{10,14},{12... | collective-permute-start | bytes 393224 | tf_op jit(solution)/shard_map/ppermute | solution.py:23
  66.3 9.9 %collective-permute-start.13 = (bf16[4,128,128]{2,1,0:T(8,128)(2,1)S(1)}, bf16[4,128,128]{2,1,0:T(8,128)(2,1)S(1)}, u32[]{:S(2)}, u32[]{:S(2)}) collective-permute-start(bf16[4,128,128]{2,1,0:T(8,128)(2,1)S(1)} %pad_maximum_fusion.refs_1_.refs_4_), channel_id=1, source_target_pairs={{0,6},{2,0},{4,2},{6,4},{1,7},{3,1},{5,3},{7,5},{8,14},{10,8},{12,... | collective-permute-start | bytes 393224 | tf_op jit(solution)/shard_map/ppermute | solution.py:23
  69.1 12.1 %collective-permute-start.18 = (bf16[112,512]{1,0:T(8,128)(2,1)S(1)}, bf16[112,512]{1,0:T(8,128)(2,1)S(1)}, u32[]{:S(2)}, u32[]{:S(2)}) collective-permute-start(bf16[112,512]{1,0:T(8,128)(2,1)S(1)} %convert_element_type.29), channel_id=1, source_target_pairs={{0,128},{128,0},{1,129},{129,1},{2,130},{130,2},{3,131},{131,3},{4... | collective-permute-start | bytes 344072 | tf_op jit(solution)/shard_map/ppermute | solution.py:23
  75.6 10.2 %collective-permute-start.8 = (bf16[4,128,128]{2,1,0:T(8,128)(2,1)S(1)}, bf16[4,128,128]{2,1,0:T(8,128)(2,1)S(1)}, u32[]{:S(2)}, u32[]{:S(2)}) collective-permute-start(bf16[4,128,128]{2,1,0:T(8,128)(2,1)S(1)} %pad_maximum_fusion.refs_1_.refs_4_), channel_id=1, source_target_pairs={{0,1},{1,0},{2,3},{3,2},{4,5},{5,4},{6,7},{7,6},{8,9},{9,8},{10,11... | collective-permute-start | bytes 393224 | tf_op jit(solution)/shard_map/ppermute | solution.py:23
  75.6 10.8 %collective-permute-start.10 = (bf16[4,128,128]{2,1,0:T(8,128)(2,1)S(1)}, bf16[4,128,128]{2,1,0:T(8,128)(2,1)S(1)}, u32[]{:S(2)}, u32[]{:S(2)}) collective-permute-start(bf16[4,128,128]{2,1,0:T(8,128)(2,1)S(1)} %collective-permute-done.9.refs_3_.refs_6_), channel_id=1, source_target_pairs={{0,1},{1,0},{2,3},{3,2},{4,5},{5,4},{6,7},{7,6},{8,9},{9,8},{10,11... | collective-permute-start | bytes 393224 | tf_op jit(solution)/shard_map/ppermute | solution.py:23
  76.1 12.9 %collective-permute-start.12 = (bf16[4,128,128]{2,1,0:T(8,128)(2,1)S(1)}, bf16[4,128,128]{2,1,0:T(8,128)(2,1)S(1)}, u32[]{:S(2)}, u32[]{:S(2)}) collective-permute-start(bf16[4,128,128]{2,1,0:T(8,128)(2,1)S(1)} %collective-permute-done.11.refs_5_.refs_4_), channel_id=1, source_target_pairs={{0,1},{1,0},{2,3},{3,2},{4,5},{5,4},{6,7},{7,6},{8,9},{9,8},{10,11... | collective-permute-start | bytes 393224 | tf_op jit(solution)/shard_map/ppermute | solution.py:23
  76.2 12.8 %collective-permute-start.14 = (bf16[4,128,128]{2,1,0:T(8,128)(2,1)S(1)}, bf16[4,128,128]{2,1,0:T(8,128)(2,1)S(1)}, u32[]{:S(2)}, u32[]{:S(2)}) collective-permute-start(bf16[4,128,128]{2,1,0:T(8,128)(2,1)S(1)} %collective-permute-done.13.refs_7_.refs_6_), channel_id=1, source_target_pairs={{0,1},{1,0},{2,3},{3,2},{4,5},{5,4},{6,7},{7,6},{8,9},{9,8},{10,11... | collective-permute-start | bytes 393224 | tf_op jit(solution)/shard_map/ppermute | solution.py:23
  81.3 11.0 %collective-permute-start.20 = (bf16[112,512]{1,0:T(8,128)(2,1)S(1)}, bf16[112,512]{1,0:T(8,128)(2,1)S(1)}, u32[]{:S(2)}, u32[]{:S(2)}) collective-permute-start(bf16[112,512]{1,0:T(8,128)(2,1)S(1)} %multiply_convert_fusion.1.refs_9_.refs_1_.refs_0_), channel_id=1, source_target_pairs={{0,16},{8,24},{16,0},{24,8},{1,17},{9,25},{17,1},{25,9},{2,18},{10... | collective-permute-start | bytes 344072 | tf_op jit(solution)/shard_map/ppermute | solution.py:23
  85.8 6.5 %collective-permute-start.21 = (bf16[112,512]{1,0:T(8,128)(2,1)S(1)}, bf16[112,512]{1,0:T(8,128)(2,1)S(1)}, u32[]{:S(2)}, u32[]{:S(2)}) collective-permute-start(bf16[112,512]{1,0:T(8,128)(2,1)S(1)} %multiply_convert_fusion.1.refs_9_.refs_1_.refs_0_), channel_id=1, source_target_pairs={{0,8},{8,16},{16,24},{24,0},{1,9},{9,17},{17,25},{25,1},{2,10},{10... | collective-permute-start | bytes 344072 | tf_op jit(solution)/shard_map/ppermute | solution.py:23
  86.3 6.0 %collective-permute-start.22 = (bf16[112,512]{1,0:T(8,128)(2,1)S(1)}, bf16[112,512]{1,0:T(8,128)(2,1)S(1)}, u32[]{:S(2)}, u32[]{:S(2)}) collective-permute-start(bf16[112,512]{1,0:T(8,128)(2,1)S(1)} %multiply_convert_fusion.1.refs_9_.refs_1_.refs_0_), channel_id=1, source_target_pairs={{0,24},{8,0},{16,8},{24,16},{1,25},{9,1},{17,9},{25,17},{2,26},{10... | collective-permute-start | bytes 344072 | tf_op jit(solution)/shard_map/ppermute | solution.py:23
  89.3 8.9 %collective-permute-start.19 = (bf16[112,512]{1,0:T(8,128)(2,1)S(1)}, bf16[112,512]{1,0:T(8,128)(2,1)S(1)}, u32[]{:S(2)}, u32[]{:S(2)}) collective-permute-start(bf16[112,512]{1,0:T(8,128)(2,1)S(1)} %convert_element_type.33), channel_id=1, source_target_pairs={{0,128},{128,0},{1,129},{129,1},{2,130},{130,2},{3,131},{131,3},{4... | collective-permute-start | bytes 344072 | tf_op jit(solution)/shard_map/ppermute | solution.py:23
  98.2 6.5 %collective-permute-start.23 = (bf16[112,512]{1,0:T(8,128)(2,1)S(1)}, bf16[112,512]{1,0:T(8,128)(2,1)S(1)}, u32[]{:S(2)}, u32[]{:S(2)}) collective-permute-start(bf16[112,512]{1,0:T(8,128)(2,1)S(1)} %multiply_convert_fusion.refs_0_), channel_id=1, source_target_pairs={{0,16},{8,24},{16,0},{24,8},{1,17},{9,25},{17,1},{25,9},{2,18},{10... | collective-permute-start | bytes 344072 | tf_op jit(solution)/shard_map/ppermute | solution.py:23
  98.9 6.9 %collective-permute-start.24 = (bf16[112,512]{1,0:T(8,128)(2,1)S(1)}, bf16[112,512]{1,0:T(8,128)(2,1)S(1)}, u32[]{:S(2)}, u32[]{:S(2)}) collective-permute-start(bf16[112,512]{1,0:T(8,128)(2,1)S(1)} %multiply_convert_fusion.refs_0_), channel_id=1, source_target_pairs={{0,8},{8,16},{16,24},{24,0},{1,9},{9,17},{17,25},{25,1},{2,10},{10... | collective-permute-start | bytes 344072 | tf_op jit(solution)/shard_map/ppermute | solution.py:23
  99.5 6.4 %collective-permute-start.25 = (bf16[112,512]{1,0:T(8,128)(2,1)S(1)}, bf16[112,512]{1,0:T(8,128)(2,1)S(1)}, u32[]{:S(2)}, u32[]{:S(2)}) collective-permute-start(bf16[112,512]{1,0:T(8,128)(2,1)S(1)} %multiply_convert_fusion.refs_0_), channel_id=1, source_target_pairs={{0,24},{8,0},{16,8},{24,16},{1,25},{9,1},{17,9},{25,17},{2,26},{10... | collective-permute-start | bytes 344072 | tf_op jit(solution)/shard_map/ppermute | solution.py:23

commit v17 on v16

--- a/solution.py
+++ b/solution.py
@@ -259,7 +259,7 @@
     far_got = gated(far_got, acts + [near_sq], jax.ShapeDtypeStruct)
     summed = jnp.sum(far_got.astype(jnp.float32), axis=0)
     other = shifted(summed.astype(jnp.bfloat16), "z_hi", 1)
-    total = summed + gated(other, near_pieces, jax.ShapeDtypeStruct).astype(jnp.float32)
+    total = summed + gated(other, near_pieces[1:2], jax.ShapeDtypeStruct).astype(jnp.float32)
     far_sq = (total * total).astype(jnp.bfloat16)
     far_pieces = [far_sq] + [shifted(far_sq, "y", step) for step in Y_STEPS]
     out = corrected(far_pieces, acts[4:], corrected(near_pieces, acts[:4]))

time: 122 us -> 122 us (level)
  waiting for transfers between devices: 32.5 us -> 28.7 us
  starting transfers between devices: 56.1 us -> 58.8 us
    ppermute x26, waiting for transfers between devices: 20.6 us -> 15.6 us  [shifted(): lax.ppermute(value, axis, [(i, (i + step) % size) for i in range(size)])]
    ppermute x26, starting transfers between devices: 39.8 us -> 42.6 us  [shifted(): lax.ppermute(value, axis, [(i, (i + step) % size) for i in range(size)])]
    all_to_all x2, waiting for transfers between devices: 0.72 us -> 2.01 us  [exchanged(): lax.all_to_all(partial.reshape(16, columns // 16, tokens), ('x', 'y'), 0,...]
  transfers between devices with their start and end apart: 29 -> 29, of which waited for: 9 -> 10; matrix products, arithmetic and copies ran while one was open for 2% -> 2% of each run, Pallas kernels for 9% -> 9%
where the time goes in v17:
time: 122 us; the launch traced here: 121 us
  starting transfers between devices  58.8 us (48%)
  waiting for transfers between devices  28.7 us (24%)
  Pallas kernels  15.9 us (13%)
  blocking collectives  14.3 us (12%)
  other arithmetic  2.24 us (2%)
    ppermute x26, starting transfers between devices, shifted(): lax.ppermute(value, axis, [(i, (i + step) % size) for i in range(size)])  42.6 us
    ppermute x26, waiting for transfers between devices, shifted(): lax.ppermute(value, axis, [(i, (i + step) % size) for i in range(size)])  15.6 us
    all_to_all x1, blocking collectives, per_device(): out = lax.all_to_all(out, 'x', 0, 0, tiled=True)  14.3 us
    all_to_all x1, waiting for transfers between devices, act_squares(): got = lax.all_to_all(partials, ('x', 'y'), 0, 0, tiled=True)  11.1 us
    all_to_all x2, starting transfers between devices, exchanged(): lax.all_to_all(partial.reshape(16, columns // 16, tokens), ('x', 'y'), 0,...  9.16 us
    pallas_call x2, Pallas kernels, grad_partials(): pl.pallas_call(lambda *refs: grad_kernel(len(parts), *refs), out_shape=pl...  8.03 us
    all_to_all x1, starting transfers between devices, act_squares(): got = lax.all_to_all(partials, ('x', 'y'), 0, 0, tiled=True)  7.09 us
    pallas_call x1, Pallas kernels, first_partials(): pl.pallas_call(first_kernel, out_shape=(pltpu.HBM(shape, jnp.bfloat16), p...  4.53 us
  transfers between devices with their start and end apart: 29, of which 10 were waited for; matrix products, arithmetic and copies ran while one was open for 2% of the time, Pallas kernels for 9%

profile of v17, /device:TPU:64, one launch (start us, length us, event | category | flops | bytes accessed | tf_op | source)
XLA Modules:
  0.0 121.1 jit_solution(3116729504798702910)
XLA Ops:
  0.0 4.5 %first.1 = (bf16[16,128,256]{2,1,0:T(8,128)(2,1)}, bf16[128,896]{1,0:T(8,128)(2,1)}) custom-call(s32[1]{0:T(128)} %bitcast.2.place, f32[1,8192]{1,0:T(1,128)} %bitcast.16, bf16[128,896]{1,0:T(8,128)(2,1)} %gate_at.1, bf16[128,896]{1,0:T(8,128)(2,1)} %grad_at.1, bf16[128,8192]{1,0:T(8,128)(2,1)} %hidden_at.1, bf16[256,4096]{1,0:T(8,128)(2,1)} %basis_at.1), custom_call_target="tpu_custom_call" | custom-call | tf_op jit(solution)/shard_map/first/pallas_call | solution.py:90
  4.5 2.0 %collective-permute-start.16 = (bf16[128,896]{1,0:T(8,128)(2,1)}, bf16[128,896]{1,0:T(8,128)(2,1)}, u32[]{:S(2)}, u32[]{:S(2)}) collective-permute-start(bf16[128,896]{1,0:T(8,128)(2,1)} %get-tuple-element.9.refs_0_), channel_id=1, source_target_pairs={{0,2},{2,4},{4,6},{6,0},{1,3},{3,5},{5,7},{7,1},{8,10},{10,12},{12... | collective-permute-start | bytes 688136 | tf_op jit(solution)/shard_map/ppermute | solution.py:23
  6.5 7.1 %all-to-all-start = ((bf16[16,128,256]{2,1,0:T(8,128)(2,1)}), bf16[16,128,256]{2,1,0:T(8,128)(2,1)}, u32[]{:S(2)}, u32[]{:S(2)}) async-start(bf16[16,128,256]{2,1,0:T(8,128)(2,1)} %get-tuple-element.10), calls=%async_computation | async-start | bytes 2097152 | tf_op jit(solution)/shard_map/all_to_all | solution.py:159
  15.7 4.1 %grad.3 = bf16[1792,512]{1,0:T(8,128)(2,1)} custom-call(bf16[128,896]{1,0:T(8,128)(2,1)} %get-tuple-element.9.refs_0_, bf16[128,896]{1,0:T(8,128)(2,1)S(1)} %collective-permute-done.15.refs_1_, bf16[128,896]{1,0:T(8,128)(2,1)} %collective-permute-done.16.refs_2_, bf16[128,896]{1,0:T(8,128)(2,1)S(1)} %collective-permute-done.17.refs_3_, ...), custom_call_target="tpu_custom_call" | custom-call | flops 8000000000 | bytes 10000000 | tf_op jit(solution)/shard_map/grad/pallas_call | solution.py:132
  19.8 11.1 %all-to-all-done.got = bf16[16,128,256]{2,1,0:T(8,128)(2,1)} async-done(((bf16[16,128,256]{2,1,0:T(8,128)(2,1)}), bf16[16,128,256]{2,1,0:T(8,128)(2,1)}, u32[]{:S(2)}, u32[]{:S(2)}) %all-to-all-start) | async-done | bytes 1048608 | tf_op jit(solution)/shard_map/all_to_all | solution.py:159
  30.9 4.4 %all-to-all-start.2 = ((bf16[16,112,512]{2,1,0:T(8,128)(2,1)}), bf16[16,112,512]{2,1,0:T(8,128)(2,1)}, u32[]{:S(2)}, u32[]{:S(2)}) async-start(bf16[16,112,512]{2,1,0:T(8,128)(2,1)} %bitcast.14), calls=%async_computation.2 | async-start | bytes 3670016 | tf_op jit(solution)/shard_map/all_to_all | solution.py:195
  35.4 1.4 %act_sum.1 = (f32[128,128]{1,0:T(8,128)S(1)}, f32[128,128]{1,0:T(8,128)S(1)}) custom-call(s32[1]{0:T(128)} %bitcast.4.place, bf16[16,128,256]{2,1,0:T(8,128)(2,1)} %all-to-all-done.got), custom_call_target="tpu_custom_call" | custom-call | flops 20000000000 | bytes 1000000 | tf_op jit(solution)/shard_map/act_sum/pallas_call | solution.py:163
  36.7 4.6 %collective-permute-start.4 = (f32[128,128]{1,0:T(8,128)S(1)}, f32[128,128]{1,0:T(8,128)S(1)}, u32[]{:S(2)}, u32[]{:S(2)}) collective-permute-start(f32[128,128]{1,0:T(8,128)S(1)} %get-tuple-element.12), channel_id=1, source_target_pairs={{0,128},{128,0},{1,129},{129,1},{2,130},{130,2},{3,131},{131,3},{4... | collective-permute-start | bytes 196616 | tf_op jit(solution)/shard_map/ppermute | solution.py:23
  41.8 3.4 %collective-permute-done.4 = f32[128,128]{1,0:T(8,128)S(1)} collective-permute-done((f32[128,128]{1,0:T(8,128)S(1)}, f32[128,128]{1,0:T(8,128)S(1)}, u32[]{:S(2)}, u32[]{:S(2)}) %collective-permute-start.4) | collective-permute-done | bytes 65568 | tf_op jit(solution)/shard_map/ppermute | solution.py:23
  45.3 1.8 %collective-permute-start.5 = (bf16[128,128]{1,0:T(8,128)(2,1)S(1)}, bf16[128,128]{1,0:T(8,128)(2,1)S(1)}, u32[]{:S(2)}, u32[]{:S(2)}) collective-permute-start(bf16[128,128]{1,0:T(8,128)(2,1)S(1)} %multiply_convert_fusion.2), channel_id=1, source_target_pairs={{0,32},{32,64},{64,96},{96,0},{1,33},{33,65},{65,97},{97,1},{2,34}... | collective-permute-start | bytes 98312 | tf_op jit(solution)/shard_map/ppermute | solution.py:23
  47.0 2.7 %collective-permute-start.6 = (bf16[128,128]{1,0:T(8,128)(2,1)S(1)}, bf16[128,128]{1,0:T(8,128)(2,1)S(1)}, u32[]{:S(2)}, u32[]{:S(2)}) collective-permute-start(bf16[128,128]{1,0:T(8,128)(2,1)S(1)} %multiply_convert_fusion.2), channel_id=1, source_target_pairs={{0,64},{32,96},{64,0},{96,32},{1,65},{33,97},{65,1},{97,33},{2,66}... | collective-permute-start | bytes 98312 | tf_op jit(solution)/shard_map/ppermute | solution.py:23
  49.8 1.4 %collective-permute-start.7 = (bf16[128,128]{1,0:T(8,128)(2,1)S(1)}, bf16[128,128]{1,0:T(8,128)(2,1)S(1)}, u32[]{:S(2)}, u32[]{:S(2)}) collective-permute-start(bf16[128,128]{1,0:T(8,128)(2,1)S(1)} %multiply_convert_fusion.2), channel_id=1, source_target_pairs={{0,96},{32,0},{64,32},{96,64},{1,97},{33,1},{65,33},{97,65},{2,98}... | collective-permute-start | bytes 98312 | tf_op jit(solution)/shard_map/ppermute | solution.py:23
  51.2 4.0 %grad.2.refs_0_ = bf16[1792,512]{1,0:T(8,128)(2,1)} custom-call(bf16[128,896]{1,0:T(8,128)(2,1)S(1)} %collective-permute-done.refs_0_, bf16[128,896]{1,0:T(8,128)(2,1)S(1)} %collective-permute-done.1.refs_1_, bf16[128,896]{1,0:T(8,128)(2,1)} %collective-permute-done.2.refs_2_, bf16[128,896]{1,0:T(8,128)(2,1)S(1)} %collective-permute-done.3.refs_3_, ...), custom_call_target="tpu_custom_call" | custom-call | tf_op jit(solution)/shard_map/grad/pallas_call | solution.py:132
  55.7 3.5 %collective-permute-done.6 = bf16[128,128]{1,0:T(8,128)(2,1)S(1)} collective-permute-done((bf16[128,128]{1,0:T(8,128)(2,1)S(1)}, bf16[128,128]{1,0:T(8,128)(2,1)S(1)}, u32[]{:S(2)}, u32[]{:S(2)}) %collective-permute-start.6) | collective-permute-done | bytes 32800 | tf_op jit(solution)/shard_map/ppermute | solution.py:23
  59.9 4.7 %all-to-all-start.1 = ((bf16[16,112,512]{2,1,0:T(8,128)(2,1)}), bf16[16,112,512]{2,1,0:T(8,128)(2,1)S(1)}, u32[]{:S(2)}, u32[]{:S(2)}) async-start(bf16[16,112,512]{2,1,0:T(8,128)(2,1)} %bitcast.12), calls=%async_computation.1 | async-start | bytes 3670016 | tf_op jit(solution)/shard_map/all_to_all | solution.py:195
  65.3 1.0 collective-permute-start.11
  66.3 1.0 collective-permute-start.13
  67.3 1.8 %convert_reduce_fusion.1 = f32[112,512]{1,0:T(8,128)S(1)} fusion(bf16[16,112,512]{2,1,0:T(8,128)(2,1)} %all-to-all-done.2), kind=kLoop, calls=%fused_computation.1 | loop fusion | flops 1777664 | bytes 2064384 | tf_op jit(solution)/shard_map/reduce_sum | solution.py:199
  69.1 6.5 %collective-permute-start.18 = (bf16[112,512]{1,0:T(8,128)(2,1)S(1)}, bf16[112,512]{1,0:T(8,128)(2,1)S(1)}, u32[]{:S(2)}, u32[]{:S(2)}) collective-permute-start(bf16[112,512]{1,0:T(8,128)(2,1)S(1)} %convert_element_type.29), channel_id=1, source_target_pairs={{0,128},{128,0},{1,129},{129,1},{2,130},{130,2},{3,131},{131,3},{4... | collective-permute-start | bytes 344072 | tf_op jit(solution)/shard_map/ppermute | solution.py:23
  76.6 4.6 %collective-permute-done.18 = bf16[112,512]{1,0:T(8,128)(2,1)S(1)} collective-permute-done((bf16[112,512]{1,0:T(8,128)(2,1)S(1)}, bf16[112,512]{1,0:T(8,128)(2,1)S(1)}, u32[]{:S(2)}, u32[]{:S(2)}) %collective-permute-start.18) | collective-permute-done | bytes 114720 | tf_op jit(solution)/shard_map/ppermute | solution.py:23
  81.3 4.5 %collective-permute-start.20 = (bf16[112,512]{1,0:T(8,128)(2,1)S(1)}, bf16[112,512]{1,0:T(8,128)(2,1)S(1)}, u32[]{:S(2)}, u32[]{:S(2)}) collective-permute-start(bf16[112,512]{1,0:T(8,128)(2,1)S(1)} %multiply_convert_fusion.1.refs_9_.refs_0_), channel_id=1, source_target_pairs={{0,16},{8,24},{16,0},{24,8},{1,17},{9,25},{17,1},{25,9},{2,18},{10... | collective-permute-start | bytes 344072 | tf_op jit(solution)/shard_map/ppermute | solution.py:23
  85.8 1.3 %all-to-all-done.1.refs_0_ = bf16[16,112,512]{2,1,0:T(8,128)(2,1)S(1)} async-done(((bf16[16,112,512]{2,1,0:T(8,128)(2,1)}), bf16[16,112,512]{2,1,0:T(8,128)(2,1)S(1)}, u32[]{:S(2)}, u32[]{:S(2)}) %all-to-all-start.1) | async-done | bytes 1835040 | tf_op jit(solution)/shard_map/all_to_all | solution.py:195
  87.4 4.6 %collective-permute-start.19 = (bf16[112,512]{1,0:T(8,128)(2,1)S(1)}, bf16[112,512]{1,0:T(8,128)(2,1)S(1)}, u32[]{:S(2)}, u32[]{:S(2)}) collective-permute-start(bf16[112,512]{1,0:T(8,128)(2,1)S(1)} %convert_element_type.33), channel_id=1, source_target_pairs={{0,128},{128,0},{1,129},{129,1},{2,130},{130,2},{3,131},{131,3},{4... | collective-permute-start | bytes 344072 | tf_op jit(solution)/shard_map/ppermute | solution.py:23
  92.7 2.5 %collective-permute-start.25 = (bf16[112,512]{1,0:T(8,128)(2,1)S(1)}, bf16[112,512]{1,0:T(8,128)(2,1)S(1)}, u32[]{:S(2)}, u32[]{:S(2)}) collective-permute-start(bf16[112,512]{1,0:T(8,128)(2,1)S(1)} %multiply_convert_fusion.1.refs_9_.refs_0_), channel_id=1, source_target_pairs={{0,24},{8,0},{16,8},{24,16},{1,25},{9,1},{17,9},{25,17},{2,26},{10... | collective-permute-start | bytes 344072 | tf_op jit(solution)/shard_map/ppermute | solution.py:23
  95.2 1.8 %collective-permute-done.19.refs_0_ = bf16[112,512]{1,0:T(8,128)(2,1)S(1)} collective-permute-done((bf16[112,512]{1,0:T(8,128)(2,1)S(1)}, bf16[112,512]{1,0:T(8,128)(2,1)S(1)}, u32[]{:S(2)}, u32[]{:S(2)}) %collective-permute-start.19) | collective-permute-done | bytes 114720 | tf_op jit(solution)/shard_map/ppermute | solution.py:23
  97.1 1.8 %collective-permute-start.21 = (bf16[112,512]{1,0:T(8,128)(2,1)S(1)}, bf16[112,512]{1,0:T(8,128)(2,1)S(1)}, u32[]{:S(2)}, u32[]{:S(2)}) collective-permute-start(bf16[112,512]{1,0:T(8,128)(2,1)S(1)} %multiply_convert_fusion.refs_0_), channel_id=1, source_target_pairs={{0,16},{8,24},{16,0},{24,8},{1,17},{9,25},{17,1},{25,9},{2,18},{10... | collective-permute-start | bytes 344072 | tf_op jit(solution)/shard_map/ppermute | solution.py:23
  98.9 3.2 %collective-permute-start.23 = (bf16[112,512]{1,0:T(8,128)(2,1)S(1)}, bf16[112,512]{1,0:T(8,128)(2,1)S(1)}, u32[]{:S(2)}, u32[]{:S(2)}) collective-permute-start(bf16[112,512]{1,0:T(8,128)(2,1)S(1)} %multiply_convert_fusion.refs_0_), channel_id=1, source_target_pairs={{0,24},{8,0},{16,8},{24,16},{1,25},{9,1},{17,9},{25,17},{2,26},{10... | collective-permute-start | bytes 344072 | tf_op jit(solution)/shard_map/ppermute | solution.py:23
  102.2 1.0 correct.2.refs_8_
  103.5 1.4 %collective-permute-done.22.refs_2_ = bf16[112,512]{1,0:T(8,128)(2,1)S(1)} collective-permute-done((bf16[112,512]{1,0:T(8,128)(2,1)S(1)}, bf16[112,512]{1,0:T(8,128)(2,1)S(1)}, u32[]{:S(2)}, u32[]{:S(2)}) %collective-permute-start.22) | collective-permute-done | bytes 114720 | tf_op jit(solution)/shard_map/ppermute | solution.py:23
  104.9 1.0 correct.3
  105.9 14.3 %all_to_all.20 = f32[4,448,128]{2,1,0:T(8,128)S(1)} all-to-all(f32[4,448,128]{2,1,0:T(8,128)S(1)} %correct.3), channel_id=1, replica_groups=mesh['z_hi'=2,'x'=4,'y'=4,'z_lo'=4,'core'=2] {'x'}, dimensions={0} | all-to-all | bytes 1835008 | tf_op jit(solution)/shard_map/all_to_all | solution.py:266
  120.2 0.9 copy.14
  (48 shorter events, 6.9 us)
Async XLA Ops:
  0.0 15.7 %copy-start = (bf16[896,1792]{1,0:T(8,128)(2,1)S(1)}, bf16[896,1792]{1,0:T(8,128)(2,1)}, u32[]{:S(2)}) copy-start(bf16[896,1792]{1,0:T(8,128)(2,1)} %refs_4_.3) | copy-start | bytes 9633796
  4.5 9.2 %collective-permute-start.16 = (bf16[128,896]{1,0:T(8,128)(2,1)}, bf16[128,896]{1,0:T(8,128)(2,1)}, u32[]{:S(2)}, u32[]{:S(2)}) collective-permute-start(bf16[128,896]{1,0:T(8,128)(2,1)} %get-tuple-element.9.refs_0_), channel_id=1, source_target_pairs={{0,2},{2,4},{4,6},{6,0},{1,3},{3,5},{5,7},{7,1},{8,10},{10,12},{12... | collective-permute-start | bytes 688136 | tf_op jit(solution)/shard_map/ppermute | solution.py:23
  6.5 24.4 %all-to-all-start = ((bf16[16,128,256]{2,1,0:T(8,128)(2,1)}), bf16[16,128,256]{2,1,0:T(8,128)(2,1)}, u32[]{:S(2)}, u32[]{:S(2)}) async-start(bf16[16,128,256]{2,1,0:T(8,128)(2,1)} %get-tuple-element.10), calls=%async_computation | async-start | bytes 2097152 | tf_op jit(solution)/shard_map/all_to_all | solution.py:159
  13.6 2.1 %collective-permute-start.15 = (bf16[128,896]{1,0:T(8,128)(2,1)}, bf16[128,896]{1,0:T(8,128)(2,1)S(1)}, u32[]{:S(2)}, u32[]{:S(2)}) collective-permute-start(bf16[128,896]{1,0:T(8,128)(2,1)} %get-tuple-element.9.refs_0_), channel_id=1, source_target_pairs={{0,1},{1,0},{2,3},{3,2},{4,5},{5,4},{6,7},{7,6},{8,9},{9,8},{10,11... | collective-permute-start | bytes 688136 | tf_op jit(solution)/shard_map/ppermute | solution.py:23
  13.7 2.0 %collective-permute-start.17 = (bf16[128,896]{1,0:T(8,128)(2,1)}, bf16[128,896]{1,0:T(8,128)(2,1)S(1)}, u32[]{:S(2)}, u32[]{:S(2)}) collective-permute-start(bf16[128,896]{1,0:T(8,128)(2,1)} %collective-permute-done.16.refs_2_), channel_id=1, source_target_pairs={{0,1},{1,0},{2,3},{3,2},{4,5},{5,4},{6,7},{7,6},{8,9},{9,8},{10,11... | collective-permute-start | bytes 688136 | tf_op jit(solution)/shard_map/ppermute | solution.py:23
  14.2 27.1 %collective-permute-start = (bf16[128,896]{1,0:T(8,128)(2,1)}, bf16[128,896]{1,0:T(8,128)(2,1)S(1)}, u32[]{:S(2)}, u32[]{:S(2)}) collective-permute-start(bf16[128,896]{1,0:T(8,128)(2,1)} %get-tuple-element.9.refs_0_), channel_id=1, source_target_pairs={{0,4},{2,6},{4,0},{6,2},{1,5},{3,7},{5,1},{7,3},{8,12},{10,14},{12... | collective-permute-start | bytes 688136 | tf_op jit(solution)/shard_map/ppermute | solution.py:23
  14.8 26.5 %collective-permute-start.2 = (bf16[128,896]{1,0:T(8,128)(2,1)}, bf16[128,896]{1,0:T(8,128)(2,1)}, u32[]{:S(2)}, u32[]{:S(2)}) collective-permute-start(bf16[128,896]{1,0:T(8,128)(2,1)} %get-tuple-element.9.refs_0_), channel_id=1, source_target_pairs={{0,6},{2,0},{4,2},{6,4},{1,7},{3,1},{5,3},{7,5},{8,14},{10,8},{12,... | collective-permute-start | bytes 688136 | tf_op jit(solution)/shard_map/ppermute | solution.py:23
  30.9 29.0 %all-to-all-start.2 = ((bf16[16,112,512]{2,1,0:T(8,128)(2,1)}), bf16[16,112,512]{2,1,0:T(8,128)(2,1)}, u32[]{:S(2)}, u32[]{:S(2)}) async-start(bf16[16,112,512]{2,1,0:T(8,128)(2,1)} %bitcast.14), calls=%async_computation.2 | async-start | bytes 3670016 | tf_op jit(solution)/shard_map/all_to_all | solution.py:195
  36.7 8.5 %collective-permute-start.4 = (f32[128,128]{1,0:T(8,128)S(1)}, f32[128,128]{1,0:T(8,128)S(1)}, u32[]{:S(2)}, u32[]{:S(2)}) collective-permute-start(f32[128,128]{1,0:T(8,128)S(1)} %get-tuple-element.12), channel_id=1, source_target_pairs={{0,128},{128,0},{1,129},{129,1},{2,130},{130,2},{3,131},{131,3},{4... | collective-permute-start | bytes 196616 | tf_op jit(solution)/shard_map/ppermute | solution.py:23
  41.3 9.9 %collective-permute-start.1 = (bf16[128,896]{1,0:T(8,128)(2,1)S(1)}, bf16[128,896]{1,0:T(8,128)(2,1)S(1)}, u32[]{:S(2)}, u32[]{:S(2)}) collective-permute-start(bf16[128,896]{1,0:T(8,128)(2,1)S(1)} %collective-permute-done.refs_0_), channel_id=1, source_target_pairs={{0,1},{1,0},{2,3},{3,2},{4,5},{5,4},{6,7},{7,6},{8,9},{9,8},{10,11... | collective-permute-start | bytes 688136 | tf_op jit(solution)/shard_map/ppermute | solution.py:23
  41.3 9.9 %collective-permute-start.3 = (bf16[128,896]{1,0:T(8,128)(2,1)}, bf16[128,896]{1,0:T(8,128)(2,1)S(1)}, u32[]{:S(2)}, u32[]{:S(2)}) collective-permute-start(bf16[128,896]{1,0:T(8,128)(2,1)} %collective-permute-done.2.refs_2_), channel_id=1, source_target_pairs={{0,1},{1,0},{2,3},{3,2},{4,5},{5,4},{6,7},{7,6},{8,9},{9,8},{10,11... | collective-permute-start | bytes 688136 | tf_op jit(solution)/shard_map/ppermute | solution.py:23
  45.3 10.4 %collective-permute-start.5 = (bf16[128,128]{1,0:T(8,128)(2,1)S(1)}, bf16[128,128]{1,0:T(8,128)(2,1)S(1)}, u32[]{:S(2)}, u32[]{:S(2)}) collective-permute-start(bf16[128,128]{1,0:T(8,128)(2,1)S(1)} %multiply_convert_fusion.2), channel_id=1, source_target_pairs={{0,32},{32,64},{64,96},{96,0},{1,33},{33,65},{65,97},{97,1},{2,34}... | collective-permute-start | bytes 98312 | tf_op jit(solution)/shard_map/ppermute | solution.py:23
  47.0 12.1 %collective-permute-start.6 = (bf16[128,128]{1,0:T(8,128)(2,1)S(1)}, bf16[128,128]{1,0:T(8,128)(2,1)S(1)}, u32[]{:S(2)}, u32[]{:S(2)}) collective-permute-start(bf16[128,128]{1,0:T(8,128)(2,1)S(1)} %multiply_convert_fusion.2), channel_id=1, source_target_pairs={{0,64},{32,96},{64,0},{96,32},{1,65},{33,97},{65,1},{97,33},{2,66}... | collective-permute-start | bytes 98312 | tf_op jit(solution)/shard_map/ppermute | solution.py:23
  49.8 9.4 %collective-permute-start.7 = (bf16[128,128]{1,0:T(8,128)(2,1)S(1)}, bf16[128,128]{1,0:T(8,128)(2,1)S(1)}, u32[]{:S(2)}, u32[]{:S(2)}) collective-permute-start(bf16[128,128]{1,0:T(8,128)(2,1)S(1)} %multiply_convert_fusion.2), channel_id=1, source_target_pairs={{0,96},{32,0},{64,32},{96,64},{1,97},{33,1},{65,33},{97,65},{2,98}... | collective-permute-start | bytes 98312 | tf_op jit(solution)/shard_map/ppermute | solution.py:23
  59.9 27.2 %all-to-all-start.1 = ((bf16[16,112,512]{2,1,0:T(8,128)(2,1)}), bf16[16,112,512]{2,1,0:T(8,128)(2,1)S(1)}, u32[]{:S(2)}, u32[]{:S(2)}) async-start(bf16[16,112,512]{2,1,0:T(8,128)(2,1)} %bitcast.12), calls=%async_computation.1 | async-start | bytes 3670016 | tf_op jit(solution)/shard_map/all_to_all | solution.py:195
  64.7 10.9 %collective-permute-start.9 = (bf16[4,128,128]{2,1,0:T(8,128)(2,1)S(1)}, bf16[4,128,128]{2,1,0:T(8,128)(2,1)S(1)}, u32[]{:S(2)}, u32[]{:S(2)}) collective-permute-start(bf16[4,128,128]{2,1,0:T(8,128)(2,1)S(1)} %pad_maximum_fusion.refs_1_.refs_4_), channel_id=1, source_target_pairs={{0,2},{2,4},{4,6},{6,0},{1,3},{3,5},{5,7},{7,1},{8,10},{10,12},{12... | collective-permute-start | bytes 393224 | tf_op jit(solution)/shard_map/ppermute | solution.py:23
  65.3 10.8 %collective-permute-start.11 = (bf16[4,128,128]{2,1,0:T(8,128)(2,1)S(1)}, bf16[4,128,128]{2,1,0:T(8,128)(2,1)S(1)}, u32[]{:S(2)}, u32[]{:S(2)}) collective-permute-start(bf16[4,128,128]{2,1,0:T(8,128)(2,1)S(1)} %pad_maximum_fusion.refs_1_.refs_4_), channel_id=1, source_target_pairs={{0,4},{2,6},{4,0},{6,2},{1,5},{3,7},{5,1},{7,3},{8,12},{10,14},{12... | collective-permute-start | bytes 393224 | tf_op jit(solution)/shard_map/ppermute | solution.py:23
  66.3 9.9 %collective-permute-start.13 = (bf16[4,128,128]{2,1,0:T(8,128)(2,1)S(1)}, bf16[4,128,128]{2,1,0:T(8,128)(2,1)S(1)}, u32[]{:S(2)}, u32[]{:S(2)}) collective-permute-start(bf16[4,128,128]{2,1,0:T(8,128)(2,1)S(1)} %pad_maximum_fusion.refs_1_.refs_4_), channel_id=1, source_target_pairs={{0,6},{2,0},{4,2},{6,4},{1,7},{3,1},{5,3},{7,5},{8,14},{10,8},{12,... | collective-permute-start | bytes 393224 | tf_op jit(solution)/shard_map/ppermute | solution.py:23
  69.1 12.1 %collective-permute-start.18 = (bf16[112,512]{1,0:T(8,128)(2,1)S(1)}, bf16[112,512]{1,0:T(8,128)(2,1)S(1)}, u32[]{:S(2)}, u32[]{:S(2)}) collective-permute-start(bf16[112,512]{1,0:T(8,128)(2,1)S(1)} %convert_element_type.29), channel_id=1, source_target_pairs={{0,128},{128,0},{1,129},{129,1},{2,130},{130,2},{3,131},{131,3},{4... | collective-permute-start | bytes 344072 | tf_op jit(solution)/shard_map/ppermute | solution.py:23
  75.6 10.2 %collective-permute-start.8 = (bf16[4,128,128]{2,1,0:T(8,128)(2,1)S(1)}, bf16[4,128,128]{2,1,0:T(8,128)(2,1)S(1)}, u32[]{:S(2)}, u32[]{:S(2)}) collective-permute-start(bf16[4,128,128]{2,1,0:T(8,128)(2,1)S(1)} %pad_maximum_fusion.refs_1_.refs_4_), channel_id=1, source_target_pairs={{0,1},{1,0},{2,3},{3,2},{4,5},{5,4},{6,7},{7,6},{8,9},{9,8},{10,11... | collective-permute-start | bytes 393224 | tf_op jit(solution)/shard_map/ppermute | solution.py:23
  75.6 10.2 %collective-permute-start.10 = (bf16[4,128,128]{2,1,0:T(8,128)(2,1)S(1)}, bf16[4,128,128]{2,1,0:T(8,128)(2,1)S(1)}, u32[]{:S(2)}, u32[]{:S(2)}) collective-permute-start(bf16[4,128,128]{2,1,0:T(8,128)(2,1)S(1)} %collective-permute-done.9.refs_3_.refs_6_), channel_id=1, source_target_pairs={{0,1},{1,0},{2,3},{3,2},{4,5},{5,4},{6,7},{7,6},{8,9},{9,8},{10,11... | collective-permute-start | bytes 393224 | tf_op jit(solution)/shard_map/ppermute | solution.py:23
  76.1 9.7 %collective-permute-start.12 = (bf16[4,128,128]{2,1,0:T(8,128)(2,1)S(1)}, bf16[4,128,128]{2,1,0:T(8,128)(2,1)S(1)}, u32[]{:S(2)}, u32[]{:S(2)}) collective-permute-start(bf16[4,128,128]{2,1,0:T(8,128)(2,1)S(1)} %collective-permute-done.11.refs_5_.refs_4_), channel_id=1, source_target_pairs={{0,1},{1,0},{2,3},{3,2},{4,5},{5,4},{6,7},{7,6},{8,9},{9,8},{10,11... | collective-permute-start | bytes 393224 | tf_op jit(solution)/shard_map/ppermute | solution.py:23
  76.2 9.6 %collective-permute-start.14 = (bf16[4,128,128]{2,1,0:T(8,128)(2,1)S(1)}, bf16[4,128,128]{2,1,0:T(8,128)(2,1)S(1)}, u32[]{:S(2)}, u32[]{:S(2)}) collective-permute-start(bf16[4,128,128]{2,1,0:T(8,128)(2,1)S(1)} %collective-permute-done.13.refs_7_.refs_6_), channel_id=1, source_target_pairs={{0,1},{1,0},{2,3},{3,2},{4,5},{5,4},{6,7},{7,6},{8,9},{9,8},{10,11... | collective-permute-start | bytes 393224 | tf_op jit(solution)/shard_map/ppermute | solution.py:23
  81.3 14.0 %collective-permute-start.20 = (bf16[112,512]{1,0:T(8,128)(2,1)S(1)}, bf16[112,512]{1,0:T(8,128)(2,1)S(1)}, u32[]{:S(2)}, u32[]{:S(2)}) collective-permute-start(bf16[112,512]{1,0:T(8,128)(2,1)S(1)} %multiply_convert_fusion.1.refs_9_.refs_0_), channel_id=1, source_target_pairs={{0,16},{8,24},{16,0},{24,8},{1,17},{9,25},{17,1},{25,9},{2,18},{10... | collective-permute-start | bytes 344072 | tf_op jit(solution)/shard_map/ppermute | solution.py:23
  87.4 9.7 %collective-permute-start.19 = (bf16[112,512]{1,0:T(8,128)(2,1)S(1)}, bf16[112,512]{1,0:T(8,128)(2,1)S(1)}, u32[]{:S(2)}, u32[]{:S(2)}) collective-permute-start(bf16[112,512]{1,0:T(8,128)(2,1)S(1)} %convert_element_type.33), channel_id=1, source_target_pairs={{0,128},{128,0},{1,129},{129,1},{2,130},{130,2},{3,131},{131,3},{4... | collective-permute-start | bytes 344072 | tf_op jit(solution)/shard_map/ppermute | solution.py:23
  92.0 10.2 %collective-permute-start.24 = (bf16[112,512]{1,0:T(8,128)(2,1)S(1)}, bf16[112,512]{1,0:T(8,128)(2,1)S(1)}, u32[]{:S(2)}, u32[]{:S(2)}) collective-permute-start(bf16[112,512]{1,0:T(8,128)(2,1)S(1)} %multiply_convert_fusion.1.refs_9_.refs_0_), channel_id=1, source_target_pairs={{0,8},{8,16},{16,24},{24,0},{1,9},{9,17},{17,25},{25,1},{2,10},{10... | collective-permute-start | bytes 344072 | tf_op jit(solution)/shard_map/ppermute | solution.py:23
  92.7 9.5 %collective-permute-start.25 = (bf16[112,512]{1,0:T(8,128)(2,1)S(1)}, bf16[112,512]{1,0:T(8,128)(2,1)S(1)}, u32[]{:S(2)}, u32[]{:S(2)}) collective-permute-start(bf16[112,512]{1,0:T(8,128)(2,1)S(1)} %multiply_convert_fusion.1.refs_9_.refs_0_), channel_id=1, source_target_pairs={{0,24},{8,0},{16,8},{24,16},{1,25},{9,1},{17,9},{25,17},{2,26},{10... | collective-permute-start | bytes 344072 | tf_op jit(solution)/shard_map/ppermute | solution.py:23
  97.1 6.4 %collective-permute-start.21 = (bf16[112,512]{1,0:T(8,128)(2,1)S(1)}, bf16[112,512]{1,0:T(8,128)(2,1)S(1)}, u32[]{:S(2)}, u32[]{:S(2)}) collective-permute-start(bf16[112,512]{1,0:T(8,128)(2,1)S(1)} %multiply_convert_fusion.refs_0_), channel_id=1, source_target_pairs={{0,16},{8,24},{16,0},{24,8},{1,17},{9,25},{17,1},{25,9},{2,18},{10... | collective-permute-start | bytes 344072 | tf_op jit(solution)/shard_map/ppermute | solution.py:23
  98.9 6.0 %collective-permute-start.22 = (bf16[112,512]{1,0:T(8,128)(2,1)S(1)}, bf16[112,512]{1,0:T(8,128)(2,1)S(1)}, u32[]{:S(2)}, u32[]{:S(2)}) collective-permute-start(bf16[112,512]{1,0:T(8,128)(2,1)S(1)} %multiply_convert_fusion.refs_0_), channel_id=1, source_target_pairs={{0,8},{8,16},{16,24},{24,0},{1,9},{9,17},{17,25},{25,1},{2,10},{10... | collective-permute-start | bytes 344072 | tf_op jit(solution)/shard_map/ppermute | solution.py:23
  98.9 6.0 %collective-permute-start.23 = (bf16[112,512]{1,0:T(8,128)(2,1)S(1)}, bf16[112,512]{1,0:T(8,128)(2,1)S(1)}, u32[]{:S(2)}, u32[]{:S(2)}) collective-permute-start(bf16[112,512]{1,0:T(8,128)(2,1)S(1)} %multiply_convert_fusion.refs_0_), channel_id=1, source_target_pairs={{0,24},{8,0},{16,8},{24,16},{1,25},{9,1},{17,9},{25,17},{2,26},{10... | collective-permute-start | bytes 344072 | tf_op jit(solution)/shard_map/ppermute | solution.py:23

commit v18 on v17

--- a/solution.py
+++ b/solution.py
@@ -251,10 +251,13 @@
     near_got = exchanged(grad_partials(near_rows, grad_basis, (), cost))
     act_own = jnp.stack(act_row)
     far_got = exchanged(gated(grad_partials(far_rows, grad_basis), [act_own]))
+    near_sum = jnp.sum(near_got.astype(jnp.float32), axis=0)
+    act_own = gated(act_own, [near_sum], jax.ShapeDtypeStruct)
     acts = []
     for own in [act_own] + [shifted(act_own, "z_lo", step) for step in (1, 2, 3)]:
         acts += [own, shifted(own, "core", 1)]
-    near_sq = squared(near_got)
+    total = near_sum + shifted(near_sum.astype(jnp.bfloat16), "z_hi", 1).astype(jnp.float32)
+    near_sq = (total * total).astype(jnp.bfloat16)
     near_pieces = [near_sq] + [shifted(near_sq, "y", step) for step in Y_STEPS]
     far_got = gated(far_got, acts + [near_sq], jax.ShapeDtypeStruct)
     summed = jnp.sum(far_got.astype(jnp.float32), axis=0)

time: 122 us -> 125 us (1.025)
  waiting for transfers between devices: 28.7 us -> 35.7 us
  starting transfers between devices: 58.8 us -> 53.5 us
  blocking collectives: 14.3 us -> 16.3 us
    ppermute x26, waiting for transfers between devices: 15.6 us -> 22.7 us  [shifted(): lax.ppermute(value, axis, [(i, (i + step) % size) for i in range(size)])]
    ppermute x26, starting transfers between devices: 42.6 us -> 37.4 us  [shifted(): lax.ppermute(value, axis, [(i, (i + step) % size) for i in range(size)])]
    all_to_all x1, blocking collectives: 14.3 us -> 16.3 us  [per_device(): out = lax.all_to_all(out, 'x', 0, 0, tiled=True)]
  transfers between devices with their start and end apart: 29 -> 29, of which waited for: 10 -> 11; matrix products, arithmetic and copies ran while one was open for 2% -> 2% of each run, Pallas kernels for 9% -> 8%
where the time goes in v18:
time: 125 us
  starting transfers between devices  53.5 us (43%)
  waiting for transfers between devices  35.7 us (29%)
  blocking collectives  16.3 us (13%)
  Pallas kernels  16 us (13%)
  other arithmetic  2.23 us (2%)
    ppermute x26, starting transfers between devices, shifted(): lax.ppermute(value, axis, [(i, (i + step) % size) for i in range(size)])  37.4 us
    ppermute x26, waiting for transfers between devices, shifted(): lax.ppermute(value, axis, [(i, (i + step) % size) for i in range(size)])  22.7 us
    all_to_all x1, blocking collectives, per_device(): out = lax.all_to_all(out, 'x', 0, 0, tiled=True)  16.3 us
    all_to_all x1, waiting for transfers between devices, act_squares(): got = lax.all_to_all(partials, ('x', 'y'), 0, 0, tiled=True)  10.3 us
    all_to_all x2, starting transfers between devices, exchanged(): lax.all_to_all(partial.reshape(16, columns // 16, tokens), ('x', 'y'), 0,...  8.99 us
    pallas_call x2, Pallas kernels, grad_partials(): pl.pallas_call(lambda *refs: grad_kernel(len(parts), *refs), out_shape=pl...  8.04 us
    all_to_all x1, starting transfers between devices, act_squares(): got = lax.all_to_all(partials, ('x', 'y'), 0, 0, tiled=True)  7.09 us
    pallas_call x1, Pallas kernels, first_partials(): pl.pallas_call(first_kernel, out_shape=(pltpu.HBM(shape, jnp.bfloat16), p...  4.53 us
  transfers between devices with their start and end apart: 29, of which 11 were waited for; matrix products, arithmetic and copies ran while one was open for 2% of the time, Pallas kernels for 8%

profile of v18, /device:TPU:64, one launch (start us, length us, event | category | flops | bytes accessed | tf_op | source)
XLA Modules:
  0.0 124.8 jit_solution(11895566987836064306)
XLA Ops:
  0.0 4.5 %first.1 = (bf16[16,128,256]{2,1,0:T(8,128)(2,1)}, bf16[128,896]{1,0:T(8,128)(2,1)}) custom-call(s32[1]{0:T(128)} %bitcast.2.place, f32[1,8192]{1,0:T(1,128)} %bitcast.16, bf16[128,896]{1,0:T(8,128)(2,1)} %gate_at.1, bf16[128,896]{1,0:T(8,128)(2,1)} %grad_at.1, bf16[128,8192]{1,0:T(8,128)(2,1)} %hidden_at.1, bf16[256,4096]{1,0:T(8,128)(2,1)} %basis_at.1), custom_call_target="tpu_custom_call" | custom-call | tf_op jit(solution)/shard_map/first/pallas_call | solution.py:90
  4.5 2.0 %collective-permute-start.9 = (bf16[128,896]{1,0:T(8,128)(2,1)}, bf16[128,896]{1,0:T(8,128)(2,1)}, u32[]{:S(2)}, u32[]{:S(2)}) collective-permute-start(bf16[128,896]{1,0:T(8,128)(2,1)} %get-tuple-element.9.refs_0_), channel_id=1, source_target_pairs={{0,2},{2,4},{4,6},{6,0},{1,3},{3,5},{5,7},{7,1},{8,10},{10,12},{12... | collective-permute-start | bytes 688136 | tf_op jit(solution)/shard_map/ppermute | solution.py:23
  6.5 7.1 %all-to-all-start = ((bf16[16,128,256]{2,1,0:T(8,128)(2,1)}), bf16[16,128,256]{2,1,0:T(8,128)(2,1)}, u32[]{:S(2)}, u32[]{:S(2)}) async-start(bf16[16,128,256]{2,1,0:T(8,128)(2,1)} %get-tuple-element.10), calls=%async_computation | async-start | bytes 2097152 | tf_op jit(solution)/shard_map/all_to_all | solution.py:159
  14.3 2.3 %collective-permute-start = (bf16[128,896]{1,0:T(8,128)(2,1)}, bf16[128,896]{1,0:T(8,128)(2,1)}, u32[]{:S(2)}, u32[]{:S(2)}) collective-permute-start(bf16[128,896]{1,0:T(8,128)(2,1)} %get-tuple-element.9.refs_0_), channel_id=1, source_target_pairs={{0,4},{2,6},{4,0},{6,2},{1,5},{3,7},{5,1},{7,3},{8,12},{10,14},{12... | collective-permute-start | bytes 688136 | tf_op jit(solution)/shard_map/ppermute | solution.py:23
  16.6 4.1 %grad.3 = bf16[1792,512]{1,0:T(8,128)(2,1)} custom-call(bf16[128,896]{1,0:T(8,128)(2,1)} %get-tuple-element.9.refs_0_, bf16[128,896]{1,0:T(8,128)(2,1)S(1)} %collective-permute-done.8.refs_1_, bf16[128,896]{1,0:T(8,128)(2,1)} %collective-permute-done.9.refs_2_, bf16[128,896]{1,0:T(8,128)(2,1)S(1)} %collective-permute-done.10.refs_3_, ...), custom_call_target="tpu_custom_call" | custom-call | flops 8000000000 | bytes 10000000 | tf_op jit(solution)/shard_map/grad/pallas_call | solution.py:132
  20.7 10.3 %all-to-all-done.got = bf16[16,128,256]{2,1,0:T(8,128)(2,1)} async-done(((bf16[16,128,256]{2,1,0:T(8,128)(2,1)}), bf16[16,128,256]{2,1,0:T(8,128)(2,1)}, u32[]{:S(2)}, u32[]{:S(2)}) %all-to-all-start) | async-done | bytes 1048608 | tf_op jit(solution)/shard_map/all_to_all | solution.py:159
  30.9 4.4 %all-to-all-start.2 = ((bf16[16,112,512]{2,1,0:T(8,128)(2,1)}), bf16[16,112,512]{2,1,0:T(8,128)(2,1)}, u32[]{:S(2)}, u32[]{:S(2)}) async-start(bf16[16,112,512]{2,1,0:T(8,128)(2,1)} %bitcast.14), calls=%async_computation.2 | async-start | bytes 3670016 | tf_op jit(solution)/shard_map/all_to_all | solution.py:195
  35.4 1.4 %act_sum.1 = (f32[128,128]{1,0:T(8,128)S(1)}, f32[128,128]{1,0:T(8,128)S(1)}) custom-call(s32[1]{0:T(128)} %bitcast.4.place, bf16[16,128,256]{2,1,0:T(8,128)(2,1)} %all-to-all-done.got), custom_call_target="tpu_custom_call" | custom-call | flops 20000000000 | bytes 1000000 | tf_op jit(solution)/shard_map/act_sum/pallas_call | solution.py:163
  36.7 4.6 %collective-permute-start.4 = (f32[128,128]{1,0:T(8,128)S(1)}, f32[128,128]{1,0:T(8,128)S(1)}, u32[]{:S(2)}, u32[]{:S(2)}) collective-permute-start(f32[128,128]{1,0:T(8,128)S(1)} %get-tuple-element.12), channel_id=1, source_target_pairs={{0,128},{128,0},{1,129},{129,1},{2,130},{130,2},{3,131},{131,3},{4... | collective-permute-start | bytes 196616 | tf_op jit(solution)/shard_map/ppermute | solution.py:23
  41.8 3.4 %collective-permute-done.4 = f32[128,128]{1,0:T(8,128)S(1)} collective-permute-done((f32[128,128]{1,0:T(8,128)S(1)}, f32[128,128]{1,0:T(8,128)S(1)}, u32[]{:S(2)}, u32[]{:S(2)}) %collective-permute-start.4) | collective-permute-done | bytes 65568 | tf_op jit(solution)/shard_map/ppermute | solution.py:23
  45.3 3.0 %collective-permute-start.7 = (bf16[128,128]{1,0:T(8,128)(2,1)S(1)}, bf16[128,128]{1,0:T(8,128)(2,1)S(1)}, u32[]{:S(2)}, u32[]{:S(2)}) collective-permute-start(bf16[128,128]{1,0:T(8,128)(2,1)S(1)} %multiply_convert_fusion.2), channel_id=1, source_target_pairs={{0,96},{32,0},{64,32},{96,64},{1,97},{33,1},{65,33},{97,65},{2,98}... | collective-permute-start | bytes 98312 | tf_op jit(solution)/shard_map/ppermute | solution.py:23
  50.0 4.0 %grad.2.refs_0_ = bf16[1792,512]{1,0:T(8,128)(2,1)} custom-call(bf16[128,896]{1,0:T(8,128)(2,1)} %collective-permute-done.refs_0_, bf16[128,896]{1,0:T(8,128)(2,1)S(1)} %collective-permute-done.1.refs_1_, bf16[128,896]{1,0:T(8,128)(2,1)S(1)} %collective-permute-done.2.refs_2_, bf16[128,896]{1,0:T(8,128)(2,1)S(1)} %collective-permute-done.3.refs_3_, ...), custom_call_target="tpu_custom_call" | custom-call | tf_op jit(solution)/shard_map/grad/pallas_call | solution.py:132
  54.0 3.3 %collective-permute-done.7 = bf16[128,128]{1,0:T(8,128)(2,1)S(1)} collective-permute-done((bf16[128,128]{1,0:T(8,128)(2,1)S(1)}, bf16[128,128]{1,0:T(8,128)(2,1)S(1)}, u32[]{:S(2)}, u32[]{:S(2)}) %collective-permute-start.7) | collective-permute-done | bytes 32800 | tf_op jit(solution)/shard_map/ppermute | solution.py:23
  57.3 1.4 %collective-permute-done.6 = bf16[128,128]{1,0:T(8,128)(2,1)S(1)} collective-permute-done((bf16[128,128]{1,0:T(8,128)(2,1)S(1)}, bf16[128,128]{1,0:T(8,128)(2,1)S(1)}, u32[]{:S(2)}, u32[]{:S(2)}) %collective-permute-start.6) | collective-permute-done | bytes 32800 | tf_op jit(solution)/shard_map/ppermute | solution.py:23
  58.7 1.4 %all-to-all-done.2 = bf16[16,112,512]{2,1,0:T(8,128)(2,1)} async-done(((bf16[16,112,512]{2,1,0:T(8,128)(2,1)}), bf16[16,112,512]{2,1,0:T(8,128)(2,1)}, u32[]{:S(2)}, u32[]{:S(2)}) %all-to-all-start.2) | async-done | bytes 1835040 | tf_op jit(solution)/shard_map/all_to_all | solution.py:195
  60.1 4.6 %all-to-all-start.1 = ((bf16[16,112,512]{2,1,0:T(8,128)(2,1)}), bf16[16,112,512]{2,1,0:T(8,128)(2,1)S(1)}, u32[]{:S(2)}, u32[]{:S(2)}) async-start(bf16[16,112,512]{2,1,0:T(8,128)(2,1)} %bitcast.12), calls=%async_computation.1 | async-start | bytes 3670016 | tf_op jit(solution)/shard_map/all_to_all | solution.py:195
  64.6 1.8 %convert_reduce_fusion.1.refs_1_ = f32[112,512]{1,0:T(8,128)S(1)} fusion(bf16[16,112,512]{2,1,0:T(8,128)(2,1)} %all-to-all-done.2), kind=kLoop, calls=%fused_computation.1 | loop fusion | flops 1777664 | bytes 2064384 | tf_op jit(solution)/shard_map/reduce_sum | solution.py:254
  66.8 2.9 %collective-permute-start.14 = (bf16[4,128,128]{2,1,0:T(8,128)(2,1)S(1)}, bf16[4,128,128]{2,1,0:T(8,128)(2,1)S(1)}, u32[]{:S(2)}, u32[]{:S(2)}) collective-permute-start(bf16[4,128,128]{2,1,0:T(8,128)(2,1)S(1)} %gate.5.refs_1_.refs_4_), channel_id=1, source_target_pairs={{0,4},{2,6},{4,0},{6,2},{1,5},{3,7},{5,1},{7,3},{8,12},{10,14},{12... | collective-permute-start | bytes 393224 | tf_op jit(solution)/shard_map/ppermute | solution.py:23
  69.6 5.7 %collective-permute-start.18 = (bf16[112,512]{1,0:T(8,128)(2,1)S(1)}, bf16[112,512]{1,0:T(8,128)(2,1)S(1)}, u32[]{:S(2)}, u32[]{:S(2)}) collective-permute-start(bf16[112,512]{1,0:T(8,128)(2,1)S(1)} %convert_element_type.29), channel_id=1, source_target_pairs={{0,128},{128,0},{1,129},{129,1},{2,130},{130,2},{3,131},{131,3},{4... | collective-permute-start | bytes 344072 | tf_op jit(solution)/shard_map/ppermute | solution.py:23
  75.9 3.6 %collective-permute-done.14.refs_5_.refs_4_ = bf16[4,128,128]{2,1,0:T(8,128)(2,1)S(1)} collective-permute-done((bf16[4,128,128]{2,1,0:T(8,128)(2,1)S(1)}, bf16[4,128,128]{2,1,0:T(8,128)(2,1)S(1)}, u32[]{:S(2)}, u32[]{:S(2)}) %collective-permute-start.14) | collective-permute-done | bytes 131104 | tf_op jit(solution)/shard_map/ppermute | solution.py:23
  79.5 2.3 %collective-permute-done.12.refs_3_.refs_6_ = bf16[4,128,128]{2,1,0:T(8,128)(2,1)S(1)} collective-permute-done((bf16[4,128,128]{2,1,0:T(8,128)(2,1)S(1)}, bf16[4,128,128]{2,1,0:T(8,128)(2,1)S(1)}, u32[]{:S(2)}, u32[]{:S(2)}) %collective-permute-start.12) | collective-permute-done | bytes 131104 | tf_op jit(solution)/shard_map/ppermute | solution.py:23
  81.9 3.4 %collective-permute-start.20 = (bf16[112,512]{1,0:T(8,128)(2,1)S(1)}, bf16[112,512]{1,0:T(8,128)(2,1)S(1)}, u32[]{:S(2)}, u32[]{:S(2)}) collective-permute-start(bf16[112,512]{1,0:T(8,128)(2,1)S(1)} %multiply_convert_fusion.1.refs_9_.refs_0_), channel_id=1, source_target_pairs={{0,16},{8,24},{16,0},{24,8},{1,17},{9,25},{17,1},{25,9},{2,18},{10... | collective-permute-start | bytes 344072 | tf_op jit(solution)/shard_map/ppermute | solution.py:23
  85.3 1.4 %all-to-all-done.1.refs_0_ = bf16[16,112,512]{2,1,0:T(8,128)(2,1)S(1)} async-done(((bf16[16,112,512]{2,1,0:T(8,128)(2,1)}), bf16[16,112,512]{2,1,0:T(8,128)(2,1)S(1)}, u32[]{:S(2)}, u32[]{:S(2)}) %all-to-all-start.1) | async-done | bytes 1835040 | tf_op jit(solution)/shard_map/all_to_all | solution.py:195
  87.0 4.6 %collective-permute-start.19 = (bf16[112,512]{1,0:T(8,128)(2,1)S(1)}, bf16[112,512]{1,0:T(8,128)(2,1)S(1)}, u32[]{:S(2)}, u32[]{:S(2)}) collective-permute-start(bf16[112,512]{1,0:T(8,128)(2,1)S(1)} %convert_element_type.33), channel_id=1, source_target_pairs={{0,128},{128,0},{1,129},{129,1},{2,130},{130,2},{3,131},{131,3},{4... | collective-permute-start | bytes 344072 | tf_op jit(solution)/shard_map/ppermute | solution.py:23
  91.6 1.2 %collective-permute-start.25 = (bf16[112,512]{1,0:T(8,128)(2,1)S(1)}, bf16[112,512]{1,0:T(8,128)(2,1)S(1)}, u32[]{:S(2)}, u32[]{:S(2)}) collective-permute-start(bf16[112,512]{1,0:T(8,128)(2,1)S(1)} %multiply_convert_fusion.1.refs_9_.refs_0_), channel_id=1, source_target_pairs={{0,24},{8,0},{16,8},{24,16},{1,25},{9,1},{17,9},{25,17},{2,26},{10... | collective-permute-start | bytes 344072 | tf_op jit(solution)/shard_map/ppermute | solution.py:23
  93.6 3.8 %collective-permute-done.19.refs_0_ = bf16[112,512]{1,0:T(8,128)(2,1)S(1)} collective-permute-done((bf16[112,512]{1,0:T(8,128)(2,1)S(1)}, bf16[112,512]{1,0:T(8,128)(2,1)S(1)}, u32[]{:S(2)}, u32[]{:S(2)}) %collective-permute-start.19) | collective-permute-done | bytes 114720 | tf_op jit(solution)/shard_map/ppermute | solution.py:23
  97.5 1.3 %collective-permute-start.23 = (bf16[112,512]{1,0:T(8,128)(2,1)S(1)}, bf16[112,512]{1,0:T(8,128)(2,1)S(1)}, u32[]{:S(2)}, u32[]{:S(2)}) collective-permute-start(bf16[112,512]{1,0:T(8,128)(2,1)S(1)} %multiply_convert_fusion.refs_0_), channel_id=1, source_target_pairs={{0,24},{8,0},{16,8},{24,16},{1,25},{9,1},{17,9},{25,17},{2,26},{10... | collective-permute-start | bytes 344072 | tf_op jit(solution)/shard_map/ppermute | solution.py:23
  99.6 1.1 collective-permute-start.21
  100.8 1.0 correct.2.refs_8_
  101.8 1.1 collective-permute-done.23.refs_3_
  102.9 3.7 %collective-permute-done.22.refs_2_ = bf16[112,512]{1,0:T(8,128)(2,1)S(1)} collective-permute-done((bf16[112,512]{1,0:T(8,128)(2,1)S(1)}, bf16[112,512]{1,0:T(8,128)(2,1)S(1)}, u32[]{:S(2)}, u32[]{:S(2)}) %collective-permute-start.22) | collective-permute-done | bytes 114720 | tf_op jit(solution)/shard_map/ppermute | solution.py:23
  107.6 16.3 %all_to_all.20 = f32[4,448,128]{2,1,0:T(8,128)S(1)} all-to-all(f32[4,448,128]{2,1,0:T(8,128)S(1)} %correct.3), channel_id=1, replica_groups=mesh['z_hi'=2,'x'=4,'y'=4,'z_lo'=4,'core'=2] {'x'}, dimensions={0} | all-to-all | bytes 1835008 | tf_op jit(solution)/shard_map/all_to_all | solution.py:269
  (49 shorter events, 7.8 us)
Async XLA Ops:
  0.0 16.6 %copy-start = (bf16[896,1792]{1,0:T(8,128)(2,1)S(1)}, bf16[896,1792]{1,0:T(8,128)(2,1)}, u32[]{:S(2)}) copy-start(bf16[896,1792]{1,0:T(8,128)(2,1)} %refs_4_.3) | copy-start | bytes 9633796
  4.5 9.2 %collective-permute-start.9 = (bf16[128,896]{1,0:T(8,128)(2,1)}, bf16[128,896]{1,0:T(8,128)(2,1)}, u32[]{:S(2)}, u32[]{:S(2)}) collective-permute-start(bf16[128,896]{1,0:T(8,128)(2,1)} %get-tuple-element.9.refs_0_), channel_id=1, source_target_pairs={{0,2},{2,4},{4,6},{6,0},{1,3},{3,5},{5,7},{7,1},{8,10},{10,12},{12... | collective-permute-start | bytes 688136 | tf_op jit(solution)/shard_map/ppermute | solution.py:23
  6.5 24.4 %all-to-all-start = ((bf16[16,128,256]{2,1,0:T(8,128)(2,1)}), bf16[16,128,256]{2,1,0:T(8,128)(2,1)}, u32[]{:S(2)}, u32[]{:S(2)}) async-start(bf16[16,128,256]{2,1,0:T(8,128)(2,1)} %get-tuple-element.10), calls=%async_computation | async-start | bytes 2097152 | tf_op jit(solution)/shard_map/all_to_all | solution.py:159
  13.6 3.0 %collective-permute-start.8 = (bf16[128,896]{1,0:T(8,128)(2,1)}, bf16[128,896]{1,0:T(8,128)(2,1)S(1)}, u32[]{:S(2)}, u32[]{:S(2)}) collective-permute-start(bf16[128,896]{1,0:T(8,128)(2,1)} %get-tuple-element.9.refs_0_), channel_id=1, source_target_pairs={{0,1},{1,0},{2,3},{3,2},{4,5},{5,4},{6,7},{7,6},{8,9},{9,8},{10,11... | collective-permute-start | bytes 688136 | tf_op jit(solution)/shard_map/ppermute | solution.py:23
  13.7 2.9 %collective-permute-start.10 = (bf16[128,896]{1,0:T(8,128)(2,1)}, bf16[128,896]{1,0:T(8,128)(2,1)S(1)}, u32[]{:S(2)}, u32[]{:S(2)}) collective-permute-start(bf16[128,896]{1,0:T(8,128)(2,1)} %collective-permute-done.9.refs_2_), channel_id=1, source_target_pairs={{0,1},{1,0},{2,3},{3,2},{4,5},{5,4},{6,7},{7,6},{8,9},{9,8},{10,11... | collective-permute-start | bytes 688136 | tf_op jit(solution)/shard_map/ppermute | solution.py:23
  14.2 27.1 %collective-permute-start.2 = (bf16[128,896]{1,0:T(8,128)(2,1)}, bf16[128,896]{1,0:T(8,128)(2,1)S(1)}, u32[]{:S(2)}, u32[]{:S(2)}) collective-permute-start(bf16[128,896]{1,0:T(8,128)(2,1)} %get-tuple-element.9.refs_0_), channel_id=1, source_target_pairs={{0,6},{2,0},{4,2},{6,4},{1,7},{3,1},{5,3},{7,5},{8,14},{10,8},{12,... | collective-permute-start | bytes 688136 | tf_op jit(solution)/shard_map/ppermute | solution.py:23
  14.3 27.0 %collective-permute-start = (bf16[128,896]{1,0:T(8,128)(2,1)}, bf16[128,896]{1,0:T(8,128)(2,1)}, u32[]{:S(2)}, u32[]{:S(2)}) collective-permute-start(bf16[128,896]{1,0:T(8,128)(2,1)} %get-tuple-element.9.refs_0_), channel_id=1, source_target_pairs={{0,4},{2,6},{4,0},{6,2},{1,5},{3,7},{5,1},{7,3},{8,12},{10,14},{12... | collective-permute-start | bytes 688136 | tf_op jit(solution)/shard_map/ppermute | solution.py:23
  30.9 29.1 %all-to-all-start.2 = ((bf16[16,112,512]{2,1,0:T(8,128)(2,1)}), bf16[16,112,512]{2,1,0:T(8,128)(2,1)}, u32[]{:S(2)}, u32[]{:S(2)}) async-start(bf16[16,112,512]{2,1,0:T(8,128)(2,1)} %bitcast.14), calls=%async_computation.2 | async-start | bytes 3670016 | tf_op jit(solution)/shard_map/all_to_all | solution.py:195
  36.7 8.5 %collective-permute-start.4 = (f32[128,128]{1,0:T(8,128)S(1)}, f32[128,128]{1,0:T(8,128)S(1)}, u32[]{:S(2)}, u32[]{:S(2)}) collective-permute-start(f32[128,128]{1,0:T(8,128)S(1)} %get-tuple-element.12), channel_id=1, source_target_pairs={{0,128},{128,0},{1,129},{129,1},{2,130},{130,2},{3,131},{131,3},{4... | collective-permute-start | bytes 196616 | tf_op jit(solution)/shard_map/ppermute | solution.py:23
  41.3 8.7 %collective-permute-start.3 = (bf16[128,896]{1,0:T(8,128)(2,1)S(1)}, bf16[128,896]{1,0:T(8,128)(2,1)S(1)}, u32[]{:S(2)}, u32[]{:S(2)}) collective-permute-start(bf16[128,896]{1,0:T(8,128)(2,1)S(1)} %collective-permute-done.2.refs_2_), channel_id=1, source_target_pairs={{0,1},{1,0},{2,3},{3,2},{4,5},{5,4},{6,7},{7,6},{8,9},{9,8},{10,11... | collective-permute-start | bytes 688136 | tf_op jit(solution)/shard_map/ppermute | solution.py:23
  41.3 8.7 %collective-permute-start.1 = (bf16[128,896]{1,0:T(8,128)(2,1)}, bf16[128,896]{1,0:T(8,128)(2,1)S(1)}, u32[]{:S(2)}, u32[]{:S(2)}) collective-permute-start(bf16[128,896]{1,0:T(8,128)(2,1)} %collective-permute-done.refs_0_), channel_id=1, source_target_pairs={{0,1},{1,0},{2,3},{3,2},{4,5},{5,4},{6,7},{7,6},{8,9},{9,8},{10,11... | collective-permute-start | bytes 688136 | tf_op jit(solution)/shard_map/ppermute | solution.py:23
  45.3 12.0 %collective-permute-start.7 = (bf16[128,128]{1,0:T(8,128)(2,1)S(1)}, bf16[128,128]{1,0:T(8,128)(2,1)S(1)}, u32[]{:S(2)}, u32[]{:S(2)}) collective-permute-start(bf16[128,128]{1,0:T(8,128)(2,1)S(1)} %multiply_convert_fusion.2), channel_id=1, source_target_pairs={{0,96},{32,0},{64,32},{96,64},{1,97},{33,1},{65,33},{97,65},{2,98}... | collective-permute-start | bytes 98312 | tf_op jit(solution)/shard_map/ppermute | solution.py:23
  48.3 10.4 %collective-permute-start.6 = (bf16[128,128]{1,0:T(8,128)(2,1)S(1)}, bf16[128,128]{1,0:T(8,128)(2,1)S(1)}, u32[]{:S(2)}, u32[]{:S(2)}) collective-permute-start(bf16[128,128]{1,0:T(8,128)(2,1)S(1)} %multiply_convert_fusion.2), channel_id=1, source_target_pairs={{0,64},{32,96},{64,0},{96,32},{1,65},{33,97},{65,1},{97,33},{2,66}... | collective-permute-start | bytes 98312 | tf_op jit(solution)/shard_map/ppermute | solution.py:23
  49.1 9.6 %collective-permute-start.5 = (bf16[128,128]{1,0:T(8,128)(2,1)S(1)}, bf16[128,128]{1,0:T(8,128)(2,1)S(1)}, u32[]{:S(2)}, u32[]{:S(2)}) collective-permute-start(bf16[128,128]{1,0:T(8,128)(2,1)S(1)} %multiply_convert_fusion.2), channel_id=1, source_target_pairs={{0,32},{32,64},{64,96},{96,0},{1,33},{33,65},{65,97},{97,1},{2,34}... | collective-permute-start | bytes 98312 | tf_op jit(solution)/shard_map/ppermute | solution.py:23
  60.1 26.7 %all-to-all-start.1 = ((bf16[16,112,512]{2,1,0:T(8,128)(2,1)}), bf16[16,112,512]{2,1,0:T(8,128)(2,1)S(1)}, u32[]{:S(2)}, u32[]{:S(2)}) async-start(bf16[16,112,512]{2,1,0:T(8,128)(2,1)} %bitcast.12), calls=%async_computation.1 | async-start | bytes 3670016 | tf_op jit(solution)/shard_map/all_to_all | solution.py:195
  66.4 9.0 %collective-permute-start.16 = (bf16[4,128,128]{2,1,0:T(8,128)(2,1)S(1)}, bf16[4,128,128]{2,1,0:T(8,128)(2,1)S(1)}, u32[]{:S(2)}, u32[]{:S(2)}) collective-permute-start(bf16[4,128,128]{2,1,0:T(8,128)(2,1)S(1)} %gate.5.refs_1_.refs_4_), channel_id=1, source_target_pairs={{0,6},{2,0},{4,2},{6,4},{1,7},{3,1},{5,3},{7,5},{8,14},{10,8},{12,... | collective-permute-start | bytes 393224 | tf_op jit(solution)/shard_map/ppermute | solution.py:23
  66.8 12.8 %collective-permute-start.14 = (bf16[4,128,128]{2,1,0:T(8,128)(2,1)S(1)}, bf16[4,128,128]{2,1,0:T(8,128)(2,1)S(1)}, u32[]{:S(2)}, u32[]{:S(2)}) collective-permute-start(bf16[4,128,128]{2,1,0:T(8,128)(2,1)S(1)} %gate.5.refs_1_.refs_4_), channel_id=1, source_target_pairs={{0,4},{2,6},{4,0},{6,2},{1,5},{3,7},{5,1},{7,3},{8,12},{10,14},{12... | collective-permute-start | bytes 393224 | tf_op jit(solution)/shard_map/ppermute | solution.py:23
  69.6 12.2 %collective-permute-start.12 = (bf16[4,128,128]{2,1,0:T(8,128)(2,1)S(1)}, bf16[4,128,128]{2,1,0:T(8,128)(2,1)S(1)}, u32[]{:S(2)}, u32[]{:S(2)}) collective-permute-start(bf16[4,128,128]{2,1,0:T(8,128)(2,1)S(1)} %gate.5.refs_1_.refs_4_), channel_id=1, source_target_pairs={{0,2},{2,4},{4,6},{6,0},{1,3},{3,5},{5,7},{7,1},{8,10},{10,12},{12... | collective-permute-start | bytes 393224 | tf_op jit(solution)/shard_map/ppermute | solution.py:23
  69.6 12.2 %collective-permute-start.18 = (bf16[112,512]{1,0:T(8,128)(2,1)S(1)}, bf16[112,512]{1,0:T(8,128)(2,1)S(1)}, u32[]{:S(2)}, u32[]{:S(2)}) collective-permute-start(bf16[112,512]{1,0:T(8,128)(2,1)S(1)} %convert_element_type.29), channel_id=1, source_target_pairs={{0,128},{128,0},{1,129},{129,1},{2,130},{130,2},{3,131},{131,3},{4... | collective-permute-start | bytes 344072 | tf_op jit(solution)/shard_map/ppermute | solution.py:23
  75.4 9.9 %collective-permute-start.11 = (bf16[4,128,128]{2,1,0:T(8,128)(2,1)S(1)}, bf16[4,128,128]{2,1,0:T(8,128)(2,1)S(1)}, u32[]{:S(2)}, u32[]{:S(2)}) collective-permute-start(bf16[4,128,128]{2,1,0:T(8,128)(2,1)S(1)} %gate.5.refs_1_.refs_4_), channel_id=1, source_target_pairs={{0,1},{1,0},{2,3},{3,2},{4,5},{5,4},{6,7},{7,6},{8,9},{9,8},{10,11... | collective-permute-start | bytes 393224 | tf_op jit(solution)/shard_map/ppermute | solution.py:23
  75.4 9.9 %collective-permute-start.17 = (bf16[4,128,128]{2,1,0:T(8,128)(2,1)S(1)}, bf16[4,128,128]{2,1,0:T(8,128)(2,1)S(1)}, u32[]{:S(2)}, u32[]{:S(2)}) collective-permute-start(bf16[4,128,128]{2,1,0:T(8,128)(2,1)S(1)} %collective-permute-done.16.refs_7_.refs_6_), channel_id=1, source_target_pairs={{0,1},{1,0},{2,3},{3,2},{4,5},{5,4},{6,7},{7,6},{8,9},{9,8},{10,11... | collective-permute-start | bytes 393224 | tf_op jit(solution)/shard_map/ppermute | solution.py:23
  79.5 5.8 %collective-permute-start.15 = (bf16[4,128,128]{2,1,0:T(8,128)(2,1)S(1)}, bf16[4,128,128]{2,1,0:T(8,128)(2,1)S(1)}, u32[]{:S(2)}, u32[]{:S(2)}) collective-permute-start(bf16[4,128,128]{2,1,0:T(8,128)(2,1)S(1)} %collective-permute-done.14.refs_5_.refs_4_), channel_id=1, source_target_pairs={{0,1},{1,0},{2,3},{3,2},{4,5},{5,4},{6,7},{7,6},{8,9},{9,8},{10,11... | collective-permute-start | bytes 393224 | tf_op jit(solution)/shard_map/ppermute | solution.py:23
  81.8 3.5 %collective-permute-start.13 = (bf16[4,128,128]{2,1,0:T(8,128)(2,1)S(1)}, bf16[4,128,128]{2,1,0:T(8,128)(2,1)S(1)}, u32[]{:S(2)}, u32[]{:S(2)}) collective-permute-start(bf16[4,128,128]{2,1,0:T(8,128)(2,1)S(1)} %collective-permute-done.12.refs_3_.refs_6_), channel_id=1, source_target_pairs={{0,1},{1,0},{2,3},{3,2},{4,5},{5,4},{6,7},{7,6},{8,9},{9,8},{10,11... | collective-permute-start | bytes 393224 | tf_op jit(solution)/shard_map/ppermute | solution.py:23
  81.9 11.7 %collective-permute-start.20 = (bf16[112,512]{1,0:T(8,128)(2,1)S(1)}, bf16[112,512]{1,0:T(8,128)(2,1)S(1)}, u32[]{:S(2)}, u32[]{:S(2)}) collective-permute-start(bf16[112,512]{1,0:T(8,128)(2,1)S(1)} %multiply_convert_fusion.1.refs_9_.refs_0_), channel_id=1, source_target_pairs={{0,16},{8,24},{16,0},{24,8},{1,17},{9,25},{17,1},{25,9},{2,18},{10... | collective-permute-start | bytes 344072 | tf_op jit(solution)/shard_map/ppermute | solution.py:23
  87.0 10.5 %collective-permute-start.19 = (bf16[112,512]{1,0:T(8,128)(2,1)S(1)}, bf16[112,512]{1,0:T(8,128)(2,1)S(1)}, u32[]{:S(2)}, u32[]{:S(2)}) collective-permute-start(bf16[112,512]{1,0:T(8,128)(2,1)S(1)} %convert_element_type.33), channel_id=1, source_target_pairs={{0,128},{128,0},{1,129},{129,1},{2,130},{130,2},{3,131},{131,3},{4... | collective-permute-start | bytes 344072 | tf_op jit(solution)/shard_map/ppermute | solution.py:23
  91.6 9.2 %collective-permute-start.25 = (bf16[112,512]{1,0:T(8,128)(2,1)S(1)}, bf16[112,512]{1,0:T(8,128)(2,1)S(1)}, u32[]{:S(2)}, u32[]{:S(2)}) collective-permute-start(bf16[112,512]{1,0:T(8,128)(2,1)S(1)} %multiply_convert_fusion.1.refs_9_.refs_0_), channel_id=1, source_target_pairs={{0,24},{8,0},{16,8},{24,16},{1,25},{9,1},{17,9},{25,17},{2,26},{10... | collective-permute-start | bytes 344072 | tf_op jit(solution)/shard_map/ppermute | solution.py:23
  92.8 7.9 %collective-permute-start.24 = (bf16[112,512]{1,0:T(8,128)(2,1)S(1)}, bf16[112,512]{1,0:T(8,128)(2,1)S(1)}, u32[]{:S(2)}, u32[]{:S(2)}) collective-permute-start(bf16[112,512]{1,0:T(8,128)(2,1)S(1)} %multiply_convert_fusion.1.refs_9_.refs_0_), channel_id=1, source_target_pairs={{0,8},{8,16},{16,24},{24,0},{1,9},{9,17},{17,25},{25,1},{2,10},{10... | collective-permute-start | bytes 344072 | tf_op jit(solution)/shard_map/ppermute | solution.py:23
  97.5 5.4 %collective-permute-start.23 = (bf16[112,512]{1,0:T(8,128)(2,1)S(1)}, bf16[112,512]{1,0:T(8,128)(2,1)S(1)}, u32[]{:S(2)}, u32[]{:S(2)}) collective-permute-start(bf16[112,512]{1,0:T(8,128)(2,1)S(1)} %multiply_convert_fusion.refs_0_), channel_id=1, source_target_pairs={{0,24},{8,0},{16,8},{24,16},{1,25},{9,1},{17,9},{25,17},{2,26},{10... | collective-permute-start | bytes 344072 | tf_op jit(solution)/shard_map/ppermute | solution.py:23
  98.8 7.8 %collective-permute-start.22 = (bf16[112,512]{1,0:T(8,128)(2,1)S(1)}, bf16[112,512]{1,0:T(8,128)(2,1)S(1)}, u32[]{:S(2)}, u32[]{:S(2)}) collective-permute-start(bf16[112,512]{1,0:T(8,128)(2,1)S(1)} %multiply_convert_fusion.refs_0_), channel_id=1, source_target_pairs={{0,8},{8,16},{16,24},{24,0},{1,9},{9,17},{17,25},{25,1},{2,10},{10... | collective-permute-start | bytes 344072 | tf_op jit(solution)/shard_map/ppermute | solution.py:23
  99.6 7.0 %collective-permute-start.21 = (bf16[112,512]{1,0:T(8,128)(2,1)S(1)}, bf16[112,512]{1,0:T(8,128)(2,1)S(1)}, u32[]{:S(2)}, u32[]{:S(2)}) collective-permute-start(bf16[112,512]{1,0:T(8,128)(2,1)S(1)} %multiply_convert_fusion.refs_0_), channel_id=1, source_target_pairs={{0,16},{8,24},{16,0},{24,8},{1,17},{9,25},{17,1},{25,9},{2,18},{10... | collective-permute-start | bytes 344072 | tf_op jit(solution)/shard_map/ppermute | solution.py:23
